TPU v7x, 32 devices: a whole 2x2x4 slice. The times are simulated.
32 devices in a mesh: dp: 4 (over y, x), cent: 8 (over z, core).
Axes of the slice: x: 2, y: 2, z: 4, core: 2. Of those that a mesh axis runs over, the one named last changes fastest.
Arguments:
- embeddings: bfloat16 [8192, 1024], P('dp')
- centroids: bfloat16 [4096, 1024], P('cent')
- col_start: float32 [4096], P('cent'), may hold values from -6 to 6
Outputs:
- new_centroids: bfloat16 [4096, 1024], P('cent')
- row_potential: float32 [8192], P('dp')
- col_potential: float32 [4096], P('cent')
All inputs are finite; a program needn't handle non-finite values.
Results may differ from a plain program's by a relative error of at most 0.0048.
Values may be sent and summed in bfloat16 or wider, within the bound.
No kernel may reach another device: no remote copies, remote signals or barrier semaphores. Data moves between devices by JAX's collectives and lax.ppermute only.
A program may use at most 64 MiB of HBM per device.

v0:
```python
import functools
import math

import jax
import jax.numpy as jnp
from jax import lax
from jax.experimental import pallas as pl
from jax.experimental.pallas import tpu as pltpu
from jax.sharding import PartitionSpec as P

ITERS = 3
CHUNKS = 2
LANES = 128
VMEM_BYTES = 24 * 2**20


def bits_of(axis):
    size = lax.axis_size(axis)
    assert size & (size - 1) == 0
    return list(range(size.bit_length() - 1))


def flipped(x, axis, mask):
    size = lax.axis_size(axis)
    return lax.ppermute(x, axis, [(k, k ^ mask) for k in range(size)])


def lse(first, second):
    top = jnp.maximum(first, second)
    return top + jnp.log(jnp.exp(first - top) + jnp.exp(second - top))


def lse_over_dp(x, aligned):
    bits = bits_of("dp")

    def partner(value, mask):
        return aligned(flipped(value, "dp", mask), mask)

    for masks in ([1 << bit for bit in bits[k:k + 2]] for k in range(0, len(bits), 2)):
        if len(masks) == 2:
            far = partner(x, masks[0] | masks[1])
            near = [partner(x, mask) for mask in reversed(masks)]
            x = lse(lax.optimization_barrier(lse(x, far)), lse(*near))
        else:
            x = lse(x, partner(x, masks[0]))
    return x


def lse_over_cent(x, odd):
    size = lax.axis_size("cent")
    near, middle, *rest = [1 << bit for bit in bits_of("cent")[1:]]

    def split(value, even_mask, odd_mask):
        return lax.ppermute(value, "cent", [(k, k ^ (odd_mask if k % 2 else even_mask)) for k in range(size)])

    x = lse(x, flipped(x, "cent", 1))
    second = split(x, near, middle)
    first = split(x, near, near | middle)
    x = jnp.where(odd, lse(second, first), lse(x, first))
    for mask in [1] + rest:
        x = lse(x, flipped(x, "cent", mask))
    return x


def column(values):
    lane = lax.broadcasted_iota(jnp.int32, (LANES, LANES), 1)
    diagonal = lane == lax.broadcasted_iota(jnp.int32, (LANES, LANES), 0)
    return jnp.sum(jnp.where(diagonal, values, 0.0), axis=1, keepdims=True)


def quarter_places(orders, quarter):
    ups = [lax.axis_index("dp") >> order[0] & 1 for order in orders]
    sent = [(2 * k + 1 - up) * quarter for k, up in enumerate(ups)]
    return sent + [(2 * k + up) * quarter for k, up in enumerate(ups)]


def place_kernel(chunk, orders, *refs):
    blocks, (out, sent) = refs[:4], refs[-2:]
    quarter, width = blocks[0].shape
    copies = []
    for k, start in enumerate(quarter_places(orders, quarter)):
        rows = pl.ds(pl.multiple_of(start, LANES), quarter)
        copies.append(pltpu.make_async_copy(blocks[k], out.at[rows, pl.ds(chunk * width, width)], sent.at[k]))
        copies[-1].start()
    for copy in copies:
        copy.wait()


def placed(chunk, orders, blocks, shape, so_far):
    vmem = pl.BlockSpec(memory_space=pltpu.VMEM)
    anywhere = pl.BlockSpec(memory_space=pl.ANY)
    return pl.pallas_call(
        functools.partial(place_kernel, chunk, orders),
        out_shape=jax.ShapeDtypeStruct(shape, blocks[0].dtype),
        in_specs=[vmem] * 4 + [anywhere] * len(so_far),
        out_specs=anywhere,
        scratch_shapes=[pltpu.SemaphoreType.DMA((4,))],
        input_output_aliases={4: 0} if so_far else {},
        compiler_params=pltpu.CompilerParams(vmem_limit_bytes=VMEM_BYTES),
    )(*blocks, *so_far)


def means_kernel(is_kept, plan, embeddings, mass, *rest):
    half = plan.shape[0] // 2
    quarter = half // 2
    sums = jnp.dot(plan[pl.ds(is_kept * half, half), :], embeddings[...], preferred_element_type=jnp.float32)
    if is_kept:
        weights, row, out, row_out = rest
        row_out[...] = row[...]
    else:
        out = None
    for block in range(half // LANES):
        factor = 1.0 / column(mass[pl.ds(is_kept * (half // LANES) + block, 1), :])
        if is_kept:
            factor = factor * column(weights[pl.ds(block, 1), :])
        rows = pl.ds(block * LANES % quarter, LANES)
        values = sums[block * LANES:(block + 1) * LANES] * factor
        half_index = block * LANES // quarter
        if is_kept:
            out[half_index, rows, :] = values
        else:
            width = rest[0].shape[1]
            for chunk in range(CHUNKS):
                target = rest[2 * chunk + half_index]
                target[rows, :] = values[:, chunk * width:(chunk + 1) * width].astype(target.dtype)


def means_of(is_kept, plan, embeddings, mass, *rest):
    count, rows_here = plan.shape
    depth = embeddings.shape[1]
    vmem = pl.BlockSpec(memory_space=pltpu.VMEM)
    if is_kept:
        out_shape = (
            jax.ShapeDtypeStruct((2, count // 4, depth), jnp.float32),
            jax.ShapeDtypeStruct((1, rows_here), jnp.float32),
        )
        out_specs = (vmem, pl.BlockSpec((1, rows_here), lambda: (0, 0)))
    else:
        out_shape = [jax.ShapeDtypeStruct((count // 4, depth // CHUNKS), jnp.bfloat16)] * (2 * CHUNKS)
        out_specs = [vmem] * (2 * CHUNKS)
    return pl.pallas_call(
        functools.partial(means_kernel, is_kept),
        out_shape=out_shape,
        in_specs=[vmem] * (3 + len(rest)),
        out_specs=out_specs,
        compiler_params=pltpu.CompilerParams(vmem_limit_bytes=VMEM_BYTES),
        cost_estimate=pl.CostEstimate(
            flops=count * rows_here * depth, bytes_accessed=2 * rows_here * depth, transcendentals=0
        ),
    )(plan, embeddings, mass.reshape(count // LANES, LANES), *rest)


def last_sum(plan, part, mass, row_now, embeddings, chosen, orders, aligned):
    quarter = part.shape[0] // 4
    first, second = orders[0][:2]
    partners = {bit: aligned(flipped(part, "dp", 1 << bit), 1 << bit) for bit in (first, second)}
    sent = means_of(0, plan, embeddings, mass)
    got = [flipped(sent[2 * chunk + k], "dp", 1 << order[0]) for chunk in range(CHUNKS) for k, order in enumerate(orders)]

    def kept_of(lower, upper):
        return jnp.concatenate([lower[2 * quarter:3 * quarter], upper[3 * quarter:]])

    pairs = lax.optimization_barrier([lse(partners[first], part), lse(partners[second], part)])
    pair = kept_of(*pairs)
    weights = jnp.exp(kept_of(part, part) - pair).reshape(2 * quarter // LANES, LANES)
    kept, row_out = means_of(1, plan, embeddings, mass, weights, row_now[None, :])
    weights = jnp.exp(kept_of(partners[first], partners[second]) - pair)

    corner = flipped(partners[first], "dp", 1 << second)

    def exchanged(mine, bit, own, other):
        mine = mine.astype(jnp.bfloat16)
        theirs = flipped(mine, "dp", 1 << bit).astype(jnp.float32)
        mine = mine.astype(jnp.float32)
        lower = chosen(bit, theirs, mine) * chosen(bit, other, own)
        upper = chosen(bit, mine, theirs) * chosen(bit, own, other)
        return (lower + upper).astype(jnp.bfloat16)

    def gathered(mine, order, own, other):
        if len(order) == 1:
            return exchanged(mine, order[0], own, other)
        bit = order[0]
        low, high = jnp.split(mine, 2, axis=0)
        got = flipped(chosen(bit, low, high).astype(jnp.bfloat16), "dp", 1 << bit).astype(jnp.float32)
        own, other = (chosen(bit, high, low) for low, high in (jnp.split(x, 2, axis=0) for x in (own, other)))
        ones = jnp.ones((own.shape[0], 1), jnp.float32)
        done = gathered(chosen(bit, high, low) * own + got * other, order[1:], ones, ones)
        theirs = flipped(done, "dp", 1 << bit)
        return jnp.concatenate([chosen(bit, theirs, done), chosen(bit, done, theirs)], axis=0)

    width = kept.shape[2] // CHUNKS
    shape = (part.shape[0], kept.shape[2])
    mines = []
    for chunk in range(CHUNKS):
        columns = slice(chunk * width, (chunk + 1) * width)
        if chunk > 0:
            mines, kept, weights = lax.optimization_barrier((mines, kept, weights))
        for k in range(2):
            rows = slice(k * quarter, (k + 1) * quarter)
            mines.append(kept[k, :, columns] + got[2 * chunk + k].astype(jnp.float32) * weights[rows, None])

    pairs, partners, corner = lax.optimization_barrier((pairs, partners, corner, mines))[:3]
    corner = aligned(corner, 1 << second)
    whole = lse(pairs[0], lse(corner, partners[second]))
    for bit in orders[0][2:]:
        whole = lse(aligned(flipped(whole, "dp", 1 << bit), 1 << bit), whole)
    pair_other = kept_of(lse(partners[second], corner), lse(partners[first], corner))
    weights_own = jnp.exp(kept_of(*pairs) - kept_of(whole, whole))
    weights_other = jnp.exp(pair_other - kept_of(whole, whole))

    outs = []
    firsts = []
    for chunk in range(CHUNKS):
        dones = []
        for k, order in enumerate(orders):
            rows = slice(k * quarter, (k + 1) * quarter)
            dones.append(gathered(mines[2 * chunk + k], order[1:], weights_own[rows, None], weights_other[rows, None]))
        if chunk < CHUNKS - 1:
            dones, weights_own, weights_other = lax.optimization_barrier((dones, weights_own, weights_other))
        firsts = firsts or dones
        blocks = [flipped(done, "dp", 1 << order[0]) for done, order in zip(dones, orders)] + dones
        outs = [placed(chunk, orders, blocks, shape, outs)]
    whole = lax.optimization_barrier((whole, firsts[0]))[0]
    quarters = jnp.split(whole, 4)
    halves = []
    for k, order in enumerate(orders):
        sent, kept = quarters[k], quarters[2 + k]
        halves += [chosen(order[0], sent, kept), chosen(order[0], kept, sent)]
    return outs[0], row_out.reshape(row_now.shape), jnp.concatenate(halves)


def on_device(embeddings, centroids, col_start):
    rows_here = embeddings.shape[0]
    cent_here = centroids.shape[0]
    n_total = rows_here * lax.axis_size("dp")
    k_total = cent_here * lax.axis_size("cent")

    bits = bits_of("dp")
    orders = (bits, [bits[1], bits[0]] + bits[2:])
    place = jnp.full((1,), lax.axis_index("dp"), jnp.int32)
    ups = [place >> bit & 1 for bit in bits]
    ups = [up == 1 for up in ups]
    odd = jnp.full((1,), lax.axis_index("cent"), jnp.int32) & 1 == 1
    ups, odd, embeddings, centroids = lax.optimization_barrier((ups, odd, embeddings, centroids))

    def chosen(bit, yes, no):
        return jnp.where(ups[bit].reshape((1,) * yes.ndim), yes, no)

    def sent_and_kept(value):
        quarters = jnp.split(value, 4)
        lows, highs = quarters[0::2], quarters[1::2]
        sent = [chosen(order[0], low, high) for order, low, high in zip(orders, lows, highs)]
        kept = [chosen(order[0], high, low) for order, low, high in zip(orders, lows, highs)]
        return jnp.concatenate(sent + kept)

    def aligned(value, mask):
        quarters = jnp.split(value, 4)
        for k, order in enumerate(orders):
            if mask >> order[0] & 1:
                quarters[k], quarters[2 + k] = quarters[2 + k], quarters[k]
        return jnp.concatenate(quarters)

    scores = lax.dot_general(
        sent_and_kept(centroids), embeddings, (((1,), (1,)), ((), ())), preferred_element_type=jnp.float32
    ) * (1.0 / math.sqrt(embeddings.shape[1]))
    col_now = sent_and_kept(col_start)
    for step_index in range(ITERS):
        shifted = scores + col_now[:, None]
        top = jnp.max(shifted, axis=0)
        part = top + jnp.log(jnp.sum(jnp.exp(shifted - top[None, :]), axis=0))
        row_now = -math.log(n_total) - lse_over_cent(part, odd)
        lifted = scores + row_now[None, :]
        top = jnp.max(lifted, axis=1)
        terms = jnp.exp(lifted - top[:, None])
        mass = jnp.sum(terms, axis=1)
        part = top + jnp.log(mass)
        if step_index < ITERS - 1:
            col_now = -math.log(k_total) - lse_over_dp(part, aligned)
    plan = terms.astype(jnp.bfloat16)
    new_centroids, row_out, whole = last_sum(plan, part, mass, row_now, embeddings, chosen, orders, aligned)
    return new_centroids, row_out, -math.log(k_total) - whole


def solution(mesh):
    specs = (P("dp", None), P("cent", None), P("cent"))
    return jax.shard_map(
        on_device,
        mesh=mesh,
        in_specs=specs,
        out_specs=(P("cent", None), P("dp"), P("cent")),
        check_vma=False,
    )
```

profile of v0, /device:TPU:0, one launch (start us, length us, event | category | flops | bytes accessed | tf_op | source)
XLA Modules:
  0.0 79.6 jit_solution(4181988244224410535)
XLA Ops:
  0.6 0.8 %broadcast_select_fusion.19 = (f32[128]{0:T(128)S(1)}, f32[128]{0:T(128)S(1)}, f32[128]{0:T(128)S(1)}, f32[128]{0:T(128)S(1)}) fusion(pred[]{:T(512)} %bitcast.4, f32[512]{0:T(512)} %param.5, pred[]{:T(512)} %bitcast.3), kind=kLoop, calls=%fused_computation.160 | loop fusion | flops 512 | bytes 4098 | tf_op jit(solution)/shard_map/jit(_where)/select_n | solution.py:247
  1.5 1.3 %broadcast_select_fusion.3 = (bf16[128,1024]{1,0:T(8,128)(2,1)S(1)}, bf16[128,1024]{1,0:T(8,128)(2,1)S(1)}, bf16[128,1024]{1,0:T(8,128)(2,1)S(1)}, bf16[128,1024]{1,0:T(8,128)(2,1)S(1)}) fusion(pred[]{:T(512)} %bitcast.4, bf16[512,1024]{1,0:T(8,128)(2,1)} %param.4, pred[]{:T(512)} %bitcast.3), kind=kLoop, calls=%fused_computation.53 | loop fusion | flops 524288 | bytes 2097154 | tf_op jit(solution)/shard_map/jit(_where)/select_n | solution.py:247
  2.8 4.6 %add_reduce_fusion.5 = (f32[2048]{0:T(1024)S(1)}, f32[512,2048]{1,0:T(8,128)S(1)}) fusion(f32[512]{0:T(512)S(1)} %pad_maximum_fusion, bf16[2048,1024]{1,0:T(8,128)(2,1)} %embeddings.1, bf16[128,1024]{1,0:T(8,128)(2,1)S(1)} %get-tuple-element.67, bf16[128,1024]{1,0:T(8,128)(2,1)S(1)} %get-tuple-element.68, bf16[128,1024]{1,0:T(8,128)(2,1)S(1)} %get-tuple-element.66, ...), kind=kOutput, calls=%fused_computation.11 | convolution fusion | flops 2154821632 | bytes 9447424 | tf_op jit(solution)/shard_map/dot_general | solution.py:263
  7.3 0.8 exponential_reduce_fusion.4
  8.7 0.8 %collective-permute-done = f32[2048]{0:T(1024)S(1)} collective-permute-done((f32[2048]{0:T(1024)S(1)}, f32[2048]{0:T(1024)S(1)}, u32[]{:S(2)}, u32[]{:S(2)}) %collective-permute-start) | collective-permute-done | bytes 8224 | tf_op jit(solution)/shard_map/ppermute | solution.py:25
  9.5 3.0 %collective-permute-start.2 = (f32[2048]{0:T(1024)S(1)}, f32[2048]{0:T(1024)S(1)}, u32[]{:S(2)}, u32[]{:S(2)}) collective-permute-start(f32[2048]{0:T(1024)S(1)} %log_add_fusion.4), channel_id=1, source_target_pairs={{0,2},{1,7},{2,0},{3,5},{4,6},{5,3},{6,4},{7,1},{8,10},{9,15},{10,... | collective-permute-start | bytes 24584 | tf_op jit(solution)/shard_map/ppermute | solution.py:54
  12.6 1.6 %collective-permute-done.2 = f32[2048]{0:T(1024)S(1)} collective-permute-done((f32[2048]{0:T(1024)S(1)}, f32[2048]{0:T(1024)S(1)}, u32[]{:S(2)}, u32[]{:S(2)}) %collective-permute-start.2) | collective-permute-done | bytes 8224 | tf_op jit(solution)/shard_map/ppermute | solution.py:54
  14.1 2.0 %collective-permute-done.1 = f32[2048]{0:T(1024)S(1)} collective-permute-done((f32[2048]{0:T(1024)S(1)}, f32[2048]{0:T(1024)S(1)}, u32[]{:S(2)}, u32[]{:S(2)}) %collective-permute-start.1) | collective-permute-done | bytes 8224 | tf_op jit(solution)/shard_map/ppermute | solution.py:54
  16.2 1.7 %collective-permute-start.3 = (f32[2048]{0:T(1024)S(1)}, f32[2048]{0:T(1024)S(1)}, u32[]{:S(2)}, u32[]{:S(2)}) collective-permute-start(f32[2048]{0:T(1024)S(1)} %add_select_fusion.2), channel_id=1, source_target_pairs={{0,1},{1,0},{2,3},{3,2},{4,5},{5,4},{6,7},{7,6},{8,9},{9,8},{10,11... | collective-permute-start | bytes 24584 | tf_op jit(solution)/shard_map/ppermute | solution.py:25
  17.9 0.8 %collective-permute-done.3 = f32[2048]{0:T(1024)S(1)} collective-permute-done((f32[2048]{0:T(1024)S(1)}, f32[2048]{0:T(1024)S(1)}, u32[]{:S(2)}, u32[]{:S(2)}) %collective-permute-start.3) | collective-permute-done | bytes 8224 | tf_op jit(solution)/shard_map/ppermute | solution.py:25
  19.1 0.8 %exponential_reduce_fusion.3 = f32[512]{0:T(512)S(1)} fusion(f32[512,2048]{1,0:T(8,128)S(1)} %get-tuple-element.129, f32[512]{0:T(512)S(1)} %add_reduce_fusion.4, f32[2048]{0:T(1024)S(1)} %add_subtract_fusion.2), kind=kLoop, calls=%fused_computation.4 | loop fusion | flops 3145216 | bytes 4206592 | tf_op jit(solution)/shard_map/reduce_sum | solution.py:275
  19.9 2.5 %collective-permute-start.4 = (f32[512]{0:T(512)S(1)}, f32[512]{0:T(512)S(1)}, u32[]{:S(2)}, u32[]{:S(2)}) collective-permute-start(f32[512]{0:T(512)S(1)} %log_add_fusion.15), channel_id=1, source_target_pairs={{0,24},{8,16},{16,8},{24,0},{1,25},{9,17},{17,9},{25,1},{2,26},{10... | collective-permute-start | bytes 6152 | tf_op jit(solution)/shard_map/ppermute | solution.py:25
  23.5 1.0 %collective-permute-done.4 = f32[512]{0:T(512)S(1)} collective-permute-done((f32[512]{0:T(512)S(1)}, f32[512]{0:T(512)S(1)}, u32[]{:S(2)}, u32[]{:S(2)}) %collective-permute-start.4) | collective-permute-done | bytes 2080 | tf_op jit(solution)/shard_map/ppermute | solution.py:25
  24.5 1.5 %collective-permute-done.5 = f32[512]{0:T(512)S(1)} collective-permute-done((f32[512]{0:T(512)S(1)}, f32[512]{0:T(512)S(1)}, u32[]{:S(2)}, u32[]{:S(2)}) %collective-permute-start.5) | collective-permute-done | bytes 2080 | tf_op jit(solution)/shard_map/ppermute | solution.py:25
  27.0 0.8 exponential_reduce_fusion.2
  27.8 1.2 %collective-permute-done.7 = f32[2048]{0:T(1024)S(1)} collective-permute-done((f32[2048]{0:T(1024)S(1)}, f32[2048]{0:T(1024)S(1)}, u32[]{:S(2)}, u32[]{:S(2)}) %collective-permute-start.7) | collective-permute-done | bytes 8224 | tf_op jit(solution)/shard_map/ppermute | solution.py:25
  29.1 2.0 %collective-permute-start.8 = (f32[2048]{0:T(1024)S(1)}, f32[2048]{0:T(1024)S(1)}, u32[]{:S(2)}, u32[]{:S(2)}) collective-permute-start(f32[2048]{0:T(1024)S(1)} %log_add_fusion.2), channel_id=1, source_target_pairs={{0,2},{1,5},{2,0},{3,7},{4,6},{5,1},{6,4},{7,3},{8,10},{9,13},{10,... | collective-permute-start | bytes 24584 | tf_op jit(solution)/shard_map/ppermute | solution.py:54
  31.1 1.6 %collective-permute-done.9 = f32[2048]{0:T(1024)S(1)} collective-permute-done((f32[2048]{0:T(1024)S(1)}, f32[2048]{0:T(1024)S(1)}, u32[]{:S(2)}, u32[]{:S(2)}) %collective-permute-start.9) | collective-permute-done | bytes 8224 | tf_op jit(solution)/shard_map/ppermute | solution.py:54
  32.8 1.0 %collective-permute-start.10 = (f32[2048]{0:T(1024)S(1)}, f32[2048]{0:T(1024)S(1)}, u32[]{:S(2)}, u32[]{:S(2)}) collective-permute-start(f32[2048]{0:T(1024)S(1)} %add_select_fusion.1), channel_id=1, source_target_pairs={{0,1},{1,0},{2,3},{3,2},{4,5},{5,4},{6,7},{7,6},{8,9},{9,8},{10,11... | collective-permute-start | bytes 24584 | tf_op jit(solution)/shard_map/ppermute | solution.py:25
  33.8 0.8 %collective-permute-done.10 = f32[2048]{0:T(1024)S(1)} collective-permute-done((f32[2048]{0:T(1024)S(1)}, f32[2048]{0:T(1024)S(1)}, u32[]{:S(2)}, u32[]{:S(2)}) %collective-permute-start.10) | collective-permute-done | bytes 8224 | tf_op jit(solution)/shard_map/ppermute | solution.py:25
  35.0 0.8 %exponential_reduce_fusion.1 = f32[512]{0:T(512)S(1)} fusion(f32[512,2048]{1,0:T(8,128)S(1)} %get-tuple-element.129, f32[512]{0:T(512)S(1)} %add_reduce_fusion.2, f32[2048]{0:T(1024)S(1)} %add_subtract_fusion.1), kind=kLoop, calls=%fused_computation.2 | loop fusion | flops 3145216 | bytes 4206592 | tf_op jit(solution)/shard_map/reduce_sum | solution.py:275
  35.9 1.6 %collective-permute-start.11 = (f32[512]{0:T(512)S(1)}, f32[512]{0:T(512)S(1)}, u32[]{:S(2)}, u32[]{:S(2)}) collective-permute-start(f32[512]{0:T(512)S(1)} %log_add_fusion.13), channel_id=1, source_target_pairs={{0,24},{8,16},{16,8},{24,0},{1,25},{9,17},{17,9},{25,1},{2,26},{10... | collective-permute-start | bytes 6152 | tf_op jit(solution)/shard_map/ppermute | solution.py:25
  37.9 1.5 %collective-permute-start.13 = (f32[512]{0:T(512)S(1)}, f32[512]{0:T(512)S(1)}, u32[]{:S(2)}, u32[]{:S(2)}) collective-permute-start(f32[512]{0:T(512)S(1)} %log_add_fusion.13), channel_id=1, source_target_pairs={{0,8},{8,0},{16,24},{24,16},{1,9},{9,1},{17,25},{25,17},{2,10},{10... | collective-permute-start | bytes 6152 | tf_op jit(solution)/shard_map/ppermute | solution.py:25
  39.4 1.0 %collective-permute-done.11 = f32[512]{0:T(512)S(1)} collective-permute-done((f32[512]{0:T(512)S(1)}, f32[512]{0:T(512)S(1)}, u32[]{:S(2)}, u32[]{:S(2)}) %collective-permute-start.11) | collective-permute-done | bytes 2080 | tf_op jit(solution)/shard_map/ppermute | solution.py:25
  41.9 0.8 exponential_reduce_fusion
  42.8 1.2 %collective-permute-done.14 = f32[2048]{0:T(1024)S(1)} collective-permute-done((f32[2048]{0:T(1024)S(1)}, f32[2048]{0:T(1024)S(1)}, u32[]{:S(2)}, u32[]{:S(2)}) %collective-permute-start.14) | collective-permute-done | bytes 8224 | tf_op jit(solution)/shard_map/ppermute | solution.py:25
  44.0 1.4 %collective-permute-start.16 = (f32[2048]{0:T(1024)S(1)}, f32[2048]{0:T(1024)S(1)}, u32[]{:S(2)}, u32[]{:S(2)}) collective-permute-start(f32[2048]{0:T(1024)S(1)} %log_add_fusion), channel_id=1, source_target_pairs={{0,2},{1,7},{2,0},{3,5},{4,6},{5,3},{6,4},{7,1},{8,10},{9,15},{10,... | collective-permute-start | bytes 24584 | tf_op jit(solution)/shard_map/ppermute | solution.py:54
  46.1 1.6 %collective-permute-done.16 = f32[2048]{0:T(1024)S(1)} collective-permute-done((f32[2048]{0:T(1024)S(1)}, f32[2048]{0:T(1024)S(1)}, u32[]{:S(2)}, u32[]{:S(2)}) %collective-permute-start.16) | collective-permute-done | bytes 8224 | tf_op jit(solution)/shard_map/ppermute | solution.py:54
  47.7 1.4 %collective-permute-done.15 = f32[2048]{0:T(1024)S(1)} collective-permute-done((f32[2048]{0:T(1024)S(1)}, f32[2048]{0:T(1024)S(1)}, u32[]{:S(2)}, u32[]{:S(2)}) %collective-permute-start.15) | collective-permute-done | bytes 8224 | tf_op jit(solution)/shard_map/ppermute | solution.py:54
  49.1 0.8 collective-permute-start.17
  49.9 0.8 %collective-permute-done.17 = f32[2048]{0:T(1024)S(1)} collective-permute-done((f32[2048]{0:T(1024)S(1)}, f32[2048]{0:T(1024)S(1)}, u32[]{:S(2)}, u32[]{:S(2)}) %collective-permute-start.17) | collective-permute-done | bytes 8224 | tf_op jit(solution)/shard_map/ppermute | solution.py:25
  51.1 0.9 %fusion = (f32[512]{0:T(512)S(1)}, bf16[512,2048]{1,0:T(8,128)(2,1)S(1)}) fusion(f32[512,2048]{1,0:T(8,128)S(1)} %get-tuple-element.129, f32[512]{0:T(512)S(1)} %add_reduce_fusion, f32[2048]{0:T(1024)S(1)} %add_subtract_fusion), kind=kLoop, calls=%fused_computation.12 | loop fusion | flops 4193792 | bytes 6303744 | tf_op jit(solution)/shard_map/reduce_sum | solution.py:275
  52.0 1.6 %collective-permute-start.19 = (f32[512]{0:T(512)S(1)}, f32[512]{0:T(512)S(1)}, u32[]{:S(2)}, u32[]{:S(2)}) collective-permute-start(f32[512]{0:T(512)S(1)} %log_add_fusion.11), channel_id=1, source_target_pairs={{0,16},{8,24},{16,0},{24,8},{1,17},{9,25},{17,1},{25,9},{2,18},{10... | collective-permute-start | bytes 6152 | tf_op jit(solution)/shard_map/ppermute | solution.py:25
  53.6 1.5 %collective-permute-start.18 = (f32[512]{0:T(512)S(1)}, f32[512]{0:T(512)S(1)}, u32[]{:S(2)}, u32[]{:S(2)}) collective-permute-start(f32[512]{0:T(512)S(1)} %log_add_fusion.11), channel_id=1, source_target_pairs={{0,8},{8,0},{16,24},{24,16},{1,9},{9,1},{17,25},{25,17},{2,10},{10... | collective-permute-start | bytes 6152 | tf_op jit(solution)/shard_map/ppermute | solution.py:25
  55.1 1.2 %shard_map.59 = (bf16[128,512]{1,0:T(8,128)(2,1)S(1)}, bf16[128,512]{1,0:T(8,128)(2,1)S(1)}, bf16[128,512]{1,0:T(8,128)(2,1)S(1)}, bf16[128,512]{1,0:T(8,128)(2,1)S(1)}) custom-call(bf16[512,2048]{1,0:T(8,128)(2,1)S(1)} %get-tuple-element.60.plan, bf16[2048,1024]{1,0:T(8,128)(2,1)S(1)} %copy-done, f32[4,128]{1,0:T(4,128)S(1)} %bitcast.26), custom_call_target="tpu_custom_call" | custom-call | flops 1073741824 | bytes 4194304 | tf_op jit(solution)/shard_map/pallas_call | solution.py:141
  57.6 1.3 %collective-permute-start.22 = (bf16[128,512]{1,0:T(8,128)(2,1)S(1)}, bf16[128,512]{1,0:T(8,128)(2,1)S(1)}, u32[]{:S(2)}, u32[]{:S(2)}) collective-permute-start(bf16[128,512]{1,0:T(8,128)(2,1)S(1)} %get-tuple-element.41), channel_id=1, source_target_pairs={{0,8},{8,0},{16,24},{24,16},{1,9},{9,1},{17,25},{25,17},{2,10},{10... | collective-permute-start | bytes 393224 | tf_op jit(solution)/shard_map/ppermute | solution.py:25
  59.0 1.5 %collective-permute-start.26 = (bf16[128,512]{1,0:T(8,128)(2,1)S(1)}, bf16[128,512]{1,0:T(8,128)(2,1)S(1)}, u32[]{:S(2)}, u32[]{:S(2)}) collective-permute-start(bf16[128,512]{1,0:T(8,128)(2,1)S(1)} %get-tuple-element.45), channel_id=1, source_target_pairs={{0,16},{8,24},{16,0},{24,8},{1,17},{9,25},{17,1},{25,9},{2,18},{10... | collective-permute-start | bytes 393224 | tf_op jit(solution)/shard_map/ppermute | solution.py:25
  61.2 1.6 %shard_map.58 = (f32[2,128,1024]{2,1,0:T(8,128)S(1)}, f32[1,2048]{1,0:T(1,128)}) custom-call(bf16[512,2048]{1,0:T(8,128)(2,1)S(1)} %get-tuple-element.60.plan, bf16[2048,1024]{1,0:T(8,128)(2,1)S(1)} %copy-done, f32[4,128]{1,0:T(4,128)S(1)} %bitcast.27, f32[2,128]{1,0:T(2,128)S(1)} %fusion.51.rest_0_, f32[1,2048]{1,0:T(1,128)S(1)} %bitcast.25), custom_call_target="tpu_custom_call" | custom-call | flops 1073741824 | bytes 4194304 | tf_op jit(solution)/shard_map/pallas_call | solution.py:141
  63.5 1.1 %collective-permute-start.24 = (bf16[128,512]{1,0:T(8,128)(2,1)S(1)}, bf16[128,512]{1,0:T(8,128)(2,1)S(1)}, u32[]{:S(2)}, u32[]{:S(2)}) collective-permute-start(bf16[128,512]{1,0:T(8,128)(2,1)S(1)} %get-tuple-element.43), channel_id=1, source_target_pairs={{0,16},{8,24},{16,0},{24,8},{1,17},{9,25},{17,1},{25,9},{2,18},{10... | collective-permute-start | bytes 393224 | tf_op jit(solution)/shard_map/ppermute | solution.py:25
  64.5 1.0 %collective-permute-start.27 = (bf16[128,512]{1,0:T(8,128)(2,1)S(1)}, bf16[128,512]{1,0:T(8,128)(2,1)S(1)}, u32[]{:S(2)}, u32[]{:S(2)}) collective-permute-start(bf16[128,512]{1,0:T(8,128)(2,1)S(1)} %get-tuple-element.44), channel_id=1, source_target_pairs={{0,8},{8,0},{16,24},{24,16},{1,9},{9,1},{17,25},{25,17},{2,10},{10... | collective-permute-start | bytes 393224 | tf_op jit(solution)/shard_map/ppermute | solution.py:25
  65.6 1.6 %collective-permute-start.29 = (bf16[128,512]{1,0:T(8,128)(2,1)S(1)}, bf16[128,512]{1,0:T(8,128)(2,1)S(1)}, u32[]{:S(2)}, u32[]{:S(2)}) collective-permute-start(bf16[128,512]{1,0:T(8,128)(2,1)S(1)} %get-tuple-element.61), channel_id=1, source_target_pairs={{0,8},{8,0},{16,24},{24,16},{1,9},{9,1},{17,25},{25,17},{2,10},{10... | collective-permute-start | bytes 393224 | tf_op jit(solution)/shard_map/ppermute | solution.py:25
  67.9 1.8 %collective-permute-done.24 = bf16[128,512]{1,0:T(8,128)(2,1)S(1)} collective-permute-done((bf16[128,512]{1,0:T(8,128)(2,1)S(1)}, bf16[128,512]{1,0:T(8,128)(2,1)S(1)}, u32[]{:S(2)}, u32[]{:S(2)}) %collective-permute-start.24) | collective-permute-done | bytes 131104 | tf_op jit(solution)/shard_map/ppermute | solution.py:25
  70.0 1.1 %collective-permute-start.31 = (bf16[128,512]{1,0:T(8,128)(2,1)S(1)}, bf16[128,512]{1,0:T(8,128)(2,1)S(1)}, u32[]{:S(2)}, u32[]{:S(2)}) collective-permute-start(bf16[128,512]{1,0:T(8,128)(2,1)S(1)} %fusion.15.refs_2_), channel_id=1, source_target_pairs={{0,8},{8,0},{16,24},{24,16},{1,9},{9,1},{17,25},{25,17},{2,10},{10... | collective-permute-start | bytes 393224 | tf_op jit(solution)/shard_map/ppermute | solution.py:25
  71.0 2.2 %collective-permute-start.32 = (bf16[128,512]{1,0:T(8,128)(2,1)S(1)}, bf16[128,512]{1,0:T(8,128)(2,1)S(1)}, u32[]{:S(2)}, u32[]{:S(2)}) collective-permute-start(bf16[128,512]{1,0:T(8,128)(2,1)S(1)} %fusion.19.refs_3_), channel_id=1, source_target_pairs={{0,16},{8,24},{16,0},{24,8},{1,17},{9,25},{17,1},{25,9},{2,18},{10... | collective-permute-start | bytes 393224 | tf_op jit(solution)/shard_map/ppermute | solution.py:25
  73.7 1.4 %collective-permute-start.28 = (bf16[128,512]{1,0:T(8,128)(2,1)S(1)}, bf16[128,512]{1,0:T(8,128)(2,1)S(1)}, u32[]{:S(2)}, u32[]{:S(2)}) collective-permute-start(bf16[128,512]{1,0:T(8,128)(2,1)S(1)} %fusion.11.refs_2_), channel_id=1, source_target_pairs={{0,8},{8,0},{16,24},{24,16},{1,9},{9,1},{17,25},{25,17},{2,10},{10... | collective-permute-start | bytes 393224 | tf_op jit(solution)/shard_map/ppermute | solution.py:25
  76.2 0.8 %shard_map.60.refs_4_ = bf16[512,1024]{1,0:T(8,128)(2,1)} custom-call(bf16[128,512]{1,0:T(8,128)(2,1)S(1)} %collective-permute-done.31.refs_0_, bf16[128,512]{1,0:T(8,128)(2,1)S(1)} %collective-permute-done.32.refs_1_, bf16[128,512]{1,0:T(8,128)(2,1)S(1)} %fusion.15.refs_2_, bf16[128,512]{1,0:T(8,128)(2,1)S(1)} %fusion.19.refs_3_), custom_call_target="tpu_custom_call" | custom-call | tf_op jit(solution)/shard_map/pallas_call | solution.py:92
  77.0 1.4 %collective-permute-done.30.refs_1_ = bf16[128,512]{1,0:T(8,128)(2,1)S(1)} collective-permute-done((bf16[128,512]{1,0:T(8,128)(2,1)S(1)}, bf16[128,512]{1,0:T(8,128)(2,1)S(1)}, u32[]{:S(2)}, u32[]{:S(2)}) %collective-permute-start.30) | collective-permute-done | bytes 131104 | tf_op jit(solution)/shard_map/ppermute | solution.py:25
  78.8 0.8 %shard_map.61 = bf16[512,1024]{1,0:T(8,128)(2,1)} custom-call(bf16[128,512]{1,0:T(8,128)(2,1)S(1)} %collective-permute-done.28.refs_0_, bf16[128,512]{1,0:T(8,128)(2,1)S(1)} %collective-permute-done.30.refs_1_, bf16[128,512]{1,0:T(8,128)(2,1)S(1)} %fusion.11.refs_2_, bf16[128,512]{1,0:T(8,128)(2,1)S(1)} %fusion.23.refs_3_, ...), custom_call_target="tpu_custom_call", output_to_operand_aliasing={{}: (4, {})} | custom-call | tf_op jit(solution)/shard_map/pallas_call | solution.py:92
  (91 shorter events, 12.3 us)
Async XLA Ops:
  8.1 1.3 %collective-permute-start = (f32[2048]{0:T(1024)S(1)}, f32[2048]{0:T(1024)S(1)}, u32[]{:S(2)}, u32[]{:S(2)}) collective-permute-start(f32[2048]{0:T(1024)S(1)} %log_add_fusion.5), channel_id=1, source_target_pairs={{0,1},{1,0},{2,3},{3,2},{4,5},{5,4},{6,7},{7,6},{8,9},{9,8},{10,11... | collective-permute-start | bytes 24584 | tf_op jit(solution)/shard_map/ppermute | solution.py:25
  9.5 4.6 %collective-permute-start.2 = (f32[2048]{0:T(1024)S(1)}, f32[2048]{0:T(1024)S(1)}, u32[]{:S(2)}, u32[]{:S(2)}) collective-permute-start(f32[2048]{0:T(1024)S(1)} %log_add_fusion.4), channel_id=1, source_target_pairs={{0,2},{1,7},{2,0},{3,5},{4,6},{5,3},{6,4},{7,1},{8,10},{9,15},{10,... | collective-permute-start | bytes 24584 | tf_op jit(solution)/shard_map/ppermute | solution.py:54
  12.5 3.7 %collective-permute-start.1 = (f32[2048]{0:T(1024)S(1)}, f32[2048]{0:T(1024)S(1)}, u32[]{:S(2)}, u32[]{:S(2)}) collective-permute-start(f32[2048]{0:T(1024)S(1)} %log_add_fusion.4), channel_id=1, source_target_pairs={{0,2},{1,5},{2,0},{3,7},{4,6},{5,1},{6,4},{7,3},{8,10},{9,13},{10,... | collective-permute-start | bytes 24584 | tf_op jit(solution)/shard_map/ppermute | solution.py:54
  16.2 2.6 %collective-permute-start.3 = (f32[2048]{0:T(1024)S(1)}, f32[2048]{0:T(1024)S(1)}, u32[]{:S(2)}, u32[]{:S(2)}) collective-permute-start(f32[2048]{0:T(1024)S(1)} %add_select_fusion.2), channel_id=1, source_target_pairs={{0,1},{1,0},{2,3},{3,2},{4,5},{5,4},{6,7},{7,6},{8,9},{9,8},{10,11... | collective-permute-start | bytes 24584 | tf_op jit(solution)/shard_map/ppermute | solution.py:25
  19.9 4.5 %collective-permute-start.4 = (f32[512]{0:T(512)S(1)}, f32[512]{0:T(512)S(1)}, u32[]{:S(2)}, u32[]{:S(2)}) collective-permute-start(f32[512]{0:T(512)S(1)} %log_add_fusion.15), channel_id=1, source_target_pairs={{0,24},{8,16},{16,8},{24,0},{1,25},{9,17},{17,9},{25,1},{2,26},{10... | collective-permute-start | bytes 6152 | tf_op jit(solution)/shard_map/ppermute | solution.py:25
  22.5 3.6 %collective-permute-start.5 = (f32[512]{0:T(512)S(1)}, f32[512]{0:T(512)S(1)}, u32[]{:S(2)}, u32[]{:S(2)}) collective-permute-start(f32[512]{0:T(512)S(1)} %log_add_fusion.15), channel_id=1, source_target_pairs={{0,16},{8,24},{16,0},{24,8},{1,17},{9,25},{17,1},{25,9},{2,18},{10... | collective-permute-start | bytes 6152 | tf_op jit(solution)/shard_map/ppermute | solution.py:25
  23.0 3.6 %collective-permute-start.6 = (f32[512]{0:T(512)S(1)}, f32[512]{0:T(512)S(1)}, u32[]{:S(2)}, u32[]{:S(2)}) collective-permute-start(f32[512]{0:T(512)S(1)} %log_add_fusion.15), channel_id=1, source_target_pairs={{0,8},{8,0},{16,24},{24,16},{1,9},{9,1},{17,25},{25,17},{2,10},{10... | collective-permute-start | bytes 6152 | tf_op jit(solution)/shard_map/ppermute | solution.py:25
  27.8 1.2 %collective-permute-start.7 = (f32[2048]{0:T(1024)S(1)}, f32[2048]{0:T(1024)S(1)}, u32[]{:S(2)}, u32[]{:S(2)}) collective-permute-start(f32[2048]{0:T(1024)S(1)} %log_add_fusion.3), channel_id=1, source_target_pairs={{0,1},{1,0},{2,3},{3,2},{4,5},{5,4},{6,7},{7,6},{8,9},{9,8},{10,11... | collective-permute-start | bytes 24584 | tf_op jit(solution)/shard_map/ppermute | solution.py:25
  29.0 3.7 %collective-permute-start.9 = (f32[2048]{0:T(1024)S(1)}, f32[2048]{0:T(1024)S(1)}, u32[]{:S(2)}, u32[]{:S(2)}) collective-permute-start(f32[2048]{0:T(1024)S(1)} %log_add_fusion.2), channel_id=1, source_target_pairs={{0,2},{1,7},{2,0},{3,5},{4,6},{5,3},{6,4},{7,1},{8,10},{9,15},{10,... | collective-permute-start | bytes 24584 | tf_op jit(solution)/shard_map/ppermute | solution.py:54
  29.1 3.7 %collective-permute-start.8 = (f32[2048]{0:T(1024)S(1)}, f32[2048]{0:T(1024)S(1)}, u32[]{:S(2)}, u32[]{:S(2)}) collective-permute-start(f32[2048]{0:T(1024)S(1)} %log_add_fusion.2), channel_id=1, source_target_pairs={{0,2},{1,5},{2,0},{3,7},{4,6},{5,1},{6,4},{7,3},{8,10},{9,13},{10,... | collective-permute-start | bytes 24584 | tf_op jit(solution)/shard_map/ppermute | solution.py:54
  32.8 1.8 %collective-permute-start.10 = (f32[2048]{0:T(1024)S(1)}, f32[2048]{0:T(1024)S(1)}, u32[]{:S(2)}, u32[]{:S(2)}) collective-permute-start(f32[2048]{0:T(1024)S(1)} %add_select_fusion.1), channel_id=1, source_target_pairs={{0,1},{1,0},{2,3},{3,2},{4,5},{5,4},{6,7},{7,6},{8,9},{9,8},{10,11... | collective-permute-start | bytes 24584 | tf_op jit(solution)/shard_map/ppermute | solution.py:25
  35.9 4.5 %collective-permute-start.11 = (f32[512]{0:T(512)S(1)}, f32[512]{0:T(512)S(1)}, u32[]{:S(2)}, u32[]{:S(2)}) collective-permute-start(f32[512]{0:T(512)S(1)} %log_add_fusion.13), channel_id=1, source_target_pairs={{0,24},{8,16},{16,8},{24,0},{1,25},{9,17},{17,9},{25,1},{2,26},{10... | collective-permute-start | bytes 6152 | tf_op jit(solution)/shard_map/ppermute | solution.py:25
  37.4 3.6 %collective-permute-start.12 = (f32[512]{0:T(512)S(1)}, f32[512]{0:T(512)S(1)}, u32[]{:S(2)}, u32[]{:S(2)}) collective-permute-start(f32[512]{0:T(512)S(1)} %log_add_fusion.13), channel_id=1, source_target_pairs={{0,16},{8,24},{16,0},{24,8},{1,17},{9,25},{17,1},{25,9},{2,18},{10... | collective-permute-start | bytes 6152 | tf_op jit(solution)/shard_map/ppermute | solution.py:25
  37.9 3.6 %collective-permute-start.13 = (f32[512]{0:T(512)S(1)}, f32[512]{0:T(512)S(1)}, u32[]{:S(2)}, u32[]{:S(2)}) collective-permute-start(f32[512]{0:T(512)S(1)} %log_add_fusion.13), channel_id=1, source_target_pairs={{0,8},{8,0},{16,24},{24,16},{1,9},{9,1},{17,25},{25,17},{2,10},{10... | collective-permute-start | bytes 6152 | tf_op jit(solution)/shard_map/ppermute | solution.py:25
  42.7 1.2 %collective-permute-start.14 = (f32[2048]{0:T(1024)S(1)}, f32[2048]{0:T(1024)S(1)}, u32[]{:S(2)}, u32[]{:S(2)}) collective-permute-start(f32[2048]{0:T(1024)S(1)} %log_add_fusion.1), channel_id=1, source_target_pairs={{0,1},{1,0},{2,3},{3,2},{4,5},{5,4},{6,7},{7,6},{8,9},{9,8},{10,11... | collective-permute-start | bytes 24584 | tf_op jit(solution)/shard_map/ppermute | solution.py:25
  44.0 3.7 %collective-permute-start.16 = (f32[2048]{0:T(1024)S(1)}, f32[2048]{0:T(1024)S(1)}, u32[]{:S(2)}, u32[]{:S(2)}) collective-permute-start(f32[2048]{0:T(1024)S(1)} %log_add_fusion), channel_id=1, source_target_pairs={{0,2},{1,7},{2,0},{3,5},{4,6},{5,3},{6,4},{7,1},{8,10},{9,15},{10,... | collective-permute-start | bytes 24584 | tf_op jit(solution)/shard_map/ppermute | solution.py:54
  45.4 3.7 %collective-permute-start.15 = (f32[2048]{0:T(1024)S(1)}, f32[2048]{0:T(1024)S(1)}, u32[]{:S(2)}, u32[]{:S(2)}) collective-permute-start(f32[2048]{0:T(1024)S(1)} %log_add_fusion), channel_id=1, source_target_pairs={{0,2},{1,5},{2,0},{3,7},{4,6},{5,1},{6,4},{7,3},{8,10},{9,13},{10,... | collective-permute-start | bytes 24584 | tf_op jit(solution)/shard_map/ppermute | solution.py:54
  49.1 1.6 %collective-permute-start.17 = (f32[2048]{0:T(1024)S(1)}, f32[2048]{0:T(1024)S(1)}, u32[]{:S(2)}, u32[]{:S(2)}) collective-permute-start(f32[2048]{0:T(1024)S(1)} %add_select_fusion), channel_id=1, source_target_pairs={{0,1},{1,0},{2,3},{3,2},{4,5},{5,4},{6,7},{7,6},{8,9},{9,8},{10,11... | collective-permute-start | bytes 24584 | tf_op jit(solution)/shard_map/ppermute | solution.py:25
  51.1 4.0 %copy-start = (bf16[2048,1024]{1,0:T(8,128)(2,1)S(1)}, bf16[2048,1024]{1,0:T(8,128)(2,1)}, u32[]{:S(2)}) copy-start(bf16[2048,1024]{1,0:T(8,128)(2,1)} %embeddings.1) | copy-start | bytes 12582916
  52.0 6.9 %collective-permute-start.19 = (f32[512]{0:T(512)S(1)}, f32[512]{0:T(512)S(1)}, u32[]{:S(2)}, u32[]{:S(2)}) collective-permute-start(f32[512]{0:T(512)S(1)} %log_add_fusion.11), channel_id=1, source_target_pairs={{0,16},{8,24},{16,0},{24,8},{1,17},{9,25},{17,1},{25,9},{2,18},{10... | collective-permute-start | bytes 6152 | tf_op jit(solution)/shard_map/ppermute | solution.py:25
  53.6 6.9 %collective-permute-start.18 = (f32[512]{0:T(512)S(1)}, f32[512]{0:T(512)S(1)}, u32[]{:S(2)}, u32[]{:S(2)}) collective-permute-start(f32[512]{0:T(512)S(1)} %log_add_fusion.11), channel_id=1, source_target_pairs={{0,8},{8,0},{16,24},{24,16},{1,9},{9,1},{17,25},{25,17},{2,10},{10... | collective-permute-start | bytes 6152 | tf_op jit(solution)/shard_map/ppermute | solution.py:25
  56.4 6.5 %collective-permute-start.20 = (bf16[128,512]{1,0:T(8,128)(2,1)S(1)}, bf16[128,512]{1,0:T(8,128)(2,1)S(1)}, u32[]{:S(2)}, u32[]{:S(2)}) collective-permute-start(bf16[128,512]{1,0:T(8,128)(2,1)S(1)} %get-tuple-element.38), channel_id=1, source_target_pairs={{0,8},{8,0},{16,24},{24,16},{1,9},{9,1},{17,25},{25,17},{2,10},{10... | collective-permute-start | bytes 393224 | tf_op jit(solution)/shard_map/ppermute | solution.py:25
  57.0 6.4 %collective-permute-start.21 = (bf16[128,512]{1,0:T(8,128)(2,1)S(1)}, bf16[128,512]{1,0:T(8,128)(2,1)S(1)}, u32[]{:S(2)}, u32[]{:S(2)}) collective-permute-start(bf16[128,512]{1,0:T(8,128)(2,1)S(1)} %get-tuple-element.39), channel_id=1, source_target_pairs={{0,16},{8,24},{16,0},{24,8},{1,17},{9,25},{17,1},{25,9},{2,18},{10... | collective-permute-start | bytes 393224 | tf_op jit(solution)/shard_map/ppermute | solution.py:25
  57.6 7.9 %collective-permute-start.22 = (bf16[128,512]{1,0:T(8,128)(2,1)S(1)}, bf16[128,512]{1,0:T(8,128)(2,1)S(1)}, u32[]{:S(2)}, u32[]{:S(2)}) collective-permute-start(bf16[128,512]{1,0:T(8,128)(2,1)S(1)} %get-tuple-element.41), channel_id=1, source_target_pairs={{0,8},{8,0},{16,24},{24,16},{1,9},{9,1},{17,25},{25,17},{2,10},{10... | collective-permute-start | bytes 393224 | tf_op jit(solution)/shard_map/ppermute | solution.py:25
  59.0 6.5 %collective-permute-start.26 = (bf16[128,512]{1,0:T(8,128)(2,1)S(1)}, bf16[128,512]{1,0:T(8,128)(2,1)S(1)}, u32[]{:S(2)}, u32[]{:S(2)}) collective-permute-start(bf16[128,512]{1,0:T(8,128)(2,1)S(1)} %get-tuple-element.45), channel_id=1, source_target_pairs={{0,16},{8,24},{16,0},{24,8},{1,17},{9,25},{17,1},{25,9},{2,18},{10... | collective-permute-start | bytes 393224 | tf_op jit(solution)/shard_map/ppermute | solution.py:25
  60.6 7.2 %collective-permute-start.25 = (f32[512]{0:T(512)S(1)}, f32[512]{0:T(512)S(1)}, u32[]{:S(2)}, u32[]{:S(2)}) collective-permute-start(f32[512]{0:T(512)S(1)} %get-tuple-element.48), channel_id=1, source_target_pairs={{0,16},{8,24},{16,0},{24,8},{1,17},{9,25},{17,1},{25,9},{2,18},{10... | collective-permute-start | bytes 6152 | tf_op jit(solution)/shard_map/ppermute | solution.py:25
  63.5 6.3 %collective-permute-start.24 = (bf16[128,512]{1,0:T(8,128)(2,1)S(1)}, bf16[128,512]{1,0:T(8,128)(2,1)S(1)}, u32[]{:S(2)}, u32[]{:S(2)}) collective-permute-start(bf16[128,512]{1,0:T(8,128)(2,1)S(1)} %get-tuple-element.43), channel_id=1, source_target_pairs={{0,16},{8,24},{16,0},{24,8},{1,17},{9,25},{17,1},{25,9},{2,18},{10... | collective-permute-start | bytes 393224 | tf_op jit(solution)/shard_map/ppermute | solution.py:25
  64.5 5.3 %collective-permute-start.27 = (bf16[128,512]{1,0:T(8,128)(2,1)S(1)}, bf16[128,512]{1,0:T(8,128)(2,1)S(1)}, u32[]{:S(2)}, u32[]{:S(2)}) collective-permute-start(bf16[128,512]{1,0:T(8,128)(2,1)S(1)} %get-tuple-element.44), channel_id=1, source_target_pairs={{0,8},{8,0},{16,24},{24,16},{1,9},{9,1},{17,25},{25,17},{2,10},{10... | collective-permute-start | bytes 393224 | tf_op jit(solution)/shard_map/ppermute | solution.py:25
  65.6 7.6 %collective-permute-start.29 = (bf16[128,512]{1,0:T(8,128)(2,1)S(1)}, bf16[128,512]{1,0:T(8,128)(2,1)S(1)}, u32[]{:S(2)}, u32[]{:S(2)}) collective-permute-start(bf16[128,512]{1,0:T(8,128)(2,1)S(1)} %get-tuple-element.61), channel_id=1, source_target_pairs={{0,8},{8,0},{16,24},{24,16},{1,9},{9,1},{17,25},{25,17},{2,10},{10... | collective-permute-start | bytes 393224 | tf_op jit(solution)/shard_map/ppermute | solution.py:25
  67.3 6.4 %collective-permute-start.23 = (bf16[128,512]{1,0:T(8,128)(2,1)S(1)}, bf16[128,512]{1,0:T(8,128)(2,1)S(1)}, u32[]{:S(2)}, u32[]{:S(2)}) collective-permute-start(bf16[128,512]{1,0:T(8,128)(2,1)S(1)} %get-tuple-element.62), channel_id=1, source_target_pairs={{0,16},{8,24},{16,0},{24,8},{1,17},{9,25},{17,1},{25,9},{2,18},{10... | collective-permute-start | bytes 393224 | tf_op jit(solution)/shard_map/ppermute | solution.py:25
  70.0 6.2 %collective-permute-start.31 = (bf16[128,512]{1,0:T(8,128)(2,1)S(1)}, bf16[128,512]{1,0:T(8,128)(2,1)S(1)}, u32[]{:S(2)}, u32[]{:S(2)}) collective-permute-start(bf16[128,512]{1,0:T(8,128)(2,1)S(1)} %fusion.15.refs_2_), channel_id=1, source_target_pairs={{0,8},{8,0},{16,24},{24,16},{1,9},{9,1},{17,25},{25,17},{2,10},{10... | collective-permute-start | bytes 393224 | tf_op jit(solution)/shard_map/ppermute | solution.py:25
  71.0 5.1 %collective-permute-start.32 = (bf16[128,512]{1,0:T(8,128)(2,1)S(1)}, bf16[128,512]{1,0:T(8,128)(2,1)S(1)}, u32[]{:S(2)}, u32[]{:S(2)}) collective-permute-start(bf16[128,512]{1,0:T(8,128)(2,1)S(1)} %fusion.19.refs_3_), channel_id=1, source_target_pairs={{0,16},{8,24},{16,0},{24,8},{1,17},{9,25},{17,1},{25,9},{2,18},{10... | collective-permute-start | bytes 393224 | tf_op jit(solution)/shard_map/ppermute | solution.py:25
  73.4 5.0 %collective-permute-start.30 = (bf16[128,512]{1,0:T(8,128)(2,1)S(1)}, bf16[128,512]{1,0:T(8,128)(2,1)S(1)}, u32[]{:S(2)}, u32[]{:S(2)}) collective-permute-start(bf16[128,512]{1,0:T(8,128)(2,1)S(1)} %fusion.23.refs_3_), channel_id=1, source_target_pairs={{0,16},{8,24},{16,0},{24,8},{1,17},{9,25},{17,1},{25,9},{2,18},{10... | collective-permute-start | bytes 393224 | tf_op jit(solution)/shard_map/ppermute | solution.py:25
  73.7 5.0 %collective-permute-start.28 = (bf16[128,512]{1,0:T(8,128)(2,1)S(1)}, bf16[128,512]{1,0:T(8,128)(2,1)S(1)}, u32[]{:S(2)}, u32[]{:S(2)}) collective-permute-start(bf16[128,512]{1,0:T(8,128)(2,1)S(1)} %fusion.11.refs_2_), channel_id=1, source_target_pairs={{0,8},{8,0},{16,24},{24,16},{1,9},{9,1},{17,25},{25,17},{2,10},{10... | collective-permute-start | bytes 393224 | tf_op jit(solution)/shard_map/ppermute | solution.py:25
where the time goes:
time: 79.8 us; the launch traced here: 79.6 us
  starting transfers between devices  35.4 us (44%)
  waiting for transfers between devices  23.5 us (29%)
  other arithmetic  10.5 us (13%)
  matrix products  4.58 us (6%)
  Pallas kernels  4.52 us (6%)
  between operations  0.97 us (1%)
    ppermute x27, starting transfers between devices, flipped(): return lax.ppermute(x, axis, [(k, k ^ mask) for k in range(size)])  28.2 us
    ppermute x27, waiting for transfers between devices, flipped(): return lax.ppermute(x, axis, [(k, k ^ mask) for k in range(size)])  15.2 us
    ppermute x6, waiting for transfers between devices, split(): lax.ppermute(value, 'cent', [(k, k ^ (odd_mask if k % 2 else even_mask))...  8.29 us
    ppermute x6, starting transfers between devices, split(): lax.ppermute(value, 'cent', [(k, k ^ (odd_mask if k % 2 else even_mask))...  7.24 us
    dot_general x1, matrix products, on_device(): lax.dot_general(sent_and_kept(centroids), embeddings, (((1,), (1,)), ((),...  4.58 us
    pallas_call x2, Pallas kernels, means_of(): pl.pallas_call(functools.partial(means_kernel, is_kept), out_shape=out_sh...  2.88 us
    reduce_sum x3, other arithmetic, on_device(): mass = jnp.sum(terms, axis=1)  2.55 us
    reduce_sum x3, other arithmetic, on_device(): part = top + jnp.log(jnp.sum(jnp.exp(shifted - top[None, :]), axis=0))  2.32 us
  transfers between devices with their start and end apart: 33, of which 23 were waited for; matrix products, arithmetic and copies ran while one was open for 2% of the time, Pallas kernels for 5%

commit v1 on v0

--- a/solution.py
+++ b/solution.py
@@ -100,44 +100,54 @@
     )(*blocks, *so_far)
 
 
+def scaled(sums, factors, target, half_index=None):
+    for block in range(sums.shape[0] // LANES):
+        rows = pl.ds(block * LANES, LANES)
+        values = (sums[block * LANES:(block + 1) * LANES] * factors[block]).astype(target.dtype)
+        if half_index is None:
+            target[rows, :] = values
+        else:
+            target[half_index, rows, :] = values
+
+
 def means_kernel(is_kept, plan, embeddings, mass, *rest):
     half = plan.shape[0] // 2
     quarter = half // 2
-    sums = jnp.dot(plan[pl.ds(is_kept * half, half), :], embeddings[...], preferred_element_type=jnp.float32)
+    width = embeddings.shape[1] // CHUNKS
+    lines = half // LANES
+    per_quarter = lines // 2
+    inverse = [1.0 / column(mass[pl.ds(k, 1), :]) for k in range(2 * lines)]
     if is_kept:
-        weights, row, out, row_out = rest
+        weights, row, kept, row_out, *sent = rest
         row_out[...] = row[...]
     else:
-        out = None
-    for block in range(half // LANES):
-        factor = 1.0 / column(mass[pl.ds(is_kept * (half // LANES) + block, 1), :])
-        if is_kept:
-            factor = factor * column(weights[pl.ds(block, 1), :])
-        rows = pl.ds(block * LANES % quarter, LANES)
-        values = sums[block * LANES:(block + 1) * LANES] * factor
-        half_index = block * LANES // quarter
-        if is_kept:
-            out[half_index, rows, :] = values
-        else:
-            width = rest[0].shape[1]
-            for chunk in range(CHUNKS):
-                target = rest[2 * chunk + half_index]
-                target[rows, :] = values[:, chunk * width:(chunk + 1) * width].astype(target.dtype)
+        sent = rest
+    for chunk in range(1, CHUNKS) if is_kept else range(1):
+        columns = pl.ds(chunk * width, width)
+        sums = jnp.dot(plan[pl.ds(0, half), :], embeddings[:, columns], preferred_element_type=jnp.float32)
+        for k in range(2):
+            target = sent[2 * (chunk - is_kept) + k]
+            scaled(sums[k * quarter:(k + 1) * quarter], inverse[k * per_quarter:(k + 1) * per_quarter], target)
+    if is_kept:
+        sums = jnp.dot(plan[pl.ds(half, half), :], embeddings[...], preferred_element_type=jnp.float32)
+        factors = [inverse[lines + k] * column(weights[pl.ds(k, 1), :]) for k in range(lines)]
+        for k in range(2):
+            scaled(sums[k * quarter:(k + 1) * quarter], factors[k * per_quarter:(k + 1) * per_quarter], kept, k)
 
 
 def means_of(is_kept, plan, embeddings, mass, *rest):
     count, rows_here = plan.shape
     depth = embeddings.shape[1]
     vmem = pl.BlockSpec(memory_space=pltpu.VMEM)
+    sent = [jax.ShapeDtypeStruct((count // 4, depth // CHUNKS), jnp.bfloat16)] * 2
     if is_kept:
-        out_shape = (
-            jax.ShapeDtypeStruct((2, count // 4, depth), jnp.float32),
-            jax.ShapeDtypeStruct((1, rows_here), jnp.float32),
-        )
-        out_specs = (vmem, pl.BlockSpec((1, rows_here), lambda: (0, 0)))
+        sent = sent * (CHUNKS - 1)
+        kept = jax.ShapeDtypeStruct((2, count // 4, depth), jnp.float32)
+        row_out = jax.ShapeDtypeStruct((1, rows_here), jnp.float32)
+        out_shape = [kept, row_out] + sent
+        out_specs = [vmem, pl.BlockSpec((1, rows_here), lambda: (0, 0))] + [vmem] * len(sent)
     else:
-        out_shape = [jax.ShapeDtypeStruct((count // 4, depth // CHUNKS), jnp.bfloat16)] * (2 * CHUNKS)
-        out_specs = [vmem] * (2 * CHUNKS)
+        out_shape, out_specs = sent, [vmem] * 2
     return pl.pallas_call(
         functools.partial(means_kernel, is_kept),
         out_shape=out_shape,
@@ -155,7 +165,7 @@
     first, second = orders[0][:2]
     partners = {bit: aligned(flipped(part, "dp", 1 << bit), 1 << bit) for bit in (first, second)}
     sent = means_of(0, plan, embeddings, mass)
-    got = [flipped(sent[2 * chunk + k], "dp", 1 << order[0]) for chunk in range(CHUNKS) for k, order in enumerate(orders)]
+    got = [flipped(sent[k], "dp", 1 << order[0]) for k, order in enumerate(orders)]
 
     def kept_of(lower, upper):
         return jnp.concatenate([lower[2 * quarter:3 * quarter], upper[3 * quarter:]])
@@ -163,7 +173,8 @@
     pairs = lax.optimization_barrier([lse(partners[first], part), lse(partners[second], part)])
     pair = kept_of(*pairs)
     weights = jnp.exp(kept_of(part, part) - pair).reshape(2 * quarter // LANES, LANES)
-    kept, row_out = means_of(1, plan, embeddings, mass, weights, row_now[None, :])
+    kept, row_out, *sent = means_of(1, plan, embeddings, mass, weights, row_now[None, :])
+    got += [flipped(sent[k], "dp", 1 << orders[k % 2][0]) for k in range(len(sent))]
     weights = jnp.exp(kept_of(partners[first], partners[second]) - pair)
 
     corner = flipped(partners[first], "dp", 1 << second)

time: 79.8 us -> 80.7 us (1.011)
  waiting for transfers between devices: 23.5 us -> 26.3 us
  starting transfers between devices: 35.4 us -> 33.5 us
    ppermute x27, waiting for transfers between devices: 15.2 us -> 18.1 us  [flipped(): return lax.ppermute(x, axis, [(k, k ^ mask) for k in range(size)])]
    ppermute x27, starting transfers between devices: 28.2 us -> 26.3 us  [flipped(): return lax.ppermute(x, axis, [(k, k ^ mask) for k in range(size)])]
  transfers between devices with their start and end apart: 33 -> 33, of which waited for: 23 -> 28; matrix products, arithmetic and copies ran while one was open for 2% -> 2% of each run, Pallas kernels for 5% -> 5%
where the time goes in v1:
time: 80.7 us; the launch traced here: 80.5 us
  starting transfers between devices  33.5 us (42%)
  waiting for transfers between devices  26.3 us (33%)
  other arithmetic  10.5 us (13%)
  matrix products  4.58 us (6%)
  Pallas kernels  4.53 us (6%)
  between operations  0.94 us (1%)
    ppermute x27, starting transfers between devices, flipped(): return lax.ppermute(x, axis, [(k, k ^ mask) for k in range(size)])  26.3 us
    ppermute x27, waiting for transfers between devices, flipped(): return lax.ppermute(x, axis, [(k, k ^ mask) for k in range(size)])  18.1 us
    ppermute x6, waiting for transfers between devices, split(): lax.ppermute(value, 'cent', [(k, k ^ (odd_mask if k % 2 else even_mask))...  8.29 us
    ppermute x6, starting transfers between devices, split(): lax.ppermute(value, 'cent', [(k, k ^ (odd_mask if k % 2 else even_mask))...  7.24 us
    dot_general x1, matrix products, on_device(): lax.dot_general(sent_and_kept(centroids), embeddings, (((1,), (1,)), ((),...  4.58 us
    pallas_call x2, Pallas kernels, means_of(): pl.pallas_call(functools.partial(means_kernel, is_kept), out_shape=out_sh...  2.89 us
    reduce_sum x3, other arithmetic, on_device(): mass = jnp.sum(terms, axis=1)  2.55 us
    reduce_sum x3, other arithmetic, on_device(): part = top + jnp.log(jnp.sum(jnp.exp(shifted - top[None, :]), axis=0))  2.32 us
  transfers between devices with their start and end apart: 33, of which 28 were waited for; matrix products, arithmetic and copies ran while one was open for 2% of the time, Pallas kernels for 5%

profile of v1, /device:TPU:0, one launch (start us, length us, event | category | flops | bytes accessed | tf_op | source)
XLA Modules:
  0.0 80.5 jit_solution(13848344039013614876)
XLA Ops:
  0.6 0.8 %broadcast_select_fusion.19 = (f32[128]{0:T(128)S(1)}, f32[128]{0:T(128)S(1)}, f32[128]{0:T(128)S(1)}, f32[128]{0:T(128)S(1)}) fusion(pred[]{:T(512)} %bitcast.4, f32[512]{0:T(512)} %param.5, pred[]{:T(512)} %bitcast.3), kind=kLoop, calls=%fused_computation.160 | loop fusion | flops 512 | bytes 4098 | tf_op jit(solution)/shard_map/jit(_where)/select_n | solution.py:258
  1.5 1.3 %broadcast_select_fusion.3 = (bf16[128,1024]{1,0:T(8,128)(2,1)S(1)}, bf16[128,1024]{1,0:T(8,128)(2,1)S(1)}, bf16[128,1024]{1,0:T(8,128)(2,1)S(1)}, bf16[128,1024]{1,0:T(8,128)(2,1)S(1)}) fusion(pred[]{:T(512)} %bitcast.4, bf16[512,1024]{1,0:T(8,128)(2,1)} %param.4, pred[]{:T(512)} %bitcast.3), kind=kLoop, calls=%fused_computation.53 | loop fusion | flops 524288 | bytes 2097154 | tf_op jit(solution)/shard_map/jit(_where)/select_n | solution.py:258
  2.8 4.6 %add_reduce_fusion.5 = (f32[2048]{0:T(1024)S(1)}, f32[512,2048]{1,0:T(8,128)S(1)}) fusion(f32[512]{0:T(512)S(1)} %pad_maximum_fusion, bf16[2048,1024]{1,0:T(8,128)(2,1)} %embeddings.1, bf16[128,1024]{1,0:T(8,128)(2,1)S(1)} %get-tuple-element.67, bf16[128,1024]{1,0:T(8,128)(2,1)S(1)} %get-tuple-element.68, bf16[128,1024]{1,0:T(8,128)(2,1)S(1)} %get-tuple-element.66, ...), kind=kOutput, calls=%fused_computation.11 | convolution fusion | flops 2154821632 | bytes 9447424 | tf_op jit(solution)/shard_map/dot_general | solution.py:274
  7.3 0.8 exponential_reduce_fusion.4
  8.7 0.8 %collective-permute-done = f32[2048]{0:T(1024)S(1)} collective-permute-done((f32[2048]{0:T(1024)S(1)}, f32[2048]{0:T(1024)S(1)}, u32[]{:S(2)}, u32[]{:S(2)}) %collective-permute-start) | collective-permute-done | bytes 8224 | tf_op jit(solution)/shard_map/ppermute | solution.py:25
  9.5 3.0 %collective-permute-start.2 = (f32[2048]{0:T(1024)S(1)}, f32[2048]{0:T(1024)S(1)}, u32[]{:S(2)}, u32[]{:S(2)}) collective-permute-start(f32[2048]{0:T(1024)S(1)} %log_add_fusion.4), channel_id=1, source_target_pairs={{0,2},{1,7},{2,0},{3,5},{4,6},{5,3},{6,4},{7,1},{8,10},{9,15},{10,... | collective-permute-start | bytes 24584 | tf_op jit(solution)/shard_map/ppermute | solution.py:54
  12.6 1.6 %collective-permute-done.2 = f32[2048]{0:T(1024)S(1)} collective-permute-done((f32[2048]{0:T(1024)S(1)}, f32[2048]{0:T(1024)S(1)}, u32[]{:S(2)}, u32[]{:S(2)}) %collective-permute-start.2) | collective-permute-done | bytes 8224 | tf_op jit(solution)/shard_map/ppermute | solution.py:54
  14.1 2.0 %collective-permute-done.1 = f32[2048]{0:T(1024)S(1)} collective-permute-done((f32[2048]{0:T(1024)S(1)}, f32[2048]{0:T(1024)S(1)}, u32[]{:S(2)}, u32[]{:S(2)}) %collective-permute-start.1) | collective-permute-done | bytes 8224 | tf_op jit(solution)/shard_map/ppermute | solution.py:54
  16.2 1.7 %collective-permute-start.3 = (f32[2048]{0:T(1024)S(1)}, f32[2048]{0:T(1024)S(1)}, u32[]{:S(2)}, u32[]{:S(2)}) collective-permute-start(f32[2048]{0:T(1024)S(1)} %add_select_fusion.2), channel_id=1, source_target_pairs={{0,1},{1,0},{2,3},{3,2},{4,5},{5,4},{6,7},{7,6},{8,9},{9,8},{10,11... | collective-permute-start | bytes 24584 | tf_op jit(solution)/shard_map/ppermute | solution.py:25
  17.9 0.8 %collective-permute-done.3 = f32[2048]{0:T(1024)S(1)} collective-permute-done((f32[2048]{0:T(1024)S(1)}, f32[2048]{0:T(1024)S(1)}, u32[]{:S(2)}, u32[]{:S(2)}) %collective-permute-start.3) | collective-permute-done | bytes 8224 | tf_op jit(solution)/shard_map/ppermute | solution.py:25
  19.1 0.8 %exponential_reduce_fusion.3 = f32[512]{0:T(512)S(1)} fusion(f32[512,2048]{1,0:T(8,128)S(1)} %get-tuple-element.129, f32[512]{0:T(512)S(1)} %add_reduce_fusion.4, f32[2048]{0:T(1024)S(1)} %add_subtract_fusion.2), kind=kLoop, calls=%fused_computation.4 | loop fusion | flops 3145216 | bytes 4206592 | tf_op jit(solution)/shard_map/reduce_sum | solution.py:286
  19.9 2.5 %collective-permute-start.4 = (f32[512]{0:T(512)S(1)}, f32[512]{0:T(512)S(1)}, u32[]{:S(2)}, u32[]{:S(2)}) collective-permute-start(f32[512]{0:T(512)S(1)} %log_add_fusion.15), channel_id=1, source_target_pairs={{0,24},{8,16},{16,8},{24,0},{1,25},{9,17},{17,9},{25,1},{2,26},{10... | collective-permute-start | bytes 6152 | tf_op jit(solution)/shard_map/ppermute | solution.py:25
  23.5 1.0 %collective-permute-done.4 = f32[512]{0:T(512)S(1)} collective-permute-done((f32[512]{0:T(512)S(1)}, f32[512]{0:T(512)S(1)}, u32[]{:S(2)}, u32[]{:S(2)}) %collective-permute-start.4) | collective-permute-done | bytes 2080 | tf_op jit(solution)/shard_map/ppermute | solution.py:25
  24.5 1.5 %collective-permute-done.5 = f32[512]{0:T(512)S(1)} collective-permute-done((f32[512]{0:T(512)S(1)}, f32[512]{0:T(512)S(1)}, u32[]{:S(2)}, u32[]{:S(2)}) %collective-permute-start.5) | collective-permute-done | bytes 2080 | tf_op jit(solution)/shard_map/ppermute | solution.py:25
  27.8 1.2 %collective-permute-done.7 = f32[2048]{0:T(1024)S(1)} collective-permute-done((f32[2048]{0:T(1024)S(1)}, f32[2048]{0:T(1024)S(1)}, u32[]{:S(2)}, u32[]{:S(2)}) %collective-permute-start.7) | collective-permute-done | bytes 8224 | tf_op jit(solution)/shard_map/ppermute | solution.py:25
  29.1 2.0 %collective-permute-start.8 = (f32[2048]{0:T(1024)S(1)}, f32[2048]{0:T(1024)S(1)}, u32[]{:S(2)}, u32[]{:S(2)}) collective-permute-start(f32[2048]{0:T(1024)S(1)} %log_add_fusion.2), channel_id=1, source_target_pairs={{0,2},{1,5},{2,0},{3,7},{4,6},{5,1},{6,4},{7,3},{8,10},{9,13},{10,... | collective-permute-start | bytes 24584 | tf_op jit(solution)/shard_map/ppermute | solution.py:54
  31.1 1.6 %collective-permute-done.9 = f32[2048]{0:T(1024)S(1)} collective-permute-done((f32[2048]{0:T(1024)S(1)}, f32[2048]{0:T(1024)S(1)}, u32[]{:S(2)}, u32[]{:S(2)}) %collective-permute-start.9) | collective-permute-done | bytes 8224 | tf_op jit(solution)/shard_map/ppermute | solution.py:54
  32.8 1.0 %collective-permute-start.10 = (f32[2048]{0:T(1024)S(1)}, f32[2048]{0:T(1024)S(1)}, u32[]{:S(2)}, u32[]{:S(2)}) collective-permute-start(f32[2048]{0:T(1024)S(1)} %add_select_fusion.1), channel_id=1, source_target_pairs={{0,1},{1,0},{2,3},{3,2},{4,5},{5,4},{6,7},{7,6},{8,9},{9,8},{10,11... | collective-permute-start | bytes 24584 | tf_op jit(solution)/shard_map/ppermute | solution.py:25
  33.8 0.8 %collective-permute-done.10 = f32[2048]{0:T(1024)S(1)} collective-permute-done((f32[2048]{0:T(1024)S(1)}, f32[2048]{0:T(1024)S(1)}, u32[]{:S(2)}, u32[]{:S(2)}) %collective-permute-start.10) | collective-permute-done | bytes 8224 | tf_op jit(solution)/shard_map/ppermute | solution.py:25
  35.0 0.8 %exponential_reduce_fusion.1 = f32[512]{0:T(512)S(1)} fusion(f32[512,2048]{1,0:T(8,128)S(1)} %get-tuple-element.129, f32[512]{0:T(512)S(1)} %add_reduce_fusion.2, f32[2048]{0:T(1024)S(1)} %add_subtract_fusion.1), kind=kLoop, calls=%fused_computation.2 | loop fusion | flops 3145216 | bytes 4206592 | tf_op jit(solution)/shard_map/reduce_sum | solution.py:286
  35.9 1.6 %collective-permute-start.11 = (f32[512]{0:T(512)S(1)}, f32[512]{0:T(512)S(1)}, u32[]{:S(2)}, u32[]{:S(2)}) collective-permute-start(f32[512]{0:T(512)S(1)} %log_add_fusion.13), channel_id=1, source_target_pairs={{0,24},{8,16},{16,8},{24,0},{1,25},{9,17},{17,9},{25,1},{2,26},{10... | collective-permute-start | bytes 6152 | tf_op jit(solution)/shard_map/ppermute | solution.py:25
  37.9 1.5 %collective-permute-start.13 = (f32[512]{0:T(512)S(1)}, f32[512]{0:T(512)S(1)}, u32[]{:S(2)}, u32[]{:S(2)}) collective-permute-start(f32[512]{0:T(512)S(1)} %log_add_fusion.13), channel_id=1, source_target_pairs={{0,8},{8,0},{16,24},{24,16},{1,9},{9,1},{17,25},{25,17},{2,10},{10... | collective-permute-start | bytes 6152 | tf_op jit(solution)/shard_map/ppermute | solution.py:25
  39.4 1.0 %collective-permute-done.11 = f32[512]{0:T(512)S(1)} collective-permute-done((f32[512]{0:T(512)S(1)}, f32[512]{0:T(512)S(1)}, u32[]{:S(2)}, u32[]{:S(2)}) %collective-permute-start.11) | collective-permute-done | bytes 2080 | tf_op jit(solution)/shard_map/ppermute | solution.py:25
  41.9 0.8 exponential_reduce_fusion
  42.8 1.2 %collective-permute-done.14 = f32[2048]{0:T(1024)S(1)} collective-permute-done((f32[2048]{0:T(1024)S(1)}, f32[2048]{0:T(1024)S(1)}, u32[]{:S(2)}, u32[]{:S(2)}) %collective-permute-start.14) | collective-permute-done | bytes 8224 | tf_op jit(solution)/shard_map/ppermute | solution.py:25
  44.0 1.4 %collective-permute-start.16 = (f32[2048]{0:T(1024)S(1)}, f32[2048]{0:T(1024)S(1)}, u32[]{:S(2)}, u32[]{:S(2)}) collective-permute-start(f32[2048]{0:T(1024)S(1)} %log_add_fusion), channel_id=1, source_target_pairs={{0,2},{1,7},{2,0},{3,5},{4,6},{5,3},{6,4},{7,1},{8,10},{9,15},{10,... | collective-permute-start | bytes 24584 | tf_op jit(solution)/shard_map/ppermute | solution.py:54
  46.1 1.6 %collective-permute-done.16 = f32[2048]{0:T(1024)S(1)} collective-permute-done((f32[2048]{0:T(1024)S(1)}, f32[2048]{0:T(1024)S(1)}, u32[]{:S(2)}, u32[]{:S(2)}) %collective-permute-start.16) | collective-permute-done | bytes 8224 | tf_op jit(solution)/shard_map/ppermute | solution.py:54
  47.7 1.4 %collective-permute-done.15 = f32[2048]{0:T(1024)S(1)} collective-permute-done((f32[2048]{0:T(1024)S(1)}, f32[2048]{0:T(1024)S(1)}, u32[]{:S(2)}, u32[]{:S(2)}) %collective-permute-start.15) | collective-permute-done | bytes 8224 | tf_op jit(solution)/shard_map/ppermute | solution.py:54
  49.1 0.8 collective-permute-start.17
  49.9 0.8 %collective-permute-done.17 = f32[2048]{0:T(1024)S(1)} collective-permute-done((f32[2048]{0:T(1024)S(1)}, f32[2048]{0:T(1024)S(1)}, u32[]{:S(2)}, u32[]{:S(2)}) %collective-permute-start.17) | collective-permute-done | bytes 8224 | tf_op jit(solution)/shard_map/ppermute | solution.py:25
  51.1 0.9 %fusion = (f32[512]{0:T(512)S(1)}, bf16[512,2048]{1,0:T(8,128)(2,1)S(1)}) fusion(f32[512,2048]{1,0:T(8,128)S(1)} %get-tuple-element.129, f32[512]{0:T(512)S(1)} %add_reduce_fusion, f32[2048]{0:T(1024)S(1)} %add_subtract_fusion), kind=kLoop, calls=%fused_computation.12 | loop fusion | flops 4193792 | bytes 6303744 | tf_op jit(solution)/shard_map/reduce_sum | solution.py:286
  52.0 1.6 %collective-permute-start.19 = (f32[512]{0:T(512)S(1)}, f32[512]{0:T(512)S(1)}, u32[]{:S(2)}, u32[]{:S(2)}) collective-permute-start(f32[512]{0:T(512)S(1)} %log_add_fusion.11), channel_id=1, source_target_pairs={{0,16},{8,24},{16,0},{24,8},{1,17},{9,25},{17,1},{25,9},{2,18},{10... | collective-permute-start | bytes 6152 | tf_op jit(solution)/shard_map/ppermute | solution.py:25
  53.6 1.5 %collective-permute-start.18 = (f32[512]{0:T(512)S(1)}, f32[512]{0:T(512)S(1)}, u32[]{:S(2)}, u32[]{:S(2)}) collective-permute-start(f32[512]{0:T(512)S(1)} %log_add_fusion.11), channel_id=1, source_target_pairs={{0,8},{8,0},{16,24},{24,16},{1,9},{9,1},{17,25},{25,17},{2,10},{10... | collective-permute-start | bytes 6152 | tf_op jit(solution)/shard_map/ppermute | solution.py:25
  57.3 1.3 %collective-permute-start.25 = (f32[512]{0:T(512)S(1)}, f32[512]{0:T(512)S(1)}, u32[]{:S(2)}, u32[]{:S(2)}) collective-permute-start(f32[512]{0:T(512)S(1)} %get-tuple-element.48), channel_id=1, source_target_pairs={{0,16},{8,24},{16,0},{24,8},{1,17},{9,25},{17,1},{25,9},{2,18},{10... | collective-permute-start | bytes 6152 | tf_op jit(solution)/shard_map/ppermute | solution.py:25
  58.6 2.2 %shard_map.58 = (f32[2,128,1024]{2,1,0:T(8,128)S(1)}, f32[1,2048]{1,0:T(1,128)}, bf16[128,512]{1,0:T(8,128)(2,1)S(1)}, bf16[128,512]{1,0:T(8,128)(2,1)S(1)}) custom-call(bf16[512,2048]{1,0:T(8,128)(2,1)S(1)} %get-tuple-element.60.plan, bf16[2048,1024]{1,0:T(8,128)(2,1)S(1)} %copy-done, f32[4,128]{1,0:T(4,128)S(1)} %bitcast.27, f32[2,128]{1,0:T(2,128)S(1)} %fusion.51.rest_0_, ...), custom_call_target="tpu_custom_call" | custom-call | flops 1073741824 | bytes 4194304 | tf_op jit(solution)/shard_map/pallas_call | solution.py:151
  60.8 1.5 %collective-permute-start.22 = (bf16[128,512]{1,0:T(8,128)(2,1)S(1)}, bf16[128,512]{1,0:T(8,128)(2,1)S(1)}, u32[]{:S(2)}, u32[]{:S(2)}) collective-permute-start(bf16[128,512]{1,0:T(8,128)(2,1)S(1)} %get-tuple-element.41), channel_id=1, source_target_pairs={{0,8},{8,0},{16,24},{24,16},{1,9},{9,1},{17,25},{25,17},{2,10},{10... | collective-permute-start | bytes 393224 | tf_op jit(solution)/shard_map/ppermute | solution.py:25
  63.2 1.3 %collective-permute-start.24 = (bf16[128,512]{1,0:T(8,128)(2,1)S(1)}, bf16[128,512]{1,0:T(8,128)(2,1)S(1)}, u32[]{:S(2)}, u32[]{:S(2)}) collective-permute-start(bf16[128,512]{1,0:T(8,128)(2,1)S(1)} %get-tuple-element.43), channel_id=1, source_target_pairs={{0,16},{8,24},{16,0},{24,8},{1,17},{9,25},{17,1},{25,9},{2,18},{10... | collective-permute-start | bytes 393224 | tf_op jit(solution)/shard_map/ppermute | solution.py:25
  65.1 1.2 %collective-permute-done.22 = bf16[128,512]{1,0:T(8,128)(2,1)S(1)} collective-permute-done((bf16[128,512]{1,0:T(8,128)(2,1)S(1)}, bf16[128,512]{1,0:T(8,128)(2,1)S(1)}, u32[]{:S(2)}, u32[]{:S(2)}) %collective-permute-start.22) | collective-permute-done | bytes 131104 | tf_op jit(solution)/shard_map/ppermute | solution.py:25
  66.3 1.4 %collective-permute-done.26 = bf16[128,512]{1,0:T(8,128)(2,1)S(1)} collective-permute-done((bf16[128,512]{1,0:T(8,128)(2,1)S(1)}, bf16[128,512]{1,0:T(8,128)(2,1)S(1)}, u32[]{:S(2)}, u32[]{:S(2)}) %collective-permute-start.26) | collective-permute-done | bytes 131104 | tf_op jit(solution)/shard_map/ppermute | solution.py:25
  67.9 1.0 %collective-permute-start.29 = (bf16[128,512]{1,0:T(8,128)(2,1)S(1)}, bf16[128,512]{1,0:T(8,128)(2,1)S(1)}, u32[]{:S(2)}, u32[]{:S(2)}) collective-permute-start(bf16[128,512]{1,0:T(8,128)(2,1)S(1)} %get-tuple-element.61), channel_id=1, source_target_pairs={{0,8},{8,0},{16,24},{24,16},{1,9},{9,1},{17,25},{25,17},{2,10},{10... | collective-permute-start | bytes 393224 | tf_op jit(solution)/shard_map/ppermute | solution.py:25
  68.9 0.9 %collective-permute-start.23 = (bf16[128,512]{1,0:T(8,128)(2,1)S(1)}, bf16[128,512]{1,0:T(8,128)(2,1)S(1)}, u32[]{:S(2)}, u32[]{:S(2)}) collective-permute-start(bf16[128,512]{1,0:T(8,128)(2,1)S(1)} %get-tuple-element.62), channel_id=1, source_target_pairs={{0,16},{8,24},{16,0},{24,8},{1,17},{9,25},{17,1},{25,9},{2,18},{10... | collective-permute-start | bytes 393224 | tf_op jit(solution)/shard_map/ppermute | solution.py:25
  71.6 0.9 %collective-permute-start.32 = (bf16[128,512]{1,0:T(8,128)(2,1)S(1)}, bf16[128,512]{1,0:T(8,128)(2,1)S(1)}, u32[]{:S(2)}, u32[]{:S(2)}) collective-permute-start(bf16[128,512]{1,0:T(8,128)(2,1)S(1)} %fusion.19.refs_3_), channel_id=1, source_target_pairs={{0,16},{8,24},{16,0},{24,8},{1,17},{9,25},{17,1},{25,9},{2,18},{10... | collective-permute-start | bytes 393224 | tf_op jit(solution)/shard_map/ppermute | solution.py:25
  72.5 1.0 %collective-permute-done.29 = bf16[128,512]{1,0:T(8,128)(2,1)S(1)} collective-permute-done((bf16[128,512]{1,0:T(8,128)(2,1)S(1)}, bf16[128,512]{1,0:T(8,128)(2,1)S(1)}, u32[]{:S(2)}, u32[]{:S(2)}) %collective-permute-start.29) | collective-permute-done | bytes 131104 | tf_op jit(solution)/shard_map/ppermute | solution.py:25
  74.6 1.4 %collective-permute-start.28 = (bf16[128,512]{1,0:T(8,128)(2,1)S(1)}, bf16[128,512]{1,0:T(8,128)(2,1)S(1)}, u32[]{:S(2)}, u32[]{:S(2)}) collective-permute-start(bf16[128,512]{1,0:T(8,128)(2,1)S(1)} %fusion.11.refs_2_), channel_id=1, source_target_pairs={{0,8},{8,0},{16,24},{24,16},{1,9},{9,1},{17,25},{25,17},{2,10},{10... | collective-permute-start | bytes 393224 | tf_op jit(solution)/shard_map/ppermute | solution.py:25
  76.7 0.8 %shard_map.60.refs_4_ = bf16[512,1024]{1,0:T(8,128)(2,1)} custom-call(bf16[128,512]{1,0:T(8,128)(2,1)S(1)} %collective-permute-done.31.refs_0_, bf16[128,512]{1,0:T(8,128)(2,1)S(1)} %collective-permute-done.32.refs_1_, bf16[128,512]{1,0:T(8,128)(2,1)S(1)} %fusion.15.refs_2_, bf16[128,512]{1,0:T(8,128)(2,1)S(1)} %fusion.19.refs_3_), custom_call_target="tpu_custom_call" | custom-call | tf_op jit(solution)/shard_map/pallas_call | solution.py:92
  77.5 1.1 %collective-permute-done.30.refs_1_ = bf16[128,512]{1,0:T(8,128)(2,1)S(1)} collective-permute-done((bf16[128,512]{1,0:T(8,128)(2,1)S(1)}, bf16[128,512]{1,0:T(8,128)(2,1)S(1)}, u32[]{:S(2)}, u32[]{:S(2)}) %collective-permute-start.30) | collective-permute-done | bytes 131104 | tf_op jit(solution)/shard_map/ppermute | solution.py:25
  78.6 1.0 %collective-permute-done.28.refs_0_ = bf16[128,512]{1,0:T(8,128)(2,1)S(1)} collective-permute-done((bf16[128,512]{1,0:T(8,128)(2,1)S(1)}, bf16[128,512]{1,0:T(8,128)(2,1)S(1)}, u32[]{:S(2)}, u32[]{:S(2)}) %collective-permute-start.28) | collective-permute-done | bytes 131104 | tf_op jit(solution)/shard_map/ppermute | solution.py:25
  79.6 0.8 %shard_map.61 = bf16[512,1024]{1,0:T(8,128)(2,1)} custom-call(bf16[128,512]{1,0:T(8,128)(2,1)S(1)} %collective-permute-done.28.refs_0_, bf16[128,512]{1,0:T(8,128)(2,1)S(1)} %collective-permute-done.30.refs_1_, bf16[128,512]{1,0:T(8,128)(2,1)S(1)} %fusion.11.refs_2_, bf16[128,512]{1,0:T(8,128)(2,1)S(1)} %fusion.23.refs_3_, ...), custom_call_target="tpu_custom_call", output_to_operand_aliasing={{}: (4, {})} | custom-call | tf_op jit(solution)/shard_map/pallas_call | solution.py:92
  (91 shorter events, 15.0 us)
Async XLA Ops:
  8.1 1.3 %collective-permute-start = (f32[2048]{0:T(1024)S(1)}, f32[2048]{0:T(1024)S(1)}, u32[]{:S(2)}, u32[]{:S(2)}) collective-permute-start(f32[2048]{0:T(1024)S(1)} %log_add_fusion.5), channel_id=1, source_target_pairs={{0,1},{1,0},{2,3},{3,2},{4,5},{5,4},{6,7},{7,6},{8,9},{9,8},{10,11... | collective-permute-start | bytes 24584 | tf_op jit(solution)/shard_map/ppermute | solution.py:25
  9.5 4.6 %collective-permute-start.2 = (f32[2048]{0:T(1024)S(1)}, f32[2048]{0:T(1024)S(1)}, u32[]{:S(2)}, u32[]{:S(2)}) collective-permute-start(f32[2048]{0:T(1024)S(1)} %log_add_fusion.4), channel_id=1, source_target_pairs={{0,2},{1,7},{2,0},{3,5},{4,6},{5,3},{6,4},{7,1},{8,10},{9,15},{10,... | collective-permute-start | bytes 24584 | tf_op jit(solution)/shard_map/ppermute | solution.py:54
  12.5 3.7 %collective-permute-start.1 = (f32[2048]{0:T(1024)S(1)}, f32[2048]{0:T(1024)S(1)}, u32[]{:S(2)}, u32[]{:S(2)}) collective-permute-start(f32[2048]{0:T(1024)S(1)} %log_add_fusion.4), channel_id=1, source_target_pairs={{0,2},{1,5},{2,0},{3,7},{4,6},{5,1},{6,4},{7,3},{8,10},{9,13},{10,... | collective-permute-start | bytes 24584 | tf_op jit(solution)/shard_map/ppermute | solution.py:54
  16.2 2.6 %collective-permute-start.3 = (f32[2048]{0:T(1024)S(1)}, f32[2048]{0:T(1024)S(1)}, u32[]{:S(2)}, u32[]{:S(2)}) collective-permute-start(f32[2048]{0:T(1024)S(1)} %add_select_fusion.2), channel_id=1, source_target_pairs={{0,1},{1,0},{2,3},{3,2},{4,5},{5,4},{6,7},{7,6},{8,9},{9,8},{10,11... | collective-permute-start | bytes 24584 | tf_op jit(solution)/shard_map/ppermute | solution.py:25
  19.9 4.5 %collective-permute-start.4 = (f32[512]{0:T(512)S(1)}, f32[512]{0:T(512)S(1)}, u32[]{:S(2)}, u32[]{:S(2)}) collective-permute-start(f32[512]{0:T(512)S(1)} %log_add_fusion.15), channel_id=1, source_target_pairs={{0,24},{8,16},{16,8},{24,0},{1,25},{9,17},{17,9},{25,1},{2,26},{10... | collective-permute-start | bytes 6152 | tf_op jit(solution)/shard_map/ppermute | solution.py:25
  22.5 3.6 %collective-permute-start.5 = (f32[512]{0:T(512)S(1)}, f32[512]{0:T(512)S(1)}, u32[]{:S(2)}, u32[]{:S(2)}) collective-permute-start(f32[512]{0:T(512)S(1)} %log_add_fusion.15), channel_id=1, source_target_pairs={{0,16},{8,24},{16,0},{24,8},{1,17},{9,25},{17,1},{25,9},{2,18},{10... | collective-permute-start | bytes 6152 | tf_op jit(solution)/shard_map/ppermute | solution.py:25
  23.0 3.6 %collective-permute-start.6 = (f32[512]{0:T(512)S(1)}, f32[512]{0:T(512)S(1)}, u32[]{:S(2)}, u32[]{:S(2)}) collective-permute-start(f32[512]{0:T(512)S(1)} %log_add_fusion.15), channel_id=1, source_target_pairs={{0,8},{8,0},{16,24},{24,16},{1,9},{9,1},{17,25},{25,17},{2,10},{10... | collective-permute-start | bytes 6152 | tf_op jit(solution)/shard_map/ppermute | solution.py:25
  27.8 1.2 %collective-permute-start.7 = (f32[2048]{0:T(1024)S(1)}, f32[2048]{0:T(1024)S(1)}, u32[]{:S(2)}, u32[]{:S(2)}) collective-permute-start(f32[2048]{0:T(1024)S(1)} %log_add_fusion.3), channel_id=1, source_target_pairs={{0,1},{1,0},{2,3},{3,2},{4,5},{5,4},{6,7},{7,6},{8,9},{9,8},{10,11... | collective-permute-start | bytes 24584 | tf_op jit(solution)/shard_map/ppermute | solution.py:25
  29.0 3.7 %collective-permute-start.9 = (f32[2048]{0:T(1024)S(1)}, f32[2048]{0:T(1024)S(1)}, u32[]{:S(2)}, u32[]{:S(2)}) collective-permute-start(f32[2048]{0:T(1024)S(1)} %log_add_fusion.2), channel_id=1, source_target_pairs={{0,2},{1,7},{2,0},{3,5},{4,6},{5,3},{6,4},{7,1},{8,10},{9,15},{10,... | collective-permute-start | bytes 24584 | tf_op jit(solution)/shard_map/ppermute | solution.py:54
  29.1 3.7 %collective-permute-start.8 = (f32[2048]{0:T(1024)S(1)}, f32[2048]{0:T(1024)S(1)}, u32[]{:S(2)}, u32[]{:S(2)}) collective-permute-start(f32[2048]{0:T(1024)S(1)} %log_add_fusion.2), channel_id=1, source_target_pairs={{0,2},{1,5},{2,0},{3,7},{4,6},{5,1},{6,4},{7,3},{8,10},{9,13},{10,... | collective-permute-start | bytes 24584 | tf_op jit(solution)/shard_map/ppermute | solution.py:54
  32.8 1.8 %collective-permute-start.10 = (f32[2048]{0:T(1024)S(1)}, f32[2048]{0:T(1024)S(1)}, u32[]{:S(2)}, u32[]{:S(2)}) collective-permute-start(f32[2048]{0:T(1024)S(1)} %add_select_fusion.1), channel_id=1, source_target_pairs={{0,1},{1,0},{2,3},{3,2},{4,5},{5,4},{6,7},{7,6},{8,9},{9,8},{10,11... | collective-permute-start | bytes 24584 | tf_op jit(solution)/shard_map/ppermute | solution.py:25
  35.9 4.5 %collective-permute-start.11 = (f32[512]{0:T(512)S(1)}, f32[512]{0:T(512)S(1)}, u32[]{:S(2)}, u32[]{:S(2)}) collective-permute-start(f32[512]{0:T(512)S(1)} %log_add_fusion.13), channel_id=1, source_target_pairs={{0,24},{8,16},{16,8},{24,0},{1,25},{9,17},{17,9},{25,1},{2,26},{10... | collective-permute-start | bytes 6152 | tf_op jit(solution)/shard_map/ppermute | solution.py:25
  37.4 3.6 %collective-permute-start.12 = (f32[512]{0:T(512)S(1)}, f32[512]{0:T(512)S(1)}, u32[]{:S(2)}, u32[]{:S(2)}) collective-permute-start(f32[512]{0:T(512)S(1)} %log_add_fusion.13), channel_id=1, source_target_pairs={{0,16},{8,24},{16,0},{24,8},{1,17},{9,25},{17,1},{25,9},{2,18},{10... | collective-permute-start | bytes 6152 | tf_op jit(solution)/shard_map/ppermute | solution.py:25
  37.9 3.6 %collective-permute-start.13 = (f32[512]{0:T(512)S(1)}, f32[512]{0:T(512)S(1)}, u32[]{:S(2)}, u32[]{:S(2)}) collective-permute-start(f32[512]{0:T(512)S(1)} %log_add_fusion.13), channel_id=1, source_target_pairs={{0,8},{8,0},{16,24},{24,16},{1,9},{9,1},{17,25},{25,17},{2,10},{10... | collective-permute-start | bytes 6152 | tf_op jit(solution)/shard_map/ppermute | solution.py:25
  42.7 1.2 %collective-permute-start.14 = (f32[2048]{0:T(1024)S(1)}, f32[2048]{0:T(1024)S(1)}, u32[]{:S(2)}, u32[]{:S(2)}) collective-permute-start(f32[2048]{0:T(1024)S(1)} %log_add_fusion.1), channel_id=1, source_target_pairs={{0,1},{1,0},{2,3},{3,2},{4,5},{5,4},{6,7},{7,6},{8,9},{9,8},{10,11... | collective-permute-start | bytes 24584 | tf_op jit(solution)/shard_map/ppermute | solution.py:25
  44.0 3.7 %collective-permute-start.16 = (f32[2048]{0:T(1024)S(1)}, f32[2048]{0:T(1024)S(1)}, u32[]{:S(2)}, u32[]{:S(2)}) collective-permute-start(f32[2048]{0:T(1024)S(1)} %log_add_fusion), channel_id=1, source_target_pairs={{0,2},{1,7},{2,0},{3,5},{4,6},{5,3},{6,4},{7,1},{8,10},{9,15},{10,... | collective-permute-start | bytes 24584 | tf_op jit(solution)/shard_map/ppermute | solution.py:54
  45.4 3.7 %collective-permute-start.15 = (f32[2048]{0:T(1024)S(1)}, f32[2048]{0:T(1024)S(1)}, u32[]{:S(2)}, u32[]{:S(2)}) collective-permute-start(f32[2048]{0:T(1024)S(1)} %log_add_fusion), channel_id=1, source_target_pairs={{0,2},{1,5},{2,0},{3,7},{4,6},{5,1},{6,4},{7,3},{8,10},{9,13},{10,... | collective-permute-start | bytes 24584 | tf_op jit(solution)/shard_map/ppermute | solution.py:54
  49.1 1.6 %collective-permute-start.17 = (f32[2048]{0:T(1024)S(1)}, f32[2048]{0:T(1024)S(1)}, u32[]{:S(2)}, u32[]{:S(2)}) collective-permute-start(f32[2048]{0:T(1024)S(1)} %add_select_fusion), channel_id=1, source_target_pairs={{0,1},{1,0},{2,3},{3,2},{4,5},{5,4},{6,7},{7,6},{8,9},{9,8},{10,11... | collective-permute-start | bytes 24584 | tf_op jit(solution)/shard_map/ppermute | solution.py:25
  51.1 4.0 %copy-start = (bf16[2048,1024]{1,0:T(8,128)(2,1)S(1)}, bf16[2048,1024]{1,0:T(8,128)(2,1)}, u32[]{:S(2)}) copy-start(bf16[2048,1024]{1,0:T(8,128)(2,1)} %embeddings.1) | copy-start | bytes 12582916
  52.0 5.1 %collective-permute-start.19 = (f32[512]{0:T(512)S(1)}, f32[512]{0:T(512)S(1)}, u32[]{:S(2)}, u32[]{:S(2)}) collective-permute-start(f32[512]{0:T(512)S(1)} %log_add_fusion.11), channel_id=1, source_target_pairs={{0,16},{8,24},{16,0},{24,8},{1,17},{9,25},{17,1},{25,9},{2,18},{10... | collective-permute-start | bytes 6152 | tf_op jit(solution)/shard_map/ppermute | solution.py:25
  53.6 3.6 %collective-permute-start.18 = (f32[512]{0:T(512)S(1)}, f32[512]{0:T(512)S(1)}, u32[]{:S(2)}, u32[]{:S(2)}) collective-permute-start(f32[512]{0:T(512)S(1)} %log_add_fusion.11), channel_id=1, source_target_pairs={{0,8},{8,0},{16,24},{24,16},{1,9},{9,1},{17,25},{25,17},{2,10},{10... | collective-permute-start | bytes 6152 | tf_op jit(solution)/shard_map/ppermute | solution.py:25
  55.8 7.2 %collective-permute-start.20 = (bf16[128,512]{1,0:T(8,128)(2,1)S(1)}, bf16[128,512]{1,0:T(8,128)(2,1)S(1)}, u32[]{:S(2)}, u32[]{:S(2)}) collective-permute-start(bf16[128,512]{1,0:T(8,128)(2,1)S(1)} %get-tuple-element.38), channel_id=1, source_target_pairs={{0,8},{8,0},{16,24},{24,16},{1,9},{9,1},{17,25},{25,17},{2,10},{10... | collective-permute-start | bytes 393224 | tf_op jit(solution)/shard_map/ppermute | solution.py:25
  56.4 6.6 %collective-permute-start.21 = (bf16[128,512]{1,0:T(8,128)(2,1)S(1)}, bf16[128,512]{1,0:T(8,128)(2,1)S(1)}, u32[]{:S(2)}, u32[]{:S(2)}) collective-permute-start(bf16[128,512]{1,0:T(8,128)(2,1)S(1)} %get-tuple-element.39), channel_id=1, source_target_pairs={{0,16},{8,24},{16,0},{24,8},{1,17},{9,25},{17,1},{25,9},{2,18},{10... | collective-permute-start | bytes 393224 | tf_op jit(solution)/shard_map/ppermute | solution.py:25
  57.3 12.5 %collective-permute-start.25 = (f32[512]{0:T(512)S(1)}, f32[512]{0:T(512)S(1)}, u32[]{:S(2)}, u32[]{:S(2)}) collective-permute-start(f32[512]{0:T(512)S(1)} %get-tuple-element.48), channel_id=1, source_target_pairs={{0,16},{8,24},{16,0},{24,8},{1,17},{9,25},{17,1},{25,9},{2,18},{10... | collective-permute-start | bytes 6152 | tf_op jit(solution)/shard_map/ppermute | solution.py:25
  60.8 5.5 %collective-permute-start.22 = (bf16[128,512]{1,0:T(8,128)(2,1)S(1)}, bf16[128,512]{1,0:T(8,128)(2,1)S(1)}, u32[]{:S(2)}, u32[]{:S(2)}) collective-permute-start(bf16[128,512]{1,0:T(8,128)(2,1)S(1)} %get-tuple-element.41), channel_id=1, source_target_pairs={{0,8},{8,0},{16,24},{24,16},{1,9},{9,1},{17,25},{25,17},{2,10},{10... | collective-permute-start | bytes 393224 | tf_op jit(solution)/shard_map/ppermute | solution.py:25
  62.3 5.5 %collective-permute-start.26 = (bf16[128,512]{1,0:T(8,128)(2,1)S(1)}, bf16[128,512]{1,0:T(8,128)(2,1)S(1)}, u32[]{:S(2)}, u32[]{:S(2)}) collective-permute-start(bf16[128,512]{1,0:T(8,128)(2,1)S(1)} %get-tuple-element.45), channel_id=1, source_target_pairs={{0,16},{8,24},{16,0},{24,8},{1,17},{9,25},{17,1},{25,9},{2,18},{10... | collective-permute-start | bytes 393224 | tf_op jit(solution)/shard_map/ppermute | solution.py:25
  63.2 7.1 %collective-permute-start.24 = (bf16[128,512]{1,0:T(8,128)(2,1)S(1)}, bf16[128,512]{1,0:T(8,128)(2,1)S(1)}, u32[]{:S(2)}, u32[]{:S(2)}) collective-permute-start(bf16[128,512]{1,0:T(8,128)(2,1)S(1)} %get-tuple-element.43), channel_id=1, source_target_pairs={{0,16},{8,24},{16,0},{24,8},{1,17},{9,25},{17,1},{25,9},{2,18},{10... | collective-permute-start | bytes 393224 | tf_op jit(solution)/shard_map/ppermute | solution.py:25
  64.5 6.4 %collective-permute-start.27 = (bf16[128,512]{1,0:T(8,128)(2,1)S(1)}, bf16[128,512]{1,0:T(8,128)(2,1)S(1)}, u32[]{:S(2)}, u32[]{:S(2)}) collective-permute-start(bf16[128,512]{1,0:T(8,128)(2,1)S(1)} %get-tuple-element.44), channel_id=1, source_target_pairs={{0,8},{8,0},{16,24},{24,16},{1,9},{9,1},{17,25},{25,17},{2,10},{10... | collective-permute-start | bytes 393224 | tf_op jit(solution)/shard_map/ppermute | solution.py:25
  67.9 5.6 %collective-permute-start.29 = (bf16[128,512]{1,0:T(8,128)(2,1)S(1)}, bf16[128,512]{1,0:T(8,128)(2,1)S(1)}, u32[]{:S(2)}, u32[]{:S(2)}) collective-permute-start(bf16[128,512]{1,0:T(8,128)(2,1)S(1)} %get-tuple-element.61), channel_id=1, source_target_pairs={{0,8},{8,0},{16,24},{24,16},{1,9},{9,1},{17,25},{25,17},{2,10},{10... | collective-permute-start | bytes 393224 | tf_op jit(solution)/shard_map/ppermute | solution.py:25
  68.9 5.6 %collective-permute-start.23 = (bf16[128,512]{1,0:T(8,128)(2,1)S(1)}, bf16[128,512]{1,0:T(8,128)(2,1)S(1)}, u32[]{:S(2)}, u32[]{:S(2)}) collective-permute-start(bf16[128,512]{1,0:T(8,128)(2,1)S(1)} %get-tuple-element.62), channel_id=1, source_target_pairs={{0,16},{8,24},{16,0},{24,8},{1,17},{9,25},{17,1},{25,9},{2,18},{10... | collective-permute-start | bytes 393224 | tf_op jit(solution)/shard_map/ppermute | solution.py:25
  71.0 5.7 %collective-permute-start.31 = (bf16[128,512]{1,0:T(8,128)(2,1)S(1)}, bf16[128,512]{1,0:T(8,128)(2,1)S(1)}, u32[]{:S(2)}, u32[]{:S(2)}) collective-permute-start(bf16[128,512]{1,0:T(8,128)(2,1)S(1)} %fusion.15.refs_2_), channel_id=1, source_target_pairs={{0,8},{8,0},{16,24},{24,16},{1,9},{9,1},{17,25},{25,17},{2,10},{10... | collective-permute-start | bytes 393224 | tf_op jit(solution)/shard_map/ppermute | solution.py:25
  71.6 5.1 %collective-permute-start.32 = (bf16[128,512]{1,0:T(8,128)(2,1)S(1)}, bf16[128,512]{1,0:T(8,128)(2,1)S(1)}, u32[]{:S(2)}, u32[]{:S(2)}) collective-permute-start(bf16[128,512]{1,0:T(8,128)(2,1)S(1)} %fusion.19.refs_3_), channel_id=1, source_target_pairs={{0,16},{8,24},{16,0},{24,8},{1,17},{9,25},{17,1},{25,9},{2,18},{10... | collective-permute-start | bytes 393224 | tf_op jit(solution)/shard_map/ppermute | solution.py:25
  73.6 5.0 %collective-permute-start.30 = (bf16[128,512]{1,0:T(8,128)(2,1)S(1)}, bf16[128,512]{1,0:T(8,128)(2,1)S(1)}, u32[]{:S(2)}, u32[]{:S(2)}) collective-permute-start(bf16[128,512]{1,0:T(8,128)(2,1)S(1)} %fusion.23.refs_3_), channel_id=1, source_target_pairs={{0,16},{8,24},{16,0},{24,8},{1,17},{9,25},{17,1},{25,9},{2,18},{10... | collective-permute-start | bytes 393224 | tf_op jit(solution)/shard_map/ppermute | solution.py:25
  74.6 5.0 %collective-permute-start.28 = (bf16[128,512]{1,0:T(8,128)(2,1)S(1)}, bf16[128,512]{1,0:T(8,128)(2,1)S(1)}, u32[]{:S(2)}, u32[]{:S(2)}) collective-permute-start(bf16[128,512]{1,0:T(8,128)(2,1)S(1)} %fusion.11.refs_2_), channel_id=1, source_target_pairs={{0,8},{8,0},{16,24},{24,16},{1,9},{9,1},{17,25},{25,17},{2,10},{10... | collective-permute-start | bytes 393224 | tf_op jit(solution)/shard_map/ppermute | solution.py:25

commit v2 on v0

--- a/solution.py
+++ b/solution.py
@@ -11,6 +11,7 @@
 ITERS = 3
 CHUNKS = 2
 LANES = 128
+EXTRA = 16
 VMEM_BYTES = 24 * 2**20
 
 
@@ -150,7 +151,7 @@
     )(plan, embeddings, mass.reshape(count // LANES, LANES), *rest)
 
 
-def last_sum(plan, part, mass, row_now, embeddings, chosen, orders, aligned):
+def last_sum_by_vectors(plan, part, mass, row_now, embeddings, chosen, orders, aligned):
     quarter = part.shape[0] // 4
     first, second = orders[0][:2]
     partners = {bit: aligned(flipped(part, "dp", 1 << bit), 1 << bit) for bit in (first, second)}
@@ -229,6 +230,193 @@
     return outs[0], row_out.reshape(row_now.shape), jnp.concatenate(halves)
 
 
+def parts_of(lines):
+    row = lax.broadcasted_iota(jnp.int32, (EXTRA, LANES), 0)
+    rows = jnp.zeros((EXTRA, LANES), jnp.float32)
+    for index, line in enumerate(lines):
+        for part in range(3):
+            rounded = line.astype(jnp.bfloat16).astype(jnp.float32)
+            rows = jnp.where(row == 3 * index + part, rounded, rows)
+            line = line - rounded
+    return rows.astype(jnp.bfloat16)
+
+
+def lines_of(message, count):
+    rows = message[pl.ds(message.shape[0] - EXTRA, EXTRA), pl.ds(0, LANES)].astype(jnp.float32)
+    return [(rows[k:k + 1] + rows[k + 1:k + 2]) + rows[k + 2:k + 3] for k in range(0, 3 * count, 3)]
+
+
+def put(message, values, lines):
+    quarter, width = values.shape
+    message[pl.ds(0, quarter), :] = values.astype(message.dtype)
+    if lines:
+        message[pl.ds(quarter, EXTRA), pl.ds(0, LANES)] = parts_of(lines)
+        message[pl.ds(quarter, EXTRA), pl.ds(LANES, width - LANES)] = jnp.zeros((EXTRA, width - LANES), message.dtype)
+
+
+def columns_of(lines):
+    return jnp.concatenate([column(line) for line in lines], axis=0)
+
+
+def read(ref, start, count):
+    return [ref[pl.ds(start + k, 1), :] for k in range(count)]
+
+
+def write(ref, start, lines):
+    for k, line in enumerate(lines):
+        ref[pl.ds(start + k, 1), :] = line
+
+
+def joined(first, second):
+    whole = [lse(a, b) for a, b in zip(first, second)]
+    return whole, [jnp.exp(a - b) for a, b in zip(first, whole)], [jnp.exp(a - b) for a, b in zip(second, whole)]
+
+
+def sent_kernel(plan, embeddings, mass, part, *sent):
+    quarter = plan.shape[0] // 4
+    count = quarter // LANES
+    width = embeddings.shape[1] // CHUNKS
+    sums = jnp.dot(plan[pl.ds(0, 2 * quarter), :], embeddings[...], preferred_element_type=jnp.float32)
+    for k in range(2):
+        values = sums[k * quarter:(k + 1) * quarter] / columns_of(read(mass, k * count, count))
+        for chunk in range(CHUNKS):
+            lines = read(part, k * count, count) if chunk == 0 else []
+            put(sent[2 * chunk + k], values[:, chunk * width:(chunk + 1) * width], lines)
+
+
+def kept_kernel(plan, embeddings, mass, row, kept, row_out):
+    quarter = plan.shape[0] // 4
+    count = quarter // LANES
+    row_out[...] = row[...]
+    sums = jnp.dot(plan[pl.ds(2 * quarter, 2 * quarter), :], embeddings[...], preferred_element_type=jnp.float32)
+    for k in range(2):
+        kept[k] = sums[k * quarter:(k + 1) * quarter] / columns_of(read(mass, (2 + k) * count, count))
+
+
+def pair_kernel(chunk, kept, lower, upper, known, out_lower, out_upper, *weights_out):
+    quarter = kept.shape[1]
+    count = quarter // LANES
+    for k, (got, out) in enumerate(((lower, out_lower), (upper, out_upper))):
+        if chunk == 0:
+            pair, own, other = joined(read(known, (2 + k) * count, count), lines_of(got, count))
+            write(weights_out[0], 2 * k * count, own + other)
+        else:
+            pair = []
+            own, other = read(known, 2 * k * count, count), read(known, (2 * k + 1) * count, count)
+        width = got.shape[1]
+        values = kept[k, :, pl.ds(chunk * width, width)] * columns_of(own)
+        put(out, values + got[pl.ds(0, quarter), :].astype(jnp.float32) * columns_of(other), pair)
+
+
+def whole_kernel(chunk, bit, quarter, mine, theirs, *rest):
+    count = quarter // LANES
+    up = lax.axis_index("dp") >> bit & 1 == 1
+    if chunk == 0:
+        out, weights_out = rest
+        own, other = lines_of(mine, count), lines_of(theirs, count)
+        lower = [jnp.where(up, b, a) for a, b in zip(own, other)]
+        upper = [jnp.where(up, a, b) for a, b in zip(own, other)]
+        whole, low, high = joined(lower, upper)
+        write(weights_out, 0, low + high)
+    else:
+        known, out = rest
+        whole = []
+        low, high = read(known, 0, count), read(known, count, count)
+    own, other = (ref[pl.ds(0, quarter), :].astype(jnp.float32) for ref in (mine, theirs))
+    values = jnp.where(up, other, own) * columns_of(low) + jnp.where(up, own, other) * columns_of(high)
+    put(out, values, whole)
+
+
+def place_first_kernel(orders, log_k, lower_sent, upper_sent, lower_kept, upper_kept, out, col_out, sent):
+    blocks = (lower_sent, upper_sent, lower_kept, upper_kept)
+    quarter = blocks[0].shape[0] - EXTRA
+    count = quarter // LANES
+    copies = []
+    for k, start in enumerate(quarter_places(orders, quarter)):
+        rows = pl.ds(pl.multiple_of(start, LANES), quarter)
+        source = blocks[k].at[pl.ds(0, quarter)]
+        copies.append(pltpu.make_async_copy(source, out.at[rows, pl.ds(0, blocks[k].shape[1])], sent.at[k]))
+        copies[-1].start()
+    for block, start in zip(blocks, quarter_places(orders, count)):
+        write(col_out, start, [-log_k - line for line in lines_of(block, count)])
+    for copy in copies:
+        copy.wait()
+
+
+def last_sum(plan, part, mass, row_now, embeddings, log_k, orders):
+    columns, rows_here = plan.shape
+    depth = embeddings.shape[1]
+    quarter = columns // 4
+    width = depth // CHUNKS
+    lines = quarter // LANES
+    f32 = jnp.float32
+    vmem = pl.BlockSpec(memory_space=pltpu.VMEM)
+
+    def call(kernel, operands, outs, specs=None, flops=0, **options):
+        return pl.pallas_call(
+            kernel,
+            out_shape=outs,
+            in_specs=[vmem] * len(operands),
+            out_specs=specs or [vmem] * len(outs),
+            compiler_params=pltpu.CompilerParams(vmem_limit_bytes=VMEM_BYTES),
+            cost_estimate=pl.CostEstimate(flops=flops, bytes_accessed=columns * depth, transcendentals=0),
+            **options,
+        )(*operands)
+
+    def message(chunk):
+        return jax.ShapeDtypeStruct((quarter + (EXTRA if chunk == 0 else 0), width), jnp.bfloat16)
+
+    def table(count):
+        return jax.ShapeDtypeStruct((count * lines, LANES), f32)
+
+    mass, part = mass.reshape(table(4).shape), part.reshape(table(4).shape)
+    flops = columns * rows_here * depth
+    chunks = range(CHUNKS)
+    sent = call(sent_kernel, [plan, embeddings, mass, part], [message(chunk) for chunk in chunks for _ in range(2)], flops=flops)
+    got = [flipped(sent[2 * chunk + k], "dp", 1 << orders[k][0]) for chunk in chunks for k in range(2)]
+    row = row_now[None, :]
+    kept, row_out = call(
+        kept_kernel,
+        [plan, embeddings, mass, row],
+        [jax.ShapeDtypeStruct((2, quarter, depth), f32), jax.ShapeDtypeStruct(row.shape, f32)],
+        specs=[vmem, pl.BlockSpec(row.shape, lambda: (0, 0))],
+        flops=flops,
+    )
+    pairs = []
+    known = part
+    for chunk in chunks:
+        outs = [message(chunk)] * 2 + ([table(4)] if chunk == 0 else [])
+        results = call(functools.partial(pair_kernel, chunk), [kept, got[2 * chunk], got[2 * chunk + 1], known], outs)
+        both = results[:2]
+        known = results[2] if chunk == 0 else known
+        pairs += both
+    known = [None, None]
+    out = None
+    for chunk in chunks:
+        dones = []
+        for k, order in enumerate(orders):
+            mine = pairs[2 * chunk + k]
+            theirs = flipped(mine, "dp", 1 << order[1])
+            kernel = functools.partial(whole_kernel, chunk, order[1], quarter)
+            if chunk == 0:
+                done, known[k] = call(kernel, [mine, theirs], [message(chunk), table(2)])
+            else:
+                done, = call(kernel, [mine, theirs, known[k]], [message(chunk)])
+            dones.append(done)
+        blocks = [flipped(done, "dp", 1 << order[0]) for done, order in zip(dones, orders)] + dones
+        if chunk == 0:
+            out, col_out = call(
+                functools.partial(place_first_kernel, orders, log_k),
+                blocks,
+                [jax.ShapeDtypeStruct((columns, depth), jnp.bfloat16), table(4)],
+                specs=[pl.BlockSpec(memory_space=pl.ANY), pl.BlockSpec(table(4).shape, lambda: (0, 0))],
+                scratch_shapes=[pltpu.SemaphoreType.DMA((4,))],
+            )
+        else:
+            out = placed(chunk, orders, blocks, (columns, depth), [out])
+    return out, row_out.reshape(row_now.shape), col_out.reshape(columns)
+
+
 def on_device(embeddings, centroids, col_start):
     rows_here = embeddings.shape[0]
     cent_here = centroids.shape[0]
@@ -277,7 +465,9 @@
         if step_index < ITERS - 1:
             col_now = -math.log(k_total) - lse_over_dp(part, aligned)
     plan = terms.astype(jnp.bfloat16)
-    new_centroids, row_out, whole = last_sum(plan, part, mass, row_now, embeddings, chosen, orders, aligned)
+    if len(bits) == 2:
+        return last_sum(plan, part, mass, row_now, embeddings, math.log(k_total), orders)
+    new_centroids, row_out, whole = last_sum_by_vectors(plan, part, mass, row_now, embeddings, chosen, orders, aligned)
     return new_centroids, row_out, -math.log(k_total) - whole
 
 

time: 79.8 us -> 80.4 us (level)
  starting transfers between devices: 35.4 us -> 29.8 us
  waiting for transfers between devices: 23.5 us -> 28.3 us
  Pallas kernels: 4.52 us -> 6.14 us
  other arithmetic: 10.5 us -> 9.11 us
  local copies, waits for them, and re-layouts: 0.08 us -> 1.32 us
    ppermute x27 -> x24, starting transfers between devices: 28.2 us -> 22.5 us  [flipped(): return lax.ppermute(x, axis, [(k, k ^ mask) for k in range(size)])]
    ppermute x27 -> x24, waiting for transfers between devices: 15.2 us -> 20.1 us  [flipped(): return lax.ppermute(x, axis, [(k, k ^ mask) for k in range(size)])]
    pallas_call x2 -> x9, Pallas kernels: 2.88 us -> 5.32 us  [call(): pl.pallas_call(kernel, out_shape=outs, in_specs=[vmem] * len(operands), o...]
    unnamed x2, local copies, waits for them, and re-layouts: 0.01 us -> 1.3 us
    pallas_call x2 -> x1, Pallas kernels: 1.64 us -> 0.82 us  [placed(): pl.pallas_call(functools.partial(place_kernel, chunk, orders), out_shape=...]
    select_n x5 -> x2, other arithmetic: 2.11 us -> 2.1 us  [chosen(): return jnp.where(ups[bit].reshape((1,) * yes.ndim), yes, no)]
  transfers between devices with their start and end apart: 33 -> 30, of which waited for: 23 -> 26; matrix products, arithmetic and copies ran while one was open for 2% -> 0% of each run, Pallas kernels for 5% -> 5%
where the time goes in v2:
time: 80.4 us; the launch traced here: 80.1 us
  starting transfers between devices  29.8 us (37%)
  waiting for transfers between devices  28.3 us (35%)
  other arithmetic  9.11 us (11%)
  Pallas kernels  6.14 us (8%)
  matrix products  4.57 us (6%)
  local copies, waits for them, and re-layouts  1.32 us (2%)
  between operations  0.89 us (1%)
    ppermute x24, starting transfers between devices, flipped(): return lax.ppermute(x, axis, [(k, k ^ mask) for k in range(size)])  22.5 us
    ppermute x24, waiting for transfers between devices, flipped(): return lax.ppermute(x, axis, [(k, k ^ mask) for k in range(size)])  20.1 us
    ppermute x6, waiting for transfers between devices, split(): lax.ppermute(value, 'cent', [(k, k ^ (odd_mask if k % 2 else even_mask))...  8.29 us
    ppermute x6, starting transfers between devices, split(): lax.ppermute(value, 'cent', [(k, k ^ (odd_mask if k % 2 else even_mask))...  7.23 us
    pallas_call x9, Pallas kernels, call(): pl.pallas_call(kernel, out_shape=outs, in_specs=[vmem] * len(operands), o...  5.32 us
    dot_general x1, matrix products, on_device(): lax.dot_general(sent_and_kept(centroids), embeddings, (((1,), (1,)), ((),...  4.57 us
    reduce_sum x3, other arithmetic, on_device(): mass = jnp.sum(terms, axis=1)  2.55 us
    reduce_sum x3, other arithmetic, on_device(): part = top + jnp.log(jnp.sum(jnp.exp(shifted - top[None, :]), axis=0))  2.32 us
  transfers between devices with their start and end apart: 30, of which 26 were waited for; matrix products, arithmetic and copies ran while one was open for 0% of the time, Pallas kernels for 5%

profile of v2, /device:TPU:0, one launch (start us, length us, event | category | flops | bytes accessed | tf_op | source)
XLA Modules:
  0.0 80.1 jit_solution(11175373630008739507)
XLA Ops:
  0.6 0.8 %broadcast_select_fusion.7 = (f32[128]{0:T(128)S(1)}, f32[128]{0:T(128)S(1)}, f32[128]{0:T(128)S(1)}, f32[128]{0:T(128)S(1)}) fusion(pred[]{:T(512)} %bitcast.3, f32[512]{0:T(512)} %param.5, pred[]{:T(512)} %bitcast.4), kind=kLoop, calls=%fused_computation.91 | loop fusion | flops 512 | bytes 4098 | tf_op jit(solution)/shard_map/jit(_where)/select_n | solution.py:435
  1.5 1.3 %broadcast_select_fusion.3 = (bf16[128,1024]{1,0:T(8,128)(2,1)S(1)}, bf16[128,1024]{1,0:T(8,128)(2,1)S(1)}, bf16[128,1024]{1,0:T(8,128)(2,1)S(1)}, bf16[128,1024]{1,0:T(8,128)(2,1)S(1)}) fusion(pred[]{:T(512)} %bitcast.3, bf16[512,1024]{1,0:T(8,128)(2,1)} %param.4, pred[]{:T(512)} %bitcast.4), kind=kLoop, calls=%fused_computation.25 | loop fusion | flops 524288 | bytes 2097154 | tf_op jit(solution)/shard_map/jit(_where)/select_n | solution.py:435
  2.8 4.6 %add_reduce_fusion.5 = (f32[2048]{0:T(1024)S(1)}, f32[512,2048]{1,0:T(8,128)S(1)}) fusion(f32[512]{0:T(512)S(1)} %pad_maximum_fusion, bf16[2048,1024]{1,0:T(8,128)(2,1)} %embeddings.1, bf16[128,1024]{1,0:T(8,128)(2,1)S(1)} %get-tuple-element.51, bf16[128,1024]{1,0:T(8,128)(2,1)S(1)} %get-tuple-element.52, bf16[128,1024]{1,0:T(8,128)(2,1)S(1)} %get-tuple-element.50, ...), kind=kOutput, calls=%fused_computation.11 | convolution fusion | flops 2154821632 | bytes 9447424 | tf_op jit(solution)/shard_map/dot_general | solution.py:451
  7.3 0.8 exponential_reduce_fusion.4
  8.7 0.8 %collective-permute-done = f32[2048]{0:T(1024)S(1)} collective-permute-done((f32[2048]{0:T(1024)S(1)}, f32[2048]{0:T(1024)S(1)}, u32[]{:S(2)}, u32[]{:S(2)}) %collective-permute-start) | collective-permute-done | bytes 8224 | tf_op jit(solution)/shard_map/ppermute | solution.py:26
  9.5 3.0 %collective-permute-start.2 = (f32[2048]{0:T(1024)S(1)}, f32[2048]{0:T(1024)S(1)}, u32[]{:S(2)}, u32[]{:S(2)}) collective-permute-start(f32[2048]{0:T(1024)S(1)} %log_add_fusion.4), channel_id=1, source_target_pairs={{0,2},{1,7},{2,0},{3,5},{4,6},{5,3},{6,4},{7,1},{8,10},{9,15},{10,... | collective-permute-start | bytes 24584 | tf_op jit(solution)/shard_map/ppermute | solution.py:55
  12.6 1.6 %collective-permute-done.2 = f32[2048]{0:T(1024)S(1)} collective-permute-done((f32[2048]{0:T(1024)S(1)}, f32[2048]{0:T(1024)S(1)}, u32[]{:S(2)}, u32[]{:S(2)}) %collective-permute-start.2) | collective-permute-done | bytes 8224 | tf_op jit(solution)/shard_map/ppermute | solution.py:55
  14.1 2.0 %collective-permute-done.1 = f32[2048]{0:T(1024)S(1)} collective-permute-done((f32[2048]{0:T(1024)S(1)}, f32[2048]{0:T(1024)S(1)}, u32[]{:S(2)}, u32[]{:S(2)}) %collective-permute-start.1) | collective-permute-done | bytes 8224 | tf_op jit(solution)/shard_map/ppermute | solution.py:55
  16.2 1.7 %collective-permute-start.3 = (f32[2048]{0:T(1024)S(1)}, f32[2048]{0:T(1024)S(1)}, u32[]{:S(2)}, u32[]{:S(2)}) collective-permute-start(f32[2048]{0:T(1024)S(1)} %add_select_fusion.2), channel_id=1, source_target_pairs={{0,1},{1,0},{2,3},{3,2},{4,5},{5,4},{6,7},{7,6},{8,9},{9,8},{10,11... | collective-permute-start | bytes 24584 | tf_op jit(solution)/shard_map/ppermute | solution.py:26
  17.9 0.8 %collective-permute-done.3 = f32[2048]{0:T(1024)S(1)} collective-permute-done((f32[2048]{0:T(1024)S(1)}, f32[2048]{0:T(1024)S(1)}, u32[]{:S(2)}, u32[]{:S(2)}) %collective-permute-start.3) | collective-permute-done | bytes 8224 | tf_op jit(solution)/shard_map/ppermute | solution.py:26
  19.1 0.8 %exponential_reduce_fusion.3 = f32[512]{0:T(512)S(1)} fusion(f32[512,2048]{1,0:T(8,128)S(1)} %get-tuple-element.78, f32[512]{0:T(512)S(1)} %add_reduce_fusion.4, f32[2048]{0:T(1024)S(1)} %add_subtract_fusion.2), kind=kLoop, calls=%fused_computation.4 | loop fusion | flops 3145216 | bytes 4206592 | tf_op jit(solution)/shard_map/reduce_sum | solution.py:463
  19.9 2.5 %collective-permute-start.4 = (f32[512]{0:T(512)S(1)}, f32[512]{0:T(512)S(1)}, u32[]{:S(2)}, u32[]{:S(2)}) collective-permute-start(f32[512]{0:T(512)S(1)} %log_add_fusion.9), channel_id=1, source_target_pairs={{0,24},{8,16},{16,8},{24,0},{1,25},{9,17},{17,9},{25,1},{2,26},{10... | collective-permute-start | bytes 6152 | tf_op jit(solution)/shard_map/ppermute | solution.py:26
  23.5 1.0 %collective-permute-done.4 = f32[512]{0:T(512)S(1)} collective-permute-done((f32[512]{0:T(512)S(1)}, f32[512]{0:T(512)S(1)}, u32[]{:S(2)}, u32[]{:S(2)}) %collective-permute-start.4) | collective-permute-done | bytes 2080 | tf_op jit(solution)/shard_map/ppermute | solution.py:26
  24.5 1.5 %collective-permute-done.5 = f32[512]{0:T(512)S(1)} collective-permute-done((f32[512]{0:T(512)S(1)}, f32[512]{0:T(512)S(1)}, u32[]{:S(2)}, u32[]{:S(2)}) %collective-permute-start.5) | collective-permute-done | bytes 2080 | tf_op jit(solution)/shard_map/ppermute | solution.py:26
  27.0 0.8 exponential_reduce_fusion.2
  27.8 1.2 %collective-permute-done.7 = f32[2048]{0:T(1024)S(1)} collective-permute-done((f32[2048]{0:T(1024)S(1)}, f32[2048]{0:T(1024)S(1)}, u32[]{:S(2)}, u32[]{:S(2)}) %collective-permute-start.7) | collective-permute-done | bytes 8224 | tf_op jit(solution)/shard_map/ppermute | solution.py:26
  29.1 2.0 %collective-permute-start.8 = (f32[2048]{0:T(1024)S(1)}, f32[2048]{0:T(1024)S(1)}, u32[]{:S(2)}, u32[]{:S(2)}) collective-permute-start(f32[2048]{0:T(1024)S(1)} %log_add_fusion.2), channel_id=1, source_target_pairs={{0,2},{1,5},{2,0},{3,7},{4,6},{5,1},{6,4},{7,3},{8,10},{9,13},{10,... | collective-permute-start | bytes 24584 | tf_op jit(solution)/shard_map/ppermute | solution.py:55
  31.1 1.6 %collective-permute-done.9 = f32[2048]{0:T(1024)S(1)} collective-permute-done((f32[2048]{0:T(1024)S(1)}, f32[2048]{0:T(1024)S(1)}, u32[]{:S(2)}, u32[]{:S(2)}) %collective-permute-start.9) | collective-permute-done | bytes 8224 | tf_op jit(solution)/shard_map/ppermute | solution.py:55
  32.8 1.0 %collective-permute-start.10 = (f32[2048]{0:T(1024)S(1)}, f32[2048]{0:T(1024)S(1)}, u32[]{:S(2)}, u32[]{:S(2)}) collective-permute-start(f32[2048]{0:T(1024)S(1)} %add_select_fusion.1), channel_id=1, source_target_pairs={{0,1},{1,0},{2,3},{3,2},{4,5},{5,4},{6,7},{7,6},{8,9},{9,8},{10,11... | collective-permute-start | bytes 24584 | tf_op jit(solution)/shard_map/ppermute | solution.py:26
  33.8 0.8 %collective-permute-done.10 = f32[2048]{0:T(1024)S(1)} collective-permute-done((f32[2048]{0:T(1024)S(1)}, f32[2048]{0:T(1024)S(1)}, u32[]{:S(2)}, u32[]{:S(2)}) %collective-permute-start.10) | collective-permute-done | bytes 8224 | tf_op jit(solution)/shard_map/ppermute | solution.py:26
  35.0 0.8 %exponential_reduce_fusion.1 = f32[512]{0:T(512)S(1)} fusion(f32[512,2048]{1,0:T(8,128)S(1)} %get-tuple-element.78, f32[512]{0:T(512)S(1)} %add_reduce_fusion.2, f32[2048]{0:T(1024)S(1)} %add_subtract_fusion.1), kind=kLoop, calls=%fused_computation.2 | loop fusion | flops 3145216 | bytes 4206592 | tf_op jit(solution)/shard_map/reduce_sum | solution.py:463
  35.9 1.6 %collective-permute-start.11 = (f32[512]{0:T(512)S(1)}, f32[512]{0:T(512)S(1)}, u32[]{:S(2)}, u32[]{:S(2)}) collective-permute-start(f32[512]{0:T(512)S(1)} %log_add_fusion.7), channel_id=1, source_target_pairs={{0,24},{8,16},{16,8},{24,0},{1,25},{9,17},{17,9},{25,1},{2,26},{10... | collective-permute-start | bytes 6152 | tf_op jit(solution)/shard_map/ppermute | solution.py:26
  37.9 1.5 %collective-permute-start.13 = (f32[512]{0:T(512)S(1)}, f32[512]{0:T(512)S(1)}, u32[]{:S(2)}, u32[]{:S(2)}) collective-permute-start(f32[512]{0:T(512)S(1)} %log_add_fusion.7), channel_id=1, source_target_pairs={{0,8},{8,0},{16,24},{24,16},{1,9},{9,1},{17,25},{25,17},{2,10},{10... | collective-permute-start | bytes 6152 | tf_op jit(solution)/shard_map/ppermute | solution.py:26
  39.4 1.0 %collective-permute-done.11 = f32[512]{0:T(512)S(1)} collective-permute-done((f32[512]{0:T(512)S(1)}, f32[512]{0:T(512)S(1)}, u32[]{:S(2)}, u32[]{:S(2)}) %collective-permute-start.11) | collective-permute-done | bytes 2080 | tf_op jit(solution)/shard_map/ppermute | solution.py:26
  41.9 0.8 exponential_reduce_fusion
  42.8 1.2 %collective-permute-done.14 = f32[2048]{0:T(1024)S(1)} collective-permute-done((f32[2048]{0:T(1024)S(1)}, f32[2048]{0:T(1024)S(1)}, u32[]{:S(2)}, u32[]{:S(2)}) %collective-permute-start.14) | collective-permute-done | bytes 8224 | tf_op jit(solution)/shard_map/ppermute | solution.py:26
  44.0 1.4 %collective-permute-start.16 = (f32[2048]{0:T(1024)S(1)}, f32[2048]{0:T(1024)S(1)}, u32[]{:S(2)}, u32[]{:S(2)}) collective-permute-start(f32[2048]{0:T(1024)S(1)} %log_add_fusion), channel_id=1, source_target_pairs={{0,2},{1,7},{2,0},{3,5},{4,6},{5,3},{6,4},{7,1},{8,10},{9,15},{10,... | collective-permute-start | bytes 24584 | tf_op jit(solution)/shard_map/ppermute | solution.py:55
  46.1 1.6 %collective-permute-done.16 = f32[2048]{0:T(1024)S(1)} collective-permute-done((f32[2048]{0:T(1024)S(1)}, f32[2048]{0:T(1024)S(1)}, u32[]{:S(2)}, u32[]{:S(2)}) %collective-permute-start.16) | collective-permute-done | bytes 8224 | tf_op jit(solution)/shard_map/ppermute | solution.py:55
  47.7 1.4 %collective-permute-done.15 = f32[2048]{0:T(1024)S(1)} collective-permute-done((f32[2048]{0:T(1024)S(1)}, f32[2048]{0:T(1024)S(1)}, u32[]{:S(2)}, u32[]{:S(2)}) %collective-permute-start.15) | collective-permute-done | bytes 8224 | tf_op jit(solution)/shard_map/ppermute | solution.py:55
  49.1 0.8 collective-permute-start.17
  49.9 0.8 %collective-permute-done.17 = f32[2048]{0:T(1024)S(1)} collective-permute-done((f32[2048]{0:T(1024)S(1)}, f32[2048]{0:T(1024)S(1)}, u32[]{:S(2)}, u32[]{:S(2)}) %collective-permute-start.17) | collective-permute-done | bytes 8224 | tf_op jit(solution)/shard_map/ppermute | solution.py:26
  51.1 0.9 %fusion = (f32[512]{0:T(512)S(1)}, bf16[512,2048]{1,0:T(8,128)(2,1)S(1)}) fusion(f32[512,2048]{1,0:T(8,128)S(1)} %get-tuple-element.78, f32[512]{0:T(512)S(1)} %add_reduce_fusion, f32[2048]{0:T(1024)S(1)} %add_subtract_fusion), kind=kLoop, calls=%fused_computation.12 | loop fusion | flops 4193792 | bytes 6303744 | tf_op jit(solution)/shard_map/reduce_sum | solution.py:463
  52.0 1.3 %copy-done = bf16[2048,1024]{1,0:T(8,128)(2,1)S(1)} copy-done((bf16[2048,1024]{1,0:T(8,128)(2,1)S(1)}, bf16[2048,1024]{1,0:T(8,128)(2,1)}, u32[]{:S(2)}) %copy-start) | copy-done | bytes 4194328
  53.3 1.2 %shard_map.59 = (bf16[144,512]{1,0:T(8,128)(2,1)S(1)}, bf16[144,512]{1,0:T(8,128)(2,1)S(1)}, bf16[128,512]{1,0:T(8,128)(2,1)S(1)}, bf16[128,512]{1,0:T(8,128)(2,1)S(1)}) custom-call(bf16[512,2048]{1,0:T(8,128)(2,1)S(1)} %get-tuple-element.48.plan, bf16[2048,1024]{1,0:T(8,128)(2,1)S(1)} %copy-done, f32[4,128]{1,0:T(4,128)S(1)} %bitcast.15, ...), custom_call_target="tpu_custom_call" | custom-call | flops 1073741824 | bytes 524288 | tf_op jit(solution)/shard_map/pallas_call | solution.py:356
  54.6 1.6 %collective-permute-start.20 = (bf16[144,512]{1,0:T(8,128)(2,1)S(1)}, bf16[144,512]{1,0:T(8,128)(2,1)S(1)}, u32[]{:S(2)}, u32[]{:S(2)}) collective-permute-start(bf16[144,512]{1,0:T(8,128)(2,1)S(1)} %get-tuple-element.33), channel_id=1, source_target_pairs={{0,8},{8,0},{16,24},{24,16},{1,9},{9,1},{17,25},{25,17},{2,10},{10... | collective-permute-start | bytes 442376 | tf_op jit(solution)/shard_map/ppermute | solution.py:26
  56.1 1.5 %collective-permute-start.21 = (bf16[144,512]{1,0:T(8,128)(2,1)S(1)}, bf16[144,512]{1,0:T(8,128)(2,1)S(1)}, u32[]{:S(2)}, u32[]{:S(2)}) collective-permute-start(bf16[144,512]{1,0:T(8,128)(2,1)S(1)} %get-tuple-element.34), channel_id=1, source_target_pairs={{0,16},{8,24},{16,0},{24,8},{1,17},{9,25},{17,1},{25,9},{2,18},{10... | collective-permute-start | bytes 442376 | tf_op jit(solution)/shard_map/ppermute | solution.py:26
  58.7 1.7 %shard_map.58 = (f32[2,128,1024]{2,1,0:T(8,128)S(1)}, f32[1,2048]{1,0:T(1,128)}) custom-call(bf16[512,2048]{1,0:T(8,128)(2,1)S(1)} %get-tuple-element.48.plan, bf16[2048,1024]{1,0:T(8,128)(2,1)S(1)} %copy-done, f32[4,128]{1,0:T(4,128)S(1)} %bitcast.16, f32[1,2048]{1,0:T(1,128)S(1)} %bitcast.14), custom_call_target="tpu_custom_call" | custom-call | flops 1073741824 | bytes 524288 | tf_op jit(solution)/shard_map/pallas_call | solution.py:356
  60.4 0.9 %collective-permute-done.20.lower = bf16[144,512]{1,0:T(8,128)(2,1)S(1)} collective-permute-done((bf16[144,512]{1,0:T(8,128)(2,1)S(1)}, bf16[144,512]{1,0:T(8,128)(2,1)S(1)}, u32[]{:S(2)}, u32[]{:S(2)}) %collective-permute-start.20) | collective-permute-done | bytes 147488 | tf_op jit(solution)/shard_map/ppermute | solution.py:26
  61.3 1.5 %collective-permute-done.21.upper = bf16[144,512]{1,0:T(8,128)(2,1)S(1)} collective-permute-done((bf16[144,512]{1,0:T(8,128)(2,1)S(1)}, bf16[144,512]{1,0:T(8,128)(2,1)S(1)}, u32[]{:S(2)}, u32[]{:S(2)}) %collective-permute-start.21) | collective-permute-done | bytes 147488 | tf_op jit(solution)/shard_map/ppermute | solution.py:26
  63.0 1.6 %collective-permute-start.23 = (bf16[144,512]{1,0:T(8,128)(2,1)S(1)}, bf16[144,512]{1,0:T(8,128)(2,1)S(1)}, u32[]{:S(2)}, u32[]{:S(2)}) collective-permute-start(bf16[144,512]{1,0:T(8,128)(2,1)S(1)} %get-tuple-element.37.mine), channel_id=1, source_target_pairs={{0,16},{8,24},{16,0},{24,8},{1,17},{9,25},{17,1},{25,9},{2,18},{10... | collective-permute-start | bytes 442376 | tf_op jit(solution)/shard_map/ppermute | solution.py:26
  65.6 1.6 %collective-permute-start.22 = (bf16[128,512]{1,0:T(8,128)(2,1)S(1)}, bf16[128,512]{1,0:T(8,128)(2,1)S(1)}, u32[]{:S(2)}, u32[]{:S(2)}) collective-permute-start(bf16[128,512]{1,0:T(8,128)(2,1)S(1)} %get-tuple-element.36.mine), channel_id=1, source_target_pairs={{0,16},{8,24},{16,0},{24,8},{1,17},{9,25},{17,1},{25,9},{2,18},{10... | collective-permute-start | bytes 393224 | tf_op jit(solution)/shard_map/ppermute | solution.py:26
  67.6 2.0 %collective-permute-done.23.theirs = bf16[144,512]{1,0:T(8,128)(2,1)S(1)} collective-permute-done((bf16[144,512]{1,0:T(8,128)(2,1)S(1)}, bf16[144,512]{1,0:T(8,128)(2,1)S(1)}, u32[]{:S(2)}, u32[]{:S(2)}) %collective-permute-start.23) | collective-permute-done | bytes 147488 | tf_op jit(solution)/shard_map/ppermute | solution.py:26
  70.0 1.4 %collective-permute-done.26.theirs = bf16[144,512]{1,0:T(8,128)(2,1)S(1)} collective-permute-done((bf16[144,512]{1,0:T(8,128)(2,1)S(1)}, bf16[144,512]{1,0:T(8,128)(2,1)S(1)}, u32[]{:S(2)}, u32[]{:S(2)}) %collective-permute-start.26) | collective-permute-done | bytes 147488 | tf_op jit(solution)/shard_map/ppermute | solution.py:26
  72.3 1.6 %collective-permute-start.24 = (bf16[128,512]{1,0:T(8,128)(2,1)S(1)}, bf16[128,512]{1,0:T(8,128)(2,1)S(1)}, u32[]{:S(2)}, u32[]{:S(2)}) collective-permute-start(bf16[128,512]{1,0:T(8,128)(2,1)S(1)} %shard_map.63.refs_2_), channel_id=1, source_target_pairs={{0,8},{8,0},{16,24},{24,16},{1,9},{9,1},{17,25},{25,17},{2,10},{10... | collective-permute-start | bytes 393224 | tf_op jit(solution)/shard_map/ppermute | solution.py:26
  74.9 2.1 %collective-permute-done.28.lower_sent = bf16[144,512]{1,0:T(8,128)(2,1)S(1)} collective-permute-done((bf16[144,512]{1,0:T(8,128)(2,1)S(1)}, bf16[144,512]{1,0:T(8,128)(2,1)S(1)}, u32[]{:S(2)}, u32[]{:S(2)}) %collective-permute-start.28) | collective-permute-done | bytes 147488 | tf_op jit(solution)/shard_map/ppermute | solution.py:26
  77.0 1.4 %shard_map.66 = (bf16[512,1024]{1,0:T(8,128)(2,1)}, f32[4,128]{1,0:T(4,128)}) custom-call(bf16[144,512]{1,0:T(8,128)(2,1)S(1)} %collective-permute-done.28.lower_sent, bf16[144,512]{1,0:T(8,128)(2,1)S(1)} %collective-permute-done.29.upper_sent, bf16[144,512]{1,0:T(8,128)(2,1)S(1)} %get-tuple-element.42.lower_kept, ...), custom_call_target="tpu_custom_call" | custom-call | bytes 524288 | tf_op jit(solution)/shard_map/pallas_call | solution.py:356
  78.4 0.9 %collective-permute-done.27.refs_1_ = bf16[128,512]{1,0:T(8,128)(2,1)S(1)} collective-permute-done((bf16[128,512]{1,0:T(8,128)(2,1)S(1)}, bf16[128,512]{1,0:T(8,128)(2,1)S(1)}, u32[]{:S(2)}, u32[]{:S(2)}) %collective-permute-start.27) | collective-permute-done | bytes 131104 | tf_op jit(solution)/shard_map/ppermute | solution.py:26
  79.3 0.8 %shard_map.67 = bf16[512,1024]{1,0:T(8,128)(2,1)} custom-call(bf16[128,512]{1,0:T(8,128)(2,1)S(1)} %collective-permute-done.24.refs_0_, bf16[128,512]{1,0:T(8,128)(2,1)S(1)} %collective-permute-done.27.refs_1_, bf16[128,512]{1,0:T(8,128)(2,1)S(1)} %shard_map.63.refs_2_, bf16[128,512]{1,0:T(8,128)(2,1)S(1)} %shard_map.65.refs_3_, ...), custom_call_target="tpu_custom_call", output_to_operand_aliasing={{}: (4, {})} | custom-call | tf_op jit(solution)/shard_map/pallas_call | solution.py:93
  (64 shorter events, 11.7 us)
Async XLA Ops:
  8.1 1.4 %collective-permute-start = (f32[2048]{0:T(1024)S(1)}, f32[2048]{0:T(1024)S(1)}, u32[]{:S(2)}, u32[]{:S(2)}) collective-permute-start(f32[2048]{0:T(1024)S(1)} %log_add_fusion.5), channel_id=1, source_target_pairs={{0,1},{1,0},{2,3},{3,2},{4,5},{5,4},{6,7},{7,6},{8,9},{9,8},{10,11... | collective-permute-start | bytes 24584 | tf_op jit(solution)/shard_map/ppermute | solution.py:26
  9.5 4.6 %collective-permute-start.2 = (f32[2048]{0:T(1024)S(1)}, f32[2048]{0:T(1024)S(1)}, u32[]{:S(2)}, u32[]{:S(2)}) collective-permute-start(f32[2048]{0:T(1024)S(1)} %log_add_fusion.4), channel_id=1, source_target_pairs={{0,2},{1,7},{2,0},{3,5},{4,6},{5,3},{6,4},{7,1},{8,10},{9,15},{10,... | collective-permute-start | bytes 24584 | tf_op jit(solution)/shard_map/ppermute | solution.py:55
  12.5 3.7 %collective-permute-start.1 = (f32[2048]{0:T(1024)S(1)}, f32[2048]{0:T(1024)S(1)}, u32[]{:S(2)}, u32[]{:S(2)}) collective-permute-start(f32[2048]{0:T(1024)S(1)} %log_add_fusion.4), channel_id=1, source_target_pairs={{0,2},{1,5},{2,0},{3,7},{4,6},{5,1},{6,4},{7,3},{8,10},{9,13},{10,... | collective-permute-start | bytes 24584 | tf_op jit(solution)/shard_map/ppermute | solution.py:55
  16.2 2.6 %collective-permute-start.3 = (f32[2048]{0:T(1024)S(1)}, f32[2048]{0:T(1024)S(1)}, u32[]{:S(2)}, u32[]{:S(2)}) collective-permute-start(f32[2048]{0:T(1024)S(1)} %add_select_fusion.2), channel_id=1, source_target_pairs={{0,1},{1,0},{2,3},{3,2},{4,5},{5,4},{6,7},{7,6},{8,9},{9,8},{10,11... | collective-permute-start | bytes 24584 | tf_op jit(solution)/shard_map/ppermute | solution.py:26
  19.9 4.5 %collective-permute-start.4 = (f32[512]{0:T(512)S(1)}, f32[512]{0:T(512)S(1)}, u32[]{:S(2)}, u32[]{:S(2)}) collective-permute-start(f32[512]{0:T(512)S(1)} %log_add_fusion.9), channel_id=1, source_target_pairs={{0,24},{8,16},{16,8},{24,0},{1,25},{9,17},{17,9},{25,1},{2,26},{10... | collective-permute-start | bytes 6152 | tf_op jit(solution)/shard_map/ppermute | solution.py:26
  22.5 3.6 %collective-permute-start.5 = (f32[512]{0:T(512)S(1)}, f32[512]{0:T(512)S(1)}, u32[]{:S(2)}, u32[]{:S(2)}) collective-permute-start(f32[512]{0:T(512)S(1)} %log_add_fusion.9), channel_id=1, source_target_pairs={{0,16},{8,24},{16,0},{24,8},{1,17},{9,25},{17,1},{25,9},{2,18},{10... | collective-permute-start | bytes 6152 | tf_op jit(solution)/shard_map/ppermute | solution.py:26
  23.0 3.6 %collective-permute-start.6 = (f32[512]{0:T(512)S(1)}, f32[512]{0:T(512)S(1)}, u32[]{:S(2)}, u32[]{:S(2)}) collective-permute-start(f32[512]{0:T(512)S(1)} %log_add_fusion.9), channel_id=1, source_target_pairs={{0,8},{8,0},{16,24},{24,16},{1,9},{9,1},{17,25},{25,17},{2,10},{10... | collective-permute-start | bytes 6152 | tf_op jit(solution)/shard_map/ppermute | solution.py:26
  27.8 1.2 %collective-permute-start.7 = (f32[2048]{0:T(1024)S(1)}, f32[2048]{0:T(1024)S(1)}, u32[]{:S(2)}, u32[]{:S(2)}) collective-permute-start(f32[2048]{0:T(1024)S(1)} %log_add_fusion.3), channel_id=1, source_target_pairs={{0,1},{1,0},{2,3},{3,2},{4,5},{5,4},{6,7},{7,6},{8,9},{9,8},{10,11... | collective-permute-start | bytes 24584 | tf_op jit(solution)/shard_map/ppermute | solution.py:26
  29.0 3.7 %collective-permute-start.9 = (f32[2048]{0:T(1024)S(1)}, f32[2048]{0:T(1024)S(1)}, u32[]{:S(2)}, u32[]{:S(2)}) collective-permute-start(f32[2048]{0:T(1024)S(1)} %log_add_fusion.2), channel_id=1, source_target_pairs={{0,2},{1,7},{2,0},{3,5},{4,6},{5,3},{6,4},{7,1},{8,10},{9,15},{10,... | collective-permute-start | bytes 24584 | tf_op jit(solution)/shard_map/ppermute | solution.py:55
  29.1 3.7 %collective-permute-start.8 = (f32[2048]{0:T(1024)S(1)}, f32[2048]{0:T(1024)S(1)}, u32[]{:S(2)}, u32[]{:S(2)}) collective-permute-start(f32[2048]{0:T(1024)S(1)} %log_add_fusion.2), channel_id=1, source_target_pairs={{0,2},{1,5},{2,0},{3,7},{4,6},{5,1},{6,4},{7,3},{8,10},{9,13},{10,... | collective-permute-start | bytes 24584 | tf_op jit(solution)/shard_map/ppermute | solution.py:55
  32.8 1.8 %collective-permute-start.10 = (f32[2048]{0:T(1024)S(1)}, f32[2048]{0:T(1024)S(1)}, u32[]{:S(2)}, u32[]{:S(2)}) collective-permute-start(f32[2048]{0:T(1024)S(1)} %add_select_fusion.1), channel_id=1, source_target_pairs={{0,1},{1,0},{2,3},{3,2},{4,5},{5,4},{6,7},{7,6},{8,9},{9,8},{10,11... | collective-permute-start | bytes 24584 | tf_op jit(solution)/shard_map/ppermute | solution.py:26
  35.9 4.5 %collective-permute-start.11 = (f32[512]{0:T(512)S(1)}, f32[512]{0:T(512)S(1)}, u32[]{:S(2)}, u32[]{:S(2)}) collective-permute-start(f32[512]{0:T(512)S(1)} %log_add_fusion.7), channel_id=1, source_target_pairs={{0,24},{8,16},{16,8},{24,0},{1,25},{9,17},{17,9},{25,1},{2,26},{10... | collective-permute-start | bytes 6152 | tf_op jit(solution)/shard_map/ppermute | solution.py:26
  37.4 3.6 %collective-permute-start.12 = (f32[512]{0:T(512)S(1)}, f32[512]{0:T(512)S(1)}, u32[]{:S(2)}, u32[]{:S(2)}) collective-permute-start(f32[512]{0:T(512)S(1)} %log_add_fusion.7), channel_id=1, source_target_pairs={{0,16},{8,24},{16,0},{24,8},{1,17},{9,25},{17,1},{25,9},{2,18},{10... | collective-permute-start | bytes 6152 | tf_op jit(solution)/shard_map/ppermute | solution.py:26
  37.9 3.6 %collective-permute-start.13 = (f32[512]{0:T(512)S(1)}, f32[512]{0:T(512)S(1)}, u32[]{:S(2)}, u32[]{:S(2)}) collective-permute-start(f32[512]{0:T(512)S(1)} %log_add_fusion.7), channel_id=1, source_target_pairs={{0,8},{8,0},{16,24},{24,16},{1,9},{9,1},{17,25},{25,17},{2,10},{10... | collective-permute-start | bytes 6152 | tf_op jit(solution)/shard_map/ppermute | solution.py:26
  42.7 1.2 %collective-permute-start.14 = (f32[2048]{0:T(1024)S(1)}, f32[2048]{0:T(1024)S(1)}, u32[]{:S(2)}, u32[]{:S(2)}) collective-permute-start(f32[2048]{0:T(1024)S(1)} %log_add_fusion.1), channel_id=1, source_target_pairs={{0,1},{1,0},{2,3},{3,2},{4,5},{5,4},{6,7},{7,6},{8,9},{9,8},{10,11... | collective-permute-start | bytes 24584 | tf_op jit(solution)/shard_map/ppermute | solution.py:26
  44.0 3.7 %collective-permute-start.16 = (f32[2048]{0:T(1024)S(1)}, f32[2048]{0:T(1024)S(1)}, u32[]{:S(2)}, u32[]{:S(2)}) collective-permute-start(f32[2048]{0:T(1024)S(1)} %log_add_fusion), channel_id=1, source_target_pairs={{0,2},{1,7},{2,0},{3,5},{4,6},{5,3},{6,4},{7,1},{8,10},{9,15},{10,... | collective-permute-start | bytes 24584 | tf_op jit(solution)/shard_map/ppermute | solution.py:55
  45.4 3.7 %collective-permute-start.15 = (f32[2048]{0:T(1024)S(1)}, f32[2048]{0:T(1024)S(1)}, u32[]{:S(2)}, u32[]{:S(2)}) collective-permute-start(f32[2048]{0:T(1024)S(1)} %log_add_fusion), channel_id=1, source_target_pairs={{0,2},{1,5},{2,0},{3,7},{4,6},{5,1},{6,4},{7,3},{8,10},{9,13},{10,... | collective-permute-start | bytes 24584 | tf_op jit(solution)/shard_map/ppermute | solution.py:55
  49.1 1.6 %collective-permute-start.17 = (f32[2048]{0:T(1024)S(1)}, f32[2048]{0:T(1024)S(1)}, u32[]{:S(2)}, u32[]{:S(2)}) collective-permute-start(f32[2048]{0:T(1024)S(1)} %add_select_fusion), channel_id=1, source_target_pairs={{0,1},{1,0},{2,3},{3,2},{4,5},{5,4},{6,7},{7,6},{8,9},{9,8},{10,11... | collective-permute-start | bytes 24584 | tf_op jit(solution)/shard_map/ppermute | solution.py:26
  51.1 2.2 %copy-start = (bf16[2048,1024]{1,0:T(8,128)(2,1)S(1)}, bf16[2048,1024]{1,0:T(8,128)(2,1)}, u32[]{:S(2)}) copy-start(bf16[2048,1024]{1,0:T(8,128)(2,1)} %embeddings.1) | copy-start | bytes 12582916
  54.6 6.7 %collective-permute-start.20 = (bf16[144,512]{1,0:T(8,128)(2,1)S(1)}, bf16[144,512]{1,0:T(8,128)(2,1)S(1)}, u32[]{:S(2)}, u32[]{:S(2)}) collective-permute-start(bf16[144,512]{1,0:T(8,128)(2,1)S(1)} %get-tuple-element.33), channel_id=1, source_target_pairs={{0,8},{8,0},{16,24},{24,16},{1,9},{9,1},{17,25},{25,17},{2,10},{10... | collective-permute-start | bytes 442376 | tf_op jit(solution)/shard_map/ppermute | solution.py:26
  56.1 6.7 %collective-permute-start.21 = (bf16[144,512]{1,0:T(8,128)(2,1)S(1)}, bf16[144,512]{1,0:T(8,128)(2,1)S(1)}, u32[]{:S(2)}, u32[]{:S(2)}) collective-permute-start(bf16[144,512]{1,0:T(8,128)(2,1)S(1)} %get-tuple-element.34), channel_id=1, source_target_pairs={{0,16},{8,24},{16,0},{24,8},{1,17},{9,25},{17,1},{25,9},{2,18},{10... | collective-permute-start | bytes 442376 | tf_op jit(solution)/shard_map/ppermute | solution.py:26
  57.6 7.5 %collective-permute-start.18 = (bf16[128,512]{1,0:T(8,128)(2,1)S(1)}, bf16[128,512]{1,0:T(8,128)(2,1)S(1)}, u32[]{:S(2)}, u32[]{:S(2)}) collective-permute-start(bf16[128,512]{1,0:T(8,128)(2,1)S(1)} %get-tuple-element.31), channel_id=1, source_target_pairs={{0,8},{8,0},{16,24},{24,16},{1,9},{9,1},{17,25},{25,17},{2,10},{10... | collective-permute-start | bytes 393224 | tf_op jit(solution)/shard_map/ppermute | solution.py:26
  58.2 7.2 %collective-permute-start.19 = (bf16[128,512]{1,0:T(8,128)(2,1)S(1)}, bf16[128,512]{1,0:T(8,128)(2,1)S(1)}, u32[]{:S(2)}, u32[]{:S(2)}) collective-permute-start(bf16[128,512]{1,0:T(8,128)(2,1)S(1)} %get-tuple-element.32), channel_id=1, source_target_pairs={{0,16},{8,24},{16,0},{24,8},{1,17},{9,25},{17,1},{25,9},{2,18},{10... | collective-permute-start | bytes 393224 | tf_op jit(solution)/shard_map/ppermute | solution.py:26
  63.0 6.6 %collective-permute-start.23 = (bf16[144,512]{1,0:T(8,128)(2,1)S(1)}, bf16[144,512]{1,0:T(8,128)(2,1)S(1)}, u32[]{:S(2)}, u32[]{:S(2)}) collective-permute-start(bf16[144,512]{1,0:T(8,128)(2,1)S(1)} %get-tuple-element.37.mine), channel_id=1, source_target_pairs={{0,16},{8,24},{16,0},{24,8},{1,17},{9,25},{17,1},{25,9},{2,18},{10... | collective-permute-start | bytes 442376 | tf_op jit(solution)/shard_map/ppermute | solution.py:26
  64.6 6.7 %collective-permute-start.26 = (bf16[144,512]{1,0:T(8,128)(2,1)S(1)}, bf16[144,512]{1,0:T(8,128)(2,1)S(1)}, u32[]{:S(2)}, u32[]{:S(2)}) collective-permute-start(bf16[144,512]{1,0:T(8,128)(2,1)S(1)} %get-tuple-element.40.mine), channel_id=1, source_target_pairs={{0,8},{8,0},{16,24},{24,16},{1,9},{9,1},{17,25},{25,17},{2,10},{10... | collective-permute-start | bytes 442376 | tf_op jit(solution)/shard_map/ppermute | solution.py:26
  65.6 6.6 %collective-permute-start.22 = (bf16[128,512]{1,0:T(8,128)(2,1)S(1)}, bf16[128,512]{1,0:T(8,128)(2,1)S(1)}, u32[]{:S(2)}, u32[]{:S(2)}) collective-permute-start(bf16[128,512]{1,0:T(8,128)(2,1)S(1)} %get-tuple-element.36.mine), channel_id=1, source_target_pairs={{0,16},{8,24},{16,0},{24,8},{1,17},{9,25},{17,1},{25,9},{2,18},{10... | collective-permute-start | bytes 393224 | tf_op jit(solution)/shard_map/ppermute | solution.py:26
  67.2 7.0 %collective-permute-start.25 = (bf16[128,512]{1,0:T(8,128)(2,1)S(1)}, bf16[128,512]{1,0:T(8,128)(2,1)S(1)}, u32[]{:S(2)}, u32[]{:S(2)}) collective-permute-start(bf16[128,512]{1,0:T(8,128)(2,1)S(1)} %get-tuple-element.39.mine), channel_id=1, source_target_pairs={{0,8},{8,0},{16,24},{24,16},{1,9},{9,1},{17,25},{25,17},{2,10},{10... | collective-permute-start | bytes 393224 | tf_op jit(solution)/shard_map/ppermute | solution.py:26
  69.8 7.2 %collective-permute-start.28 = (bf16[144,512]{1,0:T(8,128)(2,1)S(1)}, bf16[144,512]{1,0:T(8,128)(2,1)S(1)}, u32[]{:S(2)}, u32[]{:S(2)}) collective-permute-start(bf16[144,512]{1,0:T(8,128)(2,1)S(1)} %get-tuple-element.42.lower_kept), channel_id=1, source_target_pairs={{0,8},{8,0},{16,24},{24,16},{1,9},{9,1},{17,25},{25,17},{2,10},{10... | collective-permute-start | bytes 442376 | tf_op jit(solution)/shard_map/ppermute | solution.py:26
  71.5 5.5 %collective-permute-start.29 = (bf16[144,512]{1,0:T(8,128)(2,1)S(1)}, bf16[144,512]{1,0:T(8,128)(2,1)S(1)}, u32[]{:S(2)}, u32[]{:S(2)}) collective-permute-start(bf16[144,512]{1,0:T(8,128)(2,1)S(1)} %get-tuple-element.43.upper_kept), channel_id=1, source_target_pairs={{0,16},{8,24},{16,0},{24,8},{1,17},{9,25},{17,1},{25,9},{2,18},{10... | collective-permute-start | bytes 442376 | tf_op jit(solution)/shard_map/ppermute | solution.py:26
  72.3 6.1 %collective-permute-start.24 = (bf16[128,512]{1,0:T(8,128)(2,1)S(1)}, bf16[128,512]{1,0:T(8,128)(2,1)S(1)}, u32[]{:S(2)}, u32[]{:S(2)}) collective-permute-start(bf16[128,512]{1,0:T(8,128)(2,1)S(1)} %shard_map.63.refs_2_), channel_id=1, source_target_pairs={{0,8},{8,0},{16,24},{24,16},{1,9},{9,1},{17,25},{25,17},{2,10},{10... | collective-permute-start | bytes 393224 | tf_op jit(solution)/shard_map/ppermute | solution.py:26
  74.3 5.0 %collective-permute-start.27 = (bf16[128,512]{1,0:T(8,128)(2,1)S(1)}, bf16[128,512]{1,0:T(8,128)(2,1)S(1)}, u32[]{:S(2)}, u32[]{:S(2)}) collective-permute-start(bf16[128,512]{1,0:T(8,128)(2,1)S(1)} %shard_map.65.refs_3_), channel_id=1, source_target_pairs={{0,16},{8,24},{16,0},{24,8},{1,17},{9,25},{17,1},{25,9},{2,18},{10... | collective-permute-start | bytes 393224 | tf_op jit(solution)/shard_map/ppermute | solution.py:26

commit v3 on v2

--- a/solution.py
+++ b/solution.py
@@ -47,7 +47,7 @@
     return x
 
 
-def lse_over_cent(x, odd):
+def lse_over_cent(x, odd, joined_by):
     size = lax.axis_size("cent")
     near, middle, *rest = [1 << bit for bit in bits_of("cent")[1:]]
 
@@ -57,7 +57,7 @@
     x = lse(x, flipped(x, "cent", 1))
     second = split(x, near, middle)
     first = split(x, near, near | middle)
-    x = jnp.where(odd, lse(second, first), lse(x, first))
+    x = joined_by(jnp.where(odd, lse(second, first), lse(x, first)))
     for mask in [1] + rest:
         x = lse(x, flipped(x, "cent", mask))
     return x
@@ -417,6 +417,22 @@
     return out, row_out.reshape(row_now.shape), col_out.reshape(columns)
 
 
+def beside_kernel(x, embeddings, out):
+    out[...] = x[...]
+
+
+def beside(x, embeddings):
+    lines = (x.shape[0] // LANES, LANES)
+    vmem = pl.BlockSpec(memory_space=pltpu.VMEM)
+    return pl.pallas_call(
+        beside_kernel,
+        out_shape=jax.ShapeDtypeStruct(lines, x.dtype),
+        in_specs=[vmem, pl.BlockSpec(memory_space=pl.ANY)],
+        out_specs=vmem,
+        compiler_params=pltpu.CompilerParams(vmem_limit_bytes=VMEM_BYTES),
+    )(x.reshape(lines), embeddings).reshape(x.shape)
+
+
 def on_device(embeddings, centroids, col_start):
     rows_here = embeddings.shape[0]
     cent_here = centroids.shape[0]
@@ -456,7 +472,9 @@
         shifted = scores + col_now[:, None]
         top = jnp.max(shifted, axis=0)
         part = top + jnp.log(jnp.sum(jnp.exp(shifted - top[None, :]), axis=0))
-        row_now = -math.log(n_total) - lse_over_cent(part, odd)
+        last = step_index == ITERS - 1
+        part = lse_over_cent(part, odd, lambda x: beside(x, embeddings) if last else x)
+        row_now = -math.log(n_total) - part
         lifted = scores + row_now[None, :]
         top = jnp.max(lifted, axis=1)
         terms = jnp.exp(lifted - top[:, None])

time: 80.4 us -> 79.1 us (0.984)
  local copies, waits for them, and re-layouts: 1.32 us -> 0.03 us
    unnamed x2, local copies, waits for them, and re-layouts: 1.3 us -> 0.01 us
where the time goes in v3:
time: 79.1 us; the launch traced here: 78.9 us
  starting transfers between devices  29.8 us (38%)
  waiting for transfers between devices  28.3 us (36%)
  other arithmetic  9.16 us (12%)
  Pallas kernels  6.19 us (8%)
  matrix products  4.57 us (6%)
  between operations  0.9 us (1%)
    ppermute x24, starting transfers between devices, flipped(): return lax.ppermute(x, axis, [(k, k ^ mask) for k in range(size)])  22.5 us
    ppermute x24, waiting for transfers between devices, flipped(): return lax.ppermute(x, axis, [(k, k ^ mask) for k in range(size)])  20 us
    ppermute x6, waiting for transfers between devices, split(): lax.ppermute(value, 'cent', [(k, k ^ (odd_mask if k % 2 else even_mask))...  8.29 us
    ppermute x6, starting transfers between devices, split(): lax.ppermute(value, 'cent', [(k, k ^ (odd_mask if k % 2 else even_mask))...  7.23 us
    pallas_call x9, Pallas kernels, call(): pl.pallas_call(kernel, out_shape=outs, in_specs=[vmem] * len(operands), o...  5.37 us
    dot_general x1, matrix products, on_device(): lax.dot_general(sent_and_kept(centroids), embeddings, (((1,), (1,)), ((),...  4.57 us
    reduce_sum x3, other arithmetic, on_device(): mass = jnp.sum(terms, axis=1)  2.58 us
    reduce_sum x3, other arithmetic, on_device(): part = top + jnp.log(jnp.sum(jnp.exp(shifted - top[None, :]), axis=0))  2.33 us
  transfers between devices with their start and end apart: 30, of which 26 were waited for; matrix products, arithmetic and copies ran while one was open for 0% of the time, Pallas kernels for 5%

profile of v3, /device:TPU:0, one launch (start us, length us, event | category | flops | bytes accessed | tf_op | source)
XLA Modules:
  0.0 78.9 jit_solution(10420031436773301347)
XLA Ops:
  0.6 0.8 %broadcast_select_fusion.7 = (f32[128]{0:T(128)S(1)}, f32[128]{0:T(128)S(1)}, f32[128]{0:T(128)S(1)}, f32[128]{0:T(128)S(1)}) fusion(pred[]{:T(512)} %bitcast.3, f32[512]{0:T(512)} %param.5, pred[]{:T(512)} %bitcast.4), kind=kLoop, calls=%fused_computation.91 | loop fusion | flops 512 | bytes 4098 | tf_op jit(solution)/shard_map/jit(_where)/select_n | solution.py:451
  1.5 1.3 %broadcast_select_fusion.3 = (bf16[128,1024]{1,0:T(8,128)(2,1)S(1)}, bf16[128,1024]{1,0:T(8,128)(2,1)S(1)}, bf16[128,1024]{1,0:T(8,128)(2,1)S(1)}, bf16[128,1024]{1,0:T(8,128)(2,1)S(1)}) fusion(pred[]{:T(512)} %bitcast.3, bf16[512,1024]{1,0:T(8,128)(2,1)} %param.4, pred[]{:T(512)} %bitcast.4), kind=kLoop, calls=%fused_computation.25 | loop fusion | flops 524288 | bytes 2097154 | tf_op jit(solution)/shard_map/jit(_where)/select_n | solution.py:451
  2.8 4.6 %add_reduce_fusion.5 = (f32[2048]{0:T(1024)S(1)}, f32[512,2048]{1,0:T(8,128)S(1)}) fusion(f32[512]{0:T(512)S(1)} %pad_maximum_fusion, bf16[2048,1024]{1,0:T(8,128)(2,1)} %embeddings.2, bf16[128,1024]{1,0:T(8,128)(2,1)S(1)} %get-tuple-element.51, bf16[128,1024]{1,0:T(8,128)(2,1)S(1)} %get-tuple-element.52, bf16[128,1024]{1,0:T(8,128)(2,1)S(1)} %get-tuple-element.50, ...), kind=kOutput, calls=%fused_computation.11 | convolution fusion | flops 2154821632 | bytes 9447424 | tf_op jit(solution)/shard_map/dot_general | solution.py:467
  7.3 0.8 exponential_reduce_fusion.4
  8.6 0.8 %collective-permute-done = f32[2048]{0:T(1024)S(1)} collective-permute-done((f32[2048]{0:T(1024)S(1)}, f32[2048]{0:T(1024)S(1)}, u32[]{:S(2)}, u32[]{:S(2)}) %collective-permute-start) | collective-permute-done | bytes 8224 | tf_op jit(solution)/shard_map/ppermute | solution.py:26
  9.5 3.0 %collective-permute-start.2 = (f32[2048]{0:T(1024)S(1)}, f32[2048]{0:T(1024)S(1)}, u32[]{:S(2)}, u32[]{:S(2)}) collective-permute-start(f32[2048]{0:T(1024)S(1)} %log_add_fusion.4), channel_id=1, source_target_pairs={{0,2},{1,7},{2,0},{3,5},{4,6},{5,3},{6,4},{7,1},{8,10},{9,15},{10,... | collective-permute-start | bytes 24584 | tf_op jit(solution)/shard_map/ppermute | solution.py:55
  12.5 1.6 %collective-permute-done.2 = f32[2048]{0:T(1024)S(1)} collective-permute-done((f32[2048]{0:T(1024)S(1)}, f32[2048]{0:T(1024)S(1)}, u32[]{:S(2)}, u32[]{:S(2)}) %collective-permute-start.2) | collective-permute-done | bytes 8224 | tf_op jit(solution)/shard_map/ppermute | solution.py:55
  14.1 2.0 %collective-permute-done.1 = f32[2048]{0:T(1024)S(1)} collective-permute-done((f32[2048]{0:T(1024)S(1)}, f32[2048]{0:T(1024)S(1)}, u32[]{:S(2)}, u32[]{:S(2)}) %collective-permute-start.1) | collective-permute-done | bytes 8224 | tf_op jit(solution)/shard_map/ppermute | solution.py:55
  16.1 1.7 %collective-permute-start.3 = (f32[2048]{0:T(1024)S(1)}, f32[2048]{0:T(1024)S(1)}, u32[]{:S(2)}, u32[]{:S(2)}) collective-permute-start(f32[2048]{0:T(1024)S(1)} %add_select_fusion.1), channel_id=1, source_target_pairs={{0,1},{1,0},{2,3},{3,2},{4,5},{5,4},{6,7},{7,6},{8,9},{9,8},{10,11... | collective-permute-start | bytes 24584 | tf_op jit(solution)/shard_map/ppermute | solution.py:26
  17.9 0.8 %collective-permute-done.3 = f32[2048]{0:T(1024)S(1)} collective-permute-done((f32[2048]{0:T(1024)S(1)}, f32[2048]{0:T(1024)S(1)}, u32[]{:S(2)}, u32[]{:S(2)}) %collective-permute-start.3) | collective-permute-done | bytes 8224 | tf_op jit(solution)/shard_map/ppermute | solution.py:26
  19.1 0.8 %exponential_reduce_fusion.3 = f32[512]{0:T(512)S(1)} fusion(f32[512,2048]{1,0:T(8,128)S(1)} %get-tuple-element.78, f32[512]{0:T(512)S(1)} %add_reduce_fusion.4, f32[2048]{0:T(1024)S(1)} %add_subtract_fusion.2), kind=kLoop, calls=%fused_computation.4 | loop fusion | flops 3145216 | bytes 4206592 | tf_op jit(solution)/shard_map/reduce_sum | solution.py:481
  19.9 2.5 %collective-permute-start.4 = (f32[512]{0:T(512)S(1)}, f32[512]{0:T(512)S(1)}, u32[]{:S(2)}, u32[]{:S(2)}) collective-permute-start(f32[512]{0:T(512)S(1)} %log_add_fusion.9), channel_id=1, source_target_pairs={{0,24},{8,16},{16,8},{24,0},{1,25},{9,17},{17,9},{25,1},{2,26},{10... | collective-permute-start | bytes 6152 | tf_op jit(solution)/shard_map/ppermute | solution.py:26
  23.5 1.0 %collective-permute-done.4 = f32[512]{0:T(512)S(1)} collective-permute-done((f32[512]{0:T(512)S(1)}, f32[512]{0:T(512)S(1)}, u32[]{:S(2)}, u32[]{:S(2)}) %collective-permute-start.4) | collective-permute-done | bytes 2080 | tf_op jit(solution)/shard_map/ppermute | solution.py:26
  24.5 1.5 %collective-permute-done.5 = f32[512]{0:T(512)S(1)} collective-permute-done((f32[512]{0:T(512)S(1)}, f32[512]{0:T(512)S(1)}, u32[]{:S(2)}, u32[]{:S(2)}) %collective-permute-start.5) | collective-permute-done | bytes 2080 | tf_op jit(solution)/shard_map/ppermute | solution.py:26
  27.0 0.8 exponential_reduce_fusion.2
  27.8 1.2 %collective-permute-done.7 = f32[2048]{0:T(1024)S(1)} collective-permute-done((f32[2048]{0:T(1024)S(1)}, f32[2048]{0:T(1024)S(1)}, u32[]{:S(2)}, u32[]{:S(2)}) %collective-permute-start.7) | collective-permute-done | bytes 8224 | tf_op jit(solution)/shard_map/ppermute | solution.py:26
  29.1 2.0 %collective-permute-start.8 = (f32[2048]{0:T(1024)S(1)}, f32[2048]{0:T(1024)S(1)}, u32[]{:S(2)}, u32[]{:S(2)}) collective-permute-start(f32[2048]{0:T(1024)S(1)} %log_add_fusion.2), channel_id=1, source_target_pairs={{0,2},{1,5},{2,0},{3,7},{4,6},{5,1},{6,4},{7,3},{8,10},{9,13},{10,... | collective-permute-start | bytes 24584 | tf_op jit(solution)/shard_map/ppermute | solution.py:55
  31.1 1.6 %collective-permute-done.9 = f32[2048]{0:T(1024)S(1)} collective-permute-done((f32[2048]{0:T(1024)S(1)}, f32[2048]{0:T(1024)S(1)}, u32[]{:S(2)}, u32[]{:S(2)}) %collective-permute-start.9) | collective-permute-done | bytes 8224 | tf_op jit(solution)/shard_map/ppermute | solution.py:55
  32.8 1.0 %collective-permute-start.10 = (f32[2048]{0:T(1024)S(1)}, f32[2048]{0:T(1024)S(1)}, u32[]{:S(2)}, u32[]{:S(2)}) collective-permute-start(f32[2048]{0:T(1024)S(1)} %add_select_fusion), channel_id=1, source_target_pairs={{0,1},{1,0},{2,3},{3,2},{4,5},{5,4},{6,7},{7,6},{8,9},{9,8},{10,11... | collective-permute-start | bytes 24584 | tf_op jit(solution)/shard_map/ppermute | solution.py:26
  33.8 0.8 %collective-permute-done.10 = f32[2048]{0:T(1024)S(1)} collective-permute-done((f32[2048]{0:T(1024)S(1)}, f32[2048]{0:T(1024)S(1)}, u32[]{:S(2)}, u32[]{:S(2)}) %collective-permute-start.10) | collective-permute-done | bytes 8224 | tf_op jit(solution)/shard_map/ppermute | solution.py:26
  35.0 0.8 %exponential_reduce_fusion.1 = f32[512]{0:T(512)S(1)} fusion(f32[512,2048]{1,0:T(8,128)S(1)} %get-tuple-element.78, f32[512]{0:T(512)S(1)} %add_reduce_fusion.2, f32[2048]{0:T(1024)S(1)} %add_subtract_fusion.1), kind=kLoop, calls=%fused_computation.2 | loop fusion | flops 3145216 | bytes 4206592 | tf_op jit(solution)/shard_map/reduce_sum | solution.py:481
  35.9 1.6 %collective-permute-start.11 = (f32[512]{0:T(512)S(1)}, f32[512]{0:T(512)S(1)}, u32[]{:S(2)}, u32[]{:S(2)}) collective-permute-start(f32[512]{0:T(512)S(1)} %log_add_fusion.7), channel_id=1, source_target_pairs={{0,24},{8,16},{16,8},{24,0},{1,25},{9,17},{17,9},{25,1},{2,26},{10... | collective-permute-start | bytes 6152 | tf_op jit(solution)/shard_map/ppermute | solution.py:26
  37.9 1.5 %collective-permute-start.13 = (f32[512]{0:T(512)S(1)}, f32[512]{0:T(512)S(1)}, u32[]{:S(2)}, u32[]{:S(2)}) collective-permute-start(f32[512]{0:T(512)S(1)} %log_add_fusion.7), channel_id=1, source_target_pairs={{0,8},{8,0},{16,24},{24,16},{1,9},{9,1},{17,25},{25,17},{2,10},{10... | collective-permute-start | bytes 6152 | tf_op jit(solution)/shard_map/ppermute | solution.py:26
  39.4 1.0 %collective-permute-done.11 = f32[512]{0:T(512)S(1)} collective-permute-done((f32[512]{0:T(512)S(1)}, f32[512]{0:T(512)S(1)}, u32[]{:S(2)}, u32[]{:S(2)}) %collective-permute-start.11) | collective-permute-done | bytes 2080 | tf_op jit(solution)/shard_map/ppermute | solution.py:26
  41.9 0.8 exponential_reduce_fusion
  42.8 1.2 %collective-permute-done.14 = f32[2048]{0:T(1024)S(1)} collective-permute-done((f32[2048]{0:T(1024)S(1)}, f32[2048]{0:T(1024)S(1)}, u32[]{:S(2)}, u32[]{:S(2)}) %collective-permute-start.14) | collective-permute-done | bytes 8224 | tf_op jit(solution)/shard_map/ppermute | solution.py:26
  44.0 1.4 %collective-permute-start.16 = (f32[2048]{0:T(1024)S(1)}, f32[2048]{0:T(1024)S(1)}, u32[]{:S(2)}, u32[]{:S(2)}) collective-permute-start(f32[2048]{0:T(1024)S(1)} %log_add_fusion), channel_id=1, source_target_pairs={{0,2},{1,7},{2,0},{3,5},{4,6},{5,3},{6,4},{7,1},{8,10},{9,15},{10,... | collective-permute-start | bytes 24584 | tf_op jit(solution)/shard_map/ppermute | solution.py:55
  45.5 0.6 collective-permute-start.15
  46.1 1.6 %collective-permute-done.16 = f32[2048]{0:T(1024)S(1)} collective-permute-done((f32[2048]{0:T(1024)S(1)}, f32[2048]{0:T(1024)S(1)}, u32[]{:S(2)}, u32[]{:S(2)}) %collective-permute-start.16) | collective-permute-done | bytes 8224 | tf_op jit(solution)/shard_map/ppermute | solution.py:55
  47.7 1.4 %collective-permute-done.15 = f32[2048]{0:T(1024)S(1)} collective-permute-done((f32[2048]{0:T(1024)S(1)}, f32[2048]{0:T(1024)S(1)}, u32[]{:S(2)}, u32[]{:S(2)}) %collective-permute-start.15) | collective-permute-done | bytes 8224 | tf_op jit(solution)/shard_map/ppermute | solution.py:55
  49.1 0.8 %collective-permute-start.17 = (f32[2048]{0:T(1024)S(1)}, f32[2048]{0:T(1024)S(1)}, u32[]{:S(2)}, u32[]{:S(2)}) collective-permute-start(f32[2048]{0:T(1024)S(1)} %bitcast.21), channel_id=1, source_target_pairs={{0,1},{1,0},{2,3},{3,2},{4,5},{5,4},{6,7},{7,6},{8,9},{9,8},{10,11... | collective-permute-start | bytes 24584 | tf_op jit(solution)/shard_map/ppermute | solution.py:26
  49.9 0.8 %collective-permute-done.17 = f32[2048]{0:T(1024)S(1)} collective-permute-done((f32[2048]{0:T(1024)S(1)}, f32[2048]{0:T(1024)S(1)}, u32[]{:S(2)}, u32[]{:S(2)}) %collective-permute-start.17) | collective-permute-done | bytes 8224 | tf_op jit(solution)/shard_map/ppermute | solution.py:26
  51.2 0.9 %fusion = (f32[512]{0:T(512)S(1)}, bf16[512,2048]{1,0:T(8,128)(2,1)S(1)}) fusion(f32[512,2048]{1,0:T(8,128)S(1)} %get-tuple-element.78, f32[512]{0:T(512)S(1)} %add_reduce_fusion, f32[2048]{0:T(1024)S(1)} %add_subtract_fusion), kind=kLoop, calls=%fused_computation.12 | loop fusion | flops 4193792 | bytes 6303744 | tf_op jit(solution)/shard_map/reduce_sum | solution.py:481
  52.1 1.3 %shard_map.60 = (bf16[144,512]{1,0:T(8,128)(2,1)S(1)}, bf16[144,512]{1,0:T(8,128)(2,1)S(1)}, bf16[128,512]{1,0:T(8,128)(2,1)S(1)}, bf16[128,512]{1,0:T(8,128)(2,1)S(1)}) custom-call(bf16[512,2048]{1,0:T(8,128)(2,1)S(1)} %get-tuple-element.48.plan, bf16[2048,1024]{1,0:T(8,128)(2,1)S(1)} %copy-done, f32[4,128]{1,0:T(4,128)S(1)} %bitcast.19, ...), custom_call_target="tpu_custom_call" | custom-call | flops 1073741824 | bytes 524288 | tf_op jit(solution)/shard_map/pallas_call | solution.py:356
  53.4 1.6 %collective-permute-start.20 = (bf16[144,512]{1,0:T(8,128)(2,1)S(1)}, bf16[144,512]{1,0:T(8,128)(2,1)S(1)}, u32[]{:S(2)}, u32[]{:S(2)}) collective-permute-start(bf16[144,512]{1,0:T(8,128)(2,1)S(1)} %get-tuple-element.33), channel_id=1, source_target_pairs={{0,8},{8,0},{16,24},{24,16},{1,9},{9,1},{17,25},{25,17},{2,10},{10... | collective-permute-start | bytes 442376 | tf_op jit(solution)/shard_map/ppermute | solution.py:26
  54.9 1.5 %collective-permute-start.21 = (bf16[144,512]{1,0:T(8,128)(2,1)S(1)}, bf16[144,512]{1,0:T(8,128)(2,1)S(1)}, u32[]{:S(2)}, u32[]{:S(2)}) collective-permute-start(bf16[144,512]{1,0:T(8,128)(2,1)S(1)} %get-tuple-element.34), channel_id=1, source_target_pairs={{0,16},{8,24},{16,0},{24,8},{1,17},{9,25},{17,1},{25,9},{2,18},{10... | collective-permute-start | bytes 442376 | tf_op jit(solution)/shard_map/ppermute | solution.py:26
  57.5 1.7 %shard_map.59 = (f32[2,128,1024]{2,1,0:T(8,128)S(1)}, f32[1,2048]{1,0:T(1,128)}) custom-call(bf16[512,2048]{1,0:T(8,128)(2,1)S(1)} %get-tuple-element.48.plan, bf16[2048,1024]{1,0:T(8,128)(2,1)S(1)} %copy-done, f32[4,128]{1,0:T(4,128)S(1)} %bitcast.20, f32[1,2048]{1,0:T(1,128)S(1)} %bitcast.18), custom_call_target="tpu_custom_call" | custom-call | flops 1073741824 | bytes 524288 | tf_op jit(solution)/shard_map/pallas_call | solution.py:356
  59.2 0.9 %collective-permute-done.20.lower = bf16[144,512]{1,0:T(8,128)(2,1)S(1)} collective-permute-done((bf16[144,512]{1,0:T(8,128)(2,1)S(1)}, bf16[144,512]{1,0:T(8,128)(2,1)S(1)}, u32[]{:S(2)}, u32[]{:S(2)}) %collective-permute-start.20) | collective-permute-done | bytes 147488 | tf_op jit(solution)/shard_map/ppermute | solution.py:26
  60.1 1.5 %collective-permute-done.21.upper = bf16[144,512]{1,0:T(8,128)(2,1)S(1)} collective-permute-done((bf16[144,512]{1,0:T(8,128)(2,1)S(1)}, bf16[144,512]{1,0:T(8,128)(2,1)S(1)}, u32[]{:S(2)}, u32[]{:S(2)}) %collective-permute-start.21) | collective-permute-done | bytes 147488 | tf_op jit(solution)/shard_map/ppermute | solution.py:26
  61.8 1.6 %collective-permute-start.23 = (bf16[144,512]{1,0:T(8,128)(2,1)S(1)}, bf16[144,512]{1,0:T(8,128)(2,1)S(1)}, u32[]{:S(2)}, u32[]{:S(2)}) collective-permute-start(bf16[144,512]{1,0:T(8,128)(2,1)S(1)} %get-tuple-element.37.mine), channel_id=1, source_target_pairs={{0,16},{8,24},{16,0},{24,8},{1,17},{9,25},{17,1},{25,9},{2,18},{10... | collective-permute-start | bytes 442376 | tf_op jit(solution)/shard_map/ppermute | solution.py:26
  64.4 1.6 %collective-permute-start.22 = (bf16[128,512]{1,0:T(8,128)(2,1)S(1)}, bf16[128,512]{1,0:T(8,128)(2,1)S(1)}, u32[]{:S(2)}, u32[]{:S(2)}) collective-permute-start(bf16[128,512]{1,0:T(8,128)(2,1)S(1)} %get-tuple-element.36.mine), channel_id=1, source_target_pairs={{0,16},{8,24},{16,0},{24,8},{1,17},{9,25},{17,1},{25,9},{2,18},{10... | collective-permute-start | bytes 393224 | tf_op jit(solution)/shard_map/ppermute | solution.py:26
  66.4 2.0 %collective-permute-done.23.theirs = bf16[144,512]{1,0:T(8,128)(2,1)S(1)} collective-permute-done((bf16[144,512]{1,0:T(8,128)(2,1)S(1)}, bf16[144,512]{1,0:T(8,128)(2,1)S(1)}, u32[]{:S(2)}, u32[]{:S(2)}) %collective-permute-start.23) | collective-permute-done | bytes 147488 | tf_op jit(solution)/shard_map/ppermute | solution.py:26
  68.8 1.4 %collective-permute-done.26.theirs = bf16[144,512]{1,0:T(8,128)(2,1)S(1)} collective-permute-done((bf16[144,512]{1,0:T(8,128)(2,1)S(1)}, bf16[144,512]{1,0:T(8,128)(2,1)S(1)}, u32[]{:S(2)}, u32[]{:S(2)}) %collective-permute-start.26) | collective-permute-done | bytes 147488 | tf_op jit(solution)/shard_map/ppermute | solution.py:26
  71.1 1.6 %collective-permute-start.24 = (bf16[128,512]{1,0:T(8,128)(2,1)S(1)}, bf16[128,512]{1,0:T(8,128)(2,1)S(1)}, u32[]{:S(2)}, u32[]{:S(2)}) collective-permute-start(bf16[128,512]{1,0:T(8,128)(2,1)S(1)} %shard_map.64.refs_2_), channel_id=1, source_target_pairs={{0,8},{8,0},{16,24},{24,16},{1,9},{9,1},{17,25},{25,17},{2,10},{10... | collective-permute-start | bytes 393224 | tf_op jit(solution)/shard_map/ppermute | solution.py:26
  73.7 2.1 %collective-permute-done.28.lower_sent = bf16[144,512]{1,0:T(8,128)(2,1)S(1)} collective-permute-done((bf16[144,512]{1,0:T(8,128)(2,1)S(1)}, bf16[144,512]{1,0:T(8,128)(2,1)S(1)}, u32[]{:S(2)}, u32[]{:S(2)}) %collective-permute-start.28) | collective-permute-done | bytes 147488 | tf_op jit(solution)/shard_map/ppermute | solution.py:26
  75.8 1.4 %shard_map.67 = (bf16[512,1024]{1,0:T(8,128)(2,1)}, f32[4,128]{1,0:T(4,128)}) custom-call(bf16[144,512]{1,0:T(8,128)(2,1)S(1)} %collective-permute-done.28.lower_sent, bf16[144,512]{1,0:T(8,128)(2,1)S(1)} %collective-permute-done.29.upper_sent, bf16[144,512]{1,0:T(8,128)(2,1)S(1)} %get-tuple-element.42.lower_kept, ...), custom_call_target="tpu_custom_call" | custom-call | bytes 524288 | tf_op jit(solution)/shard_map/pallas_call | solution.py:356
  77.2 0.9 %collective-permute-done.27.refs_1_ = bf16[128,512]{1,0:T(8,128)(2,1)S(1)} collective-permute-done((bf16[128,512]{1,0:T(8,128)(2,1)S(1)}, bf16[128,512]{1,0:T(8,128)(2,1)S(1)}, u32[]{:S(2)}, u32[]{:S(2)}) %collective-permute-start.27) | collective-permute-done | bytes 131104 | tf_op jit(solution)/shard_map/ppermute | solution.py:26
  78.1 0.8 %shard_map.68 = bf16[512,1024]{1,0:T(8,128)(2,1)} custom-call(bf16[128,512]{1,0:T(8,128)(2,1)S(1)} %collective-permute-done.24.refs_0_, bf16[128,512]{1,0:T(8,128)(2,1)S(1)} %collective-permute-done.27.refs_1_, bf16[128,512]{1,0:T(8,128)(2,1)S(1)} %shard_map.64.refs_2_, bf16[128,512]{1,0:T(8,128)(2,1)S(1)} %shard_map.66.refs_3_, ...), custom_call_target="tpu_custom_call", output_to_operand_aliasing={{}: (4, {})} | custom-call | tf_op jit(solution)/shard_map/pallas_call | solution.py:93
  (65 shorter events, 11.1 us)
Async XLA Ops:
  8.1 1.4 %collective-permute-start = (f32[2048]{0:T(1024)S(1)}, f32[2048]{0:T(1024)S(1)}, u32[]{:S(2)}, u32[]{:S(2)}) collective-permute-start(f32[2048]{0:T(1024)S(1)} %log_add_fusion.5), channel_id=1, source_target_pairs={{0,1},{1,0},{2,3},{3,2},{4,5},{5,4},{6,7},{7,6},{8,9},{9,8},{10,11... | collective-permute-start | bytes 24584 | tf_op jit(solution)/shard_map/ppermute | solution.py:26
  9.5 4.6 %collective-permute-start.2 = (f32[2048]{0:T(1024)S(1)}, f32[2048]{0:T(1024)S(1)}, u32[]{:S(2)}, u32[]{:S(2)}) collective-permute-start(f32[2048]{0:T(1024)S(1)} %log_add_fusion.4), channel_id=1, source_target_pairs={{0,2},{1,7},{2,0},{3,5},{4,6},{5,3},{6,4},{7,1},{8,10},{9,15},{10,... | collective-permute-start | bytes 24584 | tf_op jit(solution)/shard_map/ppermute | solution.py:55
  12.5 3.7 %collective-permute-start.1 = (f32[2048]{0:T(1024)S(1)}, f32[2048]{0:T(1024)S(1)}, u32[]{:S(2)}, u32[]{:S(2)}) collective-permute-start(f32[2048]{0:T(1024)S(1)} %log_add_fusion.4), channel_id=1, source_target_pairs={{0,2},{1,5},{2,0},{3,7},{4,6},{5,1},{6,4},{7,3},{8,10},{9,13},{10,... | collective-permute-start | bytes 24584 | tf_op jit(solution)/shard_map/ppermute | solution.py:55
  16.1 2.6 %collective-permute-start.3 = (f32[2048]{0:T(1024)S(1)}, f32[2048]{0:T(1024)S(1)}, u32[]{:S(2)}, u32[]{:S(2)}) collective-permute-start(f32[2048]{0:T(1024)S(1)} %add_select_fusion.1), channel_id=1, source_target_pairs={{0,1},{1,0},{2,3},{3,2},{4,5},{5,4},{6,7},{7,6},{8,9},{9,8},{10,11... | collective-permute-start | bytes 24584 | tf_op jit(solution)/shard_map/ppermute | solution.py:26
  19.9 4.5 %collective-permute-start.4 = (f32[512]{0:T(512)S(1)}, f32[512]{0:T(512)S(1)}, u32[]{:S(2)}, u32[]{:S(2)}) collective-permute-start(f32[512]{0:T(512)S(1)} %log_add_fusion.9), channel_id=1, source_target_pairs={{0,24},{8,16},{16,8},{24,0},{1,25},{9,17},{17,9},{25,1},{2,26},{10... | collective-permute-start | bytes 6152 | tf_op jit(solution)/shard_map/ppermute | solution.py:26
  22.4 3.6 %collective-permute-start.5 = (f32[512]{0:T(512)S(1)}, f32[512]{0:T(512)S(1)}, u32[]{:S(2)}, u32[]{:S(2)}) collective-permute-start(f32[512]{0:T(512)S(1)} %log_add_fusion.9), channel_id=1, source_target_pairs={{0,16},{8,24},{16,0},{24,8},{1,17},{9,25},{17,1},{25,9},{2,18},{10... | collective-permute-start | bytes 6152 | tf_op jit(solution)/shard_map/ppermute | solution.py:26
  23.0 3.6 %collective-permute-start.6 = (f32[512]{0:T(512)S(1)}, f32[512]{0:T(512)S(1)}, u32[]{:S(2)}, u32[]{:S(2)}) collective-permute-start(f32[512]{0:T(512)S(1)} %log_add_fusion.9), channel_id=1, source_target_pairs={{0,8},{8,0},{16,24},{24,16},{1,9},{9,1},{17,25},{25,17},{2,10},{10... | collective-permute-start | bytes 6152 | tf_op jit(solution)/shard_map/ppermute | solution.py:26
  27.8 1.2 %collective-permute-start.7 = (f32[2048]{0:T(1024)S(1)}, f32[2048]{0:T(1024)S(1)}, u32[]{:S(2)}, u32[]{:S(2)}) collective-permute-start(f32[2048]{0:T(1024)S(1)} %log_add_fusion.3), channel_id=1, source_target_pairs={{0,1},{1,0},{2,3},{3,2},{4,5},{5,4},{6,7},{7,6},{8,9},{9,8},{10,11... | collective-permute-start | bytes 24584 | tf_op jit(solution)/shard_map/ppermute | solution.py:26
  29.0 3.7 %collective-permute-start.9 = (f32[2048]{0:T(1024)S(1)}, f32[2048]{0:T(1024)S(1)}, u32[]{:S(2)}, u32[]{:S(2)}) collective-permute-start(f32[2048]{0:T(1024)S(1)} %log_add_fusion.2), channel_id=1, source_target_pairs={{0,2},{1,7},{2,0},{3,5},{4,6},{5,3},{6,4},{7,1},{8,10},{9,15},{10,... | collective-permute-start | bytes 24584 | tf_op jit(solution)/shard_map/ppermute | solution.py:55
  29.1 3.7 %collective-permute-start.8 = (f32[2048]{0:T(1024)S(1)}, f32[2048]{0:T(1024)S(1)}, u32[]{:S(2)}, u32[]{:S(2)}) collective-permute-start(f32[2048]{0:T(1024)S(1)} %log_add_fusion.2), channel_id=1, source_target_pairs={{0,2},{1,5},{2,0},{3,7},{4,6},{5,1},{6,4},{7,3},{8,10},{9,13},{10,... | collective-permute-start | bytes 24584 | tf_op jit(solution)/shard_map/ppermute | solution.py:55
  32.8 1.8 %collective-permute-start.10 = (f32[2048]{0:T(1024)S(1)}, f32[2048]{0:T(1024)S(1)}, u32[]{:S(2)}, u32[]{:S(2)}) collective-permute-start(f32[2048]{0:T(1024)S(1)} %add_select_fusion), channel_id=1, source_target_pairs={{0,1},{1,0},{2,3},{3,2},{4,5},{5,4},{6,7},{7,6},{8,9},{9,8},{10,11... | collective-permute-start | bytes 24584 | tf_op jit(solution)/shard_map/ppermute | solution.py:26
  35.9 4.5 %collective-permute-start.11 = (f32[512]{0:T(512)S(1)}, f32[512]{0:T(512)S(1)}, u32[]{:S(2)}, u32[]{:S(2)}) collective-permute-start(f32[512]{0:T(512)S(1)} %log_add_fusion.7), channel_id=1, source_target_pairs={{0,24},{8,16},{16,8},{24,0},{1,25},{9,17},{17,9},{25,1},{2,26},{10... | collective-permute-start | bytes 6152 | tf_op jit(solution)/shard_map/ppermute | solution.py:26
  37.4 3.6 %collective-permute-start.12 = (f32[512]{0:T(512)S(1)}, f32[512]{0:T(512)S(1)}, u32[]{:S(2)}, u32[]{:S(2)}) collective-permute-start(f32[512]{0:T(512)S(1)} %log_add_fusion.7), channel_id=1, source_target_pairs={{0,16},{8,24},{16,0},{24,8},{1,17},{9,25},{17,1},{25,9},{2,18},{10... | collective-permute-start | bytes 6152 | tf_op jit(solution)/shard_map/ppermute | solution.py:26
  37.9 3.6 %collective-permute-start.13 = (f32[512]{0:T(512)S(1)}, f32[512]{0:T(512)S(1)}, u32[]{:S(2)}, u32[]{:S(2)}) collective-permute-start(f32[512]{0:T(512)S(1)} %log_add_fusion.7), channel_id=1, source_target_pairs={{0,8},{8,0},{16,24},{24,16},{1,9},{9,1},{17,25},{25,17},{2,10},{10... | collective-permute-start | bytes 6152 | tf_op jit(solution)/shard_map/ppermute | solution.py:26
  41.6 7.6 %copy-start = (bf16[2048,1024]{1,0:T(8,128)(2,1)S(1)}, bf16[2048,1024]{1,0:T(8,128)(2,1)}, u32[]{:S(2)}) copy-start(bf16[2048,1024]{1,0:T(8,128)(2,1)} %embeddings.2) | copy-start | bytes 12582916
  42.8 1.2 %collective-permute-start.14 = (f32[2048]{0:T(1024)S(1)}, f32[2048]{0:T(1024)S(1)}, u32[]{:S(2)}, u32[]{:S(2)}) collective-permute-start(f32[2048]{0:T(1024)S(1)} %log_add_fusion.1), channel_id=1, source_target_pairs={{0,1},{1,0},{2,3},{3,2},{4,5},{5,4},{6,7},{7,6},{8,9},{9,8},{10,11... | collective-permute-start | bytes 24584 | tf_op jit(solution)/shard_map/ppermute | solution.py:26
  44.0 3.7 %collective-permute-start.16 = (f32[2048]{0:T(1024)S(1)}, f32[2048]{0:T(1024)S(1)}, u32[]{:S(2)}, u32[]{:S(2)}) collective-permute-start(f32[2048]{0:T(1024)S(1)} %log_add_fusion), channel_id=1, source_target_pairs={{0,2},{1,7},{2,0},{3,5},{4,6},{5,3},{6,4},{7,1},{8,10},{9,15},{10,... | collective-permute-start | bytes 24584 | tf_op jit(solution)/shard_map/ppermute | solution.py:55
  45.5 3.7 %collective-permute-start.15 = (f32[2048]{0:T(1024)S(1)}, f32[2048]{0:T(1024)S(1)}, u32[]{:S(2)}, u32[]{:S(2)}) collective-permute-start(f32[2048]{0:T(1024)S(1)} %log_add_fusion), channel_id=1, source_target_pairs={{0,2},{1,5},{2,0},{3,7},{4,6},{5,1},{6,4},{7,3},{8,10},{9,13},{10,... | collective-permute-start | bytes 24584 | tf_op jit(solution)/shard_map/ppermute | solution.py:55
  49.1 1.6 %collective-permute-start.17 = (f32[2048]{0:T(1024)S(1)}, f32[2048]{0:T(1024)S(1)}, u32[]{:S(2)}, u32[]{:S(2)}) collective-permute-start(f32[2048]{0:T(1024)S(1)} %bitcast.21), channel_id=1, source_target_pairs={{0,1},{1,0},{2,3},{3,2},{4,5},{5,4},{6,7},{7,6},{8,9},{9,8},{10,11... | collective-permute-start | bytes 24584 | tf_op jit(solution)/shard_map/ppermute | solution.py:26
  53.4 6.7 %collective-permute-start.20 = (bf16[144,512]{1,0:T(8,128)(2,1)S(1)}, bf16[144,512]{1,0:T(8,128)(2,1)S(1)}, u32[]{:S(2)}, u32[]{:S(2)}) collective-permute-start(bf16[144,512]{1,0:T(8,128)(2,1)S(1)} %get-tuple-element.33), channel_id=1, source_target_pairs={{0,8},{8,0},{16,24},{24,16},{1,9},{9,1},{17,25},{25,17},{2,10},{10... | collective-permute-start | bytes 442376 | tf_op jit(solution)/shard_map/ppermute | solution.py:26
  54.9 6.7 %collective-permute-start.21 = (bf16[144,512]{1,0:T(8,128)(2,1)S(1)}, bf16[144,512]{1,0:T(8,128)(2,1)S(1)}, u32[]{:S(2)}, u32[]{:S(2)}) collective-permute-start(bf16[144,512]{1,0:T(8,128)(2,1)S(1)} %get-tuple-element.34), channel_id=1, source_target_pairs={{0,16},{8,24},{16,0},{24,8},{1,17},{9,25},{17,1},{25,9},{2,18},{10... | collective-permute-start | bytes 442376 | tf_op jit(solution)/shard_map/ppermute | solution.py:26
  56.4 7.5 %collective-permute-start.18 = (bf16[128,512]{1,0:T(8,128)(2,1)S(1)}, bf16[128,512]{1,0:T(8,128)(2,1)S(1)}, u32[]{:S(2)}, u32[]{:S(2)}) collective-permute-start(bf16[128,512]{1,0:T(8,128)(2,1)S(1)} %get-tuple-element.31), channel_id=1, source_target_pairs={{0,8},{8,0},{16,24},{24,16},{1,9},{9,1},{17,25},{25,17},{2,10},{10... | collective-permute-start | bytes 393224 | tf_op jit(solution)/shard_map/ppermute | solution.py:26
  57.0 7.2 %collective-permute-start.19 = (bf16[128,512]{1,0:T(8,128)(2,1)S(1)}, bf16[128,512]{1,0:T(8,128)(2,1)S(1)}, u32[]{:S(2)}, u32[]{:S(2)}) collective-permute-start(bf16[128,512]{1,0:T(8,128)(2,1)S(1)} %get-tuple-element.32), channel_id=1, source_target_pairs={{0,16},{8,24},{16,0},{24,8},{1,17},{9,25},{17,1},{25,9},{2,18},{10... | collective-permute-start | bytes 393224 | tf_op jit(solution)/shard_map/ppermute | solution.py:26
  61.8 6.6 %collective-permute-start.23 = (bf16[144,512]{1,0:T(8,128)(2,1)S(1)}, bf16[144,512]{1,0:T(8,128)(2,1)S(1)}, u32[]{:S(2)}, u32[]{:S(2)}) collective-permute-start(bf16[144,512]{1,0:T(8,128)(2,1)S(1)} %get-tuple-element.37.mine), channel_id=1, source_target_pairs={{0,16},{8,24},{16,0},{24,8},{1,17},{9,25},{17,1},{25,9},{2,18},{10... | collective-permute-start | bytes 442376 | tf_op jit(solution)/shard_map/ppermute | solution.py:26
  63.4 6.7 %collective-permute-start.26 = (bf16[144,512]{1,0:T(8,128)(2,1)S(1)}, bf16[144,512]{1,0:T(8,128)(2,1)S(1)}, u32[]{:S(2)}, u32[]{:S(2)}) collective-permute-start(bf16[144,512]{1,0:T(8,128)(2,1)S(1)} %get-tuple-element.40.mine), channel_id=1, source_target_pairs={{0,8},{8,0},{16,24},{24,16},{1,9},{9,1},{17,25},{25,17},{2,10},{10... | collective-permute-start | bytes 442376 | tf_op jit(solution)/shard_map/ppermute | solution.py:26
  64.4 6.6 %collective-permute-start.22 = (bf16[128,512]{1,0:T(8,128)(2,1)S(1)}, bf16[128,512]{1,0:T(8,128)(2,1)S(1)}, u32[]{:S(2)}, u32[]{:S(2)}) collective-permute-start(bf16[128,512]{1,0:T(8,128)(2,1)S(1)} %get-tuple-element.36.mine), channel_id=1, source_target_pairs={{0,16},{8,24},{16,0},{24,8},{1,17},{9,25},{17,1},{25,9},{2,18},{10... | collective-permute-start | bytes 393224 | tf_op jit(solution)/shard_map/ppermute | solution.py:26
  66.0 7.0 %collective-permute-start.25 = (bf16[128,512]{1,0:T(8,128)(2,1)S(1)}, bf16[128,512]{1,0:T(8,128)(2,1)S(1)}, u32[]{:S(2)}, u32[]{:S(2)}) collective-permute-start(bf16[128,512]{1,0:T(8,128)(2,1)S(1)} %get-tuple-element.39.mine), channel_id=1, source_target_pairs={{0,8},{8,0},{16,24},{24,16},{1,9},{9,1},{17,25},{25,17},{2,10},{10... | collective-permute-start | bytes 393224 | tf_op jit(solution)/shard_map/ppermute | solution.py:26
  68.6 7.2 %collective-permute-start.28 = (bf16[144,512]{1,0:T(8,128)(2,1)S(1)}, bf16[144,512]{1,0:T(8,128)(2,1)S(1)}, u32[]{:S(2)}, u32[]{:S(2)}) collective-permute-start(bf16[144,512]{1,0:T(8,128)(2,1)S(1)} %get-tuple-element.42.lower_kept), channel_id=1, source_target_pairs={{0,8},{8,0},{16,24},{24,16},{1,9},{9,1},{17,25},{25,17},{2,10},{10... | collective-permute-start | bytes 442376 | tf_op jit(solution)/shard_map/ppermute | solution.py:26
  70.3 5.5 %collective-permute-start.29 = (bf16[144,512]{1,0:T(8,128)(2,1)S(1)}, bf16[144,512]{1,0:T(8,128)(2,1)S(1)}, u32[]{:S(2)}, u32[]{:S(2)}) collective-permute-start(bf16[144,512]{1,0:T(8,128)(2,1)S(1)} %get-tuple-element.43.upper_kept), channel_id=1, source_target_pairs={{0,16},{8,24},{16,0},{24,8},{1,17},{9,25},{17,1},{25,9},{2,18},{10... | collective-permute-start | bytes 442376 | tf_op jit(solution)/shard_map/ppermute | solution.py:26
  71.1 6.1 %collective-permute-start.24 = (bf16[128,512]{1,0:T(8,128)(2,1)S(1)}, bf16[128,512]{1,0:T(8,128)(2,1)S(1)}, u32[]{:S(2)}, u32[]{:S(2)}) collective-permute-start(bf16[128,512]{1,0:T(8,128)(2,1)S(1)} %shard_map.64.refs_2_), channel_id=1, source_target_pairs={{0,8},{8,0},{16,24},{24,16},{1,9},{9,1},{17,25},{25,17},{2,10},{10... | collective-permute-start | bytes 393224 | tf_op jit(solution)/shard_map/ppermute | solution.py:26
  73.1 5.0 %collective-permute-start.27 = (bf16[128,512]{1,0:T(8,128)(2,1)S(1)}, bf16[128,512]{1,0:T(8,128)(2,1)S(1)}, u32[]{:S(2)}, u32[]{:S(2)}) collective-permute-start(bf16[128,512]{1,0:T(8,128)(2,1)S(1)} %shard_map.66.refs_3_), channel_id=1, source_target_pairs={{0,16},{8,24},{16,0},{24,8},{1,17},{9,25},{17,1},{25,9},{2,18},{10... | collective-permute-start | bytes 393224 | tf_op jit(solution)/shard_map/ppermute | solution.py:26

commit v4 on v3

--- a/solution.py
+++ b/solution.py
@@ -272,16 +272,15 @@
     return whole, [jnp.exp(a - b) for a, b in zip(first, whole)], [jnp.exp(a - b) for a, b in zip(second, whole)]
 
 
-def sent_kernel(plan, embeddings, mass, part, *sent):
+def sent_kernel(chunk, plan, embeddings, mass, part, *sent):
     quarter = plan.shape[0] // 4
     count = quarter // LANES
     width = embeddings.shape[1] // CHUNKS
-    sums = jnp.dot(plan[pl.ds(0, 2 * quarter), :], embeddings[...], preferred_element_type=jnp.float32)
+    columns = embeddings[:, pl.ds(chunk * width, width)]
+    sums = jnp.dot(plan[pl.ds(0, 2 * quarter), :], columns, preferred_element_type=jnp.float32)
     for k in range(2):
         values = sums[k * quarter:(k + 1) * quarter] / columns_of(read(mass, k * count, count))
-        for chunk in range(CHUNKS):
-            lines = read(part, k * count, count) if chunk == 0 else []
-            put(sent[2 * chunk + k], values[:, chunk * width:(chunk + 1) * width], lines)
+        put(sent[k], values, read(part, k * count, count) if chunk == 0 else [])
 
 
 def kept_kernel(plan, embeddings, mass, row, kept, row_out):
@@ -372,7 +371,10 @@
     mass, part = mass.reshape(table(4).shape), part.reshape(table(4).shape)
     flops = columns * rows_here * depth
     chunks = range(CHUNKS)
-    sent = call(sent_kernel, [plan, embeddings, mass, part], [message(chunk) for chunk in chunks for _ in range(2)], flops=flops)
+    sent = []
+    for chunk in chunks:
+        kernel = functools.partial(sent_kernel, chunk)
+        sent += call(kernel, [plan, embeddings, mass, part], [message(chunk)] * 2, flops=flops // CHUNKS)
     got = [flipped(sent[2 * chunk + k], "dp", 1 << orders[k][0]) for chunk in chunks for k in range(2)]
     row = row_now[None, :]
     kept, row_out = call(

time: 79.1 us -> 78.6 us (level)
  waiting for transfers between devices: 28.3 us -> 27.5 us
    ppermute x24, waiting for transfers between devices: 20 us -> 19.2 us  [flipped(): return lax.ppermute(x, axis, [(k, k ^ mask) for k in range(size)])]
    pallas_call x9 -> x10, Pallas kernels: 5.37 us -> 5.54 us  [call(): pl.pallas_call(kernel, out_shape=outs, in_specs=[vmem] * len(operands), o...]
  transfers between devices with their start and end apart: 30 -> 30, of which waited for: 26 -> 25; matrix products, arithmetic and copies ran while one was open for 0% -> 0% of each run, Pallas kernels for 5% -> 6%
where the time goes in v4:
time: 78.6 us; the launch traced here: 78.4 us
  starting transfers between devices  29.9 us (38%)
  waiting for transfers between devices  27.5 us (35%)
  other arithmetic  9.16 us (12%)
  Pallas kernels  6.36 us (8%)
  matrix products  4.57 us (6%)
  between operations  0.9 us (1%)
    ppermute x24, starting transfers between devices, flipped(): return lax.ppermute(x, axis, [(k, k ^ mask) for k in range(size)])  22.7 us
    ppermute x24, waiting for transfers between devices, flipped(): return lax.ppermute(x, axis, [(k, k ^ mask) for k in range(size)])  19.2 us
    ppermute x6, waiting for transfers between devices, split(): lax.ppermute(value, 'cent', [(k, k ^ (odd_mask if k % 2 else even_mask))...  8.29 us
    ppermute x6, starting transfers between devices, split(): lax.ppermute(value, 'cent', [(k, k ^ (odd_mask if k % 2 else even_mask))...  7.23 us
    pallas_call x10, Pallas kernels, call(): pl.pallas_call(kernel, out_shape=outs, in_specs=[vmem] * len(operands), o...  5.54 us
    dot_general x1, matrix products, on_device(): lax.dot_general(sent_and_kept(centroids), embeddings, (((1,), (1,)), ((),...  4.57 us
    reduce_sum x3, other arithmetic, on_device(): mass = jnp.sum(terms, axis=1)  2.58 us
    reduce_sum x3, other arithmetic, on_device(): part = top + jnp.log(jnp.sum(jnp.exp(shifted - top[None, :]), axis=0))  2.33 us
  transfers between devices with their start and end apart: 30, of which 25 were waited for; matrix products, arithmetic and copies ran while one was open for 0% of the time, Pallas kernels for 6%

profile of v4, /device:TPU:0, one launch (start us, length us, event | category | flops | bytes accessed | tf_op | source)
XLA Modules:
  0.0 78.4 jit_solution(16108576097556629633)
XLA Ops:
  0.6 0.8 %broadcast_select_fusion.7 = (f32[128]{0:T(128)S(1)}, f32[128]{0:T(128)S(1)}, f32[128]{0:T(128)S(1)}, f32[128]{0:T(128)S(1)}) fusion(pred[]{:T(512)} %bitcast.3, f32[512]{0:T(512)} %param.5, pred[]{:T(512)} %bitcast.4), kind=kLoop, calls=%fused_computation.91 | loop fusion | flops 512 | bytes 4098 | tf_op jit(solution)/shard_map/jit(_where)/select_n | solution.py:453
  1.5 1.3 %broadcast_select_fusion.3 = (bf16[128,1024]{1,0:T(8,128)(2,1)S(1)}, bf16[128,1024]{1,0:T(8,128)(2,1)S(1)}, bf16[128,1024]{1,0:T(8,128)(2,1)S(1)}, bf16[128,1024]{1,0:T(8,128)(2,1)S(1)}) fusion(pred[]{:T(512)} %bitcast.3, bf16[512,1024]{1,0:T(8,128)(2,1)} %param.4, pred[]{:T(512)} %bitcast.4), kind=kLoop, calls=%fused_computation.25 | loop fusion | flops 524288 | bytes 2097154 | tf_op jit(solution)/shard_map/jit(_where)/select_n | solution.py:453
  2.8 4.6 %add_reduce_fusion.5 = (f32[2048]{0:T(1024)S(1)}, f32[512,2048]{1,0:T(8,128)S(1)}) fusion(f32[512]{0:T(512)S(1)} %pad_maximum_fusion, bf16[2048,1024]{1,0:T(8,128)(2,1)} %embeddings.3, bf16[128,1024]{1,0:T(8,128)(2,1)S(1)} %get-tuple-element.51, bf16[128,1024]{1,0:T(8,128)(2,1)S(1)} %get-tuple-element.52, bf16[128,1024]{1,0:T(8,128)(2,1)S(1)} %get-tuple-element.50, ...), kind=kOutput, calls=%fused_computation.11 | convolution fusion | flops 2154821632 | bytes 9447424 | tf_op jit(solution)/shard_map/dot_general | solution.py:469
  7.3 0.8 exponential_reduce_fusion.4
  8.6 0.8 %collective-permute-done = f32[2048]{0:T(1024)S(1)} collective-permute-done((f32[2048]{0:T(1024)S(1)}, f32[2048]{0:T(1024)S(1)}, u32[]{:S(2)}, u32[]{:S(2)}) %collective-permute-start) | collective-permute-done | bytes 8224 | tf_op jit(solution)/shard_map/ppermute | solution.py:26
  9.5 3.0 %collective-permute-start.2 = (f32[2048]{0:T(1024)S(1)}, f32[2048]{0:T(1024)S(1)}, u32[]{:S(2)}, u32[]{:S(2)}) collective-permute-start(f32[2048]{0:T(1024)S(1)} %log_add_fusion.4), channel_id=1, source_target_pairs={{0,2},{1,7},{2,0},{3,5},{4,6},{5,3},{6,4},{7,1},{8,10},{9,15},{10,... | collective-permute-start | bytes 24584 | tf_op jit(solution)/shard_map/ppermute | solution.py:55
  12.5 1.6 %collective-permute-done.2 = f32[2048]{0:T(1024)S(1)} collective-permute-done((f32[2048]{0:T(1024)S(1)}, f32[2048]{0:T(1024)S(1)}, u32[]{:S(2)}, u32[]{:S(2)}) %collective-permute-start.2) | collective-permute-done | bytes 8224 | tf_op jit(solution)/shard_map/ppermute | solution.py:55
  14.1 2.0 %collective-permute-done.1 = f32[2048]{0:T(1024)S(1)} collective-permute-done((f32[2048]{0:T(1024)S(1)}, f32[2048]{0:T(1024)S(1)}, u32[]{:S(2)}, u32[]{:S(2)}) %collective-permute-start.1) | collective-permute-done | bytes 8224 | tf_op jit(solution)/shard_map/ppermute | solution.py:55
  16.1 1.7 %collective-permute-start.3 = (f32[2048]{0:T(1024)S(1)}, f32[2048]{0:T(1024)S(1)}, u32[]{:S(2)}, u32[]{:S(2)}) collective-permute-start(f32[2048]{0:T(1024)S(1)} %add_select_fusion.1), channel_id=1, source_target_pairs={{0,1},{1,0},{2,3},{3,2},{4,5},{5,4},{6,7},{7,6},{8,9},{9,8},{10,11... | collective-permute-start | bytes 24584 | tf_op jit(solution)/shard_map/ppermute | solution.py:26
  17.9 0.8 %collective-permute-done.3 = f32[2048]{0:T(1024)S(1)} collective-permute-done((f32[2048]{0:T(1024)S(1)}, f32[2048]{0:T(1024)S(1)}, u32[]{:S(2)}, u32[]{:S(2)}) %collective-permute-start.3) | collective-permute-done | bytes 8224 | tf_op jit(solution)/shard_map/ppermute | solution.py:26
  19.1 0.8 %exponential_reduce_fusion.3 = f32[512]{0:T(512)S(1)} fusion(f32[512,2048]{1,0:T(8,128)S(1)} %get-tuple-element.78, f32[512]{0:T(512)S(1)} %add_reduce_fusion.4, f32[2048]{0:T(1024)S(1)} %add_subtract_fusion.2), kind=kLoop, calls=%fused_computation.4 | loop fusion | flops 3145216 | bytes 4206592 | tf_op jit(solution)/shard_map/reduce_sum | solution.py:483
  19.9 2.5 %collective-permute-start.4 = (f32[512]{0:T(512)S(1)}, f32[512]{0:T(512)S(1)}, u32[]{:S(2)}, u32[]{:S(2)}) collective-permute-start(f32[512]{0:T(512)S(1)} %log_add_fusion.9), channel_id=1, source_target_pairs={{0,24},{8,16},{16,8},{24,0},{1,25},{9,17},{17,9},{25,1},{2,26},{10... | collective-permute-start | bytes 6152 | tf_op jit(solution)/shard_map/ppermute | solution.py:26
  23.5 1.0 %collective-permute-done.4 = f32[512]{0:T(512)S(1)} collective-permute-done((f32[512]{0:T(512)S(1)}, f32[512]{0:T(512)S(1)}, u32[]{:S(2)}, u32[]{:S(2)}) %collective-permute-start.4) | collective-permute-done | bytes 2080 | tf_op jit(solution)/shard_map/ppermute | solution.py:26
  24.5 1.5 %collective-permute-done.5 = f32[512]{0:T(512)S(1)} collective-permute-done((f32[512]{0:T(512)S(1)}, f32[512]{0:T(512)S(1)}, u32[]{:S(2)}, u32[]{:S(2)}) %collective-permute-start.5) | collective-permute-done | bytes 2080 | tf_op jit(solution)/shard_map/ppermute | solution.py:26
  27.0 0.8 exponential_reduce_fusion.2
  27.8 1.2 %collective-permute-done.7 = f32[2048]{0:T(1024)S(1)} collective-permute-done((f32[2048]{0:T(1024)S(1)}, f32[2048]{0:T(1024)S(1)}, u32[]{:S(2)}, u32[]{:S(2)}) %collective-permute-start.7) | collective-permute-done | bytes 8224 | tf_op jit(solution)/shard_map/ppermute | solution.py:26
  29.1 2.0 %collective-permute-start.8 = (f32[2048]{0:T(1024)S(1)}, f32[2048]{0:T(1024)S(1)}, u32[]{:S(2)}, u32[]{:S(2)}) collective-permute-start(f32[2048]{0:T(1024)S(1)} %log_add_fusion.2), channel_id=1, source_target_pairs={{0,2},{1,5},{2,0},{3,7},{4,6},{5,1},{6,4},{7,3},{8,10},{9,13},{10,... | collective-permute-start | bytes 24584 | tf_op jit(solution)/shard_map/ppermute | solution.py:55
  31.1 1.6 %collective-permute-done.9 = f32[2048]{0:T(1024)S(1)} collective-permute-done((f32[2048]{0:T(1024)S(1)}, f32[2048]{0:T(1024)S(1)}, u32[]{:S(2)}, u32[]{:S(2)}) %collective-permute-start.9) | collective-permute-done | bytes 8224 | tf_op jit(solution)/shard_map/ppermute | solution.py:55
  32.8 1.0 %collective-permute-start.10 = (f32[2048]{0:T(1024)S(1)}, f32[2048]{0:T(1024)S(1)}, u32[]{:S(2)}, u32[]{:S(2)}) collective-permute-start(f32[2048]{0:T(1024)S(1)} %add_select_fusion), channel_id=1, source_target_pairs={{0,1},{1,0},{2,3},{3,2},{4,5},{5,4},{6,7},{7,6},{8,9},{9,8},{10,11... | collective-permute-start | bytes 24584 | tf_op jit(solution)/shard_map/ppermute | solution.py:26
  33.8 0.8 %collective-permute-done.10 = f32[2048]{0:T(1024)S(1)} collective-permute-done((f32[2048]{0:T(1024)S(1)}, f32[2048]{0:T(1024)S(1)}, u32[]{:S(2)}, u32[]{:S(2)}) %collective-permute-start.10) | collective-permute-done | bytes 8224 | tf_op jit(solution)/shard_map/ppermute | solution.py:26
  35.0 0.8 %exponential_reduce_fusion.1 = f32[512]{0:T(512)S(1)} fusion(f32[512,2048]{1,0:T(8,128)S(1)} %get-tuple-element.78, f32[512]{0:T(512)S(1)} %add_reduce_fusion.2, f32[2048]{0:T(1024)S(1)} %add_subtract_fusion.1), kind=kLoop, calls=%fused_computation.2 | loop fusion | flops 3145216 | bytes 4206592 | tf_op jit(solution)/shard_map/reduce_sum | solution.py:483
  35.9 1.6 %collective-permute-start.11 = (f32[512]{0:T(512)S(1)}, f32[512]{0:T(512)S(1)}, u32[]{:S(2)}, u32[]{:S(2)}) collective-permute-start(f32[512]{0:T(512)S(1)} %log_add_fusion.7), channel_id=1, source_target_pairs={{0,24},{8,16},{16,8},{24,0},{1,25},{9,17},{17,9},{25,1},{2,26},{10... | collective-permute-start | bytes 6152 | tf_op jit(solution)/shard_map/ppermute | solution.py:26
  37.9 1.5 %collective-permute-start.13 = (f32[512]{0:T(512)S(1)}, f32[512]{0:T(512)S(1)}, u32[]{:S(2)}, u32[]{:S(2)}) collective-permute-start(f32[512]{0:T(512)S(1)} %log_add_fusion.7), channel_id=1, source_target_pairs={{0,8},{8,0},{16,24},{24,16},{1,9},{9,1},{17,25},{25,17},{2,10},{10... | collective-permute-start | bytes 6152 | tf_op jit(solution)/shard_map/ppermute | solution.py:26
  39.4 1.0 %collective-permute-done.11 = f32[512]{0:T(512)S(1)} collective-permute-done((f32[512]{0:T(512)S(1)}, f32[512]{0:T(512)S(1)}, u32[]{:S(2)}, u32[]{:S(2)}) %collective-permute-start.11) | collective-permute-done | bytes 2080 | tf_op jit(solution)/shard_map/ppermute | solution.py:26
  41.9 0.8 exponential_reduce_fusion
  42.8 1.2 %collective-permute-done.14 = f32[2048]{0:T(1024)S(1)} collective-permute-done((f32[2048]{0:T(1024)S(1)}, f32[2048]{0:T(1024)S(1)}, u32[]{:S(2)}, u32[]{:S(2)}) %collective-permute-start.14) | collective-permute-done | bytes 8224 | tf_op jit(solution)/shard_map/ppermute | solution.py:26
  44.0 1.4 %collective-permute-start.16 = (f32[2048]{0:T(1024)S(1)}, f32[2048]{0:T(1024)S(1)}, u32[]{:S(2)}, u32[]{:S(2)}) collective-permute-start(f32[2048]{0:T(1024)S(1)} %log_add_fusion), channel_id=1, source_target_pairs={{0,2},{1,7},{2,0},{3,5},{4,6},{5,3},{6,4},{7,1},{8,10},{9,15},{10,... | collective-permute-start | bytes 24584 | tf_op jit(solution)/shard_map/ppermute | solution.py:55
  46.1 1.6 %collective-permute-done.16 = f32[2048]{0:T(1024)S(1)} collective-permute-done((f32[2048]{0:T(1024)S(1)}, f32[2048]{0:T(1024)S(1)}, u32[]{:S(2)}, u32[]{:S(2)}) %collective-permute-start.16) | collective-permute-done | bytes 8224 | tf_op jit(solution)/shard_map/ppermute | solution.py:55
  47.7 1.4 %collective-permute-done.15 = f32[2048]{0:T(1024)S(1)} collective-permute-done((f32[2048]{0:T(1024)S(1)}, f32[2048]{0:T(1024)S(1)}, u32[]{:S(2)}, u32[]{:S(2)}) %collective-permute-start.15) | collective-permute-done | bytes 8224 | tf_op jit(solution)/shard_map/ppermute | solution.py:55
  49.1 0.8 %collective-permute-start.17 = (f32[2048]{0:T(1024)S(1)}, f32[2048]{0:T(1024)S(1)}, u32[]{:S(2)}, u32[]{:S(2)}) collective-permute-start(f32[2048]{0:T(1024)S(1)} %bitcast.22), channel_id=1, source_target_pairs={{0,1},{1,0},{2,3},{3,2},{4,5},{5,4},{6,7},{7,6},{8,9},{9,8},{10,11... | collective-permute-start | bytes 24584 | tf_op jit(solution)/shard_map/ppermute | solution.py:26
  49.9 0.8 %collective-permute-done.17 = f32[2048]{0:T(1024)S(1)} collective-permute-done((f32[2048]{0:T(1024)S(1)}, f32[2048]{0:T(1024)S(1)}, u32[]{:S(2)}, u32[]{:S(2)}) %collective-permute-start.17) | collective-permute-done | bytes 8224 | tf_op jit(solution)/shard_map/ppermute | solution.py:26
  51.2 0.9 %fusion = (f32[512]{0:T(512)S(1)}, bf16[512,2048]{1,0:T(8,128)(2,1)S(1)}) fusion(f32[512,2048]{1,0:T(8,128)S(1)} %get-tuple-element.78, f32[512]{0:T(512)S(1)} %add_reduce_fusion, f32[2048]{0:T(1024)S(1)} %add_subtract_fusion), kind=kLoop, calls=%fused_computation.12 | loop fusion | flops 4193792 | bytes 6303744 | tf_op jit(solution)/shard_map/reduce_sum | solution.py:483
  52.1 0.7 shard_map.61
  52.8 1.6 %collective-permute-start.20 = (bf16[144,512]{1,0:T(8,128)(2,1)S(1)}, bf16[144,512]{1,0:T(8,128)(2,1)S(1)}, u32[]{:S(2)}, u32[]{:S(2)}) collective-permute-start(bf16[144,512]{1,0:T(8,128)(2,1)S(1)} %get-tuple-element.33), channel_id=1, source_target_pairs={{0,8},{8,0},{16,24},{24,16},{1,9},{9,1},{17,25},{25,17},{2,10},{10... | collective-permute-start | bytes 442376 | tf_op jit(solution)/shard_map/ppermute | solution.py:26
  54.4 1.5 %collective-permute-start.21 = (bf16[144,512]{1,0:T(8,128)(2,1)S(1)}, bf16[144,512]{1,0:T(8,128)(2,1)S(1)}, u32[]{:S(2)}, u32[]{:S(2)}) collective-permute-start(bf16[144,512]{1,0:T(8,128)(2,1)S(1)} %get-tuple-element.34), channel_id=1, source_target_pairs={{0,16},{8,24},{16,0},{24,8},{1,17},{9,25},{17,1},{25,9},{2,18},{10... | collective-permute-start | bytes 442376 | tf_op jit(solution)/shard_map/ppermute | solution.py:26
  55.9 0.7 shard_map.60
  57.7 1.7 %shard_map.59 = (f32[2,128,1024]{2,1,0:T(8,128)S(1)}, f32[1,2048]{1,0:T(1,128)}) custom-call(bf16[512,2048]{1,0:T(8,128)(2,1)S(1)} %get-tuple-element.48.plan, bf16[2048,1024]{1,0:T(8,128)(2,1)S(1)} %copy-done, f32[4,128]{1,0:T(4,128)S(1)} %bitcast.21, f32[1,2048]{1,0:T(1,128)S(1)} %bitcast.18), custom_call_target="tpu_custom_call" | custom-call | flops 1073741824 | bytes 524288 | tf_op jit(solution)/shard_map/pallas_call | solution.py:355
  59.4 1.6 %collective-permute-done.21.upper = bf16[144,512]{1,0:T(8,128)(2,1)S(1)} collective-permute-done((bf16[144,512]{1,0:T(8,128)(2,1)S(1)}, bf16[144,512]{1,0:T(8,128)(2,1)S(1)}, u32[]{:S(2)}, u32[]{:S(2)}) %collective-permute-start.21) | collective-permute-done | bytes 147488 | tf_op jit(solution)/shard_map/ppermute | solution.py:26
  61.2 1.6 %collective-permute-start.23 = (bf16[144,512]{1,0:T(8,128)(2,1)S(1)}, bf16[144,512]{1,0:T(8,128)(2,1)S(1)}, u32[]{:S(2)}, u32[]{:S(2)}) collective-permute-start(bf16[144,512]{1,0:T(8,128)(2,1)S(1)} %get-tuple-element.37.mine), channel_id=1, source_target_pairs={{0,16},{8,24},{16,0},{24,8},{1,17},{9,25},{17,1},{25,9},{2,18},{10... | collective-permute-start | bytes 442376 | tf_op jit(solution)/shard_map/ppermute | solution.py:26
  63.8 1.6 %collective-permute-start.22 = (bf16[128,512]{1,0:T(8,128)(2,1)S(1)}, bf16[128,512]{1,0:T(8,128)(2,1)S(1)}, u32[]{:S(2)}, u32[]{:S(2)}) collective-permute-start(bf16[128,512]{1,0:T(8,128)(2,1)S(1)} %get-tuple-element.36.mine), channel_id=1, source_target_pairs={{0,16},{8,24},{16,0},{24,8},{1,17},{9,25},{17,1},{25,9},{2,18},{10... | collective-permute-start | bytes 393224 | tf_op jit(solution)/shard_map/ppermute | solution.py:26
  65.7 2.0 %collective-permute-done.23.theirs = bf16[144,512]{1,0:T(8,128)(2,1)S(1)} collective-permute-done((bf16[144,512]{1,0:T(8,128)(2,1)S(1)}, bf16[144,512]{1,0:T(8,128)(2,1)S(1)}, u32[]{:S(2)}, u32[]{:S(2)}) %collective-permute-start.23) | collective-permute-done | bytes 147488 | tf_op jit(solution)/shard_map/ppermute | solution.py:26
  68.3 1.3 %collective-permute-done.26.theirs = bf16[144,512]{1,0:T(8,128)(2,1)S(1)} collective-permute-done((bf16[144,512]{1,0:T(8,128)(2,1)S(1)}, bf16[144,512]{1,0:T(8,128)(2,1)S(1)}, u32[]{:S(2)}, u32[]{:S(2)}) %collective-permute-start.26) | collective-permute-done | bytes 147488 | tf_op jit(solution)/shard_map/ppermute | solution.py:26
  69.8 0.6 collective-permute-start.29
  70.6 1.6 %collective-permute-start.24 = (bf16[128,512]{1,0:T(8,128)(2,1)S(1)}, bf16[128,512]{1,0:T(8,128)(2,1)S(1)}, u32[]{:S(2)}, u32[]{:S(2)}) collective-permute-start(bf16[128,512]{1,0:T(8,128)(2,1)S(1)} %shard_map.65.refs_2_), channel_id=1, source_target_pairs={{0,8},{8,0},{16,24},{24,16},{1,9},{9,1},{17,25},{25,17},{2,10},{10... | collective-permute-start | bytes 393224 | tf_op jit(solution)/shard_map/ppermute | solution.py:26
  73.0 2.2 %collective-permute-done.28.lower_sent = bf16[144,512]{1,0:T(8,128)(2,1)S(1)} collective-permute-done((bf16[144,512]{1,0:T(8,128)(2,1)S(1)}, bf16[144,512]{1,0:T(8,128)(2,1)S(1)}, u32[]{:S(2)}, u32[]{:S(2)}) %collective-permute-start.28) | collective-permute-done | bytes 147488 | tf_op jit(solution)/shard_map/ppermute | solution.py:26
  75.2 1.4 %shard_map.68 = (bf16[512,1024]{1,0:T(8,128)(2,1)}, f32[4,128]{1,0:T(4,128)}) custom-call(bf16[144,512]{1,0:T(8,128)(2,1)S(1)} %collective-permute-done.28.lower_sent, bf16[144,512]{1,0:T(8,128)(2,1)S(1)} %collective-permute-done.29.upper_sent, bf16[144,512]{1,0:T(8,128)(2,1)S(1)} %get-tuple-element.42.lower_kept, ...), custom_call_target="tpu_custom_call" | custom-call | bytes 524288 | tf_op jit(solution)/shard_map/pallas_call | solution.py:355
  76.7 0.9 %collective-permute-done.27.refs_1_ = bf16[128,512]{1,0:T(8,128)(2,1)S(1)} collective-permute-done((bf16[128,512]{1,0:T(8,128)(2,1)S(1)}, bf16[128,512]{1,0:T(8,128)(2,1)S(1)}, u32[]{:S(2)}, u32[]{:S(2)}) %collective-permute-start.27) | collective-permute-done | bytes 131104 | tf_op jit(solution)/shard_map/ppermute | solution.py:26
  77.6 0.8 %shard_map.69 = bf16[512,1024]{1,0:T(8,128)(2,1)} custom-call(bf16[128,512]{1,0:T(8,128)(2,1)S(1)} %collective-permute-done.24.refs_0_, bf16[128,512]{1,0:T(8,128)(2,1)S(1)} %collective-permute-done.27.refs_1_, bf16[128,512]{1,0:T(8,128)(2,1)S(1)} %shard_map.65.refs_2_, bf16[128,512]{1,0:T(8,128)(2,1)S(1)} %shard_map.67.refs_3_, ...), custom_call_target="tpu_custom_call", output_to_operand_aliasing={{}: (4, {})} | custom-call | tf_op jit(solution)/shard_map/pallas_call | solution.py:93
  (66 shorter events, 11.2 us)
Async XLA Ops:
  8.1 1.4 %collective-permute-start = (f32[2048]{0:T(1024)S(1)}, f32[2048]{0:T(1024)S(1)}, u32[]{:S(2)}, u32[]{:S(2)}) collective-permute-start(f32[2048]{0:T(1024)S(1)} %log_add_fusion.5), channel_id=1, source_target_pairs={{0,1},{1,0},{2,3},{3,2},{4,5},{5,4},{6,7},{7,6},{8,9},{9,8},{10,11... | collective-permute-start | bytes 24584 | tf_op jit(solution)/shard_map/ppermute | solution.py:26
  9.5 4.6 %collective-permute-start.2 = (f32[2048]{0:T(1024)S(1)}, f32[2048]{0:T(1024)S(1)}, u32[]{:S(2)}, u32[]{:S(2)}) collective-permute-start(f32[2048]{0:T(1024)S(1)} %log_add_fusion.4), channel_id=1, source_target_pairs={{0,2},{1,7},{2,0},{3,5},{4,6},{5,3},{6,4},{7,1},{8,10},{9,15},{10,... | collective-permute-start | bytes 24584 | tf_op jit(solution)/shard_map/ppermute | solution.py:55
  12.5 3.7 %collective-permute-start.1 = (f32[2048]{0:T(1024)S(1)}, f32[2048]{0:T(1024)S(1)}, u32[]{:S(2)}, u32[]{:S(2)}) collective-permute-start(f32[2048]{0:T(1024)S(1)} %log_add_fusion.4), channel_id=1, source_target_pairs={{0,2},{1,5},{2,0},{3,7},{4,6},{5,1},{6,4},{7,3},{8,10},{9,13},{10,... | collective-permute-start | bytes 24584 | tf_op jit(solution)/shard_map/ppermute | solution.py:55
  16.1 2.6 %collective-permute-start.3 = (f32[2048]{0:T(1024)S(1)}, f32[2048]{0:T(1024)S(1)}, u32[]{:S(2)}, u32[]{:S(2)}) collective-permute-start(f32[2048]{0:T(1024)S(1)} %add_select_fusion.1), channel_id=1, source_target_pairs={{0,1},{1,0},{2,3},{3,2},{4,5},{5,4},{6,7},{7,6},{8,9},{9,8},{10,11... | collective-permute-start | bytes 24584 | tf_op jit(solution)/shard_map/ppermute | solution.py:26
  19.9 4.5 %collective-permute-start.4 = (f32[512]{0:T(512)S(1)}, f32[512]{0:T(512)S(1)}, u32[]{:S(2)}, u32[]{:S(2)}) collective-permute-start(f32[512]{0:T(512)S(1)} %log_add_fusion.9), channel_id=1, source_target_pairs={{0,24},{8,16},{16,8},{24,0},{1,25},{9,17},{17,9},{25,1},{2,26},{10... | collective-permute-start | bytes 6152 | tf_op jit(solution)/shard_map/ppermute | solution.py:26
  22.4 3.6 %collective-permute-start.5 = (f32[512]{0:T(512)S(1)}, f32[512]{0:T(512)S(1)}, u32[]{:S(2)}, u32[]{:S(2)}) collective-permute-start(f32[512]{0:T(512)S(1)} %log_add_fusion.9), channel_id=1, source_target_pairs={{0,16},{8,24},{16,0},{24,8},{1,17},{9,25},{17,1},{25,9},{2,18},{10... | collective-permute-start | bytes 6152 | tf_op jit(solution)/shard_map/ppermute | solution.py:26
  23.0 3.6 %collective-permute-start.6 = (f32[512]{0:T(512)S(1)}, f32[512]{0:T(512)S(1)}, u32[]{:S(2)}, u32[]{:S(2)}) collective-permute-start(f32[512]{0:T(512)S(1)} %log_add_fusion.9), channel_id=1, source_target_pairs={{0,8},{8,0},{16,24},{24,16},{1,9},{9,1},{17,25},{25,17},{2,10},{10... | collective-permute-start | bytes 6152 | tf_op jit(solution)/shard_map/ppermute | solution.py:26
  27.8 1.2 %collective-permute-start.7 = (f32[2048]{0:T(1024)S(1)}, f32[2048]{0:T(1024)S(1)}, u32[]{:S(2)}, u32[]{:S(2)}) collective-permute-start(f32[2048]{0:T(1024)S(1)} %log_add_fusion.3), channel_id=1, source_target_pairs={{0,1},{1,0},{2,3},{3,2},{4,5},{5,4},{6,7},{7,6},{8,9},{9,8},{10,11... | collective-permute-start | bytes 24584 | tf_op jit(solution)/shard_map/ppermute | solution.py:26
  29.0 3.7 %collective-permute-start.9 = (f32[2048]{0:T(1024)S(1)}, f32[2048]{0:T(1024)S(1)}, u32[]{:S(2)}, u32[]{:S(2)}) collective-permute-start(f32[2048]{0:T(1024)S(1)} %log_add_fusion.2), channel_id=1, source_target_pairs={{0,2},{1,7},{2,0},{3,5},{4,6},{5,3},{6,4},{7,1},{8,10},{9,15},{10,... | collective-permute-start | bytes 24584 | tf_op jit(solution)/shard_map/ppermute | solution.py:55
  29.1 3.7 %collective-permute-start.8 = (f32[2048]{0:T(1024)S(1)}, f32[2048]{0:T(1024)S(1)}, u32[]{:S(2)}, u32[]{:S(2)}) collective-permute-start(f32[2048]{0:T(1024)S(1)} %log_add_fusion.2), channel_id=1, source_target_pairs={{0,2},{1,5},{2,0},{3,7},{4,6},{5,1},{6,4},{7,3},{8,10},{9,13},{10,... | collective-permute-start | bytes 24584 | tf_op jit(solution)/shard_map/ppermute | solution.py:55
  32.8 1.8 %collective-permute-start.10 = (f32[2048]{0:T(1024)S(1)}, f32[2048]{0:T(1024)S(1)}, u32[]{:S(2)}, u32[]{:S(2)}) collective-permute-start(f32[2048]{0:T(1024)S(1)} %add_select_fusion), channel_id=1, source_target_pairs={{0,1},{1,0},{2,3},{3,2},{4,5},{5,4},{6,7},{7,6},{8,9},{9,8},{10,11... | collective-permute-start | bytes 24584 | tf_op jit(solution)/shard_map/ppermute | solution.py:26
  35.9 4.5 %collective-permute-start.11 = (f32[512]{0:T(512)S(1)}, f32[512]{0:T(512)S(1)}, u32[]{:S(2)}, u32[]{:S(2)}) collective-permute-start(f32[512]{0:T(512)S(1)} %log_add_fusion.7), channel_id=1, source_target_pairs={{0,24},{8,16},{16,8},{24,0},{1,25},{9,17},{17,9},{25,1},{2,26},{10... | collective-permute-start | bytes 6152 | tf_op jit(solution)/shard_map/ppermute | solution.py:26
  37.4 3.6 %collective-permute-start.12 = (f32[512]{0:T(512)S(1)}, f32[512]{0:T(512)S(1)}, u32[]{:S(2)}, u32[]{:S(2)}) collective-permute-start(f32[512]{0:T(512)S(1)} %log_add_fusion.7), channel_id=1, source_target_pairs={{0,16},{8,24},{16,0},{24,8},{1,17},{9,25},{17,1},{25,9},{2,18},{10... | collective-permute-start | bytes 6152 | tf_op jit(solution)/shard_map/ppermute | solution.py:26
  37.9 3.6 %collective-permute-start.13 = (f32[512]{0:T(512)S(1)}, f32[512]{0:T(512)S(1)}, u32[]{:S(2)}, u32[]{:S(2)}) collective-permute-start(f32[512]{0:T(512)S(1)} %log_add_fusion.7), channel_id=1, source_target_pairs={{0,8},{8,0},{16,24},{24,16},{1,9},{9,1},{17,25},{25,17},{2,10},{10... | collective-permute-start | bytes 6152 | tf_op jit(solution)/shard_map/ppermute | solution.py:26
  41.6 7.6 %copy-start = (bf16[2048,1024]{1,0:T(8,128)(2,1)S(1)}, bf16[2048,1024]{1,0:T(8,128)(2,1)}, u32[]{:S(2)}) copy-start(bf16[2048,1024]{1,0:T(8,128)(2,1)} %embeddings.3) | copy-start | bytes 12582916
  42.8 1.2 %collective-permute-start.14 = (f32[2048]{0:T(1024)S(1)}, f32[2048]{0:T(1024)S(1)}, u32[]{:S(2)}, u32[]{:S(2)}) collective-permute-start(f32[2048]{0:T(1024)S(1)} %log_add_fusion.1), channel_id=1, source_target_pairs={{0,1},{1,0},{2,3},{3,2},{4,5},{5,4},{6,7},{7,6},{8,9},{9,8},{10,11... | collective-permute-start | bytes 24584 | tf_op jit(solution)/shard_map/ppermute | solution.py:26
  44.0 3.7 %collective-permute-start.16 = (f32[2048]{0:T(1024)S(1)}, f32[2048]{0:T(1024)S(1)}, u32[]{:S(2)}, u32[]{:S(2)}) collective-permute-start(f32[2048]{0:T(1024)S(1)} %log_add_fusion), channel_id=1, source_target_pairs={{0,2},{1,7},{2,0},{3,5},{4,6},{5,3},{6,4},{7,1},{8,10},{9,15},{10,... | collective-permute-start | bytes 24584 | tf_op jit(solution)/shard_map/ppermute | solution.py:55
  45.5 3.7 %collective-permute-start.15 = (f32[2048]{0:T(1024)S(1)}, f32[2048]{0:T(1024)S(1)}, u32[]{:S(2)}, u32[]{:S(2)}) collective-permute-start(f32[2048]{0:T(1024)S(1)} %log_add_fusion), channel_id=1, source_target_pairs={{0,2},{1,5},{2,0},{3,7},{4,6},{5,1},{6,4},{7,3},{8,10},{9,13},{10,... | collective-permute-start | bytes 24584 | tf_op jit(solution)/shard_map/ppermute | solution.py:55
  49.1 1.6 %collective-permute-start.17 = (f32[2048]{0:T(1024)S(1)}, f32[2048]{0:T(1024)S(1)}, u32[]{:S(2)}, u32[]{:S(2)}) collective-permute-start(f32[2048]{0:T(1024)S(1)} %bitcast.22), channel_id=1, source_target_pairs={{0,1},{1,0},{2,3},{3,2},{4,5},{5,4},{6,7},{7,6},{8,9},{9,8},{10,11... | collective-permute-start | bytes 24584 | tf_op jit(solution)/shard_map/ppermute | solution.py:26
  52.8 6.6 %collective-permute-start.20 = (bf16[144,512]{1,0:T(8,128)(2,1)S(1)}, bf16[144,512]{1,0:T(8,128)(2,1)S(1)}, u32[]{:S(2)}, u32[]{:S(2)}) collective-permute-start(bf16[144,512]{1,0:T(8,128)(2,1)S(1)} %get-tuple-element.33), channel_id=1, source_target_pairs={{0,8},{8,0},{16,24},{24,16},{1,9},{9,1},{17,25},{25,17},{2,10},{10... | collective-permute-start | bytes 442376 | tf_op jit(solution)/shard_map/ppermute | solution.py:26
  54.4 6.6 %collective-permute-start.21 = (bf16[144,512]{1,0:T(8,128)(2,1)S(1)}, bf16[144,512]{1,0:T(8,128)(2,1)S(1)}, u32[]{:S(2)}, u32[]{:S(2)}) collective-permute-start(bf16[144,512]{1,0:T(8,128)(2,1)S(1)} %get-tuple-element.34), channel_id=1, source_target_pairs={{0,16},{8,24},{16,0},{24,8},{1,17},{9,25},{17,1},{25,9},{2,18},{10... | collective-permute-start | bytes 442376 | tf_op jit(solution)/shard_map/ppermute | solution.py:26
  56.6 6.8 %collective-permute-start.18 = (bf16[128,512]{1,0:T(8,128)(2,1)S(1)}, bf16[128,512]{1,0:T(8,128)(2,1)S(1)}, u32[]{:S(2)}, u32[]{:S(2)}) collective-permute-start(bf16[128,512]{1,0:T(8,128)(2,1)S(1)} %get-tuple-element.31), channel_id=1, source_target_pairs={{0,8},{8,0},{16,24},{24,16},{1,9},{9,1},{17,25},{25,17},{2,10},{10... | collective-permute-start | bytes 393224 | tf_op jit(solution)/shard_map/ppermute | solution.py:26
  57.2 6.4 %collective-permute-start.19 = (bf16[128,512]{1,0:T(8,128)(2,1)S(1)}, bf16[128,512]{1,0:T(8,128)(2,1)S(1)}, u32[]{:S(2)}, u32[]{:S(2)}) collective-permute-start(bf16[128,512]{1,0:T(8,128)(2,1)S(1)} %get-tuple-element.32), channel_id=1, source_target_pairs={{0,16},{8,24},{16,0},{24,8},{1,17},{9,25},{17,1},{25,9},{2,18},{10... | collective-permute-start | bytes 393224 | tf_op jit(solution)/shard_map/ppermute | solution.py:26
  61.2 6.5 %collective-permute-start.23 = (bf16[144,512]{1,0:T(8,128)(2,1)S(1)}, bf16[144,512]{1,0:T(8,128)(2,1)S(1)}, u32[]{:S(2)}, u32[]{:S(2)}) collective-permute-start(bf16[144,512]{1,0:T(8,128)(2,1)S(1)} %get-tuple-element.37.mine), channel_id=1, source_target_pairs={{0,16},{8,24},{16,0},{24,8},{1,17},{9,25},{17,1},{25,9},{2,18},{10... | collective-permute-start | bytes 442376 | tf_op jit(solution)/shard_map/ppermute | solution.py:26
  62.9 6.7 %collective-permute-start.26 = (bf16[144,512]{1,0:T(8,128)(2,1)S(1)}, bf16[144,512]{1,0:T(8,128)(2,1)S(1)}, u32[]{:S(2)}, u32[]{:S(2)}) collective-permute-start(bf16[144,512]{1,0:T(8,128)(2,1)S(1)} %get-tuple-element.40.mine), channel_id=1, source_target_pairs={{0,8},{8,0},{16,24},{24,16},{1,9},{9,1},{17,25},{25,17},{2,10},{10... | collective-permute-start | bytes 442376 | tf_op jit(solution)/shard_map/ppermute | solution.py:26
  63.8 6.6 %collective-permute-start.22 = (bf16[128,512]{1,0:T(8,128)(2,1)S(1)}, bf16[128,512]{1,0:T(8,128)(2,1)S(1)}, u32[]{:S(2)}, u32[]{:S(2)}) collective-permute-start(bf16[128,512]{1,0:T(8,128)(2,1)S(1)} %get-tuple-element.36.mine), channel_id=1, source_target_pairs={{0,16},{8,24},{16,0},{24,8},{1,17},{9,25},{17,1},{25,9},{2,18},{10... | collective-permute-start | bytes 393224 | tf_op jit(solution)/shard_map/ppermute | solution.py:26
  65.4 7.0 %collective-permute-start.25 = (bf16[128,512]{1,0:T(8,128)(2,1)S(1)}, bf16[128,512]{1,0:T(8,128)(2,1)S(1)}, u32[]{:S(2)}, u32[]{:S(2)}) collective-permute-start(bf16[128,512]{1,0:T(8,128)(2,1)S(1)} %get-tuple-element.39.mine), channel_id=1, source_target_pairs={{0,8},{8,0},{16,24},{24,16},{1,9},{9,1},{17,25},{25,17},{2,10},{10... | collective-permute-start | bytes 393224 | tf_op jit(solution)/shard_map/ppermute | solution.py:26
  67.9 7.3 %collective-permute-start.28 = (bf16[144,512]{1,0:T(8,128)(2,1)S(1)}, bf16[144,512]{1,0:T(8,128)(2,1)S(1)}, u32[]{:S(2)}, u32[]{:S(2)}) collective-permute-start(bf16[144,512]{1,0:T(8,128)(2,1)S(1)} %get-tuple-element.42.lower_kept), channel_id=1, source_target_pairs={{0,8},{8,0},{16,24},{24,16},{1,9},{9,1},{17,25},{25,17},{2,10},{10... | collective-permute-start | bytes 442376 | tf_op jit(solution)/shard_map/ppermute | solution.py:26
  69.8 5.5 %collective-permute-start.29 = (bf16[144,512]{1,0:T(8,128)(2,1)S(1)}, bf16[144,512]{1,0:T(8,128)(2,1)S(1)}, u32[]{:S(2)}, u32[]{:S(2)}) collective-permute-start(bf16[144,512]{1,0:T(8,128)(2,1)S(1)} %get-tuple-element.43.upper_kept), channel_id=1, source_target_pairs={{0,16},{8,24},{16,0},{24,8},{1,17},{9,25},{17,1},{25,9},{2,18},{10... | collective-permute-start | bytes 442376 | tf_op jit(solution)/shard_map/ppermute | solution.py:26
  70.6 6.1 %collective-permute-start.24 = (bf16[128,512]{1,0:T(8,128)(2,1)S(1)}, bf16[128,512]{1,0:T(8,128)(2,1)S(1)}, u32[]{:S(2)}, u32[]{:S(2)}) collective-permute-start(bf16[128,512]{1,0:T(8,128)(2,1)S(1)} %shard_map.65.refs_2_), channel_id=1, source_target_pairs={{0,8},{8,0},{16,24},{24,16},{1,9},{9,1},{17,25},{25,17},{2,10},{10... | collective-permute-start | bytes 393224 | tf_op jit(solution)/shard_map/ppermute | solution.py:26
  72.5 5.0 %collective-permute-start.27 = (bf16[128,512]{1,0:T(8,128)(2,1)S(1)}, bf16[128,512]{1,0:T(8,128)(2,1)S(1)}, u32[]{:S(2)}, u32[]{:S(2)}) collective-permute-start(bf16[128,512]{1,0:T(8,128)(2,1)S(1)} %shard_map.67.refs_3_), channel_id=1, source_target_pairs={{0,16},{8,24},{16,0},{24,8},{1,17},{9,25},{17,1},{25,9},{2,18},{10... | collective-permute-start | bytes 393224 | tf_op jit(solution)/shard_map/ppermute | solution.py:26

commit v5 on v4

--- a/solution.py
+++ b/solution.py
@@ -273,23 +273,23 @@
 
 
 def sent_kernel(chunk, plan, embeddings, mass, part, *sent):
-    quarter = plan.shape[0] // 4
+    quarter = plan.shape[0] // 2
     count = quarter // LANES
     width = embeddings.shape[1] // CHUNKS
     columns = embeddings[:, pl.ds(chunk * width, width)]
-    sums = jnp.dot(plan[pl.ds(0, 2 * quarter), :], columns, preferred_element_type=jnp.float32)
+    sums = jnp.dot(plan[...], columns, preferred_element_type=jnp.float32)
     for k in range(2):
         values = sums[k * quarter:(k + 1) * quarter] / columns_of(read(mass, k * count, count))
         put(sent[k], values, read(part, k * count, count) if chunk == 0 else [])
 
 
 def kept_kernel(plan, embeddings, mass, row, kept, row_out):
-    quarter = plan.shape[0] // 4
+    quarter = plan.shape[0] // 2
     count = quarter // LANES
     row_out[...] = row[...]
-    sums = jnp.dot(plan[pl.ds(2 * quarter, 2 * quarter), :], embeddings[...], preferred_element_type=jnp.float32)
+    sums = jnp.dot(plan[...], embeddings[...], preferred_element_type=jnp.float32)
     for k in range(2):
-        kept[k] = sums[k * quarter:(k + 1) * quarter] / columns_of(read(mass, (2 + k) * count, count))
+        kept[k] = sums[k * quarter:(k + 1) * quarter] / columns_of(read(mass, k * count, count))
 
 
 def pair_kernel(chunk, kept, lower, upper, known, out_lower, out_upper, *weights_out):
@@ -297,7 +297,7 @@
     count = quarter // LANES
     for k, (got, out) in enumerate(((lower, out_lower), (upper, out_upper))):
         if chunk == 0:
-            pair, own, other = joined(read(known, (2 + k) * count, count), lines_of(got, count))
+            pair, own, other = joined(read(known, k * count, count), lines_of(got, count))
             write(weights_out[0], 2 * k * count, own + other)
         else:
             pair = []
@@ -342,8 +342,16 @@
         copy.wait()
 
 
-def last_sum(plan, part, mass, row_now, embeddings, log_k, orders):
-    columns, rows_here = plan.shape
+def last_terms(scores, row):
+    lifted = scores + row[None, :]
+    top = jnp.max(lifted, axis=1)
+    terms = jnp.exp(lifted - top[:, None])
+    mass = jnp.sum(terms, axis=1)
+    return terms.astype(jnp.bfloat16), mass, top + jnp.log(mass)
+
+
+def last_sum(scores, row_now, embeddings, log_k, orders):
+    columns, rows_here = scores.shape
     depth = embeddings.shape[1]
     quarter = columns // 4
     width = depth // CHUNKS
@@ -368,24 +376,26 @@
     def table(count):
         return jax.ShapeDtypeStruct((count * lines, LANES), f32)
 
-    mass, part = mass.reshape(table(4).shape), part.reshape(table(4).shape)
     flops = columns * rows_here * depth
     chunks = range(CHUNKS)
+    plan, mass, part = last_terms(scores[:2 * quarter], row_now)
+    operands = [plan, embeddings, mass.reshape(table(2).shape), part.reshape(table(2).shape)]
     sent = []
     for chunk in chunks:
-        kernel = functools.partial(sent_kernel, chunk)
-        sent += call(kernel, [plan, embeddings, mass, part], [message(chunk)] * 2, flops=flops // CHUNKS)
+        sent += call(functools.partial(sent_kernel, chunk), operands, [message(chunk)] * 2, flops=flops // CHUNKS)
     got = [flipped(sent[2 * chunk + k], "dp", 1 << orders[k][0]) for chunk in chunks for k in range(2)]
+    row_now = lax.optimization_barrier((row_now, sent[:2]))[0]
+    plan, mass, part = last_terms(scores[2 * quarter:], row_now)
     row = row_now[None, :]
     kept, row_out = call(
         kept_kernel,
-        [plan, embeddings, mass, row],
+        [plan, embeddings, mass.reshape(table(2).shape), row],
         [jax.ShapeDtypeStruct((2, quarter, depth), f32), jax.ShapeDtypeStruct(row.shape, f32)],
         specs=[vmem, pl.BlockSpec(row.shape, lambda: (0, 0))],
         flops=flops,
     )
     pairs = []
-    known = part
+    known = part.reshape(table(2).shape)
     for chunk in chunks:
         outs = [message(chunk)] * 2 + ([table(4)] if chunk == 0 else [])
         results = call(functools.partial(pair_kernel, chunk), [kept, got[2 * chunk], got[2 * chunk + 1], known], outs)
@@ -477,16 +487,11 @@
         last = step_index == ITERS - 1
         part = lse_over_cent(part, odd, lambda x: beside(x, embeddings) if last else x)
         row_now = -math.log(n_total) - part
-        lifted = scores + row_now[None, :]
-        top = jnp.max(lifted, axis=1)
-        terms = jnp.exp(lifted - top[:, None])
-        mass = jnp.sum(terms, axis=1)
-        part = top + jnp.log(mass)
-        if step_index < ITERS - 1:
+        if last and len(bits) == 2:
+            return last_sum(scores, row_now, embeddings, math.log(k_total), orders)
+        plan, mass, part = last_terms(scores, row_now)
+        if not last:
             col_now = -math.log(k_total) - lse_over_dp(part, aligned)
-    plan = terms.astype(jnp.bfloat16)
-    if len(bits) == 2:
-        return last_sum(plan, part, mass, row_now, embeddings, math.log(k_total), orders)
     new_centroids, row_out, whole = last_sum_by_vectors(plan, part, mass, row_now, embeddings, chosen, orders, aligned)
     return new_centroids, row_out, -math.log(k_total) - whole
 

time: 78.6 us -> 78.1 us (level)
  waiting for transfers between devices: 27.5 us -> 25.3 us
  starting transfers between devices: 29.9 us -> 31.3 us
    ppermute x24, waiting for transfers between devices: 19.2 us -> 17 us  [flipped(): return lax.ppermute(x, axis, [(k, k ^ mask) for k in range(size)])]
    ppermute x24, starting transfers between devices: 22.7 us -> 24 us  [flipped(): return lax.ppermute(x, axis, [(k, k ^ mask) for k in range(size)])]
    reduce_sum x3 -> x4, other arithmetic: 2.58 us -> 2.72 us  [last_terms(): mass = jnp.sum(terms, axis=1)]
  transfers between devices with their start and end apart: 30 -> 30, of which waited for: 25 -> 24; matrix products, arithmetic and copies ran while one was open for 0% -> 1% of each run, Pallas kernels for 6% -> 6%
where the time goes in v5:
time: 78.1 us; the launch traced here: 77.9 us
  starting transfers between devices  31.3 us (40%)
  waiting for transfers between devices  25.3 us (32%)
  other arithmetic  9.39 us (12%)
  Pallas kernels  6.35 us (8%)
  matrix products  4.57 us (6%)
  between operations  0.91 us (1%)
    ppermute x24, starting transfers between devices, flipped(): return lax.ppermute(x, axis, [(k, k ^ mask) for k in range(size)])  24 us
    ppermute x24, waiting for transfers between devices, flipped(): return lax.ppermute(x, axis, [(k, k ^ mask) for k in range(size)])  17 us
    ppermute x6, waiting for transfers between devices, split(): lax.ppermute(value, 'cent', [(k, k ^ (odd_mask if k % 2 else even_mask))...  8.29 us
    ppermute x6, starting transfers between devices, split(): lax.ppermute(value, 'cent', [(k, k ^ (odd_mask if k % 2 else even_mask))...  7.23 us
    pallas_call x10, Pallas kernels, call(): pl.pallas_call(kernel, out_shape=outs, in_specs=[vmem] * len(operands), o...  5.53 us
    dot_general x1, matrix products, on_device(): lax.dot_general(sent_and_kept(centroids), embeddings, (((1,), (1,)), ((),...  4.57 us
    reduce_sum x4, other arithmetic, last_terms(): mass = jnp.sum(terms, axis=1)  2.72 us
    reduce_sum x3, other arithmetic, on_device(): part = top + jnp.log(jnp.sum(jnp.exp(shifted - top[None, :]), axis=0))  2.33 us
  transfers between devices with their start and end apart: 30, of which 24 were waited for; matrix products, arithmetic and copies ran while one was open for 1% of the time, Pallas kernels for 6%

profile of v5, /device:TPU:0, one launch (start us, length us, event | category | flops | bytes accessed | tf_op | source)
XLA Modules:
  0.0 77.9 jit_solution(4543791911898898073)
XLA Ops:
  0.6 0.8 %broadcast_select_fusion.7 = (f32[128]{0:T(128)S(1)}, f32[128]{0:T(128)S(1)}, f32[128]{0:T(128)S(1)}, f32[128]{0:T(128)S(1)}) fusion(pred[]{:T(512)} %bitcast.3, f32[512]{0:T(512)} %param.5, pred[]{:T(512)} %bitcast.4), kind=kLoop, calls=%fused_computation.98 | loop fusion | flops 512 | bytes 4098 | tf_op jit(solution)/shard_map/jit(_where)/select_n | solution.py:463
  1.5 1.3 %broadcast_select_fusion.3 = (bf16[128,1024]{1,0:T(8,128)(2,1)S(1)}, bf16[128,1024]{1,0:T(8,128)(2,1)S(1)}, bf16[128,1024]{1,0:T(8,128)(2,1)S(1)}, bf16[128,1024]{1,0:T(8,128)(2,1)S(1)}) fusion(pred[]{:T(512)} %bitcast.3, bf16[512,1024]{1,0:T(8,128)(2,1)} %param.4, pred[]{:T(512)} %bitcast.4), kind=kLoop, calls=%fused_computation.31 | loop fusion | flops 524288 | bytes 2097154 | tf_op jit(solution)/shard_map/jit(_where)/select_n | solution.py:463
  2.8 4.6 %add_reduce_fusion.4 = (f32[2048]{0:T(1024)S(1)}, f32[512,2048]{1,0:T(8,128)S(1)}) fusion(f32[512]{0:T(512)S(1)} %pad_maximum_fusion, bf16[2048,1024]{1,0:T(8,128)(2,1)} %embeddings.3, bf16[128,1024]{1,0:T(8,128)(2,1)S(1)} %get-tuple-element.55, bf16[128,1024]{1,0:T(8,128)(2,1)S(1)} %get-tuple-element.56, bf16[128,1024]{1,0:T(8,128)(2,1)S(1)} %get-tuple-element.54, ...), kind=kOutput, calls=%fused_computation.9 | convolution fusion | flops 2154821632 | bytes 9447424 | tf_op jit(solution)/shard_map/dot_general | solution.py:479
  7.3 0.8 exponential_reduce_fusion.4
  8.6 0.8 %collective-permute-done = f32[2048]{0:T(1024)S(1)} collective-permute-done((f32[2048]{0:T(1024)S(1)}, f32[2048]{0:T(1024)S(1)}, u32[]{:S(2)}, u32[]{:S(2)}) %collective-permute-start) | collective-permute-done | bytes 8224 | tf_op jit(solution)/shard_map/ppermute | solution.py:26
  9.5 3.0 %collective-permute-start.2 = (f32[2048]{0:T(1024)S(1)}, f32[2048]{0:T(1024)S(1)}, u32[]{:S(2)}, u32[]{:S(2)}) collective-permute-start(f32[2048]{0:T(1024)S(1)} %log_add_fusion.4), channel_id=1, source_target_pairs={{0,2},{1,7},{2,0},{3,5},{4,6},{5,3},{6,4},{7,1},{8,10},{9,15},{10,... | collective-permute-start | bytes 24584 | tf_op jit(solution)/shard_map/ppermute | solution.py:55
  12.5 1.6 %collective-permute-done.2 = f32[2048]{0:T(1024)S(1)} collective-permute-done((f32[2048]{0:T(1024)S(1)}, f32[2048]{0:T(1024)S(1)}, u32[]{:S(2)}, u32[]{:S(2)}) %collective-permute-start.2) | collective-permute-done | bytes 8224 | tf_op jit(solution)/shard_map/ppermute | solution.py:55
  14.1 2.0 %collective-permute-done.1 = f32[2048]{0:T(1024)S(1)} collective-permute-done((f32[2048]{0:T(1024)S(1)}, f32[2048]{0:T(1024)S(1)}, u32[]{:S(2)}, u32[]{:S(2)}) %collective-permute-start.1) | collective-permute-done | bytes 8224 | tf_op jit(solution)/shard_map/ppermute | solution.py:55
  16.1 1.7 %collective-permute-start.3 = (f32[2048]{0:T(1024)S(1)}, f32[2048]{0:T(1024)S(1)}, u32[]{:S(2)}, u32[]{:S(2)}) collective-permute-start(f32[2048]{0:T(1024)S(1)} %add_select_fusion.1), channel_id=1, source_target_pairs={{0,1},{1,0},{2,3},{3,2},{4,5},{5,4},{6,7},{7,6},{8,9},{9,8},{10,11... | collective-permute-start | bytes 24584 | tf_op jit(solution)/shard_map/ppermute | solution.py:26
  17.9 0.8 %collective-permute-done.3 = f32[2048]{0:T(1024)S(1)} collective-permute-done((f32[2048]{0:T(1024)S(1)}, f32[2048]{0:T(1024)S(1)}, u32[]{:S(2)}, u32[]{:S(2)}) %collective-permute-start.3) | collective-permute-done | bytes 8224 | tf_op jit(solution)/shard_map/ppermute | solution.py:26
  19.1 0.8 %exponential_reduce_fusion.3 = f32[512]{0:T(512)S(1)} fusion(f32[512,2048]{1,0:T(8,128)S(1)} %get-tuple-element.82, f32[512]{0:T(512)S(1)} %add_reduce_fusion.3, f32[2048]{0:T(1024)S(1)} %add_subtract_fusion.2), kind=kLoop, calls=%fused_computation.3 | loop fusion | flops 3145216 | bytes 4206592 | tf_op jit(solution)/shard_map/reduce_sum | solution.py:349
  19.9 2.5 %collective-permute-start.4 = (f32[512]{0:T(512)S(1)}, f32[512]{0:T(512)S(1)}, u32[]{:S(2)}, u32[]{:S(2)}) collective-permute-start(f32[512]{0:T(512)S(1)} %log_add_fusion.9), channel_id=1, source_target_pairs={{0,24},{8,16},{16,8},{24,0},{1,25},{9,17},{17,9},{25,1},{2,26},{10... | collective-permute-start | bytes 6152 | tf_op jit(solution)/shard_map/ppermute | solution.py:26
  23.5 1.0 %collective-permute-done.4 = f32[512]{0:T(512)S(1)} collective-permute-done((f32[512]{0:T(512)S(1)}, f32[512]{0:T(512)S(1)}, u32[]{:S(2)}, u32[]{:S(2)}) %collective-permute-start.4) | collective-permute-done | bytes 2080 | tf_op jit(solution)/shard_map/ppermute | solution.py:26
  24.5 1.5 %collective-permute-done.5 = f32[512]{0:T(512)S(1)} collective-permute-done((f32[512]{0:T(512)S(1)}, f32[512]{0:T(512)S(1)}, u32[]{:S(2)}, u32[]{:S(2)}) %collective-permute-start.5) | collective-permute-done | bytes 2080 | tf_op jit(solution)/shard_map/ppermute | solution.py:26
  27.0 0.8 %exponential_reduce_fusion.2 = f32[2048]{0:T(1024)S(1)} fusion(f32[512,2048]{1,0:T(8,128)S(1)} %get-tuple-element.82, f32[2048]{0:T(1024)S(1)} %add_reduce_fusion.2, f32[512]{0:T(512)S(1)} %add_subtract_fusion.4), kind=kLoop, calls=%fused_computation.2 | loop fusion | flops 3143680 | bytes 4212736 | tf_op jit(solution)/shard_map/reduce_sum | solution.py:486
  27.8 1.2 %collective-permute-done.7 = f32[2048]{0:T(1024)S(1)} collective-permute-done((f32[2048]{0:T(1024)S(1)}, f32[2048]{0:T(1024)S(1)}, u32[]{:S(2)}, u32[]{:S(2)}) %collective-permute-start.7) | collective-permute-done | bytes 8224 | tf_op jit(solution)/shard_map/ppermute | solution.py:26
  29.1 2.0 %collective-permute-start.8 = (f32[2048]{0:T(1024)S(1)}, f32[2048]{0:T(1024)S(1)}, u32[]{:S(2)}, u32[]{:S(2)}) collective-permute-start(f32[2048]{0:T(1024)S(1)} %log_add_fusion.2), channel_id=1, source_target_pairs={{0,2},{1,5},{2,0},{3,7},{4,6},{5,1},{6,4},{7,3},{8,10},{9,13},{10,... | collective-permute-start | bytes 24584 | tf_op jit(solution)/shard_map/ppermute | solution.py:55
  31.1 1.6 %collective-permute-done.9 = f32[2048]{0:T(1024)S(1)} collective-permute-done((f32[2048]{0:T(1024)S(1)}, f32[2048]{0:T(1024)S(1)}, u32[]{:S(2)}, u32[]{:S(2)}) %collective-permute-start.9) | collective-permute-done | bytes 8224 | tf_op jit(solution)/shard_map/ppermute | solution.py:55
  32.8 1.0 %collective-permute-start.10 = (f32[2048]{0:T(1024)S(1)}, f32[2048]{0:T(1024)S(1)}, u32[]{:S(2)}, u32[]{:S(2)}) collective-permute-start(f32[2048]{0:T(1024)S(1)} %add_select_fusion), channel_id=1, source_target_pairs={{0,1},{1,0},{2,3},{3,2},{4,5},{5,4},{6,7},{7,6},{8,9},{9,8},{10,11... | collective-permute-start | bytes 24584 | tf_op jit(solution)/shard_map/ppermute | solution.py:26
  33.8 0.8 %collective-permute-done.10 = f32[2048]{0:T(1024)S(1)} collective-permute-done((f32[2048]{0:T(1024)S(1)}, f32[2048]{0:T(1024)S(1)}, u32[]{:S(2)}, u32[]{:S(2)}) %collective-permute-start.10) | collective-permute-done | bytes 8224 | tf_op jit(solution)/shard_map/ppermute | solution.py:26
  35.0 0.8 %exponential_reduce_fusion.1 = f32[512]{0:T(512)S(1)} fusion(f32[512,2048]{1,0:T(8,128)S(1)} %get-tuple-element.82, f32[512]{0:T(512)S(1)} %add_reduce_fusion.1, f32[2048]{0:T(1024)S(1)} %add_subtract_fusion.1), kind=kLoop, calls=%fused_computation.1 | loop fusion | flops 3145216 | bytes 4206592 | tf_op jit(solution)/shard_map/reduce_sum | solution.py:349
  35.9 1.6 %collective-permute-start.11 = (f32[512]{0:T(512)S(1)}, f32[512]{0:T(512)S(1)}, u32[]{:S(2)}, u32[]{:S(2)}) collective-permute-start(f32[512]{0:T(512)S(1)} %log_add_fusion.7), channel_id=1, source_target_pairs={{0,24},{8,16},{16,8},{24,0},{1,25},{9,17},{17,9},{25,1},{2,26},{10... | collective-permute-start | bytes 6152 | tf_op jit(solution)/shard_map/ppermute | solution.py:26
  37.9 1.5 %collective-permute-start.13 = (f32[512]{0:T(512)S(1)}, f32[512]{0:T(512)S(1)}, u32[]{:S(2)}, u32[]{:S(2)}) collective-permute-start(f32[512]{0:T(512)S(1)} %log_add_fusion.7), channel_id=1, source_target_pairs={{0,8},{8,0},{16,24},{24,16},{1,9},{9,1},{17,25},{25,17},{2,10},{10... | collective-permute-start | bytes 6152 | tf_op jit(solution)/shard_map/ppermute | solution.py:26
  39.4 1.0 %collective-permute-done.11 = f32[512]{0:T(512)S(1)} collective-permute-done((f32[512]{0:T(512)S(1)}, f32[512]{0:T(512)S(1)}, u32[]{:S(2)}, u32[]{:S(2)}) %collective-permute-start.11) | collective-permute-done | bytes 2080 | tf_op jit(solution)/shard_map/ppermute | solution.py:26
  41.9 0.8 %exponential_reduce_fusion = f32[2048]{0:T(1024)S(1)} fusion(f32[512,2048]{1,0:T(8,128)S(1)} %get-tuple-element.82, f32[2048]{0:T(1024)S(1)} %add_reduce_fusion, f32[512]{0:T(512)S(1)} %add_subtract_fusion.3), kind=kLoop, calls=%fused_computation | loop fusion | flops 3143680 | bytes 4212736 | tf_op jit(solution)/shard_map/reduce_sum | solution.py:486
  42.8 1.2 %collective-permute-done.14 = f32[2048]{0:T(1024)S(1)} collective-permute-done((f32[2048]{0:T(1024)S(1)}, f32[2048]{0:T(1024)S(1)}, u32[]{:S(2)}, u32[]{:S(2)}) %collective-permute-start.14) | collective-permute-done | bytes 8224 | tf_op jit(solution)/shard_map/ppermute | solution.py:26
  44.0 1.4 %collective-permute-start.16 = (f32[2048]{0:T(1024)S(1)}, f32[2048]{0:T(1024)S(1)}, u32[]{:S(2)}, u32[]{:S(2)}) collective-permute-start(f32[2048]{0:T(1024)S(1)} %log_add_fusion), channel_id=1, source_target_pairs={{0,2},{1,7},{2,0},{3,5},{4,6},{5,3},{6,4},{7,1},{8,10},{9,15},{10,... | collective-permute-start | bytes 24584 | tf_op jit(solution)/shard_map/ppermute | solution.py:55
  45.5 0.6 collective-permute-start.15
  46.1 1.6 %collective-permute-done.16 = f32[2048]{0:T(1024)S(1)} collective-permute-done((f32[2048]{0:T(1024)S(1)}, f32[2048]{0:T(1024)S(1)}, u32[]{:S(2)}, u32[]{:S(2)}) %collective-permute-start.16) | collective-permute-done | bytes 8224 | tf_op jit(solution)/shard_map/ppermute | solution.py:55
  47.7 1.4 %collective-permute-done.15 = f32[2048]{0:T(1024)S(1)} collective-permute-done((f32[2048]{0:T(1024)S(1)}, f32[2048]{0:T(1024)S(1)}, u32[]{:S(2)}, u32[]{:S(2)}) %collective-permute-start.15) | collective-permute-done | bytes 8224 | tf_op jit(solution)/shard_map/ppermute | solution.py:55
  49.1 0.8 %collective-permute-start.17 = (f32[2048]{0:T(1024)S(1)}, f32[2048]{0:T(1024)S(1)}, u32[]{:S(2)}, u32[]{:S(2)}) collective-permute-start(f32[2048]{0:T(1024)S(1)} %bitcast.23), channel_id=1, source_target_pairs={{0,1},{1,0},{2,3},{3,2},{4,5},{5,4},{6,7},{7,6},{8,9},{9,8},{10,11... | collective-permute-start | bytes 24584 | tf_op jit(solution)/shard_map/ppermute | solution.py:26
  49.9 0.8 %collective-permute-done.17 = f32[2048]{0:T(1024)S(1)} collective-permute-done((f32[2048]{0:T(1024)S(1)}, f32[2048]{0:T(1024)S(1)}, u32[]{:S(2)}, u32[]{:S(2)}) %collective-permute-start.17) | collective-permute-done | bytes 8224 | tf_op jit(solution)/shard_map/ppermute | solution.py:26
  51.6 0.7 shard_map.59
  52.3 1.6 %collective-permute-start.20 = (bf16[144,512]{1,0:T(8,128)(2,1)S(1)}, bf16[144,512]{1,0:T(8,128)(2,1)S(1)}, u32[]{:S(2)}, u32[]{:S(2)}) collective-permute-start(bf16[144,512]{1,0:T(8,128)(2,1)S(1)} %get-tuple-element.31), channel_id=1, source_target_pairs={{0,8},{8,0},{16,24},{24,16},{1,9},{9,1},{17,25},{25,17},{2,10},{10... | collective-permute-start | bytes 442376 | tf_op jit(solution)/shard_map/ppermute | solution.py:26
  53.8 1.5 %collective-permute-start.21 = (bf16[144,512]{1,0:T(8,128)(2,1)S(1)}, bf16[144,512]{1,0:T(8,128)(2,1)S(1)}, u32[]{:S(2)}, u32[]{:S(2)}) collective-permute-start(bf16[144,512]{1,0:T(8,128)(2,1)S(1)} %get-tuple-element.32), channel_id=1, source_target_pairs={{0,16},{8,24},{16,0},{24,8},{1,17},{9,25},{17,1},{25,9},{2,18},{10... | collective-permute-start | bytes 442376 | tf_op jit(solution)/shard_map/ppermute | solution.py:26
  56.1 0.7 shard_map.61
  58.0 1.7 %shard_map.60 = (f32[2,128,1024]{2,1,0:T(8,128)S(1)}, f32[1,2048]{1,0:T(1,128)}) custom-call(bf16[256,2048]{1,0:T(8,128)(2,1)S(1)} %get-tuple-element.50.plan, bf16[2048,1024]{1,0:T(8,128)(2,1)S(1)} %copy-done, f32[2,128]{1,0:T(2,128)S(1)} %bitcast.26, f32[1,2048]{1,0:T(1,128)S(1)} %bitcast.22), custom_call_target="tpu_custom_call" | custom-call | flops 1073741824 | bytes 524288 | tf_op jit(solution)/shard_map/pallas_call | solution.py:363
  59.9 2.4 %collective-permute-start.23 = (bf16[144,512]{1,0:T(8,128)(2,1)S(1)}, bf16[144,512]{1,0:T(8,128)(2,1)S(1)}, u32[]{:S(2)}, u32[]{:S(2)}) collective-permute-start(bf16[144,512]{1,0:T(8,128)(2,1)S(1)} %get-tuple-element.39.mine), channel_id=1, source_target_pairs={{0,16},{8,24},{16,0},{24,8},{1,17},{9,25},{17,1},{25,9},{2,18},{10... | collective-permute-start | bytes 442376 | tf_op jit(solution)/shard_map/ppermute | solution.py:26
  62.3 0.6 collective-permute-start.26
  63.4 1.5 %collective-permute-start.22 = (bf16[128,512]{1,0:T(8,128)(2,1)S(1)}, bf16[128,512]{1,0:T(8,128)(2,1)S(1)}, u32[]{:S(2)}, u32[]{:S(2)}) collective-permute-start(bf16[128,512]{1,0:T(8,128)(2,1)S(1)} %get-tuple-element.38.mine), channel_id=1, source_target_pairs={{0,16},{8,24},{16,0},{24,8},{1,17},{9,25},{17,1},{25,9},{2,18},{10... | collective-permute-start | bytes 393224 | tf_op jit(solution)/shard_map/ppermute | solution.py:26
  64.9 1.9 %collective-permute-done.23.theirs = bf16[144,512]{1,0:T(8,128)(2,1)S(1)} collective-permute-done((bf16[144,512]{1,0:T(8,128)(2,1)S(1)}, bf16[144,512]{1,0:T(8,128)(2,1)S(1)}, u32[]{:S(2)}, u32[]{:S(2)}) %collective-permute-start.23) | collective-permute-done | bytes 147488 | tf_op jit(solution)/shard_map/ppermute | solution.py:26
  67.0 1.4 %collective-permute-start.28 = (bf16[144,512]{1,0:T(8,128)(2,1)S(1)}, bf16[144,512]{1,0:T(8,128)(2,1)S(1)}, u32[]{:S(2)}, u32[]{:S(2)}) collective-permute-start(bf16[144,512]{1,0:T(8,128)(2,1)S(1)} %get-tuple-element.44.lower_kept), channel_id=1, source_target_pairs={{0,8},{8,0},{16,24},{24,16},{1,9},{9,1},{17,25},{25,17},{2,10},{10... | collective-permute-start | bytes 442376 | tf_op jit(solution)/shard_map/ppermute | solution.py:26
  69.2 0.8 collective-permute-start.29
  70.1 1.5 %collective-permute-start.24 = (bf16[128,512]{1,0:T(8,128)(2,1)S(1)}, bf16[128,512]{1,0:T(8,128)(2,1)S(1)}, u32[]{:S(2)}, u32[]{:S(2)}) collective-permute-start(bf16[128,512]{1,0:T(8,128)(2,1)S(1)} %shard_map.65.refs_2_), channel_id=1, source_target_pairs={{0,8},{8,0},{16,24},{24,16},{1,9},{9,1},{17,25},{25,17},{2,10},{10... | collective-permute-start | bytes 393224 | tf_op jit(solution)/shard_map/ppermute | solution.py:26
  72.4 2.4 %collective-permute-done.28.lower_sent = bf16[144,512]{1,0:T(8,128)(2,1)S(1)} collective-permute-done((bf16[144,512]{1,0:T(8,128)(2,1)S(1)}, bf16[144,512]{1,0:T(8,128)(2,1)S(1)}, u32[]{:S(2)}, u32[]{:S(2)}) %collective-permute-start.28) | collective-permute-done | bytes 147488 | tf_op jit(solution)/shard_map/ppermute | solution.py:26
  74.7 1.4 %shard_map.68 = (bf16[512,1024]{1,0:T(8,128)(2,1)}, f32[4,128]{1,0:T(4,128)}) custom-call(bf16[144,512]{1,0:T(8,128)(2,1)S(1)} %collective-permute-done.28.lower_sent, bf16[144,512]{1,0:T(8,128)(2,1)S(1)} %collective-permute-done.29.upper_sent, bf16[144,512]{1,0:T(8,128)(2,1)S(1)} %get-tuple-element.44.lower_kept, ...), custom_call_target="tpu_custom_call" | custom-call | bytes 524288 | tf_op jit(solution)/shard_map/pallas_call | solution.py:363
  76.2 0.9 %collective-permute-done.27.refs_1_ = bf16[128,512]{1,0:T(8,128)(2,1)S(1)} collective-permute-done((bf16[128,512]{1,0:T(8,128)(2,1)S(1)}, bf16[128,512]{1,0:T(8,128)(2,1)S(1)}, u32[]{:S(2)}, u32[]{:S(2)}) %collective-permute-start.27) | collective-permute-done | bytes 131104 | tf_op jit(solution)/shard_map/ppermute | solution.py:26
  77.0 0.8 %shard_map.69 = bf16[512,1024]{1,0:T(8,128)(2,1)} custom-call(bf16[128,512]{1,0:T(8,128)(2,1)S(1)} %collective-permute-done.24.refs_0_, bf16[128,512]{1,0:T(8,128)(2,1)S(1)} %collective-permute-done.27.refs_1_, bf16[128,512]{1,0:T(8,128)(2,1)S(1)} %shard_map.65.refs_2_, bf16[128,512]{1,0:T(8,128)(2,1)S(1)} %shard_map.67.refs_3_, ...), custom_call_target="tpu_custom_call", output_to_operand_aliasing={{}: (4, {})} | custom-call | tf_op jit(solution)/shard_map/pallas_call | solution.py:93
  (69 shorter events, 11.0 us)
Async XLA Ops:
  8.1 1.4 %collective-permute-start = (f32[2048]{0:T(1024)S(1)}, f32[2048]{0:T(1024)S(1)}, u32[]{:S(2)}, u32[]{:S(2)}) collective-permute-start(f32[2048]{0:T(1024)S(1)} %log_add_fusion.5), channel_id=1, source_target_pairs={{0,1},{1,0},{2,3},{3,2},{4,5},{5,4},{6,7},{7,6},{8,9},{9,8},{10,11... | collective-permute-start | bytes 24584 | tf_op jit(solution)/shard_map/ppermute | solution.py:26
  9.5 4.6 %collective-permute-start.2 = (f32[2048]{0:T(1024)S(1)}, f32[2048]{0:T(1024)S(1)}, u32[]{:S(2)}, u32[]{:S(2)}) collective-permute-start(f32[2048]{0:T(1024)S(1)} %log_add_fusion.4), channel_id=1, source_target_pairs={{0,2},{1,7},{2,0},{3,5},{4,6},{5,3},{6,4},{7,1},{8,10},{9,15},{10,... | collective-permute-start | bytes 24584 | tf_op jit(solution)/shard_map/ppermute | solution.py:55
  12.5 3.7 %collective-permute-start.1 = (f32[2048]{0:T(1024)S(1)}, f32[2048]{0:T(1024)S(1)}, u32[]{:S(2)}, u32[]{:S(2)}) collective-permute-start(f32[2048]{0:T(1024)S(1)} %log_add_fusion.4), channel_id=1, source_target_pairs={{0,2},{1,5},{2,0},{3,7},{4,6},{5,1},{6,4},{7,3},{8,10},{9,13},{10,... | collective-permute-start | bytes 24584 | tf_op jit(solution)/shard_map/ppermute | solution.py:55
  16.1 2.6 %collective-permute-start.3 = (f32[2048]{0:T(1024)S(1)}, f32[2048]{0:T(1024)S(1)}, u32[]{:S(2)}, u32[]{:S(2)}) collective-permute-start(f32[2048]{0:T(1024)S(1)} %add_select_fusion.1), channel_id=1, source_target_pairs={{0,1},{1,0},{2,3},{3,2},{4,5},{5,4},{6,7},{7,6},{8,9},{9,8},{10,11... | collective-permute-start | bytes 24584 | tf_op jit(solution)/shard_map/ppermute | solution.py:26
  19.9 4.5 %collective-permute-start.4 = (f32[512]{0:T(512)S(1)}, f32[512]{0:T(512)S(1)}, u32[]{:S(2)}, u32[]{:S(2)}) collective-permute-start(f32[512]{0:T(512)S(1)} %log_add_fusion.9), channel_id=1, source_target_pairs={{0,24},{8,16},{16,8},{24,0},{1,25},{9,17},{17,9},{25,1},{2,26},{10... | collective-permute-start | bytes 6152 | tf_op jit(solution)/shard_map/ppermute | solution.py:26
  22.4 3.6 %collective-permute-start.5 = (f32[512]{0:T(512)S(1)}, f32[512]{0:T(512)S(1)}, u32[]{:S(2)}, u32[]{:S(2)}) collective-permute-start(f32[512]{0:T(512)S(1)} %log_add_fusion.9), channel_id=1, source_target_pairs={{0,16},{8,24},{16,0},{24,8},{1,17},{9,25},{17,1},{25,9},{2,18},{10... | collective-permute-start | bytes 6152 | tf_op jit(solution)/shard_map/ppermute | solution.py:26
  23.0 3.6 %collective-permute-start.6 = (f32[512]{0:T(512)S(1)}, f32[512]{0:T(512)S(1)}, u32[]{:S(2)}, u32[]{:S(2)}) collective-permute-start(f32[512]{0:T(512)S(1)} %log_add_fusion.9), channel_id=1, source_target_pairs={{0,8},{8,0},{16,24},{24,16},{1,9},{9,1},{17,25},{25,17},{2,10},{10... | collective-permute-start | bytes 6152 | tf_op jit(solution)/shard_map/ppermute | solution.py:26
  27.8 1.2 %collective-permute-start.7 = (f32[2048]{0:T(1024)S(1)}, f32[2048]{0:T(1024)S(1)}, u32[]{:S(2)}, u32[]{:S(2)}) collective-permute-start(f32[2048]{0:T(1024)S(1)} %log_add_fusion.3), channel_id=1, source_target_pairs={{0,1},{1,0},{2,3},{3,2},{4,5},{5,4},{6,7},{7,6},{8,9},{9,8},{10,11... | collective-permute-start | bytes 24584 | tf_op jit(solution)/shard_map/ppermute | solution.py:26
  29.0 3.7 %collective-permute-start.9 = (f32[2048]{0:T(1024)S(1)}, f32[2048]{0:T(1024)S(1)}, u32[]{:S(2)}, u32[]{:S(2)}) collective-permute-start(f32[2048]{0:T(1024)S(1)} %log_add_fusion.2), channel_id=1, source_target_pairs={{0,2},{1,7},{2,0},{3,5},{4,6},{5,3},{6,4},{7,1},{8,10},{9,15},{10,... | collective-permute-start | bytes 24584 | tf_op jit(solution)/shard_map/ppermute | solution.py:55
  29.1 3.7 %collective-permute-start.8 = (f32[2048]{0:T(1024)S(1)}, f32[2048]{0:T(1024)S(1)}, u32[]{:S(2)}, u32[]{:S(2)}) collective-permute-start(f32[2048]{0:T(1024)S(1)} %log_add_fusion.2), channel_id=1, source_target_pairs={{0,2},{1,5},{2,0},{3,7},{4,6},{5,1},{6,4},{7,3},{8,10},{9,13},{10,... | collective-permute-start | bytes 24584 | tf_op jit(solution)/shard_map/ppermute | solution.py:55
  32.8 1.8 %collective-permute-start.10 = (f32[2048]{0:T(1024)S(1)}, f32[2048]{0:T(1024)S(1)}, u32[]{:S(2)}, u32[]{:S(2)}) collective-permute-start(f32[2048]{0:T(1024)S(1)} %add_select_fusion), channel_id=1, source_target_pairs={{0,1},{1,0},{2,3},{3,2},{4,5},{5,4},{6,7},{7,6},{8,9},{9,8},{10,11... | collective-permute-start | bytes 24584 | tf_op jit(solution)/shard_map/ppermute | solution.py:26
  35.9 4.5 %collective-permute-start.11 = (f32[512]{0:T(512)S(1)}, f32[512]{0:T(512)S(1)}, u32[]{:S(2)}, u32[]{:S(2)}) collective-permute-start(f32[512]{0:T(512)S(1)} %log_add_fusion.7), channel_id=1, source_target_pairs={{0,24},{8,16},{16,8},{24,0},{1,25},{9,17},{17,9},{25,1},{2,26},{10... | collective-permute-start | bytes 6152 | tf_op jit(solution)/shard_map/ppermute | solution.py:26
  37.4 3.6 %collective-permute-start.12 = (f32[512]{0:T(512)S(1)}, f32[512]{0:T(512)S(1)}, u32[]{:S(2)}, u32[]{:S(2)}) collective-permute-start(f32[512]{0:T(512)S(1)} %log_add_fusion.7), channel_id=1, source_target_pairs={{0,16},{8,24},{16,0},{24,8},{1,17},{9,25},{17,1},{25,9},{2,18},{10... | collective-permute-start | bytes 6152 | tf_op jit(solution)/shard_map/ppermute | solution.py:26
  37.9 3.6 %collective-permute-start.13 = (f32[512]{0:T(512)S(1)}, f32[512]{0:T(512)S(1)}, u32[]{:S(2)}, u32[]{:S(2)}) collective-permute-start(f32[512]{0:T(512)S(1)} %log_add_fusion.7), channel_id=1, source_target_pairs={{0,8},{8,0},{16,24},{24,16},{1,9},{9,1},{17,25},{25,17},{2,10},{10... | collective-permute-start | bytes 6152 | tf_op jit(solution)/shard_map/ppermute | solution.py:26
  41.6 7.6 %copy-start = (bf16[2048,1024]{1,0:T(8,128)(2,1)S(1)}, bf16[2048,1024]{1,0:T(8,128)(2,1)}, u32[]{:S(2)}) copy-start(bf16[2048,1024]{1,0:T(8,128)(2,1)} %embeddings.3) | copy-start | bytes 12582916
  42.8 1.2 %collective-permute-start.14 = (f32[2048]{0:T(1024)S(1)}, f32[2048]{0:T(1024)S(1)}, u32[]{:S(2)}, u32[]{:S(2)}) collective-permute-start(f32[2048]{0:T(1024)S(1)} %log_add_fusion.1), channel_id=1, source_target_pairs={{0,1},{1,0},{2,3},{3,2},{4,5},{5,4},{6,7},{7,6},{8,9},{9,8},{10,11... | collective-permute-start | bytes 24584 | tf_op jit(solution)/shard_map/ppermute | solution.py:26
  44.0 3.7 %collective-permute-start.16 = (f32[2048]{0:T(1024)S(1)}, f32[2048]{0:T(1024)S(1)}, u32[]{:S(2)}, u32[]{:S(2)}) collective-permute-start(f32[2048]{0:T(1024)S(1)} %log_add_fusion), channel_id=1, source_target_pairs={{0,2},{1,7},{2,0},{3,5},{4,6},{5,3},{6,4},{7,1},{8,10},{9,15},{10,... | collective-permute-start | bytes 24584 | tf_op jit(solution)/shard_map/ppermute | solution.py:55
  45.5 3.7 %collective-permute-start.15 = (f32[2048]{0:T(1024)S(1)}, f32[2048]{0:T(1024)S(1)}, u32[]{:S(2)}, u32[]{:S(2)}) collective-permute-start(f32[2048]{0:T(1024)S(1)} %log_add_fusion), channel_id=1, source_target_pairs={{0,2},{1,5},{2,0},{3,7},{4,6},{5,1},{6,4},{7,3},{8,10},{9,13},{10,... | collective-permute-start | bytes 24584 | tf_op jit(solution)/shard_map/ppermute | solution.py:55
  49.1 1.6 %collective-permute-start.17 = (f32[2048]{0:T(1024)S(1)}, f32[2048]{0:T(1024)S(1)}, u32[]{:S(2)}, u32[]{:S(2)}) collective-permute-start(f32[2048]{0:T(1024)S(1)} %bitcast.23), channel_id=1, source_target_pairs={{0,1},{1,0},{2,3},{3,2},{4,5},{5,4},{6,7},{7,6},{8,9},{9,8},{10,11... | collective-permute-start | bytes 24584 | tf_op jit(solution)/shard_map/ppermute | solution.py:26
  52.3 7.4 %collective-permute-start.20 = (bf16[144,512]{1,0:T(8,128)(2,1)S(1)}, bf16[144,512]{1,0:T(8,128)(2,1)S(1)}, u32[]{:S(2)}, u32[]{:S(2)}) collective-permute-start(bf16[144,512]{1,0:T(8,128)(2,1)S(1)} %get-tuple-element.31), channel_id=1, source_target_pairs={{0,8},{8,0},{16,24},{24,16},{1,9},{9,1},{17,25},{25,17},{2,10},{10... | collective-permute-start | bytes 442376 | tf_op jit(solution)/shard_map/ppermute | solution.py:26
  53.8 5.9 %collective-permute-start.21 = (bf16[144,512]{1,0:T(8,128)(2,1)S(1)}, bf16[144,512]{1,0:T(8,128)(2,1)S(1)}, u32[]{:S(2)}, u32[]{:S(2)}) collective-permute-start(bf16[144,512]{1,0:T(8,128)(2,1)S(1)} %get-tuple-element.32), channel_id=1, source_target_pairs={{0,16},{8,24},{16,0},{24,8},{1,17},{9,25},{17,1},{25,9},{2,18},{10... | collective-permute-start | bytes 442376 | tf_op jit(solution)/shard_map/ppermute | solution.py:26
  56.8 6.1 %collective-permute-start.18 = (bf16[128,512]{1,0:T(8,128)(2,1)S(1)}, bf16[128,512]{1,0:T(8,128)(2,1)S(1)}, u32[]{:S(2)}, u32[]{:S(2)}) collective-permute-start(bf16[128,512]{1,0:T(8,128)(2,1)S(1)} %get-tuple-element.35), channel_id=1, source_target_pairs={{0,8},{8,0},{16,24},{24,16},{1,9},{9,1},{17,25},{25,17},{2,10},{10... | collective-permute-start | bytes 393224 | tf_op jit(solution)/shard_map/ppermute | solution.py:26
  57.5 5.7 %collective-permute-start.19 = (bf16[128,512]{1,0:T(8,128)(2,1)S(1)}, bf16[128,512]{1,0:T(8,128)(2,1)S(1)}, u32[]{:S(2)}, u32[]{:S(2)}) collective-permute-start(bf16[128,512]{1,0:T(8,128)(2,1)S(1)} %get-tuple-element.36), channel_id=1, source_target_pairs={{0,16},{8,24},{16,0},{24,8},{1,17},{9,25},{17,1},{25,9},{2,18},{10... | collective-permute-start | bytes 393224 | tf_op jit(solution)/shard_map/ppermute | solution.py:26
  59.9 6.9 %collective-permute-start.23 = (bf16[144,512]{1,0:T(8,128)(2,1)S(1)}, bf16[144,512]{1,0:T(8,128)(2,1)S(1)}, u32[]{:S(2)}, u32[]{:S(2)}) collective-permute-start(bf16[144,512]{1,0:T(8,128)(2,1)S(1)} %get-tuple-element.39.mine), channel_id=1, source_target_pairs={{0,16},{8,24},{16,0},{24,8},{1,17},{9,25},{17,1},{25,9},{2,18},{10... | collective-permute-start | bytes 442376 | tf_op jit(solution)/shard_map/ppermute | solution.py:26
  62.3 6.7 %collective-permute-start.26 = (bf16[144,512]{1,0:T(8,128)(2,1)S(1)}, bf16[144,512]{1,0:T(8,128)(2,1)S(1)}, u32[]{:S(2)}, u32[]{:S(2)}) collective-permute-start(bf16[144,512]{1,0:T(8,128)(2,1)S(1)} %get-tuple-element.42.mine), channel_id=1, source_target_pairs={{0,8},{8,0},{16,24},{24,16},{1,9},{9,1},{17,25},{25,17},{2,10},{10... | collective-permute-start | bytes 442376 | tf_op jit(solution)/shard_map/ppermute | solution.py:26
  63.4 6.6 %collective-permute-start.22 = (bf16[128,512]{1,0:T(8,128)(2,1)S(1)}, bf16[128,512]{1,0:T(8,128)(2,1)S(1)}, u32[]{:S(2)}, u32[]{:S(2)}) collective-permute-start(bf16[128,512]{1,0:T(8,128)(2,1)S(1)} %get-tuple-element.38.mine), channel_id=1, source_target_pairs={{0,16},{8,24},{16,0},{24,8},{1,17},{9,25},{17,1},{25,9},{2,18},{10... | collective-permute-start | bytes 393224 | tf_op jit(solution)/shard_map/ppermute | solution.py:26
  64.9 7.0 %collective-permute-start.25 = (bf16[128,512]{1,0:T(8,128)(2,1)S(1)}, bf16[128,512]{1,0:T(8,128)(2,1)S(1)}, u32[]{:S(2)}, u32[]{:S(2)}) collective-permute-start(bf16[128,512]{1,0:T(8,128)(2,1)S(1)} %get-tuple-element.41.mine), channel_id=1, source_target_pairs={{0,8},{8,0},{16,24},{24,16},{1,9},{9,1},{17,25},{25,17},{2,10},{10... | collective-permute-start | bytes 393224 | tf_op jit(solution)/shard_map/ppermute | solution.py:26
  67.0 7.7 %collective-permute-start.28 = (bf16[144,512]{1,0:T(8,128)(2,1)S(1)}, bf16[144,512]{1,0:T(8,128)(2,1)S(1)}, u32[]{:S(2)}, u32[]{:S(2)}) collective-permute-start(bf16[144,512]{1,0:T(8,128)(2,1)S(1)} %get-tuple-element.44.lower_kept), channel_id=1, source_target_pairs={{0,8},{8,0},{16,24},{24,16},{1,9},{9,1},{17,25},{25,17},{2,10},{10... | collective-permute-start | bytes 442376 | tf_op jit(solution)/shard_map/ppermute | solution.py:26
  69.2 5.5 %collective-permute-start.29 = (bf16[144,512]{1,0:T(8,128)(2,1)S(1)}, bf16[144,512]{1,0:T(8,128)(2,1)S(1)}, u32[]{:S(2)}, u32[]{:S(2)}) collective-permute-start(bf16[144,512]{1,0:T(8,128)(2,1)S(1)} %get-tuple-element.45.upper_kept), channel_id=1, source_target_pairs={{0,16},{8,24},{16,0},{24,8},{1,17},{9,25},{17,1},{25,9},{2,18},{10... | collective-permute-start | bytes 442376 | tf_op jit(solution)/shard_map/ppermute | solution.py:26
  70.1 6.0 %collective-permute-start.24 = (bf16[128,512]{1,0:T(8,128)(2,1)S(1)}, bf16[128,512]{1,0:T(8,128)(2,1)S(1)}, u32[]{:S(2)}, u32[]{:S(2)}) collective-permute-start(bf16[128,512]{1,0:T(8,128)(2,1)S(1)} %shard_map.65.refs_2_), channel_id=1, source_target_pairs={{0,8},{8,0},{16,24},{24,16},{1,9},{9,1},{17,25},{25,17},{2,10},{10... | collective-permute-start | bytes 393224 | tf_op jit(solution)/shard_map/ppermute | solution.py:26
  72.0 5.0 %collective-permute-start.27 = (bf16[128,512]{1,0:T(8,128)(2,1)S(1)}, bf16[128,512]{1,0:T(8,128)(2,1)S(1)}, u32[]{:S(2)}, u32[]{:S(2)}) collective-permute-start(bf16[128,512]{1,0:T(8,128)(2,1)S(1)} %shard_map.67.refs_3_), channel_id=1, source_target_pairs={{0,16},{8,24},{16,0},{24,8},{1,17},{9,25},{17,1},{25,9},{2,18},{10... | collective-permute-start | bytes 393224 | tf_op jit(solution)/shard_map/ppermute | solution.py:26

commit v6 on v5

--- a/solution.py
+++ b/solution.py
@@ -283,10 +283,9 @@
         put(sent[k], values, read(part, k * count, count) if chunk == 0 else [])
 
 
-def kept_kernel(plan, embeddings, mass, row, kept, row_out):
+def kept_kernel(plan, embeddings, mass, kept):
     quarter = plan.shape[0] // 2
     count = quarter // LANES
-    row_out[...] = row[...]
     sums = jnp.dot(plan[...], embeddings[...], preferred_element_type=jnp.float32)
     for k in range(2):
         kept[k] = sums[k * quarter:(k + 1) * quarter] / columns_of(read(mass, k * count, count))
@@ -326,7 +325,7 @@
     put(out, values, whole)
 
 
-def place_first_kernel(orders, log_k, lower_sent, upper_sent, lower_kept, upper_kept, out, col_out, sent):
+def place_first_kernel(orders, log_k, lower_sent, upper_sent, lower_kept, upper_kept, row, out, col_out, row_out, sent):
     blocks = (lower_sent, upper_sent, lower_kept, upper_kept)
     quarter = blocks[0].shape[0] - EXTRA
     count = quarter // LANES
@@ -336,6 +335,7 @@
         source = blocks[k].at[pl.ds(0, quarter)]
         copies.append(pltpu.make_async_copy(source, out.at[rows, pl.ds(0, blocks[k].shape[1])], sent.at[k]))
         copies[-1].start()
+    row_out[...] = row[...]
     for block, start in zip(blocks, quarter_places(orders, count)):
         write(col_out, start, [-log_k - line for line in lines_of(block, count)])
     for copy in copies:
@@ -387,11 +387,10 @@
     row_now = lax.optimization_barrier((row_now, sent[:2]))[0]
     plan, mass, part = last_terms(scores[2 * quarter:], row_now)
     row = row_now[None, :]
-    kept, row_out = call(
+    kept, = call(
         kept_kernel,
-        [plan, embeddings, mass.reshape(table(2).shape), row],
-        [jax.ShapeDtypeStruct((2, quarter, depth), f32), jax.ShapeDtypeStruct(row.shape, f32)],
-        specs=[vmem, pl.BlockSpec(row.shape, lambda: (0, 0))],
+        [plan, embeddings, mass.reshape(table(2).shape)],
+        [jax.ShapeDtypeStruct((2, quarter, depth), f32)],
         flops=flops,
     )
     pairs = []
@@ -417,11 +416,12 @@
             dones.append(done)
         blocks = [flipped(done, "dp", 1 << order[0]) for done, order in zip(dones, orders)] + dones
         if chunk == 0:
-            out, col_out = call(
+            whole = [table(4), jax.ShapeDtypeStruct(row.shape, f32)]
+            out, col_out, row_out = call(
                 functools.partial(place_first_kernel, orders, log_k),
-                blocks,
-                [jax.ShapeDtypeStruct((columns, depth), jnp.bfloat16), table(4)],
-                specs=[pl.BlockSpec(memory_space=pl.ANY), pl.BlockSpec(table(4).shape, lambda: (0, 0))],
+                blocks + [row],
+                [jax.ShapeDtypeStruct((columns, depth), jnp.bfloat16)] + whole,
+                specs=[pl.BlockSpec(memory_space=pl.ANY)] + [pl.BlockSpec(x.shape, lambda: (0, 0)) for x in whole],
                 scratch_shapes=[pltpu.SemaphoreType.DMA((4,))],
             )
         else:

time: 78.1 us -> 78 us (level)
  waiting for transfers between devices: 25.3 us -> 26.2 us
    ppermute x24, waiting for transfers between devices: 17 us -> 17.9 us  [flipped(): return lax.ppermute(x, axis, [(k, k ^ mask) for k in range(size)])]
  transfers between devices with their start and end apart: 30 -> 30, of which waited for: 24 -> 25; matrix products, arithmetic and copies ran while one was open for 1% -> 1% of each run, Pallas kernels for 6% -> 6%
where the time goes in v6:
time: 78 us; the launch traced here: 77.8 us
  starting transfers between devices  30.8 us (39%)
  waiting for transfers between devices  26.2 us (34%)
  other arithmetic  9.32 us (12%)
  Pallas kernels  5.97 us (8%)
  matrix products  4.57 us (6%)
  between operations  0.92 us (1%)
    ppermute x24, starting transfers between devices, flipped(): return lax.ppermute(x, axis, [(k, k ^ mask) for k in range(size)])  23.6 us
    ppermute x24, waiting for transfers between devices, flipped(): return lax.ppermute(x, axis, [(k, k ^ mask) for k in range(size)])  17.9 us
    ppermute x6, waiting for transfers between devices, split(): lax.ppermute(value, 'cent', [(k, k ^ (odd_mask if k % 2 else even_mask))...  8.29 us
    ppermute x6, starting transfers between devices, split(): lax.ppermute(value, 'cent', [(k, k ^ (odd_mask if k % 2 else even_mask))...  7.23 us
    pallas_call x10, Pallas kernels, call(): pl.pallas_call(kernel, out_shape=outs, in_specs=[vmem] * len(operands), o...  5.15 us
    dot_general x1, matrix products, on_device(): lax.dot_general(sent_and_kept(centroids), embeddings, (((1,), (1,)), ((),...  4.57 us
    reduce_sum x4, other arithmetic, last_terms(): mass = jnp.sum(terms, axis=1)  2.69 us
    reduce_sum x3, other arithmetic, on_device(): part = top + jnp.log(jnp.sum(jnp.exp(shifted - top[None, :]), axis=0))  2.31 us
  transfers between devices with their start and end apart: 30, of which 25 were waited for; matrix products, arithmetic and copies ran while one was open for 1% of the time, Pallas kernels for 6%

profile of v6, /device:TPU:0, one launch (start us, length us, event | category | flops | bytes accessed | tf_op | source)
XLA Modules:
  0.0 77.8 jit_solution(5938984467130944972)
XLA Ops:
  0.6 0.8 %broadcast_select_fusion.7 = (f32[128]{0:T(128)S(1)}, f32[128]{0:T(128)S(1)}, f32[128]{0:T(128)S(1)}, f32[128]{0:T(128)S(1)}) fusion(pred[]{:T(512)} %bitcast.3, f32[512]{0:T(512)} %param.5, pred[]{:T(512)} %bitcast.4), kind=kLoop, calls=%fused_computation.98 | loop fusion | flops 512 | bytes 4098 | tf_op jit(solution)/shard_map/jit(_where)/select_n | solution.py:463
  1.5 1.3 %broadcast_select_fusion.3 = (bf16[128,1024]{1,0:T(8,128)(2,1)S(1)}, bf16[128,1024]{1,0:T(8,128)(2,1)S(1)}, bf16[128,1024]{1,0:T(8,128)(2,1)S(1)}, bf16[128,1024]{1,0:T(8,128)(2,1)S(1)}) fusion(pred[]{:T(512)} %bitcast.3, bf16[512,1024]{1,0:T(8,128)(2,1)} %param.4, pred[]{:T(512)} %bitcast.4), kind=kLoop, calls=%fused_computation.31 | loop fusion | flops 524288 | bytes 2097154 | tf_op jit(solution)/shard_map/jit(_where)/select_n | solution.py:463
  2.8 4.6 %add_reduce_fusion.4 = (f32[2048]{0:T(1024)S(1)}, f32[512,2048]{1,0:T(8,128)S(1)}) fusion(f32[512]{0:T(512)S(1)} %pad_maximum_fusion, bf16[2048,1024]{1,0:T(8,128)(2,1)} %embeddings.3, bf16[128,1024]{1,0:T(8,128)(2,1)S(1)} %get-tuple-element.53, bf16[128,1024]{1,0:T(8,128)(2,1)S(1)} %get-tuple-element.54, bf16[128,1024]{1,0:T(8,128)(2,1)S(1)} %get-tuple-element.52, ...), kind=kOutput, calls=%fused_computation.9 | convolution fusion | flops 2154821632 | bytes 9447424 | tf_op jit(solution)/shard_map/dot_general | solution.py:479
  7.3 0.8 %exponential_reduce_fusion.4 = f32[2048]{0:T(1024)S(1)} fusion(f32[512,2048]{1,0:T(8,128)S(1)} %get-tuple-element.80, f32[2048]{0:T(1024)S(1)} %get-tuple-element.79, f32[512]{0:T(512)S(1)} %pad_maximum_fusion), kind=kLoop, calls=%fused_computation.4 | loop fusion | flops 3143680 | bytes 4212736 | tf_op jit(solution)/shard_map/reduce_sum | solution.py:486
  8.7 0.8 %collective-permute-done = f32[2048]{0:T(1024)S(1)} collective-permute-done((f32[2048]{0:T(1024)S(1)}, f32[2048]{0:T(1024)S(1)}, u32[]{:S(2)}, u32[]{:S(2)}) %collective-permute-start) | collective-permute-done | bytes 8224 | tf_op jit(solution)/shard_map/ppermute | solution.py:26
  9.5 3.0 %collective-permute-start.2 = (f32[2048]{0:T(1024)S(1)}, f32[2048]{0:T(1024)S(1)}, u32[]{:S(2)}, u32[]{:S(2)}) collective-permute-start(f32[2048]{0:T(1024)S(1)} %log_add_fusion.4), channel_id=1, source_target_pairs={{0,2},{1,7},{2,0},{3,5},{4,6},{5,3},{6,4},{7,1},{8,10},{9,15},{10,... | collective-permute-start | bytes 24584 | tf_op jit(solution)/shard_map/ppermute | solution.py:55
  12.6 1.6 %collective-permute-done.2 = f32[2048]{0:T(1024)S(1)} collective-permute-done((f32[2048]{0:T(1024)S(1)}, f32[2048]{0:T(1024)S(1)}, u32[]{:S(2)}, u32[]{:S(2)}) %collective-permute-start.2) | collective-permute-done | bytes 8224 | tf_op jit(solution)/shard_map/ppermute | solution.py:55
  14.1 2.0 %collective-permute-done.1 = f32[2048]{0:T(1024)S(1)} collective-permute-done((f32[2048]{0:T(1024)S(1)}, f32[2048]{0:T(1024)S(1)}, u32[]{:S(2)}, u32[]{:S(2)}) %collective-permute-start.1) | collective-permute-done | bytes 8224 | tf_op jit(solution)/shard_map/ppermute | solution.py:55
  16.2 1.7 %collective-permute-start.3 = (f32[2048]{0:T(1024)S(1)}, f32[2048]{0:T(1024)S(1)}, u32[]{:S(2)}, u32[]{:S(2)}) collective-permute-start(f32[2048]{0:T(1024)S(1)} %add_select_fusion.1), channel_id=1, source_target_pairs={{0,1},{1,0},{2,3},{3,2},{4,5},{5,4},{6,7},{7,6},{8,9},{9,8},{10,11... | collective-permute-start | bytes 24584 | tf_op jit(solution)/shard_map/ppermute | solution.py:26
  17.9 0.8 %collective-permute-done.3 = f32[2048]{0:T(1024)S(1)} collective-permute-done((f32[2048]{0:T(1024)S(1)}, f32[2048]{0:T(1024)S(1)}, u32[]{:S(2)}, u32[]{:S(2)}) %collective-permute-start.3) | collective-permute-done | bytes 8224 | tf_op jit(solution)/shard_map/ppermute | solution.py:26
  19.1 0.8 %exponential_reduce_fusion.3 = f32[512]{0:T(512)S(1)} fusion(f32[512,2048]{1,0:T(8,128)S(1)} %get-tuple-element.80, f32[512]{0:T(512)S(1)} %add_reduce_fusion.3, f32[2048]{0:T(1024)S(1)} %add_subtract_fusion.2), kind=kLoop, calls=%fused_computation.3 | loop fusion | flops 3145216 | bytes 4206592 | tf_op jit(solution)/shard_map/reduce_sum | solution.py:349
  19.9 2.5 %collective-permute-start.4 = (f32[512]{0:T(512)S(1)}, f32[512]{0:T(512)S(1)}, u32[]{:S(2)}, u32[]{:S(2)}) collective-permute-start(f32[512]{0:T(512)S(1)} %log_add_fusion.9), channel_id=1, source_target_pairs={{0,24},{8,16},{16,8},{24,0},{1,25},{9,17},{17,9},{25,1},{2,26},{10... | collective-permute-start | bytes 6152 | tf_op jit(solution)/shard_map/ppermute | solution.py:26
  23.5 1.0 %collective-permute-done.4 = f32[512]{0:T(512)S(1)} collective-permute-done((f32[512]{0:T(512)S(1)}, f32[512]{0:T(512)S(1)}, u32[]{:S(2)}, u32[]{:S(2)}) %collective-permute-start.4) | collective-permute-done | bytes 2080 | tf_op jit(solution)/shard_map/ppermute | solution.py:26
  24.5 1.5 %collective-permute-done.5 = f32[512]{0:T(512)S(1)} collective-permute-done((f32[512]{0:T(512)S(1)}, f32[512]{0:T(512)S(1)}, u32[]{:S(2)}, u32[]{:S(2)}) %collective-permute-start.5) | collective-permute-done | bytes 2080 | tf_op jit(solution)/shard_map/ppermute | solution.py:26
  26.9 0.8 exponential_reduce_fusion.2
  27.8 1.2 %collective-permute-done.7 = f32[2048]{0:T(1024)S(1)} collective-permute-done((f32[2048]{0:T(1024)S(1)}, f32[2048]{0:T(1024)S(1)}, u32[]{:S(2)}, u32[]{:S(2)}) %collective-permute-start.7) | collective-permute-done | bytes 8224 | tf_op jit(solution)/shard_map/ppermute | solution.py:26
  29.1 2.0 %collective-permute-start.8 = (f32[2048]{0:T(1024)S(1)}, f32[2048]{0:T(1024)S(1)}, u32[]{:S(2)}, u32[]{:S(2)}) collective-permute-start(f32[2048]{0:T(1024)S(1)} %log_add_fusion.2), channel_id=1, source_target_pairs={{0,2},{1,5},{2,0},{3,7},{4,6},{5,1},{6,4},{7,3},{8,10},{9,13},{10,... | collective-permute-start | bytes 24584 | tf_op jit(solution)/shard_map/ppermute | solution.py:55
  31.1 1.6 %collective-permute-done.9 = f32[2048]{0:T(1024)S(1)} collective-permute-done((f32[2048]{0:T(1024)S(1)}, f32[2048]{0:T(1024)S(1)}, u32[]{:S(2)}, u32[]{:S(2)}) %collective-permute-start.9) | collective-permute-done | bytes 8224 | tf_op jit(solution)/shard_map/ppermute | solution.py:55
  32.8 1.0 %collective-permute-start.10 = (f32[2048]{0:T(1024)S(1)}, f32[2048]{0:T(1024)S(1)}, u32[]{:S(2)}, u32[]{:S(2)}) collective-permute-start(f32[2048]{0:T(1024)S(1)} %add_select_fusion), channel_id=1, source_target_pairs={{0,1},{1,0},{2,3},{3,2},{4,5},{5,4},{6,7},{7,6},{8,9},{9,8},{10,11... | collective-permute-start | bytes 24584 | tf_op jit(solution)/shard_map/ppermute | solution.py:26
  33.8 0.8 %collective-permute-done.10 = f32[2048]{0:T(1024)S(1)} collective-permute-done((f32[2048]{0:T(1024)S(1)}, f32[2048]{0:T(1024)S(1)}, u32[]{:S(2)}, u32[]{:S(2)}) %collective-permute-start.10) | collective-permute-done | bytes 8224 | tf_op jit(solution)/shard_map/ppermute | solution.py:26
  35.0 0.8 %exponential_reduce_fusion.1 = f32[512]{0:T(512)S(1)} fusion(f32[512,2048]{1,0:T(8,128)S(1)} %get-tuple-element.80, f32[512]{0:T(512)S(1)} %add_reduce_fusion.1, f32[2048]{0:T(1024)S(1)} %add_subtract_fusion.1), kind=kLoop, calls=%fused_computation.1 | loop fusion | flops 3145216 | bytes 4206592 | tf_op jit(solution)/shard_map/reduce_sum | solution.py:349
  35.8 1.6 %collective-permute-start.11 = (f32[512]{0:T(512)S(1)}, f32[512]{0:T(512)S(1)}, u32[]{:S(2)}, u32[]{:S(2)}) collective-permute-start(f32[512]{0:T(512)S(1)} %log_add_fusion.7), channel_id=1, source_target_pairs={{0,24},{8,16},{16,8},{24,0},{1,25},{9,17},{17,9},{25,1},{2,26},{10... | collective-permute-start | bytes 6152 | tf_op jit(solution)/shard_map/ppermute | solution.py:26
  37.9 1.5 %collective-permute-start.13 = (f32[512]{0:T(512)S(1)}, f32[512]{0:T(512)S(1)}, u32[]{:S(2)}, u32[]{:S(2)}) collective-permute-start(f32[512]{0:T(512)S(1)} %log_add_fusion.7), channel_id=1, source_target_pairs={{0,8},{8,0},{16,24},{24,16},{1,9},{9,1},{17,25},{25,17},{2,10},{10... | collective-permute-start | bytes 6152 | tf_op jit(solution)/shard_map/ppermute | solution.py:26
  39.4 1.0 %collective-permute-done.11 = f32[512]{0:T(512)S(1)} collective-permute-done((f32[512]{0:T(512)S(1)}, f32[512]{0:T(512)S(1)}, u32[]{:S(2)}, u32[]{:S(2)}) %collective-permute-start.11) | collective-permute-done | bytes 2080 | tf_op jit(solution)/shard_map/ppermute | solution.py:26
  41.9 0.8 exponential_reduce_fusion
  42.7 1.2 %collective-permute-done.14 = f32[2048]{0:T(1024)S(1)} collective-permute-done((f32[2048]{0:T(1024)S(1)}, f32[2048]{0:T(1024)S(1)}, u32[]{:S(2)}, u32[]{:S(2)}) %collective-permute-start.14) | collective-permute-done | bytes 8224 | tf_op jit(solution)/shard_map/ppermute | solution.py:26
  43.9 1.4 %collective-permute-start.16 = (f32[2048]{0:T(1024)S(1)}, f32[2048]{0:T(1024)S(1)}, u32[]{:S(2)}, u32[]{:S(2)}) collective-permute-start(f32[2048]{0:T(1024)S(1)} %log_add_fusion), channel_id=1, source_target_pairs={{0,2},{1,7},{2,0},{3,5},{4,6},{5,3},{6,4},{7,1},{8,10},{9,15},{10,... | collective-permute-start | bytes 24584 | tf_op jit(solution)/shard_map/ppermute | solution.py:55
  45.4 0.6 collective-permute-start.15
  46.0 1.6 %collective-permute-done.16 = f32[2048]{0:T(1024)S(1)} collective-permute-done((f32[2048]{0:T(1024)S(1)}, f32[2048]{0:T(1024)S(1)}, u32[]{:S(2)}, u32[]{:S(2)}) %collective-permute-start.16) | collective-permute-done | bytes 8224 | tf_op jit(solution)/shard_map/ppermute | solution.py:55
  47.6 1.4 %collective-permute-done.15 = f32[2048]{0:T(1024)S(1)} collective-permute-done((f32[2048]{0:T(1024)S(1)}, f32[2048]{0:T(1024)S(1)}, u32[]{:S(2)}, u32[]{:S(2)}) %collective-permute-start.15) | collective-permute-done | bytes 8224 | tf_op jit(solution)/shard_map/ppermute | solution.py:55
  49.1 0.8 %collective-permute-start.17 = (f32[2048]{0:T(1024)S(1)}, f32[2048]{0:T(1024)S(1)}, u32[]{:S(2)}, u32[]{:S(2)}) collective-permute-start(f32[2048]{0:T(1024)S(1)} %bitcast.23), channel_id=1, source_target_pairs={{0,1},{1,0},{2,3},{3,2},{4,5},{5,4},{6,7},{7,6},{8,9},{9,8},{10,11... | collective-permute-start | bytes 24584 | tf_op jit(solution)/shard_map/ppermute | solution.py:26
  49.9 0.8 %collective-permute-done.17 = f32[2048]{0:T(1024)S(1)} collective-permute-done((f32[2048]{0:T(1024)S(1)}, f32[2048]{0:T(1024)S(1)}, u32[]{:S(2)}, u32[]{:S(2)}) %collective-permute-start.17) | collective-permute-done | bytes 8224 | tf_op jit(solution)/shard_map/ppermute | solution.py:26
  51.5 0.7 shard_map.59
  52.2 1.6 %collective-permute-start.20 = (bf16[144,512]{1,0:T(8,128)(2,1)S(1)}, bf16[144,512]{1,0:T(8,128)(2,1)S(1)}, u32[]{:S(2)}, u32[]{:S(2)}) collective-permute-start(bf16[144,512]{1,0:T(8,128)(2,1)S(1)} %get-tuple-element.30), channel_id=1, source_target_pairs={{0,8},{8,0},{16,24},{24,16},{1,9},{9,1},{17,25},{25,17},{2,10},{10... | collective-permute-start | bytes 442376 | tf_op jit(solution)/shard_map/ppermute | solution.py:26
  53.8 1.5 %collective-permute-start.21 = (bf16[144,512]{1,0:T(8,128)(2,1)S(1)}, bf16[144,512]{1,0:T(8,128)(2,1)S(1)}, u32[]{:S(2)}, u32[]{:S(2)}) collective-permute-start(bf16[144,512]{1,0:T(8,128)(2,1)S(1)} %get-tuple-element.31), channel_id=1, source_target_pairs={{0,16},{8,24},{16,0},{24,8},{1,17},{9,25},{17,1},{25,9},{2,18},{10... | collective-permute-start | bytes 442376 | tf_op jit(solution)/shard_map/ppermute | solution.py:26
  56.0 0.7 shard_map.61
  57.9 1.3 %shard_map.60.kept = f32[2,128,1024]{2,1,0:T(8,128)S(1)} custom-call(bf16[256,2048]{1,0:T(8,128)(2,1)S(1)} %get-tuple-element.48.plan, bf16[2048,1024]{1,0:T(8,128)(2,1)S(1)} %copy-done, f32[2,128]{1,0:T(2,128)S(1)} %bitcast.26), custom_call_target="tpu_custom_call" | custom-call | flops 1073741824 | bytes 524288 | tf_op jit(solution)/shard_map/pallas_call | solution.py:363
  59.8 2.4 %collective-permute-start.23 = (bf16[144,512]{1,0:T(8,128)(2,1)S(1)}, bf16[144,512]{1,0:T(8,128)(2,1)S(1)}, u32[]{:S(2)}, u32[]{:S(2)}) collective-permute-start(bf16[144,512]{1,0:T(8,128)(2,1)S(1)} %get-tuple-element.37.mine), channel_id=1, source_target_pairs={{0,16},{8,24},{16,0},{24,8},{1,17},{9,25},{17,1},{25,9},{2,18},{10... | collective-permute-start | bytes 442376 | tf_op jit(solution)/shard_map/ppermute | solution.py:26
  62.5 0.7 collective-permute-done.19.upper
  63.3 1.5 %collective-permute-start.22 = (bf16[128,512]{1,0:T(8,128)(2,1)S(1)}, bf16[128,512]{1,0:T(8,128)(2,1)S(1)}, u32[]{:S(2)}, u32[]{:S(2)}) collective-permute-start(bf16[128,512]{1,0:T(8,128)(2,1)S(1)} %get-tuple-element.36.mine), channel_id=1, source_target_pairs={{0,16},{8,24},{16,0},{24,8},{1,17},{9,25},{17,1},{25,9},{2,18},{10... | collective-permute-start | bytes 393224 | tf_op jit(solution)/shard_map/ppermute | solution.py:26
  65.2 1.7 %collective-permute-done.23.theirs = bf16[144,512]{1,0:T(8,128)(2,1)S(1)} collective-permute-done((bf16[144,512]{1,0:T(8,128)(2,1)S(1)}, bf16[144,512]{1,0:T(8,128)(2,1)S(1)}, u32[]{:S(2)}, u32[]{:S(2)}) %collective-permute-start.23) | collective-permute-done | bytes 147488 | tf_op jit(solution)/shard_map/ppermute | solution.py:26
  67.1 1.3 %collective-permute-start.28 = (bf16[144,512]{1,0:T(8,128)(2,1)S(1)}, bf16[144,512]{1,0:T(8,128)(2,1)S(1)}, u32[]{:S(2)}, u32[]{:S(2)}) collective-permute-start(bf16[144,512]{1,0:T(8,128)(2,1)S(1)} %get-tuple-element.42.lower_kept), channel_id=1, source_target_pairs={{0,8},{8,0},{16,24},{24,16},{1,9},{9,1},{17,25},{25,17},{2,10},{10... | collective-permute-start | bytes 442376 | tf_op jit(solution)/shard_map/ppermute | solution.py:26
  68.3 0.7 collective-permute-done.26.theirs
  69.5 2.1 %collective-permute-start.24 = (bf16[128,512]{1,0:T(8,128)(2,1)S(1)}, bf16[128,512]{1,0:T(8,128)(2,1)S(1)}, u32[]{:S(2)}, u32[]{:S(2)}) collective-permute-start(bf16[128,512]{1,0:T(8,128)(2,1)S(1)} %shard_map.65.refs_2_), channel_id=1, source_target_pairs={{0,8},{8,0},{16,24},{24,16},{1,9},{9,1},{17,25},{25,17},{2,10},{10... | collective-permute-start | bytes 393224 | tf_op jit(solution)/shard_map/ppermute | solution.py:26
  72.1 2.6 %collective-permute-done.28.lower_sent = bf16[144,512]{1,0:T(8,128)(2,1)S(1)} collective-permute-done((bf16[144,512]{1,0:T(8,128)(2,1)S(1)}, bf16[144,512]{1,0:T(8,128)(2,1)S(1)}, u32[]{:S(2)}, u32[]{:S(2)}) %collective-permute-start.28) | collective-permute-done | bytes 147488 | tf_op jit(solution)/shard_map/ppermute | solution.py:26
  74.6 1.4 %shard_map.68 = (bf16[512,1024]{1,0:T(8,128)(2,1)}, f32[4,128]{1,0:T(4,128)}, f32[1,2048]{1,0:T(1,128)}) custom-call(bf16[144,512]{1,0:T(8,128)(2,1)S(1)} %collective-permute-done.28.lower_sent, bf16[144,512]{1,0:T(8,128)(2,1)S(1)} %collective-permute-done.29.upper_sent, bf16[144,512]{1,0:T(8,128)(2,1)S(1)} %get-tuple-element.42.lower_kept, ...), custom_call_target="tpu_custom_call" | custom-call | bytes 524288 | tf_op jit(solution)/shard_map/pallas_call | solution.py:363
  76.1 0.9 %collective-permute-done.27.refs_1_ = bf16[128,512]{1,0:T(8,128)(2,1)S(1)} collective-permute-done((bf16[128,512]{1,0:T(8,128)(2,1)S(1)}, bf16[128,512]{1,0:T(8,128)(2,1)S(1)}, u32[]{:S(2)}, u32[]{:S(2)}) %collective-permute-start.27) | collective-permute-done | bytes 131104 | tf_op jit(solution)/shard_map/ppermute | solution.py:26
  77.0 0.8 %shard_map.69 = bf16[512,1024]{1,0:T(8,128)(2,1)} custom-call(bf16[128,512]{1,0:T(8,128)(2,1)S(1)} %collective-permute-done.24.refs_0_, bf16[128,512]{1,0:T(8,128)(2,1)S(1)} %collective-permute-done.27.refs_1_, bf16[128,512]{1,0:T(8,128)(2,1)S(1)} %shard_map.65.refs_2_, bf16[128,512]{1,0:T(8,128)(2,1)S(1)} %shard_map.67.refs_3_, ...), custom_call_target="tpu_custom_call", output_to_operand_aliasing={{}: (4, {})} | custom-call | tf_op jit(solution)/shard_map/pallas_call | solution.py:93
  (69 shorter events, 11.1 us)
Async XLA Ops:
  8.1 1.4 %collective-permute-start = (f32[2048]{0:T(1024)S(1)}, f32[2048]{0:T(1024)S(1)}, u32[]{:S(2)}, u32[]{:S(2)}) collective-permute-start(f32[2048]{0:T(1024)S(1)} %log_add_fusion.5), channel_id=1, source_target_pairs={{0,1},{1,0},{2,3},{3,2},{4,5},{5,4},{6,7},{7,6},{8,9},{9,8},{10,11... | collective-permute-start | bytes 24584 | tf_op jit(solution)/shard_map/ppermute | solution.py:26
  9.5 4.6 %collective-permute-start.2 = (f32[2048]{0:T(1024)S(1)}, f32[2048]{0:T(1024)S(1)}, u32[]{:S(2)}, u32[]{:S(2)}) collective-permute-start(f32[2048]{0:T(1024)S(1)} %log_add_fusion.4), channel_id=1, source_target_pairs={{0,2},{1,7},{2,0},{3,5},{4,6},{5,3},{6,4},{7,1},{8,10},{9,15},{10,... | collective-permute-start | bytes 24584 | tf_op jit(solution)/shard_map/ppermute | solution.py:55
  12.5 3.7 %collective-permute-start.1 = (f32[2048]{0:T(1024)S(1)}, f32[2048]{0:T(1024)S(1)}, u32[]{:S(2)}, u32[]{:S(2)}) collective-permute-start(f32[2048]{0:T(1024)S(1)} %log_add_fusion.4), channel_id=1, source_target_pairs={{0,2},{1,5},{2,0},{3,7},{4,6},{5,1},{6,4},{7,3},{8,10},{9,13},{10,... | collective-permute-start | bytes 24584 | tf_op jit(solution)/shard_map/ppermute | solution.py:55
  16.2 2.6 %collective-permute-start.3 = (f32[2048]{0:T(1024)S(1)}, f32[2048]{0:T(1024)S(1)}, u32[]{:S(2)}, u32[]{:S(2)}) collective-permute-start(f32[2048]{0:T(1024)S(1)} %add_select_fusion.1), channel_id=1, source_target_pairs={{0,1},{1,0},{2,3},{3,2},{4,5},{5,4},{6,7},{7,6},{8,9},{9,8},{10,11... | collective-permute-start | bytes 24584 | tf_op jit(solution)/shard_map/ppermute | solution.py:26
  19.9 4.5 %collective-permute-start.4 = (f32[512]{0:T(512)S(1)}, f32[512]{0:T(512)S(1)}, u32[]{:S(2)}, u32[]{:S(2)}) collective-permute-start(f32[512]{0:T(512)S(1)} %log_add_fusion.9), channel_id=1, source_target_pairs={{0,24},{8,16},{16,8},{24,0},{1,25},{9,17},{17,9},{25,1},{2,26},{10... | collective-permute-start | bytes 6152 | tf_op jit(solution)/shard_map/ppermute | solution.py:26
  22.4 3.6 %collective-permute-start.5 = (f32[512]{0:T(512)S(1)}, f32[512]{0:T(512)S(1)}, u32[]{:S(2)}, u32[]{:S(2)}) collective-permute-start(f32[512]{0:T(512)S(1)} %log_add_fusion.9), channel_id=1, source_target_pairs={{0,16},{8,24},{16,0},{24,8},{1,17},{9,25},{17,1},{25,9},{2,18},{10... | collective-permute-start | bytes 6152 | tf_op jit(solution)/shard_map/ppermute | solution.py:26
  22.9 3.6 %collective-permute-start.6 = (f32[512]{0:T(512)S(1)}, f32[512]{0:T(512)S(1)}, u32[]{:S(2)}, u32[]{:S(2)}) collective-permute-start(f32[512]{0:T(512)S(1)} %log_add_fusion.9), channel_id=1, source_target_pairs={{0,8},{8,0},{16,24},{24,16},{1,9},{9,1},{17,25},{25,17},{2,10},{10... | collective-permute-start | bytes 6152 | tf_op jit(solution)/shard_map/ppermute | solution.py:26
  27.7 1.2 %collective-permute-start.7 = (f32[2048]{0:T(1024)S(1)}, f32[2048]{0:T(1024)S(1)}, u32[]{:S(2)}, u32[]{:S(2)}) collective-permute-start(f32[2048]{0:T(1024)S(1)} %log_add_fusion.3), channel_id=1, source_target_pairs={{0,1},{1,0},{2,3},{3,2},{4,5},{5,4},{6,7},{7,6},{8,9},{9,8},{10,11... | collective-permute-start | bytes 24584 | tf_op jit(solution)/shard_map/ppermute | solution.py:26
  29.0 3.7 %collective-permute-start.9 = (f32[2048]{0:T(1024)S(1)}, f32[2048]{0:T(1024)S(1)}, u32[]{:S(2)}, u32[]{:S(2)}) collective-permute-start(f32[2048]{0:T(1024)S(1)} %log_add_fusion.2), channel_id=1, source_target_pairs={{0,2},{1,7},{2,0},{3,5},{4,6},{5,3},{6,4},{7,1},{8,10},{9,15},{10,... | collective-permute-start | bytes 24584 | tf_op jit(solution)/shard_map/ppermute | solution.py:55
  29.1 3.7 %collective-permute-start.8 = (f32[2048]{0:T(1024)S(1)}, f32[2048]{0:T(1024)S(1)}, u32[]{:S(2)}, u32[]{:S(2)}) collective-permute-start(f32[2048]{0:T(1024)S(1)} %log_add_fusion.2), channel_id=1, source_target_pairs={{0,2},{1,5},{2,0},{3,7},{4,6},{5,1},{6,4},{7,3},{8,10},{9,13},{10,... | collective-permute-start | bytes 24584 | tf_op jit(solution)/shard_map/ppermute | solution.py:55
  32.8 1.8 %collective-permute-start.10 = (f32[2048]{0:T(1024)S(1)}, f32[2048]{0:T(1024)S(1)}, u32[]{:S(2)}, u32[]{:S(2)}) collective-permute-start(f32[2048]{0:T(1024)S(1)} %add_select_fusion), channel_id=1, source_target_pairs={{0,1},{1,0},{2,3},{3,2},{4,5},{5,4},{6,7},{7,6},{8,9},{9,8},{10,11... | collective-permute-start | bytes 24584 | tf_op jit(solution)/shard_map/ppermute | solution.py:26
  35.8 4.5 %collective-permute-start.11 = (f32[512]{0:T(512)S(1)}, f32[512]{0:T(512)S(1)}, u32[]{:S(2)}, u32[]{:S(2)}) collective-permute-start(f32[512]{0:T(512)S(1)} %log_add_fusion.7), channel_id=1, source_target_pairs={{0,24},{8,16},{16,8},{24,0},{1,25},{9,17},{17,9},{25,1},{2,26},{10... | collective-permute-start | bytes 6152 | tf_op jit(solution)/shard_map/ppermute | solution.py:26
  37.4 3.6 %collective-permute-start.12 = (f32[512]{0:T(512)S(1)}, f32[512]{0:T(512)S(1)}, u32[]{:S(2)}, u32[]{:S(2)}) collective-permute-start(f32[512]{0:T(512)S(1)} %log_add_fusion.7), channel_id=1, source_target_pairs={{0,16},{8,24},{16,0},{24,8},{1,17},{9,25},{17,1},{25,9},{2,18},{10... | collective-permute-start | bytes 6152 | tf_op jit(solution)/shard_map/ppermute | solution.py:26
  37.9 3.6 %collective-permute-start.13 = (f32[512]{0:T(512)S(1)}, f32[512]{0:T(512)S(1)}, u32[]{:S(2)}, u32[]{:S(2)}) collective-permute-start(f32[512]{0:T(512)S(1)} %log_add_fusion.7), channel_id=1, source_target_pairs={{0,8},{8,0},{16,24},{24,16},{1,9},{9,1},{17,25},{25,17},{2,10},{10... | collective-permute-start | bytes 6152 | tf_op jit(solution)/shard_map/ppermute | solution.py:26
  41.5 7.5 %copy-start = (bf16[2048,1024]{1,0:T(8,128)(2,1)S(1)}, bf16[2048,1024]{1,0:T(8,128)(2,1)}, u32[]{:S(2)}) copy-start(bf16[2048,1024]{1,0:T(8,128)(2,1)} %embeddings.3) | copy-start | bytes 12582916
  42.7 1.2 %collective-permute-start.14 = (f32[2048]{0:T(1024)S(1)}, f32[2048]{0:T(1024)S(1)}, u32[]{:S(2)}, u32[]{:S(2)}) collective-permute-start(f32[2048]{0:T(1024)S(1)} %log_add_fusion.1), channel_id=1, source_target_pairs={{0,1},{1,0},{2,3},{3,2},{4,5},{5,4},{6,7},{7,6},{8,9},{9,8},{10,11... | collective-permute-start | bytes 24584 | tf_op jit(solution)/shard_map/ppermute | solution.py:26
  43.9 3.7 %collective-permute-start.16 = (f32[2048]{0:T(1024)S(1)}, f32[2048]{0:T(1024)S(1)}, u32[]{:S(2)}, u32[]{:S(2)}) collective-permute-start(f32[2048]{0:T(1024)S(1)} %log_add_fusion), channel_id=1, source_target_pairs={{0,2},{1,7},{2,0},{3,5},{4,6},{5,3},{6,4},{7,1},{8,10},{9,15},{10,... | collective-permute-start | bytes 24584 | tf_op jit(solution)/shard_map/ppermute | solution.py:55
  45.4 3.7 %collective-permute-start.15 = (f32[2048]{0:T(1024)S(1)}, f32[2048]{0:T(1024)S(1)}, u32[]{:S(2)}, u32[]{:S(2)}) collective-permute-start(f32[2048]{0:T(1024)S(1)} %log_add_fusion), channel_id=1, source_target_pairs={{0,2},{1,5},{2,0},{3,7},{4,6},{5,1},{6,4},{7,3},{8,10},{9,13},{10,... | collective-permute-start | bytes 24584 | tf_op jit(solution)/shard_map/ppermute | solution.py:55
  49.1 1.6 %collective-permute-start.17 = (f32[2048]{0:T(1024)S(1)}, f32[2048]{0:T(1024)S(1)}, u32[]{:S(2)}, u32[]{:S(2)}) collective-permute-start(f32[2048]{0:T(1024)S(1)} %bitcast.23), channel_id=1, source_target_pairs={{0,1},{1,0},{2,3},{3,2},{4,5},{5,4},{6,7},{7,6},{8,9},{9,8},{10,11... | collective-permute-start | bytes 24584 | tf_op jit(solution)/shard_map/ppermute | solution.py:26
  52.2 7.0 %collective-permute-start.20 = (bf16[144,512]{1,0:T(8,128)(2,1)S(1)}, bf16[144,512]{1,0:T(8,128)(2,1)S(1)}, u32[]{:S(2)}, u32[]{:S(2)}) collective-permute-start(bf16[144,512]{1,0:T(8,128)(2,1)S(1)} %get-tuple-element.30), channel_id=1, source_target_pairs={{0,8},{8,0},{16,24},{24,16},{1,9},{9,1},{17,25},{25,17},{2,10},{10... | collective-permute-start | bytes 442376 | tf_op jit(solution)/shard_map/ppermute | solution.py:26
  53.8 5.9 %collective-permute-start.21 = (bf16[144,512]{1,0:T(8,128)(2,1)S(1)}, bf16[144,512]{1,0:T(8,128)(2,1)S(1)}, u32[]{:S(2)}, u32[]{:S(2)}) collective-permute-start(bf16[144,512]{1,0:T(8,128)(2,1)S(1)} %get-tuple-element.31), channel_id=1, source_target_pairs={{0,16},{8,24},{16,0},{24,8},{1,17},{9,25},{17,1},{25,9},{2,18},{10... | collective-permute-start | bytes 442376 | tf_op jit(solution)/shard_map/ppermute | solution.py:26
  56.8 5.7 %collective-permute-start.18 = (bf16[128,512]{1,0:T(8,128)(2,1)S(1)}, bf16[128,512]{1,0:T(8,128)(2,1)S(1)}, u32[]{:S(2)}, u32[]{:S(2)}) collective-permute-start(bf16[128,512]{1,0:T(8,128)(2,1)S(1)} %get-tuple-element.33), channel_id=1, source_target_pairs={{0,8},{8,0},{16,24},{24,16},{1,9},{9,1},{17,25},{25,17},{2,10},{10... | collective-permute-start | bytes 393224 | tf_op jit(solution)/shard_map/ppermute | solution.py:26
  57.4 5.8 %collective-permute-start.19 = (bf16[128,512]{1,0:T(8,128)(2,1)S(1)}, bf16[128,512]{1,0:T(8,128)(2,1)S(1)}, u32[]{:S(2)}, u32[]{:S(2)}) collective-permute-start(bf16[128,512]{1,0:T(8,128)(2,1)S(1)} %get-tuple-element.34), channel_id=1, source_target_pairs={{0,16},{8,24},{16,0},{24,8},{1,17},{9,25},{17,1},{25,9},{2,18},{10... | collective-permute-start | bytes 393224 | tf_op jit(solution)/shard_map/ppermute | solution.py:26
  59.8 7.0 %collective-permute-start.23 = (bf16[144,512]{1,0:T(8,128)(2,1)S(1)}, bf16[144,512]{1,0:T(8,128)(2,1)S(1)}, u32[]{:S(2)}, u32[]{:S(2)}) collective-permute-start(bf16[144,512]{1,0:T(8,128)(2,1)S(1)} %get-tuple-element.37.mine), channel_id=1, source_target_pairs={{0,16},{8,24},{16,0},{24,8},{1,17},{9,25},{17,1},{25,9},{2,18},{10... | collective-permute-start | bytes 442376 | tf_op jit(solution)/shard_map/ppermute | solution.py:26
  62.3 6.7 %collective-permute-start.26 = (bf16[144,512]{1,0:T(8,128)(2,1)S(1)}, bf16[144,512]{1,0:T(8,128)(2,1)S(1)}, u32[]{:S(2)}, u32[]{:S(2)}) collective-permute-start(bf16[144,512]{1,0:T(8,128)(2,1)S(1)} %get-tuple-element.40.mine), channel_id=1, source_target_pairs={{0,8},{8,0},{16,24},{24,16},{1,9},{9,1},{17,25},{25,17},{2,10},{10... | collective-permute-start | bytes 442376 | tf_op jit(solution)/shard_map/ppermute | solution.py:26
  63.3 6.0 %collective-permute-start.22 = (bf16[128,512]{1,0:T(8,128)(2,1)S(1)}, bf16[128,512]{1,0:T(8,128)(2,1)S(1)}, u32[]{:S(2)}, u32[]{:S(2)}) collective-permute-start(bf16[128,512]{1,0:T(8,128)(2,1)S(1)} %get-tuple-element.36.mine), channel_id=1, source_target_pairs={{0,16},{8,24},{16,0},{24,8},{1,17},{9,25},{17,1},{25,9},{2,18},{10... | collective-permute-start | bytes 393224 | tf_op jit(solution)/shard_map/ppermute | solution.py:26
  64.8 7.0 %collective-permute-start.25 = (bf16[128,512]{1,0:T(8,128)(2,1)S(1)}, bf16[128,512]{1,0:T(8,128)(2,1)S(1)}, u32[]{:S(2)}, u32[]{:S(2)}) collective-permute-start(bf16[128,512]{1,0:T(8,128)(2,1)S(1)} %get-tuple-element.39.mine), channel_id=1, source_target_pairs={{0,8},{8,0},{16,24},{24,16},{1,9},{9,1},{17,25},{25,17},{2,10},{10... | collective-permute-start | bytes 393224 | tf_op jit(solution)/shard_map/ppermute | solution.py:26
  67.1 7.6 %collective-permute-start.28 = (bf16[144,512]{1,0:T(8,128)(2,1)S(1)}, bf16[144,512]{1,0:T(8,128)(2,1)S(1)}, u32[]{:S(2)}, u32[]{:S(2)}) collective-permute-start(bf16[144,512]{1,0:T(8,128)(2,1)S(1)} %get-tuple-element.42.lower_kept), channel_id=1, source_target_pairs={{0,8},{8,0},{16,24},{24,16},{1,9},{9,1},{17,25},{25,17},{2,10},{10... | collective-permute-start | bytes 442376 | tf_op jit(solution)/shard_map/ppermute | solution.py:26
  69.2 5.5 %collective-permute-start.29 = (bf16[144,512]{1,0:T(8,128)(2,1)S(1)}, bf16[144,512]{1,0:T(8,128)(2,1)S(1)}, u32[]{:S(2)}, u32[]{:S(2)}) collective-permute-start(bf16[144,512]{1,0:T(8,128)(2,1)S(1)} %get-tuple-element.43.upper_kept), channel_id=1, source_target_pairs={{0,16},{8,24},{16,0},{24,8},{1,17},{9,25},{17,1},{25,9},{2,18},{10... | collective-permute-start | bytes 442376 | tf_op jit(solution)/shard_map/ppermute | solution.py:26
  69.5 6.6 %collective-permute-start.24 = (bf16[128,512]{1,0:T(8,128)(2,1)S(1)}, bf16[128,512]{1,0:T(8,128)(2,1)S(1)}, u32[]{:S(2)}, u32[]{:S(2)}) collective-permute-start(bf16[128,512]{1,0:T(8,128)(2,1)S(1)} %shard_map.65.refs_2_), channel_id=1, source_target_pairs={{0,8},{8,0},{16,24},{24,16},{1,9},{9,1},{17,25},{25,17},{2,10},{10... | collective-permute-start | bytes 393224 | tf_op jit(solution)/shard_map/ppermute | solution.py:26
  71.9 5.0 %collective-permute-start.27 = (bf16[128,512]{1,0:T(8,128)(2,1)S(1)}, bf16[128,512]{1,0:T(8,128)(2,1)S(1)}, u32[]{:S(2)}, u32[]{:S(2)}) collective-permute-start(bf16[128,512]{1,0:T(8,128)(2,1)S(1)} %shard_map.67.refs_3_), channel_id=1, source_target_pairs={{0,16},{8,24},{16,0},{24,8},{1,17},{9,25},{17,1},{25,9},{2,18},{10... | collective-permute-start | bytes 393224 | tf_op jit(solution)/shard_map/ppermute | solution.py:26

commit v7 on v6

--- a/solution.py
+++ b/solution.py
@@ -31,7 +31,7 @@
     return top + jnp.log(jnp.exp(first - top) + jnp.exp(second - top))
 
 
-def lse_over_dp(x, aligned):
+def lse_over_dp(x, aligned, joined_by):
     bits = bits_of("dp")
 
     def partner(value, mask):
@@ -41,13 +41,13 @@
         if len(masks) == 2:
             far = partner(x, masks[0] | masks[1])
             near = [partner(x, mask) for mask in reversed(masks)]
-            x = lse(lax.optimization_barrier(lse(x, far)), lse(*near))
+            x = lse(joined_by(lax.optimization_barrier(lse(x, far))), lse(*near))
         else:
             x = lse(x, partner(x, masks[0]))
     return x
 
 
-def lse_over_cent(x, odd, joined_by):
+def lse_over_cent(x, odd):
     size = lax.axis_size("cent")
     near, middle, *rest = [1 << bit for bit in bits_of("cent")[1:]]
 
@@ -57,7 +57,7 @@
     x = lse(x, flipped(x, "cent", 1))
     second = split(x, near, middle)
     first = split(x, near, near | middle)
-    x = joined_by(jnp.where(odd, lse(second, first), lse(x, first)))
+    x = jnp.where(odd, lse(second, first), lse(x, first))
     for mask in [1] + rest:
         x = lse(x, flipped(x, "cent", mask))
     return x
@@ -485,13 +485,15 @@
         top = jnp.max(shifted, axis=0)
         part = top + jnp.log(jnp.sum(jnp.exp(shifted - top[None, :]), axis=0))
         last = step_index == ITERS - 1
-        part = lse_over_cent(part, odd, lambda x: beside(x, embeddings) if last else x)
+        part = lse_over_cent(part, odd)
         row_now = -math.log(n_total) - part
         if last and len(bits) == 2:
             return last_sum(scores, row_now, embeddings, math.log(k_total), orders)
         plan, mass, part = last_terms(scores, row_now)
         if not last:
-            col_now = -math.log(k_total) - lse_over_dp(part, aligned)
+            near_end = step_index == ITERS - 2
+            part = lse_over_dp(part, aligned, lambda x: beside(x, embeddings) if near_end else x)
+            col_now = -math.log(k_total) - part
     new_centroids, row_out, whole = last_sum_by_vectors(plan, part, mass, row_now, embeddings, chosen, orders, aligned)
     return new_centroids, row_out, -math.log(k_total) - whole
 

time: 78 us -> 78 us (level)
  no operation moved by 1% of the time
where the time goes in v7:
time: 78 us; the launch traced here: 77.8 us
  starting transfers between devices  30.8 us (39%)
  waiting for transfers between devices  26.1 us (33%)
  other arithmetic  9.32 us (12%)
  Pallas kernels  5.97 us (8%)
  matrix products  4.57 us (6%)
  between operations  0.91 us (1%)
    ppermute x24, starting transfers between devices, flipped(): return lax.ppermute(x, axis, [(k, k ^ mask) for k in range(size)])  23.6 us
    ppermute x24, waiting for transfers between devices, flipped(): return lax.ppermute(x, axis, [(k, k ^ mask) for k in range(size)])  17.8 us
    ppermute x6, waiting for transfers between devices, split(): lax.ppermute(value, 'cent', [(k, k ^ (odd_mask if k % 2 else even_mask))...  8.29 us
    ppermute x6, starting transfers between devices, split(): lax.ppermute(value, 'cent', [(k, k ^ (odd_mask if k % 2 else even_mask))...  7.23 us
    pallas_call x10, Pallas kernels, call(): pl.pallas_call(kernel, out_shape=outs, in_specs=[vmem] * len(operands), o...  5.15 us
    dot_general x1, matrix products, on_device(): lax.dot_general(sent_and_kept(centroids), embeddings, (((1,), (1,)), ((),...  4.57 us
    reduce_sum x4, other arithmetic, last_terms(): mass = jnp.sum(terms, axis=1)  2.69 us
    reduce_sum x3, other arithmetic, on_device(): part = top + jnp.log(jnp.sum(jnp.exp(shifted - top[None, :]), axis=0))  2.31 us
  transfers between devices with their start and end apart: 30, of which 25 were waited for; matrix products, arithmetic and copies ran while one was open for 1% of the time, Pallas kernels for 6%

profile of v7, /device:TPU:0, one launch (start us, length us, event | category | flops | bytes accessed | tf_op | source)
XLA Modules:
  0.0 77.8 jit_solution(11884686914906806997)
XLA Ops:
  0.6 0.8 %broadcast_select_fusion.7 = (f32[128]{0:T(128)S(1)}, f32[128]{0:T(128)S(1)}, f32[128]{0:T(128)S(1)}, f32[128]{0:T(128)S(1)}) fusion(pred[]{:T(512)} %bitcast.3, f32[512]{0:T(512)} %param.5, pred[]{:T(512)} %bitcast.4), kind=kLoop, calls=%fused_computation.104 | loop fusion | flops 512 | bytes 4098 | tf_op jit(solution)/shard_map/jit(_where)/select_n | solution.py:463
  1.5 1.3 %broadcast_select_fusion.3 = (bf16[128,1024]{1,0:T(8,128)(2,1)S(1)}, bf16[128,1024]{1,0:T(8,128)(2,1)S(1)}, bf16[128,1024]{1,0:T(8,128)(2,1)S(1)}, bf16[128,1024]{1,0:T(8,128)(2,1)S(1)}) fusion(pred[]{:T(512)} %bitcast.3, bf16[512,1024]{1,0:T(8,128)(2,1)} %param.4, pred[]{:T(512)} %bitcast.4), kind=kLoop, calls=%fused_computation.31 | loop fusion | flops 524288 | bytes 2097154 | tf_op jit(solution)/shard_map/jit(_where)/select_n | solution.py:463
  2.8 4.6 %add_reduce_fusion.4 = (f32[2048]{0:T(1024)S(1)}, f32[512,2048]{1,0:T(8,128)S(1)}) fusion(f32[512]{0:T(512)S(1)} %pad_maximum_fusion, bf16[2048,1024]{1,0:T(8,128)(2,1)} %embeddings.3, bf16[128,1024]{1,0:T(8,128)(2,1)S(1)} %get-tuple-element.53, bf16[128,1024]{1,0:T(8,128)(2,1)S(1)} %get-tuple-element.54, bf16[128,1024]{1,0:T(8,128)(2,1)S(1)} %get-tuple-element.52, ...), kind=kOutput, calls=%fused_computation.9 | convolution fusion | flops 2154821632 | bytes 9447424 | tf_op jit(solution)/shard_map/dot_general | solution.py:479
  7.3 0.8 %exponential_reduce_fusion.4 = f32[2048]{0:T(1024)S(1)} fusion(f32[512,2048]{1,0:T(8,128)S(1)} %get-tuple-element.80, f32[2048]{0:T(1024)S(1)} %get-tuple-element.79, f32[512]{0:T(512)S(1)} %pad_maximum_fusion), kind=kLoop, calls=%fused_computation.4 | loop fusion | flops 3143680 | bytes 4212736 | tf_op jit(solution)/shard_map/reduce_sum | solution.py:486
  8.7 0.8 %collective-permute-done = f32[2048]{0:T(1024)S(1)} collective-permute-done((f32[2048]{0:T(1024)S(1)}, f32[2048]{0:T(1024)S(1)}, u32[]{:S(2)}, u32[]{:S(2)}) %collective-permute-start) | collective-permute-done | bytes 8224 | tf_op jit(solution)/shard_map/ppermute | solution.py:26
  9.5 3.0 %collective-permute-start.2 = (f32[2048]{0:T(1024)S(1)}, f32[2048]{0:T(1024)S(1)}, u32[]{:S(2)}, u32[]{:S(2)}) collective-permute-start(f32[2048]{0:T(1024)S(1)} %log_add_fusion.4), channel_id=1, source_target_pairs={{0,2},{1,7},{2,0},{3,5},{4,6},{5,3},{6,4},{7,1},{8,10},{9,15},{10,... | collective-permute-start | bytes 24584 | tf_op jit(solution)/shard_map/ppermute | solution.py:55
  12.6 1.6 %collective-permute-done.2 = f32[2048]{0:T(1024)S(1)} collective-permute-done((f32[2048]{0:T(1024)S(1)}, f32[2048]{0:T(1024)S(1)}, u32[]{:S(2)}, u32[]{:S(2)}) %collective-permute-start.2) | collective-permute-done | bytes 8224 | tf_op jit(solution)/shard_map/ppermute | solution.py:55
  14.1 2.0 %collective-permute-done.1 = f32[2048]{0:T(1024)S(1)} collective-permute-done((f32[2048]{0:T(1024)S(1)}, f32[2048]{0:T(1024)S(1)}, u32[]{:S(2)}, u32[]{:S(2)}) %collective-permute-start.1) | collective-permute-done | bytes 8224 | tf_op jit(solution)/shard_map/ppermute | solution.py:55
  16.2 1.7 %collective-permute-start.3 = (f32[2048]{0:T(1024)S(1)}, f32[2048]{0:T(1024)S(1)}, u32[]{:S(2)}, u32[]{:S(2)}) collective-permute-start(f32[2048]{0:T(1024)S(1)} %add_select_fusion.2), channel_id=1, source_target_pairs={{0,1},{1,0},{2,3},{3,2},{4,5},{5,4},{6,7},{7,6},{8,9},{9,8},{10,11... | collective-permute-start | bytes 24584 | tf_op jit(solution)/shard_map/ppermute | solution.py:26
  17.9 0.8 %collective-permute-done.3 = f32[2048]{0:T(1024)S(1)} collective-permute-done((f32[2048]{0:T(1024)S(1)}, f32[2048]{0:T(1024)S(1)}, u32[]{:S(2)}, u32[]{:S(2)}) %collective-permute-start.3) | collective-permute-done | bytes 8224 | tf_op jit(solution)/shard_map/ppermute | solution.py:26
  19.1 0.8 %exponential_reduce_fusion.3 = f32[512]{0:T(512)S(1)} fusion(f32[512,2048]{1,0:T(8,128)S(1)} %get-tuple-element.80, f32[512]{0:T(512)S(1)} %add_reduce_fusion.3, f32[2048]{0:T(1024)S(1)} %add_subtract_fusion.2), kind=kLoop, calls=%fused_computation.3 | loop fusion | flops 3145216 | bytes 4206592 | tf_op jit(solution)/shard_map/reduce_sum | solution.py:349
  19.9 2.5 %collective-permute-start.4 = (f32[512]{0:T(512)S(1)}, f32[512]{0:T(512)S(1)}, u32[]{:S(2)}, u32[]{:S(2)}) collective-permute-start(f32[512]{0:T(512)S(1)} %log_add_fusion.9), channel_id=1, source_target_pairs={{0,24},{8,16},{16,8},{24,0},{1,25},{9,17},{17,9},{25,1},{2,26},{10... | collective-permute-start | bytes 6152 | tf_op jit(solution)/shard_map/ppermute | solution.py:26
  23.5 1.0 %collective-permute-done.4 = f32[512]{0:T(512)S(1)} collective-permute-done((f32[512]{0:T(512)S(1)}, f32[512]{0:T(512)S(1)}, u32[]{:S(2)}, u32[]{:S(2)}) %collective-permute-start.4) | collective-permute-done | bytes 2080 | tf_op jit(solution)/shard_map/ppermute | solution.py:26
  24.5 1.5 %collective-permute-done.5 = f32[512]{0:T(512)S(1)} collective-permute-done((f32[512]{0:T(512)S(1)}, f32[512]{0:T(512)S(1)}, u32[]{:S(2)}, u32[]{:S(2)}) %collective-permute-start.5) | collective-permute-done | bytes 2080 | tf_op jit(solution)/shard_map/ppermute | solution.py:26
  26.9 0.8 exponential_reduce_fusion.2
  27.8 1.2 %collective-permute-done.7 = f32[2048]{0:T(1024)S(1)} collective-permute-done((f32[2048]{0:T(1024)S(1)}, f32[2048]{0:T(1024)S(1)}, u32[]{:S(2)}, u32[]{:S(2)}) %collective-permute-start.7) | collective-permute-done | bytes 8224 | tf_op jit(solution)/shard_map/ppermute | solution.py:26
  29.1 2.0 %collective-permute-start.8 = (f32[2048]{0:T(1024)S(1)}, f32[2048]{0:T(1024)S(1)}, u32[]{:S(2)}, u32[]{:S(2)}) collective-permute-start(f32[2048]{0:T(1024)S(1)} %log_add_fusion.2), channel_id=1, source_target_pairs={{0,2},{1,5},{2,0},{3,7},{4,6},{5,1},{6,4},{7,3},{8,10},{9,13},{10,... | collective-permute-start | bytes 24584 | tf_op jit(solution)/shard_map/ppermute | solution.py:55
  31.1 1.6 %collective-permute-done.9 = f32[2048]{0:T(1024)S(1)} collective-permute-done((f32[2048]{0:T(1024)S(1)}, f32[2048]{0:T(1024)S(1)}, u32[]{:S(2)}, u32[]{:S(2)}) %collective-permute-start.9) | collective-permute-done | bytes 8224 | tf_op jit(solution)/shard_map/ppermute | solution.py:55
  32.8 1.0 %collective-permute-start.10 = (f32[2048]{0:T(1024)S(1)}, f32[2048]{0:T(1024)S(1)}, u32[]{:S(2)}, u32[]{:S(2)}) collective-permute-start(f32[2048]{0:T(1024)S(1)} %add_select_fusion.1), channel_id=1, source_target_pairs={{0,1},{1,0},{2,3},{3,2},{4,5},{5,4},{6,7},{7,6},{8,9},{9,8},{10,11... | collective-permute-start | bytes 24584 | tf_op jit(solution)/shard_map/ppermute | solution.py:26
  33.8 0.8 %collective-permute-done.10 = f32[2048]{0:T(1024)S(1)} collective-permute-done((f32[2048]{0:T(1024)S(1)}, f32[2048]{0:T(1024)S(1)}, u32[]{:S(2)}, u32[]{:S(2)}) %collective-permute-start.10) | collective-permute-done | bytes 8224 | tf_op jit(solution)/shard_map/ppermute | solution.py:26
  35.0 0.8 %exponential_reduce_fusion.1 = f32[512]{0:T(512)S(1)} fusion(f32[512,2048]{1,0:T(8,128)S(1)} %get-tuple-element.80, f32[512]{0:T(512)S(1)} %add_reduce_fusion.1, f32[2048]{0:T(1024)S(1)} %add_subtract_fusion.1), kind=kLoop, calls=%fused_computation.1 | loop fusion | flops 3145216 | bytes 4206592 | tf_op jit(solution)/shard_map/reduce_sum | solution.py:349
  35.8 1.6 %collective-permute-start.11 = (f32[512]{0:T(512)S(1)}, f32[512]{0:T(512)S(1)}, u32[]{:S(2)}, u32[]{:S(2)}) collective-permute-start(f32[512]{0:T(512)S(1)} %log_add_fusion.7), channel_id=1, source_target_pairs={{0,24},{8,16},{16,8},{24,0},{1,25},{9,17},{17,9},{25,1},{2,26},{10... | collective-permute-start | bytes 6152 | tf_op jit(solution)/shard_map/ppermute | solution.py:26
  37.9 1.5 %collective-permute-start.13 = (f32[512]{0:T(512)S(1)}, f32[512]{0:T(512)S(1)}, u32[]{:S(2)}, u32[]{:S(2)}) collective-permute-start(f32[512]{0:T(512)S(1)} %log_add_fusion.7), channel_id=1, source_target_pairs={{0,8},{8,0},{16,24},{24,16},{1,9},{9,1},{17,25},{25,17},{2,10},{10... | collective-permute-start | bytes 6152 | tf_op jit(solution)/shard_map/ppermute | solution.py:26
  39.4 1.0 %collective-permute-done.11 = f32[512]{0:T(512)S(1)} collective-permute-done((f32[512]{0:T(512)S(1)}, f32[512]{0:T(512)S(1)}, u32[]{:S(2)}, u32[]{:S(2)}) %collective-permute-start.11) | collective-permute-done | bytes 2080 | tf_op jit(solution)/shard_map/ppermute | solution.py:26
  41.9 0.8 exponential_reduce_fusion
  42.8 1.2 %collective-permute-done.14 = f32[2048]{0:T(1024)S(1)} collective-permute-done((f32[2048]{0:T(1024)S(1)}, f32[2048]{0:T(1024)S(1)}, u32[]{:S(2)}, u32[]{:S(2)}) %collective-permute-start.14) | collective-permute-done | bytes 8224 | tf_op jit(solution)/shard_map/ppermute | solution.py:26
  43.9 1.4 %collective-permute-start.16 = (f32[2048]{0:T(1024)S(1)}, f32[2048]{0:T(1024)S(1)}, u32[]{:S(2)}, u32[]{:S(2)}) collective-permute-start(f32[2048]{0:T(1024)S(1)} %log_add_fusion), channel_id=1, source_target_pairs={{0,2},{1,7},{2,0},{3,5},{4,6},{5,3},{6,4},{7,1},{8,10},{9,15},{10,... | collective-permute-start | bytes 24584 | tf_op jit(solution)/shard_map/ppermute | solution.py:55
  45.4 0.6 collective-permute-start.15
  46.0 1.6 %collective-permute-done.16 = f32[2048]{0:T(1024)S(1)} collective-permute-done((f32[2048]{0:T(1024)S(1)}, f32[2048]{0:T(1024)S(1)}, u32[]{:S(2)}, u32[]{:S(2)}) %collective-permute-start.16) | collective-permute-done | bytes 8224 | tf_op jit(solution)/shard_map/ppermute | solution.py:55
  47.6 1.4 %collective-permute-done.15 = f32[2048]{0:T(1024)S(1)} collective-permute-done((f32[2048]{0:T(1024)S(1)}, f32[2048]{0:T(1024)S(1)}, u32[]{:S(2)}, u32[]{:S(2)}) %collective-permute-start.15) | collective-permute-done | bytes 8224 | tf_op jit(solution)/shard_map/ppermute | solution.py:55
  49.1 0.8 %collective-permute-start.17 = (f32[2048]{0:T(1024)S(1)}, f32[2048]{0:T(1024)S(1)}, u32[]{:S(2)}, u32[]{:S(2)}) collective-permute-start(f32[2048]{0:T(1024)S(1)} %add_select_fusion), channel_id=1, source_target_pairs={{0,1},{1,0},{2,3},{3,2},{4,5},{5,4},{6,7},{7,6},{8,9},{9,8},{10,11... | collective-permute-start | bytes 24584 | tf_op jit(solution)/shard_map/ppermute | solution.py:26
  49.8 0.8 %collective-permute-done.17 = f32[2048]{0:T(1024)S(1)} collective-permute-done((f32[2048]{0:T(1024)S(1)}, f32[2048]{0:T(1024)S(1)}, u32[]{:S(2)}, u32[]{:S(2)}) %collective-permute-start.17) | collective-permute-done | bytes 8224 | tf_op jit(solution)/shard_map/ppermute | solution.py:26
  51.5 0.7 shard_map.59
  52.2 1.6 %collective-permute-start.20 = (bf16[144,512]{1,0:T(8,128)(2,1)S(1)}, bf16[144,512]{1,0:T(8,128)(2,1)S(1)}, u32[]{:S(2)}, u32[]{:S(2)}) collective-permute-start(bf16[144,512]{1,0:T(8,128)(2,1)S(1)} %get-tuple-element.30), channel_id=1, source_target_pairs={{0,8},{8,0},{16,24},{24,16},{1,9},{9,1},{17,25},{25,17},{2,10},{10... | collective-permute-start | bytes 442376 | tf_op jit(solution)/shard_map/ppermute | solution.py:26
  53.7 1.5 %collective-permute-start.21 = (bf16[144,512]{1,0:T(8,128)(2,1)S(1)}, bf16[144,512]{1,0:T(8,128)(2,1)S(1)}, u32[]{:S(2)}, u32[]{:S(2)}) collective-permute-start(bf16[144,512]{1,0:T(8,128)(2,1)S(1)} %get-tuple-element.31), channel_id=1, source_target_pairs={{0,16},{8,24},{16,0},{24,8},{1,17},{9,25},{17,1},{25,9},{2,18},{10... | collective-permute-start | bytes 442376 | tf_op jit(solution)/shard_map/ppermute | solution.py:26
  56.0 0.7 shard_map.61
  57.9 1.3 %shard_map.60.kept = f32[2,128,1024]{2,1,0:T(8,128)S(1)} custom-call(bf16[256,2048]{1,0:T(8,128)(2,1)S(1)} %get-tuple-element.48.plan, bf16[2048,1024]{1,0:T(8,128)(2,1)S(1)} %copy-done, f32[2,128]{1,0:T(2,128)S(1)} %bitcast.43), custom_call_target="tpu_custom_call" | custom-call | flops 1073741824 | bytes 524288 | tf_op jit(solution)/shard_map/pallas_call | solution.py:363
  59.8 2.4 %collective-permute-start.23 = (bf16[144,512]{1,0:T(8,128)(2,1)S(1)}, bf16[144,512]{1,0:T(8,128)(2,1)S(1)}, u32[]{:S(2)}, u32[]{:S(2)}) collective-permute-start(bf16[144,512]{1,0:T(8,128)(2,1)S(1)} %get-tuple-element.37.mine), channel_id=1, source_target_pairs={{0,16},{8,24},{16,0},{24,8},{1,17},{9,25},{17,1},{25,9},{2,18},{10... | collective-permute-start | bytes 442376 | tf_op jit(solution)/shard_map/ppermute | solution.py:26
  62.5 0.7 collective-permute-done.19.upper
  63.3 1.5 %collective-permute-start.22 = (bf16[128,512]{1,0:T(8,128)(2,1)S(1)}, bf16[128,512]{1,0:T(8,128)(2,1)S(1)}, u32[]{:S(2)}, u32[]{:S(2)}) collective-permute-start(bf16[128,512]{1,0:T(8,128)(2,1)S(1)} %get-tuple-element.36.mine), channel_id=1, source_target_pairs={{0,16},{8,24},{16,0},{24,8},{1,17},{9,25},{17,1},{25,9},{2,18},{10... | collective-permute-start | bytes 393224 | tf_op jit(solution)/shard_map/ppermute | solution.py:26
  65.2 1.6 %collective-permute-done.23.theirs = bf16[144,512]{1,0:T(8,128)(2,1)S(1)} collective-permute-done((bf16[144,512]{1,0:T(8,128)(2,1)S(1)}, bf16[144,512]{1,0:T(8,128)(2,1)S(1)}, u32[]{:S(2)}, u32[]{:S(2)}) %collective-permute-start.23) | collective-permute-done | bytes 147488 | tf_op jit(solution)/shard_map/ppermute | solution.py:26
  67.0 1.3 %collective-permute-start.28 = (bf16[144,512]{1,0:T(8,128)(2,1)S(1)}, bf16[144,512]{1,0:T(8,128)(2,1)S(1)}, u32[]{:S(2)}, u32[]{:S(2)}) collective-permute-start(bf16[144,512]{1,0:T(8,128)(2,1)S(1)} %get-tuple-element.42.lower_kept), channel_id=1, source_target_pairs={{0,8},{8,0},{16,24},{24,16},{1,9},{9,1},{17,25},{25,17},{2,10},{10... | collective-permute-start | bytes 442376 | tf_op jit(solution)/shard_map/ppermute | solution.py:26
  68.3 0.7 collective-permute-done.26.theirs
  69.5 2.1 %collective-permute-start.24 = (bf16[128,512]{1,0:T(8,128)(2,1)S(1)}, bf16[128,512]{1,0:T(8,128)(2,1)S(1)}, u32[]{:S(2)}, u32[]{:S(2)}) collective-permute-start(bf16[128,512]{1,0:T(8,128)(2,1)S(1)} %shard_map.65.refs_2_), channel_id=1, source_target_pairs={{0,8},{8,0},{16,24},{24,16},{1,9},{9,1},{17,25},{25,17},{2,10},{10... | collective-permute-start | bytes 393224 | tf_op jit(solution)/shard_map/ppermute | solution.py:26
  72.1 2.6 %collective-permute-done.28.lower_sent = bf16[144,512]{1,0:T(8,128)(2,1)S(1)} collective-permute-done((bf16[144,512]{1,0:T(8,128)(2,1)S(1)}, bf16[144,512]{1,0:T(8,128)(2,1)S(1)}, u32[]{:S(2)}, u32[]{:S(2)}) %collective-permute-start.28) | collective-permute-done | bytes 147488 | tf_op jit(solution)/shard_map/ppermute | solution.py:26
  74.6 1.4 %shard_map.68 = (bf16[512,1024]{1,0:T(8,128)(2,1)}, f32[4,128]{1,0:T(4,128)}, f32[1,2048]{1,0:T(1,128)}) custom-call(bf16[144,512]{1,0:T(8,128)(2,1)S(1)} %collective-permute-done.28.lower_sent, bf16[144,512]{1,0:T(8,128)(2,1)S(1)} %collective-permute-done.29.upper_sent, bf16[144,512]{1,0:T(8,128)(2,1)S(1)} %get-tuple-element.42.lower_kept, ...), custom_call_target="tpu_custom_call" | custom-call | bytes 524288 | tf_op jit(solution)/shard_map/pallas_call | solution.py:363
  76.1 0.9 %collective-permute-done.27.refs_1_ = bf16[128,512]{1,0:T(8,128)(2,1)S(1)} collective-permute-done((bf16[128,512]{1,0:T(8,128)(2,1)S(1)}, bf16[128,512]{1,0:T(8,128)(2,1)S(1)}, u32[]{:S(2)}, u32[]{:S(2)}) %collective-permute-start.27) | collective-permute-done | bytes 131104 | tf_op jit(solution)/shard_map/ppermute | solution.py:26
  77.0 0.8 %shard_map.69 = bf16[512,1024]{1,0:T(8,128)(2,1)} custom-call(bf16[128,512]{1,0:T(8,128)(2,1)S(1)} %collective-permute-done.24.refs_0_, bf16[128,512]{1,0:T(8,128)(2,1)S(1)} %collective-permute-done.27.refs_1_, bf16[128,512]{1,0:T(8,128)(2,1)S(1)} %shard_map.65.refs_2_, bf16[128,512]{1,0:T(8,128)(2,1)S(1)} %shard_map.67.refs_3_, ...), custom_call_target="tpu_custom_call", output_to_operand_aliasing={{}: (4, {})} | custom-call | tf_op jit(solution)/shard_map/pallas_call | solution.py:93
  (69 shorter events, 11.1 us)
Async XLA Ops:
  8.1 1.4 %collective-permute-start = (f32[2048]{0:T(1024)S(1)}, f32[2048]{0:T(1024)S(1)}, u32[]{:S(2)}, u32[]{:S(2)}) collective-permute-start(f32[2048]{0:T(1024)S(1)} %log_add_fusion.5), channel_id=1, source_target_pairs={{0,1},{1,0},{2,3},{3,2},{4,5},{5,4},{6,7},{7,6},{8,9},{9,8},{10,11... | collective-permute-start | bytes 24584 | tf_op jit(solution)/shard_map/ppermute | solution.py:26
  9.5 4.6 %collective-permute-start.2 = (f32[2048]{0:T(1024)S(1)}, f32[2048]{0:T(1024)S(1)}, u32[]{:S(2)}, u32[]{:S(2)}) collective-permute-start(f32[2048]{0:T(1024)S(1)} %log_add_fusion.4), channel_id=1, source_target_pairs={{0,2},{1,7},{2,0},{3,5},{4,6},{5,3},{6,4},{7,1},{8,10},{9,15},{10,... | collective-permute-start | bytes 24584 | tf_op jit(solution)/shard_map/ppermute | solution.py:55
  12.5 3.7 %collective-permute-start.1 = (f32[2048]{0:T(1024)S(1)}, f32[2048]{0:T(1024)S(1)}, u32[]{:S(2)}, u32[]{:S(2)}) collective-permute-start(f32[2048]{0:T(1024)S(1)} %log_add_fusion.4), channel_id=1, source_target_pairs={{0,2},{1,5},{2,0},{3,7},{4,6},{5,1},{6,4},{7,3},{8,10},{9,13},{10,... | collective-permute-start | bytes 24584 | tf_op jit(solution)/shard_map/ppermute | solution.py:55
  16.2 2.6 %collective-permute-start.3 = (f32[2048]{0:T(1024)S(1)}, f32[2048]{0:T(1024)S(1)}, u32[]{:S(2)}, u32[]{:S(2)}) collective-permute-start(f32[2048]{0:T(1024)S(1)} %add_select_fusion.2), channel_id=1, source_target_pairs={{0,1},{1,0},{2,3},{3,2},{4,5},{5,4},{6,7},{7,6},{8,9},{9,8},{10,11... | collective-permute-start | bytes 24584 | tf_op jit(solution)/shard_map/ppermute | solution.py:26
  19.9 4.5 %collective-permute-start.4 = (f32[512]{0:T(512)S(1)}, f32[512]{0:T(512)S(1)}, u32[]{:S(2)}, u32[]{:S(2)}) collective-permute-start(f32[512]{0:T(512)S(1)} %log_add_fusion.9), channel_id=1, source_target_pairs={{0,24},{8,16},{16,8},{24,0},{1,25},{9,17},{17,9},{25,1},{2,26},{10... | collective-permute-start | bytes 6152 | tf_op jit(solution)/shard_map/ppermute | solution.py:26
  22.4 3.6 %collective-permute-start.5 = (f32[512]{0:T(512)S(1)}, f32[512]{0:T(512)S(1)}, u32[]{:S(2)}, u32[]{:S(2)}) collective-permute-start(f32[512]{0:T(512)S(1)} %log_add_fusion.9), channel_id=1, source_target_pairs={{0,16},{8,24},{16,0},{24,8},{1,17},{9,25},{17,1},{25,9},{2,18},{10... | collective-permute-start | bytes 6152 | tf_op jit(solution)/shard_map/ppermute | solution.py:26
  22.9 3.6 %collective-permute-start.6 = (f32[512]{0:T(512)S(1)}, f32[512]{0:T(512)S(1)}, u32[]{:S(2)}, u32[]{:S(2)}) collective-permute-start(f32[512]{0:T(512)S(1)} %log_add_fusion.9), channel_id=1, source_target_pairs={{0,8},{8,0},{16,24},{24,16},{1,9},{9,1},{17,25},{25,17},{2,10},{10... | collective-permute-start | bytes 6152 | tf_op jit(solution)/shard_map/ppermute | solution.py:26
  27.7 1.2 %collective-permute-start.7 = (f32[2048]{0:T(1024)S(1)}, f32[2048]{0:T(1024)S(1)}, u32[]{:S(2)}, u32[]{:S(2)}) collective-permute-start(f32[2048]{0:T(1024)S(1)} %log_add_fusion.3), channel_id=1, source_target_pairs={{0,1},{1,0},{2,3},{3,2},{4,5},{5,4},{6,7},{7,6},{8,9},{9,8},{10,11... | collective-permute-start | bytes 24584 | tf_op jit(solution)/shard_map/ppermute | solution.py:26
  29.0 3.7 %collective-permute-start.9 = (f32[2048]{0:T(1024)S(1)}, f32[2048]{0:T(1024)S(1)}, u32[]{:S(2)}, u32[]{:S(2)}) collective-permute-start(f32[2048]{0:T(1024)S(1)} %log_add_fusion.2), channel_id=1, source_target_pairs={{0,2},{1,7},{2,0},{3,5},{4,6},{5,3},{6,4},{7,1},{8,10},{9,15},{10,... | collective-permute-start | bytes 24584 | tf_op jit(solution)/shard_map/ppermute | solution.py:55
  29.1 3.7 %collective-permute-start.8 = (f32[2048]{0:T(1024)S(1)}, f32[2048]{0:T(1024)S(1)}, u32[]{:S(2)}, u32[]{:S(2)}) collective-permute-start(f32[2048]{0:T(1024)S(1)} %log_add_fusion.2), channel_id=1, source_target_pairs={{0,2},{1,5},{2,0},{3,7},{4,6},{5,1},{6,4},{7,3},{8,10},{9,13},{10,... | collective-permute-start | bytes 24584 | tf_op jit(solution)/shard_map/ppermute | solution.py:55
  32.8 1.8 %collective-permute-start.10 = (f32[2048]{0:T(1024)S(1)}, f32[2048]{0:T(1024)S(1)}, u32[]{:S(2)}, u32[]{:S(2)}) collective-permute-start(f32[2048]{0:T(1024)S(1)} %add_select_fusion.1), channel_id=1, source_target_pairs={{0,1},{1,0},{2,3},{3,2},{4,5},{5,4},{6,7},{7,6},{8,9},{9,8},{10,11... | collective-permute-start | bytes 24584 | tf_op jit(solution)/shard_map/ppermute | solution.py:26
  34.6 6.3 %copy-start = (bf16[2048,1024]{1,0:T(8,128)(2,1)S(1)}, bf16[2048,1024]{1,0:T(8,128)(2,1)}, u32[]{:S(2)}) copy-start(bf16[2048,1024]{1,0:T(8,128)(2,1)} %embeddings.3) | copy-start | bytes 12582916
  35.8 4.5 %collective-permute-start.11 = (f32[512]{0:T(512)S(1)}, f32[512]{0:T(512)S(1)}, u32[]{:S(2)}, u32[]{:S(2)}) collective-permute-start(f32[512]{0:T(512)S(1)} %log_add_fusion.7), channel_id=1, source_target_pairs={{0,24},{8,16},{16,8},{24,0},{1,25},{9,17},{17,9},{25,1},{2,26},{10... | collective-permute-start | bytes 6152 | tf_op jit(solution)/shard_map/ppermute | solution.py:26
  37.4 3.6 %collective-permute-start.12 = (f32[512]{0:T(512)S(1)}, f32[512]{0:T(512)S(1)}, u32[]{:S(2)}, u32[]{:S(2)}) collective-permute-start(f32[512]{0:T(512)S(1)} %log_add_fusion.7), channel_id=1, source_target_pairs={{0,16},{8,24},{16,0},{24,8},{1,17},{9,25},{17,1},{25,9},{2,18},{10... | collective-permute-start | bytes 6152 | tf_op jit(solution)/shard_map/ppermute | solution.py:26
  37.9 3.6 %collective-permute-start.13 = (f32[512]{0:T(512)S(1)}, f32[512]{0:T(512)S(1)}, u32[]{:S(2)}, u32[]{:S(2)}) collective-permute-start(f32[512]{0:T(512)S(1)} %log_add_fusion.7), channel_id=1, source_target_pairs={{0,8},{8,0},{16,24},{24,16},{1,9},{9,1},{17,25},{25,17},{2,10},{10... | collective-permute-start | bytes 6152 | tf_op jit(solution)/shard_map/ppermute | solution.py:26
  42.7 1.2 %collective-permute-start.14 = (f32[2048]{0:T(1024)S(1)}, f32[2048]{0:T(1024)S(1)}, u32[]{:S(2)}, u32[]{:S(2)}) collective-permute-start(f32[2048]{0:T(1024)S(1)} %log_add_fusion.1), channel_id=1, source_target_pairs={{0,1},{1,0},{2,3},{3,2},{4,5},{5,4},{6,7},{7,6},{8,9},{9,8},{10,11... | collective-permute-start | bytes 24584 | tf_op jit(solution)/shard_map/ppermute | solution.py:26
  43.9 3.7 %collective-permute-start.16 = (f32[2048]{0:T(1024)S(1)}, f32[2048]{0:T(1024)S(1)}, u32[]{:S(2)}, u32[]{:S(2)}) collective-permute-start(f32[2048]{0:T(1024)S(1)} %log_add_fusion), channel_id=1, source_target_pairs={{0,2},{1,7},{2,0},{3,5},{4,6},{5,3},{6,4},{7,1},{8,10},{9,15},{10,... | collective-permute-start | bytes 24584 | tf_op jit(solution)/shard_map/ppermute | solution.py:55
  45.4 3.7 %collective-permute-start.15 = (f32[2048]{0:T(1024)S(1)}, f32[2048]{0:T(1024)S(1)}, u32[]{:S(2)}, u32[]{:S(2)}) collective-permute-start(f32[2048]{0:T(1024)S(1)} %log_add_fusion), channel_id=1, source_target_pairs={{0,2},{1,5},{2,0},{3,7},{4,6},{5,1},{6,4},{7,3},{8,10},{9,13},{10,... | collective-permute-start | bytes 24584 | tf_op jit(solution)/shard_map/ppermute | solution.py:55
  49.1 1.6 %collective-permute-start.17 = (f32[2048]{0:T(1024)S(1)}, f32[2048]{0:T(1024)S(1)}, u32[]{:S(2)}, u32[]{:S(2)}) collective-permute-start(f32[2048]{0:T(1024)S(1)} %add_select_fusion), channel_id=1, source_target_pairs={{0,1},{1,0},{2,3},{3,2},{4,5},{5,4},{6,7},{7,6},{8,9},{9,8},{10,11... | collective-permute-start | bytes 24584 | tf_op jit(solution)/shard_map/ppermute | solution.py:26
  52.2 7.0 %collective-permute-start.20 = (bf16[144,512]{1,0:T(8,128)(2,1)S(1)}, bf16[144,512]{1,0:T(8,128)(2,1)S(1)}, u32[]{:S(2)}, u32[]{:S(2)}) collective-permute-start(bf16[144,512]{1,0:T(8,128)(2,1)S(1)} %get-tuple-element.30), channel_id=1, source_target_pairs={{0,8},{8,0},{16,24},{24,16},{1,9},{9,1},{17,25},{25,17},{2,10},{10... | collective-permute-start | bytes 442376 | tf_op jit(solution)/shard_map/ppermute | solution.py:26
  53.7 5.9 %collective-permute-start.21 = (bf16[144,512]{1,0:T(8,128)(2,1)S(1)}, bf16[144,512]{1,0:T(8,128)(2,1)S(1)}, u32[]{:S(2)}, u32[]{:S(2)}) collective-permute-start(bf16[144,512]{1,0:T(8,128)(2,1)S(1)} %get-tuple-element.31), channel_id=1, source_target_pairs={{0,16},{8,24},{16,0},{24,8},{1,17},{9,25},{17,1},{25,9},{2,18},{10... | collective-permute-start | bytes 442376 | tf_op jit(solution)/shard_map/ppermute | solution.py:26
  56.8 5.7 %collective-permute-start.18 = (bf16[128,512]{1,0:T(8,128)(2,1)S(1)}, bf16[128,512]{1,0:T(8,128)(2,1)S(1)}, u32[]{:S(2)}, u32[]{:S(2)}) collective-permute-start(bf16[128,512]{1,0:T(8,128)(2,1)S(1)} %get-tuple-element.33), channel_id=1, source_target_pairs={{0,8},{8,0},{16,24},{24,16},{1,9},{9,1},{17,25},{25,17},{2,10},{10... | collective-permute-start | bytes 393224 | tf_op jit(solution)/shard_map/ppermute | solution.py:26
  57.4 5.8 %collective-permute-start.19 = (bf16[128,512]{1,0:T(8,128)(2,1)S(1)}, bf16[128,512]{1,0:T(8,128)(2,1)S(1)}, u32[]{:S(2)}, u32[]{:S(2)}) collective-permute-start(bf16[128,512]{1,0:T(8,128)(2,1)S(1)} %get-tuple-element.34), channel_id=1, source_target_pairs={{0,16},{8,24},{16,0},{24,8},{1,17},{9,25},{17,1},{25,9},{2,18},{10... | collective-permute-start | bytes 393224 | tf_op jit(solution)/shard_map/ppermute | solution.py:26
  59.8 7.0 %collective-permute-start.23 = (bf16[144,512]{1,0:T(8,128)(2,1)S(1)}, bf16[144,512]{1,0:T(8,128)(2,1)S(1)}, u32[]{:S(2)}, u32[]{:S(2)}) collective-permute-start(bf16[144,512]{1,0:T(8,128)(2,1)S(1)} %get-tuple-element.37.mine), channel_id=1, source_target_pairs={{0,16},{8,24},{16,0},{24,8},{1,17},{9,25},{17,1},{25,9},{2,18},{10... | collective-permute-start | bytes 442376 | tf_op jit(solution)/shard_map/ppermute | solution.py:26
  62.2 6.7 %collective-permute-start.26 = (bf16[144,512]{1,0:T(8,128)(2,1)S(1)}, bf16[144,512]{1,0:T(8,128)(2,1)S(1)}, u32[]{:S(2)}, u32[]{:S(2)}) collective-permute-start(bf16[144,512]{1,0:T(8,128)(2,1)S(1)} %get-tuple-element.40.mine), channel_id=1, source_target_pairs={{0,8},{8,0},{16,24},{24,16},{1,9},{9,1},{17,25},{25,17},{2,10},{10... | collective-permute-start | bytes 442376 | tf_op jit(solution)/shard_map/ppermute | solution.py:26
  63.3 6.0 %collective-permute-start.22 = (bf16[128,512]{1,0:T(8,128)(2,1)S(1)}, bf16[128,512]{1,0:T(8,128)(2,1)S(1)}, u32[]{:S(2)}, u32[]{:S(2)}) collective-permute-start(bf16[128,512]{1,0:T(8,128)(2,1)S(1)} %get-tuple-element.36.mine), channel_id=1, source_target_pairs={{0,16},{8,24},{16,0},{24,8},{1,17},{9,25},{17,1},{25,9},{2,18},{10... | collective-permute-start | bytes 393224 | tf_op jit(solution)/shard_map/ppermute | solution.py:26
  64.8 7.0 %collective-permute-start.25 = (bf16[128,512]{1,0:T(8,128)(2,1)S(1)}, bf16[128,512]{1,0:T(8,128)(2,1)S(1)}, u32[]{:S(2)}, u32[]{:S(2)}) collective-permute-start(bf16[128,512]{1,0:T(8,128)(2,1)S(1)} %get-tuple-element.39.mine), channel_id=1, source_target_pairs={{0,8},{8,0},{16,24},{24,16},{1,9},{9,1},{17,25},{25,17},{2,10},{10... | collective-permute-start | bytes 393224 | tf_op jit(solution)/shard_map/ppermute | solution.py:26
  67.0 7.6 %collective-permute-start.28 = (bf16[144,512]{1,0:T(8,128)(2,1)S(1)}, bf16[144,512]{1,0:T(8,128)(2,1)S(1)}, u32[]{:S(2)}, u32[]{:S(2)}) collective-permute-start(bf16[144,512]{1,0:T(8,128)(2,1)S(1)} %get-tuple-element.42.lower_kept), channel_id=1, source_target_pairs={{0,8},{8,0},{16,24},{24,16},{1,9},{9,1},{17,25},{25,17},{2,10},{10... | collective-permute-start | bytes 442376 | tf_op jit(solution)/shard_map/ppermute | solution.py:26
  69.1 5.5 %collective-permute-start.29 = (bf16[144,512]{1,0:T(8,128)(2,1)S(1)}, bf16[144,512]{1,0:T(8,128)(2,1)S(1)}, u32[]{:S(2)}, u32[]{:S(2)}) collective-permute-start(bf16[144,512]{1,0:T(8,128)(2,1)S(1)} %get-tuple-element.43.upper_kept), channel_id=1, source_target_pairs={{0,16},{8,24},{16,0},{24,8},{1,17},{9,25},{17,1},{25,9},{2,18},{10... | collective-permute-start | bytes 442376 | tf_op jit(solution)/shard_map/ppermute | solution.py:26
  69.5 6.6 %collective-permute-start.24 = (bf16[128,512]{1,0:T(8,128)(2,1)S(1)}, bf16[128,512]{1,0:T(8,128)(2,1)S(1)}, u32[]{:S(2)}, u32[]{:S(2)}) collective-permute-start(bf16[128,512]{1,0:T(8,128)(2,1)S(1)} %shard_map.65.refs_2_), channel_id=1, source_target_pairs={{0,8},{8,0},{16,24},{24,16},{1,9},{9,1},{17,25},{25,17},{2,10},{10... | collective-permute-start | bytes 393224 | tf_op jit(solution)/shard_map/ppermute | solution.py:26
  71.9 5.0 %collective-permute-start.27 = (bf16[128,512]{1,0:T(8,128)(2,1)S(1)}, bf16[128,512]{1,0:T(8,128)(2,1)S(1)}, u32[]{:S(2)}, u32[]{:S(2)}) collective-permute-start(bf16[128,512]{1,0:T(8,128)(2,1)S(1)} %shard_map.67.refs_3_), channel_id=1, source_target_pairs={{0,16},{8,24},{16,0},{24,8},{1,17},{9,25},{17,1},{25,9},{2,18},{10... | collective-permute-start | bytes 393224 | tf_op jit(solution)/shard_map/ppermute | solution.py:26

commit v8 on v7

--- a/solution.py
+++ b/solution.py
@@ -452,7 +452,7 @@
     k_total = cent_here * lax.axis_size("cent")
 
     bits = bits_of("dp")
-    orders = (bits, [bits[1], bits[0]] + bits[2:])
+    orders = ([bits[1], bits[0]] + bits[2:], bits)
     place = jnp.full((1,), lax.axis_index("dp"), jnp.int32)
     ups = [place >> bit & 1 for bit in bits]
     ups = [up == 1 for up in ups]

time: 78 us -> 78 us (level)
  no operation moved by 1% of the time
where the time goes in v8:
time: 78 us; the launch traced here: 77.8 us
  starting transfers between devices  30.8 us (39%)
  waiting for transfers between devices  26.1 us (33%)
  other arithmetic  9.32 us (12%)
  Pallas kernels  5.97 us (8%)
  matrix products  4.57 us (6%)
  between operations  0.91 us (1%)
    ppermute x24, starting transfers between devices, flipped(): return lax.ppermute(x, axis, [(k, k ^ mask) for k in range(size)])  23.6 us
    ppermute x24, waiting for transfers between devices, flipped(): return lax.ppermute(x, axis, [(k, k ^ mask) for k in range(size)])  17.8 us
    ppermute x6, waiting for transfers between devices, split(): lax.ppermute(value, 'cent', [(k, k ^ (odd_mask if k % 2 else even_mask))...  8.29 us
    ppermute x6, starting transfers between devices, split(): lax.ppermute(value, 'cent', [(k, k ^ (odd_mask if k % 2 else even_mask))...  7.23 us
    pallas_call x10, Pallas kernels, call(): pl.pallas_call(kernel, out_shape=outs, in_specs=[vmem] * len(operands), o...  5.15 us
    dot_general x1, matrix products, on_device(): lax.dot_general(sent_and_kept(centroids), embeddings, (((1,), (1,)), ((),...  4.57 us
    reduce_sum x4, other arithmetic, last_terms(): mass = jnp.sum(terms, axis=1)  2.69 us
    reduce_sum x3, other arithmetic, on_device(): part = top + jnp.log(jnp.sum(jnp.exp(shifted - top[None, :]), axis=0))  2.31 us
  transfers between devices with their start and end apart: 30, of which 25 were waited for; matrix products, arithmetic and copies ran while one was open for 1% of the time, Pallas kernels for 6%

profile of v8, /device:TPU:0, one launch (start us, length us, event | category | flops | bytes accessed | tf_op | source)
XLA Modules:
  0.0 77.8 jit_solution(6298316021565259915)
XLA Ops:
  0.6 0.8 %broadcast_select_fusion.7 = (f32[128]{0:T(128)S(1)}, f32[128]{0:T(128)S(1)}, f32[128]{0:T(128)S(1)}, f32[128]{0:T(128)S(1)}) fusion(pred[]{:T(512)} %bitcast.3, f32[512]{0:T(512)} %param.5, pred[]{:T(512)} %bitcast.4), kind=kLoop, calls=%fused_computation.104 | loop fusion | flops 512 | bytes 4098 | tf_op jit(solution)/shard_map/jit(_where)/select_n | solution.py:463
  1.5 1.3 %broadcast_select_fusion.3 = (bf16[128,1024]{1,0:T(8,128)(2,1)S(1)}, bf16[128,1024]{1,0:T(8,128)(2,1)S(1)}, bf16[128,1024]{1,0:T(8,128)(2,1)S(1)}, bf16[128,1024]{1,0:T(8,128)(2,1)S(1)}) fusion(pred[]{:T(512)} %bitcast.3, bf16[512,1024]{1,0:T(8,128)(2,1)} %param.4, pred[]{:T(512)} %bitcast.4), kind=kLoop, calls=%fused_computation.31 | loop fusion | flops 524288 | bytes 2097154 | tf_op jit(solution)/shard_map/jit(_where)/select_n | solution.py:463
  2.8 4.6 %add_reduce_fusion.4 = (f32[2048]{0:T(1024)S(1)}, f32[512,2048]{1,0:T(8,128)S(1)}) fusion(f32[512]{0:T(512)S(1)} %pad_maximum_fusion, bf16[2048,1024]{1,0:T(8,128)(2,1)} %embeddings.3, bf16[128,1024]{1,0:T(8,128)(2,1)S(1)} %get-tuple-element.53, bf16[128,1024]{1,0:T(8,128)(2,1)S(1)} %get-tuple-element.54, bf16[128,1024]{1,0:T(8,128)(2,1)S(1)} %get-tuple-element.52, ...), kind=kOutput, calls=%fused_computation.9 | convolution fusion | flops 2154821632 | bytes 9447424 | tf_op jit(solution)/shard_map/dot_general | solution.py:479
  7.3 0.8 %exponential_reduce_fusion.4 = f32[2048]{0:T(1024)S(1)} fusion(f32[512,2048]{1,0:T(8,128)S(1)} %get-tuple-element.80, f32[2048]{0:T(1024)S(1)} %get-tuple-element.79, f32[512]{0:T(512)S(1)} %pad_maximum_fusion), kind=kLoop, calls=%fused_computation.4 | loop fusion | flops 3143680 | bytes 4212736 | tf_op jit(solution)/shard_map/reduce_sum | solution.py:486
  8.7 0.8 %collective-permute-done = f32[2048]{0:T(1024)S(1)} collective-permute-done((f32[2048]{0:T(1024)S(1)}, f32[2048]{0:T(1024)S(1)}, u32[]{:S(2)}, u32[]{:S(2)}) %collective-permute-start) | collective-permute-done | bytes 8224 | tf_op jit(solution)/shard_map/ppermute | solution.py:26
  9.5 3.0 %collective-permute-start.2 = (f32[2048]{0:T(1024)S(1)}, f32[2048]{0:T(1024)S(1)}, u32[]{:S(2)}, u32[]{:S(2)}) collective-permute-start(f32[2048]{0:T(1024)S(1)} %log_add_fusion.4), channel_id=1, source_target_pairs={{0,2},{1,7},{2,0},{3,5},{4,6},{5,3},{6,4},{7,1},{8,10},{9,15},{10,... | collective-permute-start | bytes 24584 | tf_op jit(solution)/shard_map/ppermute | solution.py:55
  12.6 1.6 %collective-permute-done.2 = f32[2048]{0:T(1024)S(1)} collective-permute-done((f32[2048]{0:T(1024)S(1)}, f32[2048]{0:T(1024)S(1)}, u32[]{:S(2)}, u32[]{:S(2)}) %collective-permute-start.2) | collective-permute-done | bytes 8224 | tf_op jit(solution)/shard_map/ppermute | solution.py:55
  14.1 2.0 %collective-permute-done.1 = f32[2048]{0:T(1024)S(1)} collective-permute-done((f32[2048]{0:T(1024)S(1)}, f32[2048]{0:T(1024)S(1)}, u32[]{:S(2)}, u32[]{:S(2)}) %collective-permute-start.1) | collective-permute-done | bytes 8224 | tf_op jit(solution)/shard_map/ppermute | solution.py:55
  16.2 1.7 %collective-permute-start.3 = (f32[2048]{0:T(1024)S(1)}, f32[2048]{0:T(1024)S(1)}, u32[]{:S(2)}, u32[]{:S(2)}) collective-permute-start(f32[2048]{0:T(1024)S(1)} %add_select_fusion.2), channel_id=1, source_target_pairs={{0,1},{1,0},{2,3},{3,2},{4,5},{5,4},{6,7},{7,6},{8,9},{9,8},{10,11... | collective-permute-start | bytes 24584 | tf_op jit(solution)/shard_map/ppermute | solution.py:26
  17.9 0.8 %collective-permute-done.3 = f32[2048]{0:T(1024)S(1)} collective-permute-done((f32[2048]{0:T(1024)S(1)}, f32[2048]{0:T(1024)S(1)}, u32[]{:S(2)}, u32[]{:S(2)}) %collective-permute-start.3) | collective-permute-done | bytes 8224 | tf_op jit(solution)/shard_map/ppermute | solution.py:26
  19.1 0.8 %exponential_reduce_fusion.3 = f32[512]{0:T(512)S(1)} fusion(f32[512,2048]{1,0:T(8,128)S(1)} %get-tuple-element.80, f32[512]{0:T(512)S(1)} %add_reduce_fusion.3, f32[2048]{0:T(1024)S(1)} %add_subtract_fusion.2), kind=kLoop, calls=%fused_computation.3 | loop fusion | flops 3145216 | bytes 4206592 | tf_op jit(solution)/shard_map/reduce_sum | solution.py:349
  19.9 2.5 %collective-permute-start.4 = (f32[512]{0:T(512)S(1)}, f32[512]{0:T(512)S(1)}, u32[]{:S(2)}, u32[]{:S(2)}) collective-permute-start(f32[512]{0:T(512)S(1)} %log_add_fusion.9), channel_id=1, source_target_pairs={{0,24},{8,16},{16,8},{24,0},{1,25},{9,17},{17,9},{25,1},{2,26},{10... | collective-permute-start | bytes 6152 | tf_op jit(solution)/shard_map/ppermute | solution.py:26
  23.5 1.0 %collective-permute-done.4 = f32[512]{0:T(512)S(1)} collective-permute-done((f32[512]{0:T(512)S(1)}, f32[512]{0:T(512)S(1)}, u32[]{:S(2)}, u32[]{:S(2)}) %collective-permute-start.4) | collective-permute-done | bytes 2080 | tf_op jit(solution)/shard_map/ppermute | solution.py:26
  24.5 1.5 %collective-permute-done.5 = f32[512]{0:T(512)S(1)} collective-permute-done((f32[512]{0:T(512)S(1)}, f32[512]{0:T(512)S(1)}, u32[]{:S(2)}, u32[]{:S(2)}) %collective-permute-start.5) | collective-permute-done | bytes 2080 | tf_op jit(solution)/shard_map/ppermute | solution.py:26
  26.9 0.8 exponential_reduce_fusion.2
  27.8 1.2 %collective-permute-done.7 = f32[2048]{0:T(1024)S(1)} collective-permute-done((f32[2048]{0:T(1024)S(1)}, f32[2048]{0:T(1024)S(1)}, u32[]{:S(2)}, u32[]{:S(2)}) %collective-permute-start.7) | collective-permute-done | bytes 8224 | tf_op jit(solution)/shard_map/ppermute | solution.py:26
  29.1 2.0 %collective-permute-start.8 = (f32[2048]{0:T(1024)S(1)}, f32[2048]{0:T(1024)S(1)}, u32[]{:S(2)}, u32[]{:S(2)}) collective-permute-start(f32[2048]{0:T(1024)S(1)} %log_add_fusion.2), channel_id=1, source_target_pairs={{0,2},{1,5},{2,0},{3,7},{4,6},{5,1},{6,4},{7,3},{8,10},{9,13},{10,... | collective-permute-start | bytes 24584 | tf_op jit(solution)/shard_map/ppermute | solution.py:55
  31.1 1.6 %collective-permute-done.9 = f32[2048]{0:T(1024)S(1)} collective-permute-done((f32[2048]{0:T(1024)S(1)}, f32[2048]{0:T(1024)S(1)}, u32[]{:S(2)}, u32[]{:S(2)}) %collective-permute-start.9) | collective-permute-done | bytes 8224 | tf_op jit(solution)/shard_map/ppermute | solution.py:55
  32.8 1.0 %collective-permute-start.10 = (f32[2048]{0:T(1024)S(1)}, f32[2048]{0:T(1024)S(1)}, u32[]{:S(2)}, u32[]{:S(2)}) collective-permute-start(f32[2048]{0:T(1024)S(1)} %add_select_fusion.1), channel_id=1, source_target_pairs={{0,1},{1,0},{2,3},{3,2},{4,5},{5,4},{6,7},{7,6},{8,9},{9,8},{10,11... | collective-permute-start | bytes 24584 | tf_op jit(solution)/shard_map/ppermute | solution.py:26
  33.8 0.8 %collective-permute-done.10 = f32[2048]{0:T(1024)S(1)} collective-permute-done((f32[2048]{0:T(1024)S(1)}, f32[2048]{0:T(1024)S(1)}, u32[]{:S(2)}, u32[]{:S(2)}) %collective-permute-start.10) | collective-permute-done | bytes 8224 | tf_op jit(solution)/shard_map/ppermute | solution.py:26
  35.0 0.8 %exponential_reduce_fusion.1 = f32[512]{0:T(512)S(1)} fusion(f32[512,2048]{1,0:T(8,128)S(1)} %get-tuple-element.80, f32[512]{0:T(512)S(1)} %add_reduce_fusion.1, f32[2048]{0:T(1024)S(1)} %add_subtract_fusion.1), kind=kLoop, calls=%fused_computation.1 | loop fusion | flops 3145216 | bytes 4206592 | tf_op jit(solution)/shard_map/reduce_sum | solution.py:349
  35.8 1.6 %collective-permute-start.11 = (f32[512]{0:T(512)S(1)}, f32[512]{0:T(512)S(1)}, u32[]{:S(2)}, u32[]{:S(2)}) collective-permute-start(f32[512]{0:T(512)S(1)} %log_add_fusion.7), channel_id=1, source_target_pairs={{0,24},{8,16},{16,8},{24,0},{1,25},{9,17},{17,9},{25,1},{2,26},{10... | collective-permute-start | bytes 6152 | tf_op jit(solution)/shard_map/ppermute | solution.py:26
  37.9 1.5 %collective-permute-start.13 = (f32[512]{0:T(512)S(1)}, f32[512]{0:T(512)S(1)}, u32[]{:S(2)}, u32[]{:S(2)}) collective-permute-start(f32[512]{0:T(512)S(1)} %log_add_fusion.7), channel_id=1, source_target_pairs={{0,8},{8,0},{16,24},{24,16},{1,9},{9,1},{17,25},{25,17},{2,10},{10... | collective-permute-start | bytes 6152 | tf_op jit(solution)/shard_map/ppermute | solution.py:26
  39.4 1.0 %collective-permute-done.11 = f32[512]{0:T(512)S(1)} collective-permute-done((f32[512]{0:T(512)S(1)}, f32[512]{0:T(512)S(1)}, u32[]{:S(2)}, u32[]{:S(2)}) %collective-permute-start.11) | collective-permute-done | bytes 2080 | tf_op jit(solution)/shard_map/ppermute | solution.py:26
  41.9 0.8 exponential_reduce_fusion
  42.8 1.2 %collective-permute-done.14 = f32[2048]{0:T(1024)S(1)} collective-permute-done((f32[2048]{0:T(1024)S(1)}, f32[2048]{0:T(1024)S(1)}, u32[]{:S(2)}, u32[]{:S(2)}) %collective-permute-start.14) | collective-permute-done | bytes 8224 | tf_op jit(solution)/shard_map/ppermute | solution.py:26
  43.9 1.4 %collective-permute-start.16 = (f32[2048]{0:T(1024)S(1)}, f32[2048]{0:T(1024)S(1)}, u32[]{:S(2)}, u32[]{:S(2)}) collective-permute-start(f32[2048]{0:T(1024)S(1)} %log_add_fusion), channel_id=1, source_target_pairs={{0,2},{1,7},{2,0},{3,5},{4,6},{5,3},{6,4},{7,1},{8,10},{9,15},{10,... | collective-permute-start | bytes 24584 | tf_op jit(solution)/shard_map/ppermute | solution.py:55
  45.4 0.6 collective-permute-start.15
  46.0 1.6 %collective-permute-done.16 = f32[2048]{0:T(1024)S(1)} collective-permute-done((f32[2048]{0:T(1024)S(1)}, f32[2048]{0:T(1024)S(1)}, u32[]{:S(2)}, u32[]{:S(2)}) %collective-permute-start.16) | collective-permute-done | bytes 8224 | tf_op jit(solution)/shard_map/ppermute | solution.py:55
  47.6 1.4 %collective-permute-done.15 = f32[2048]{0:T(1024)S(1)} collective-permute-done((f32[2048]{0:T(1024)S(1)}, f32[2048]{0:T(1024)S(1)}, u32[]{:S(2)}, u32[]{:S(2)}) %collective-permute-start.15) | collective-permute-done | bytes 8224 | tf_op jit(solution)/shard_map/ppermute | solution.py:55
  49.1 0.8 %collective-permute-start.17 = (f32[2048]{0:T(1024)S(1)}, f32[2048]{0:T(1024)S(1)}, u32[]{:S(2)}, u32[]{:S(2)}) collective-permute-start(f32[2048]{0:T(1024)S(1)} %add_select_fusion), channel_id=1, source_target_pairs={{0,1},{1,0},{2,3},{3,2},{4,5},{5,4},{6,7},{7,6},{8,9},{9,8},{10,11... | collective-permute-start | bytes 24584 | tf_op jit(solution)/shard_map/ppermute | solution.py:26
  49.8 0.8 %collective-permute-done.17 = f32[2048]{0:T(1024)S(1)} collective-permute-done((f32[2048]{0:T(1024)S(1)}, f32[2048]{0:T(1024)S(1)}, u32[]{:S(2)}, u32[]{:S(2)}) %collective-permute-start.17) | collective-permute-done | bytes 8224 | tf_op jit(solution)/shard_map/ppermute | solution.py:26
  51.5 0.7 shard_map.59
  52.2 1.6 %collective-permute-start.20 = (bf16[144,512]{1,0:T(8,128)(2,1)S(1)}, bf16[144,512]{1,0:T(8,128)(2,1)S(1)}, u32[]{:S(2)}, u32[]{:S(2)}) collective-permute-start(bf16[144,512]{1,0:T(8,128)(2,1)S(1)} %get-tuple-element.30), channel_id=1, source_target_pairs={{0,16},{8,24},{16,0},{24,8},{1,17},{9,25},{17,1},{25,9},{2,18},{10... | collective-permute-start | bytes 442376 | tf_op jit(solution)/shard_map/ppermute | solution.py:26
  53.8 1.5 %collective-permute-start.21 = (bf16[144,512]{1,0:T(8,128)(2,1)S(1)}, bf16[144,512]{1,0:T(8,128)(2,1)S(1)}, u32[]{:S(2)}, u32[]{:S(2)}) collective-permute-start(bf16[144,512]{1,0:T(8,128)(2,1)S(1)} %get-tuple-element.31), channel_id=1, source_target_pairs={{0,8},{8,0},{16,24},{24,16},{1,9},{9,1},{17,25},{25,17},{2,10},{10... | collective-permute-start | bytes 442376 | tf_op jit(solution)/shard_map/ppermute | solution.py:26
  56.0 0.7 shard_map.61
  57.9 1.3 %shard_map.60.kept = f32[2,128,1024]{2,1,0:T(8,128)S(1)} custom-call(bf16[256,2048]{1,0:T(8,128)(2,1)S(1)} %get-tuple-element.48.plan, bf16[2048,1024]{1,0:T(8,128)(2,1)S(1)} %copy-done, f32[2,128]{1,0:T(2,128)S(1)} %bitcast.43), custom_call_target="tpu_custom_call" | custom-call | flops 1073741824 | bytes 524288 | tf_op jit(solution)/shard_map/pallas_call | solution.py:363
  59.9 2.4 %collective-permute-start.23 = (bf16[144,512]{1,0:T(8,128)(2,1)S(1)}, bf16[144,512]{1,0:T(8,128)(2,1)S(1)}, u32[]{:S(2)}, u32[]{:S(2)}) collective-permute-start(bf16[144,512]{1,0:T(8,128)(2,1)S(1)} %get-tuple-element.37.mine), channel_id=1, source_target_pairs={{0,8},{8,0},{16,24},{24,16},{1,9},{9,1},{17,25},{25,17},{2,10},{10... | collective-permute-start | bytes 442376 | tf_op jit(solution)/shard_map/ppermute | solution.py:26
  62.5 0.7 collective-permute-done.19.upper
  63.3 1.5 %collective-permute-start.22 = (bf16[128,512]{1,0:T(8,128)(2,1)S(1)}, bf16[128,512]{1,0:T(8,128)(2,1)S(1)}, u32[]{:S(2)}, u32[]{:S(2)}) collective-permute-start(bf16[128,512]{1,0:T(8,128)(2,1)S(1)} %get-tuple-element.36.mine), channel_id=1, source_target_pairs={{0,8},{8,0},{16,24},{24,16},{1,9},{9,1},{17,25},{25,17},{2,10},{10... | collective-permute-start | bytes 393224 | tf_op jit(solution)/shard_map/ppermute | solution.py:26
  65.3 1.6 %collective-permute-done.23.theirs = bf16[144,512]{1,0:T(8,128)(2,1)S(1)} collective-permute-done((bf16[144,512]{1,0:T(8,128)(2,1)S(1)}, bf16[144,512]{1,0:T(8,128)(2,1)S(1)}, u32[]{:S(2)}, u32[]{:S(2)}) %collective-permute-start.23) | collective-permute-done | bytes 147488 | tf_op jit(solution)/shard_map/ppermute | solution.py:26
  67.1 1.3 %collective-permute-start.28 = (bf16[144,512]{1,0:T(8,128)(2,1)S(1)}, bf16[144,512]{1,0:T(8,128)(2,1)S(1)}, u32[]{:S(2)}, u32[]{:S(2)}) collective-permute-start(bf16[144,512]{1,0:T(8,128)(2,1)S(1)} %get-tuple-element.42.lower_kept), channel_id=1, source_target_pairs={{0,16},{8,24},{16,0},{24,8},{1,17},{9,25},{17,1},{25,9},{2,18},{10... | collective-permute-start | bytes 442376 | tf_op jit(solution)/shard_map/ppermute | solution.py:26
  68.4 0.6 collective-permute-done.26.theirs
  69.5 2.1 %collective-permute-start.24 = (bf16[128,512]{1,0:T(8,128)(2,1)S(1)}, bf16[128,512]{1,0:T(8,128)(2,1)S(1)}, u32[]{:S(2)}, u32[]{:S(2)}) collective-permute-start(bf16[128,512]{1,0:T(8,128)(2,1)S(1)} %shard_map.65.refs_2_), channel_id=1, source_target_pairs={{0,16},{8,24},{16,0},{24,8},{1,17},{9,25},{17,1},{25,9},{2,18},{10... | collective-permute-start | bytes 393224 | tf_op jit(solution)/shard_map/ppermute | solution.py:26
  72.1 2.5 %collective-permute-done.28.lower_sent = bf16[144,512]{1,0:T(8,128)(2,1)S(1)} collective-permute-done((bf16[144,512]{1,0:T(8,128)(2,1)S(1)}, bf16[144,512]{1,0:T(8,128)(2,1)S(1)}, u32[]{:S(2)}, u32[]{:S(2)}) %collective-permute-start.28) | collective-permute-done | bytes 147488 | tf_op jit(solution)/shard_map/ppermute | solution.py:26
  74.6 1.4 %shard_map.68 = (bf16[512,1024]{1,0:T(8,128)(2,1)}, f32[4,128]{1,0:T(4,128)}, f32[1,2048]{1,0:T(1,128)}) custom-call(bf16[144,512]{1,0:T(8,128)(2,1)S(1)} %collective-permute-done.28.lower_sent, bf16[144,512]{1,0:T(8,128)(2,1)S(1)} %collective-permute-done.29.upper_sent, bf16[144,512]{1,0:T(8,128)(2,1)S(1)} %get-tuple-element.42.lower_kept, ...), custom_call_target="tpu_custom_call" | custom-call | bytes 524288 | tf_op jit(solution)/shard_map/pallas_call | solution.py:363
  76.1 0.9 %collective-permute-done.27.refs_1_ = bf16[128,512]{1,0:T(8,128)(2,1)S(1)} collective-permute-done((bf16[128,512]{1,0:T(8,128)(2,1)S(1)}, bf16[128,512]{1,0:T(8,128)(2,1)S(1)}, u32[]{:S(2)}, u32[]{:S(2)}) %collective-permute-start.27) | collective-permute-done | bytes 131104 | tf_op jit(solution)/shard_map/ppermute | solution.py:26
  77.0 0.8 %shard_map.69 = bf16[512,1024]{1,0:T(8,128)(2,1)} custom-call(bf16[128,512]{1,0:T(8,128)(2,1)S(1)} %collective-permute-done.24.refs_0_, bf16[128,512]{1,0:T(8,128)(2,1)S(1)} %collective-permute-done.27.refs_1_, bf16[128,512]{1,0:T(8,128)(2,1)S(1)} %shard_map.65.refs_2_, bf16[128,512]{1,0:T(8,128)(2,1)S(1)} %shard_map.67.refs_3_, ...), custom_call_target="tpu_custom_call", output_to_operand_aliasing={{}: (4, {})} | custom-call | tf_op jit(solution)/shard_map/pallas_call | solution.py:93
  (69 shorter events, 11.2 us)
Async XLA Ops:
  8.1 1.4 %collective-permute-start = (f32[2048]{0:T(1024)S(1)}, f32[2048]{0:T(1024)S(1)}, u32[]{:S(2)}, u32[]{:S(2)}) collective-permute-start(f32[2048]{0:T(1024)S(1)} %log_add_fusion.5), channel_id=1, source_target_pairs={{0,1},{1,0},{2,3},{3,2},{4,5},{5,4},{6,7},{7,6},{8,9},{9,8},{10,11... | collective-permute-start | bytes 24584 | tf_op jit(solution)/shard_map/ppermute | solution.py:26
  9.5 4.6 %collective-permute-start.2 = (f32[2048]{0:T(1024)S(1)}, f32[2048]{0:T(1024)S(1)}, u32[]{:S(2)}, u32[]{:S(2)}) collective-permute-start(f32[2048]{0:T(1024)S(1)} %log_add_fusion.4), channel_id=1, source_target_pairs={{0,2},{1,7},{2,0},{3,5},{4,6},{5,3},{6,4},{7,1},{8,10},{9,15},{10,... | collective-permute-start | bytes 24584 | tf_op jit(solution)/shard_map/ppermute | solution.py:55
  12.5 3.7 %collective-permute-start.1 = (f32[2048]{0:T(1024)S(1)}, f32[2048]{0:T(1024)S(1)}, u32[]{:S(2)}, u32[]{:S(2)}) collective-permute-start(f32[2048]{0:T(1024)S(1)} %log_add_fusion.4), channel_id=1, source_target_pairs={{0,2},{1,5},{2,0},{3,7},{4,6},{5,1},{6,4},{7,3},{8,10},{9,13},{10,... | collective-permute-start | bytes 24584 | tf_op jit(solution)/shard_map/ppermute | solution.py:55
  16.2 2.6 %collective-permute-start.3 = (f32[2048]{0:T(1024)S(1)}, f32[2048]{0:T(1024)S(1)}, u32[]{:S(2)}, u32[]{:S(2)}) collective-permute-start(f32[2048]{0:T(1024)S(1)} %add_select_fusion.2), channel_id=1, source_target_pairs={{0,1},{1,0},{2,3},{3,2},{4,5},{5,4},{6,7},{7,6},{8,9},{9,8},{10,11... | collective-permute-start | bytes 24584 | tf_op jit(solution)/shard_map/ppermute | solution.py:26
  19.9 4.5 %collective-permute-start.4 = (f32[512]{0:T(512)S(1)}, f32[512]{0:T(512)S(1)}, u32[]{:S(2)}, u32[]{:S(2)}) collective-permute-start(f32[512]{0:T(512)S(1)} %log_add_fusion.9), channel_id=1, source_target_pairs={{0,24},{8,16},{16,8},{24,0},{1,25},{9,17},{17,9},{25,1},{2,26},{10... | collective-permute-start | bytes 6152 | tf_op jit(solution)/shard_map/ppermute | solution.py:26
  22.4 3.6 %collective-permute-start.5 = (f32[512]{0:T(512)S(1)}, f32[512]{0:T(512)S(1)}, u32[]{:S(2)}, u32[]{:S(2)}) collective-permute-start(f32[512]{0:T(512)S(1)} %log_add_fusion.9), channel_id=1, source_target_pairs={{0,16},{8,24},{16,0},{24,8},{1,17},{9,25},{17,1},{25,9},{2,18},{10... | collective-permute-start | bytes 6152 | tf_op jit(solution)/shard_map/ppermute | solution.py:26
  22.9 3.6 %collective-permute-start.6 = (f32[512]{0:T(512)S(1)}, f32[512]{0:T(512)S(1)}, u32[]{:S(2)}, u32[]{:S(2)}) collective-permute-start(f32[512]{0:T(512)S(1)} %log_add_fusion.9), channel_id=1, source_target_pairs={{0,8},{8,0},{16,24},{24,16},{1,9},{9,1},{17,25},{25,17},{2,10},{10... | collective-permute-start | bytes 6152 | tf_op jit(solution)/shard_map/ppermute | solution.py:26
  27.7 1.2 %collective-permute-start.7 = (f32[2048]{0:T(1024)S(1)}, f32[2048]{0:T(1024)S(1)}, u32[]{:S(2)}, u32[]{:S(2)}) collective-permute-start(f32[2048]{0:T(1024)S(1)} %log_add_fusion.3), channel_id=1, source_target_pairs={{0,1},{1,0},{2,3},{3,2},{4,5},{5,4},{6,7},{7,6},{8,9},{9,8},{10,11... | collective-permute-start | bytes 24584 | tf_op jit(solution)/shard_map/ppermute | solution.py:26
  29.0 3.7 %collective-permute-start.9 = (f32[2048]{0:T(1024)S(1)}, f32[2048]{0:T(1024)S(1)}, u32[]{:S(2)}, u32[]{:S(2)}) collective-permute-start(f32[2048]{0:T(1024)S(1)} %log_add_fusion.2), channel_id=1, source_target_pairs={{0,2},{1,7},{2,0},{3,5},{4,6},{5,3},{6,4},{7,1},{8,10},{9,15},{10,... | collective-permute-start | bytes 24584 | tf_op jit(solution)/shard_map/ppermute | solution.py:55
  29.1 3.7 %collective-permute-start.8 = (f32[2048]{0:T(1024)S(1)}, f32[2048]{0:T(1024)S(1)}, u32[]{:S(2)}, u32[]{:S(2)}) collective-permute-start(f32[2048]{0:T(1024)S(1)} %log_add_fusion.2), channel_id=1, source_target_pairs={{0,2},{1,5},{2,0},{3,7},{4,6},{5,1},{6,4},{7,3},{8,10},{9,13},{10,... | collective-permute-start | bytes 24584 | tf_op jit(solution)/shard_map/ppermute | solution.py:55
  32.8 1.8 %collective-permute-start.10 = (f32[2048]{0:T(1024)S(1)}, f32[2048]{0:T(1024)S(1)}, u32[]{:S(2)}, u32[]{:S(2)}) collective-permute-start(f32[2048]{0:T(1024)S(1)} %add_select_fusion.1), channel_id=1, source_target_pairs={{0,1},{1,0},{2,3},{3,2},{4,5},{5,4},{6,7},{7,6},{8,9},{9,8},{10,11... | collective-permute-start | bytes 24584 | tf_op jit(solution)/shard_map/ppermute | solution.py:26
  34.6 6.3 %copy-start = (bf16[2048,1024]{1,0:T(8,128)(2,1)S(1)}, bf16[2048,1024]{1,0:T(8,128)(2,1)}, u32[]{:S(2)}) copy-start(bf16[2048,1024]{1,0:T(8,128)(2,1)} %embeddings.3) | copy-start | bytes 12582916
  35.8 4.5 %collective-permute-start.11 = (f32[512]{0:T(512)S(1)}, f32[512]{0:T(512)S(1)}, u32[]{:S(2)}, u32[]{:S(2)}) collective-permute-start(f32[512]{0:T(512)S(1)} %log_add_fusion.7), channel_id=1, source_target_pairs={{0,24},{8,16},{16,8},{24,0},{1,25},{9,17},{17,9},{25,1},{2,26},{10... | collective-permute-start | bytes 6152 | tf_op jit(solution)/shard_map/ppermute | solution.py:26
  37.4 3.6 %collective-permute-start.12 = (f32[512]{0:T(512)S(1)}, f32[512]{0:T(512)S(1)}, u32[]{:S(2)}, u32[]{:S(2)}) collective-permute-start(f32[512]{0:T(512)S(1)} %log_add_fusion.7), channel_id=1, source_target_pairs={{0,16},{8,24},{16,0},{24,8},{1,17},{9,25},{17,1},{25,9},{2,18},{10... | collective-permute-start | bytes 6152 | tf_op jit(solution)/shard_map/ppermute | solution.py:26
  37.9 3.6 %collective-permute-start.13 = (f32[512]{0:T(512)S(1)}, f32[512]{0:T(512)S(1)}, u32[]{:S(2)}, u32[]{:S(2)}) collective-permute-start(f32[512]{0:T(512)S(1)} %log_add_fusion.7), channel_id=1, source_target_pairs={{0,8},{8,0},{16,24},{24,16},{1,9},{9,1},{17,25},{25,17},{2,10},{10... | collective-permute-start | bytes 6152 | tf_op jit(solution)/shard_map/ppermute | solution.py:26
  42.7 1.2 %collective-permute-start.14 = (f32[2048]{0:T(1024)S(1)}, f32[2048]{0:T(1024)S(1)}, u32[]{:S(2)}, u32[]{:S(2)}) collective-permute-start(f32[2048]{0:T(1024)S(1)} %log_add_fusion.1), channel_id=1, source_target_pairs={{0,1},{1,0},{2,3},{3,2},{4,5},{5,4},{6,7},{7,6},{8,9},{9,8},{10,11... | collective-permute-start | bytes 24584 | tf_op jit(solution)/shard_map/ppermute | solution.py:26
  43.9 3.7 %collective-permute-start.16 = (f32[2048]{0:T(1024)S(1)}, f32[2048]{0:T(1024)S(1)}, u32[]{:S(2)}, u32[]{:S(2)}) collective-permute-start(f32[2048]{0:T(1024)S(1)} %log_add_fusion), channel_id=1, source_target_pairs={{0,2},{1,7},{2,0},{3,5},{4,6},{5,3},{6,4},{7,1},{8,10},{9,15},{10,... | collective-permute-start | bytes 24584 | tf_op jit(solution)/shard_map/ppermute | solution.py:55
  45.4 3.7 %collective-permute-start.15 = (f32[2048]{0:T(1024)S(1)}, f32[2048]{0:T(1024)S(1)}, u32[]{:S(2)}, u32[]{:S(2)}) collective-permute-start(f32[2048]{0:T(1024)S(1)} %log_add_fusion), channel_id=1, source_target_pairs={{0,2},{1,5},{2,0},{3,7},{4,6},{5,1},{6,4},{7,3},{8,10},{9,13},{10,... | collective-permute-start | bytes 24584 | tf_op jit(solution)/shard_map/ppermute | solution.py:55
  49.1 1.6 %collective-permute-start.17 = (f32[2048]{0:T(1024)S(1)}, f32[2048]{0:T(1024)S(1)}, u32[]{:S(2)}, u32[]{:S(2)}) collective-permute-start(f32[2048]{0:T(1024)S(1)} %add_select_fusion), channel_id=1, source_target_pairs={{0,1},{1,0},{2,3},{3,2},{4,5},{5,4},{6,7},{7,6},{8,9},{9,8},{10,11... | collective-permute-start | bytes 24584 | tf_op jit(solution)/shard_map/ppermute | solution.py:26
  52.2 7.0 %collective-permute-start.20 = (bf16[144,512]{1,0:T(8,128)(2,1)S(1)}, bf16[144,512]{1,0:T(8,128)(2,1)S(1)}, u32[]{:S(2)}, u32[]{:S(2)}) collective-permute-start(bf16[144,512]{1,0:T(8,128)(2,1)S(1)} %get-tuple-element.30), channel_id=1, source_target_pairs={{0,16},{8,24},{16,0},{24,8},{1,17},{9,25},{17,1},{25,9},{2,18},{10... | collective-permute-start | bytes 442376 | tf_op jit(solution)/shard_map/ppermute | solution.py:26
  53.8 5.9 %collective-permute-start.21 = (bf16[144,512]{1,0:T(8,128)(2,1)S(1)}, bf16[144,512]{1,0:T(8,128)(2,1)S(1)}, u32[]{:S(2)}, u32[]{:S(2)}) collective-permute-start(bf16[144,512]{1,0:T(8,128)(2,1)S(1)} %get-tuple-element.31), channel_id=1, source_target_pairs={{0,8},{8,0},{16,24},{24,16},{1,9},{9,1},{17,25},{25,17},{2,10},{10... | collective-permute-start | bytes 442376 | tf_op jit(solution)/shard_map/ppermute | solution.py:26
  56.8 5.7 %collective-permute-start.18 = (bf16[128,512]{1,0:T(8,128)(2,1)S(1)}, bf16[128,512]{1,0:T(8,128)(2,1)S(1)}, u32[]{:S(2)}, u32[]{:S(2)}) collective-permute-start(bf16[128,512]{1,0:T(8,128)(2,1)S(1)} %get-tuple-element.33), channel_id=1, source_target_pairs={{0,16},{8,24},{16,0},{24,8},{1,17},{9,25},{17,1},{25,9},{2,18},{10... | collective-permute-start | bytes 393224 | tf_op jit(solution)/shard_map/ppermute | solution.py:26
  57.3 5.8 %collective-permute-start.19 = (bf16[128,512]{1,0:T(8,128)(2,1)S(1)}, bf16[128,512]{1,0:T(8,128)(2,1)S(1)}, u32[]{:S(2)}, u32[]{:S(2)}) collective-permute-start(bf16[128,512]{1,0:T(8,128)(2,1)S(1)} %get-tuple-element.34), channel_id=1, source_target_pairs={{0,8},{8,0},{16,24},{24,16},{1,9},{9,1},{17,25},{25,17},{2,10},{10... | collective-permute-start | bytes 393224 | tf_op jit(solution)/shard_map/ppermute | solution.py:26
  59.9 7.0 %collective-permute-start.23 = (bf16[144,512]{1,0:T(8,128)(2,1)S(1)}, bf16[144,512]{1,0:T(8,128)(2,1)S(1)}, u32[]{:S(2)}, u32[]{:S(2)}) collective-permute-start(bf16[144,512]{1,0:T(8,128)(2,1)S(1)} %get-tuple-element.37.mine), channel_id=1, source_target_pairs={{0,8},{8,0},{16,24},{24,16},{1,9},{9,1},{17,25},{25,17},{2,10},{10... | collective-permute-start | bytes 442376 | tf_op jit(solution)/shard_map/ppermute | solution.py:26
  62.2 6.7 %collective-permute-start.26 = (bf16[144,512]{1,0:T(8,128)(2,1)S(1)}, bf16[144,512]{1,0:T(8,128)(2,1)S(1)}, u32[]{:S(2)}, u32[]{:S(2)}) collective-permute-start(bf16[144,512]{1,0:T(8,128)(2,1)S(1)} %get-tuple-element.40.mine), channel_id=1, source_target_pairs={{0,16},{8,24},{16,0},{24,8},{1,17},{9,25},{17,1},{25,9},{2,18},{10... | collective-permute-start | bytes 442376 | tf_op jit(solution)/shard_map/ppermute | solution.py:26
  63.3 6.0 %collective-permute-start.22 = (bf16[128,512]{1,0:T(8,128)(2,1)S(1)}, bf16[128,512]{1,0:T(8,128)(2,1)S(1)}, u32[]{:S(2)}, u32[]{:S(2)}) collective-permute-start(bf16[128,512]{1,0:T(8,128)(2,1)S(1)} %get-tuple-element.36.mine), channel_id=1, source_target_pairs={{0,8},{8,0},{16,24},{24,16},{1,9},{9,1},{17,25},{25,17},{2,10},{10... | collective-permute-start | bytes 393224 | tf_op jit(solution)/shard_map/ppermute | solution.py:26
  64.8 7.0 %collective-permute-start.25 = (bf16[128,512]{1,0:T(8,128)(2,1)S(1)}, bf16[128,512]{1,0:T(8,128)(2,1)S(1)}, u32[]{:S(2)}, u32[]{:S(2)}) collective-permute-start(bf16[128,512]{1,0:T(8,128)(2,1)S(1)} %get-tuple-element.39.mine), channel_id=1, source_target_pairs={{0,16},{8,24},{16,0},{24,8},{1,17},{9,25},{17,1},{25,9},{2,18},{10... | collective-permute-start | bytes 393224 | tf_op jit(solution)/shard_map/ppermute | solution.py:26
  67.1 7.5 %collective-permute-start.28 = (bf16[144,512]{1,0:T(8,128)(2,1)S(1)}, bf16[144,512]{1,0:T(8,128)(2,1)S(1)}, u32[]{:S(2)}, u32[]{:S(2)}) collective-permute-start(bf16[144,512]{1,0:T(8,128)(2,1)S(1)} %get-tuple-element.42.lower_kept), channel_id=1, source_target_pairs={{0,16},{8,24},{16,0},{24,8},{1,17},{9,25},{17,1},{25,9},{2,18},{10... | collective-permute-start | bytes 442376 | tf_op jit(solution)/shard_map/ppermute | solution.py:26
  69.1 5.5 %collective-permute-start.29 = (bf16[144,512]{1,0:T(8,128)(2,1)S(1)}, bf16[144,512]{1,0:T(8,128)(2,1)S(1)}, u32[]{:S(2)}, u32[]{:S(2)}) collective-permute-start(bf16[144,512]{1,0:T(8,128)(2,1)S(1)} %get-tuple-element.43.upper_kept), channel_id=1, source_target_pairs={{0,8},{8,0},{16,24},{24,16},{1,9},{9,1},{17,25},{25,17},{2,10},{10... | collective-permute-start | bytes 442376 | tf_op jit(solution)/shard_map/ppermute | solution.py:26
  69.5 6.6 %collective-permute-start.24 = (bf16[128,512]{1,0:T(8,128)(2,1)S(1)}, bf16[128,512]{1,0:T(8,128)(2,1)S(1)}, u32[]{:S(2)}, u32[]{:S(2)}) collective-permute-start(bf16[128,512]{1,0:T(8,128)(2,1)S(1)} %shard_map.65.refs_2_), channel_id=1, source_target_pairs={{0,16},{8,24},{16,0},{24,8},{1,17},{9,25},{17,1},{25,9},{2,18},{10... | collective-permute-start | bytes 393224 | tf_op jit(solution)/shard_map/ppermute | solution.py:26
  71.9 5.0 %collective-permute-start.27 = (bf16[128,512]{1,0:T(8,128)(2,1)S(1)}, bf16[128,512]{1,0:T(8,128)(2,1)S(1)}, u32[]{:S(2)}, u32[]{:S(2)}) collective-permute-start(bf16[128,512]{1,0:T(8,128)(2,1)S(1)} %shard_map.67.refs_3_), channel_id=1, source_target_pairs={{0,8},{8,0},{16,24},{24,16},{1,9},{9,1},{17,25},{25,17},{2,10},{10... | collective-permute-start | bytes 393224 | tf_op jit(solution)/shard_map/ppermute | solution.py:26
